TPU v7x, 32 devices: a whole 2x2x4 slice. The times are simulated.
32 devices in a mesh: gx: 8 (over y, x, core), gy: 4 (over z).
Axes of the slice: x: 2, y: 2, z: 4, core: 2. Of those that a mesh axis runs over, the one named last changes fastest.
Arguments:
- start: float32 [16, 4, 1024], P('gx', 'gy'), may hold values from -6 to 6
- source: float32 [16, 4, 1024], P('gx', 'gy'), may hold values from -4 to 4
- diag_inverse: bfloat16 [16, 4, 16, 4096], P('gx', 'gy'), may hold values from -0.75 to 0.75
- x_lower: bfloat16 [16, 4, 16, 4096], P('gx', 'gy'), may hold values from -1 to 1
- x_upper: bfloat16 [16, 4, 16, 4096], P('gx', 'gy'), may hold values from -1 to 1
- side_blocks: bfloat16 [4, 16, 4, 16, 4096], P(None, 'gx', 'gy'), may hold values from -0.25 to 0.25
Outputs:
- forward: float32 [16, 4, 1024], P('gx', 'gy')
- result: float32 [16, 4, 1024], P('gx', 'gy')
All inputs are finite; a program needn't handle non-finite values.
Results may differ from a plain program's by a relative error of at most 0.0003.
Values sent between devices are 32-bit elements; how exact they have to be, the bound alone decides.
No kernel may reach another device: no remote copies, remote signals or barrier semaphores. Data moves between devices by JAX's collectives and lax.ppermute only.
A program may use at most 64 MiB of HBM per device.

v0:
```python
import jax
import jax.numpy as jnp
from jax import lax
from jax.sharding import PartitionSpec as P


def padded(block, sides, width):
    for axis, dim in sides:
        count = lax.axis_size(axis)
        forward = [(i, i + 1) for i in range(count - 1)]
        backward = [(target, source) for source, target in forward]
        low = lax.ppermute(
            lax.slice_in_dim(block, block.shape[dim] - width, None, axis=dim), axis, forward
        )
        high = lax.ppermute(lax.slice_in_dim(block, 0, width, axis=dim), axis, backward)
        block = jnp.concatenate([low, block, high], axis=dim)
    return block


def from_behind(block, axis, distance):
    devices = range(lax.axis_size(axis))
    route = [(i - distance, i) for i in devices if i - distance in devices]
    return lax.ppermute(block, axis, route)


def prefix_2(part, axis, combine, identity, reverse):
    count = lax.axis_size(axis)
    place = lax.axis_index(axis)
    ahead = count - 1 - place if reverse else place
    gathered = jax.tree.map(lambda a: lax.all_gather(a, axis), part)
    state = jax.tree.map(lambda a, e: jnp.zeros_like(a) + jnp.asarray(e, a.dtype), part, identity)

    def one(hop, state):
        source = count - 1 - hop if reverse else hop
        return combine(
            state, jax.tree.map(lambda a: lax.dynamic_index_in_dim(a, source, 0, False), gathered)
        )

    return lax.fori_loop(0, ahead, one, state)


def apply_block(block, column_values):
    lead = column_values.shape[:-1]
    depth = block.shape[-2]
    width = column_values.shape[-1] // depth
    matrix = block.astype(jnp.float32).reshape(lead + (depth, width, width))
    column = column_values.reshape(lead + (depth, width))
    product = jnp.einsum("...zab,...zb->...za", matrix, column, precision=lax.Precision.HIGHEST)
    return product.reshape(lead + (depth * width,))


def z_terms(side_blocks, column_values, depth):
    width = column_values.shape[-1] // depth
    cells = column_values.reshape(column_values.shape[:-1] + (depth, width))
    zero = jnp.zeros_like(cells[..., :1, :])
    below = jnp.concatenate([zero, cells[..., :-1, :]], -2).reshape(column_values.shape)
    above = jnp.concatenate([cells[..., 1:, :], zero], -2).reshape(column_values.shape)
    return apply_block(side_blocks[2], below) + apply_block(side_blocks[3], above)


def multiply_maps(later, earlier, depth):
    rows = later.shape[0]
    width = later.shape[-1]
    species = int(width**0.5 + 0.5)
    left = later.astype(jnp.float32).reshape(rows, depth, species, species)
    right = earlier.astype(jnp.float32).reshape(rows, depth, species, species)
    joined = jnp.einsum("yzab,yzbc->yzac", left, right, precision=lax.Precision.HIGHEST)
    return joined.reshape(rows, depth, width)


def compose_planes(drive, blocks, depth, order):
    first = order[0]
    product = blocks[first].astype(jnp.float32)
    offset = drive[first]
    for plane in order[1:]:
        offset = drive[plane] - apply_block(blocks[plane], offset)
        product = multiply_maps(blocks[plane], product, depth)
    return (product, offset)


def run_planes(drive, blocks, entering, order):
    planes = [None] * drive.shape[0]
    previous = entering
    for plane in order:
        previous = drive[plane] - apply_block(blocks[plane], previous)
        planes[plane] = previous
    return jnp.stack(planes, 0)


def make_combine(depth):

    def combine(earlier, later):
        matrix = multiply_maps(later[0], earlier[0], depth)
        offset = later[1] + apply_block(later[0], earlier[1])
        return (matrix, offset)

    return combine


def neutral_map(rows, depth, species):
    unit_matrix = jnp.eye(species, dtype=jnp.float32).reshape(1, 1, species * species)
    matrix = jnp.broadcast_to(unit_matrix, (rows, depth, species * species))
    return (matrix, jnp.zeros((rows, depth * species), jnp.float32))


def local(start, source, diag_inverse, x_lower, x_upper, side_blocks):
    depth = x_lower.shape[2]
    rows = start.shape[1]
    planes_here = start.shape[0]
    species = start.shape[2] // depth
    upward = list(range(planes_here))
    downward = upward[::-1]
    combine = make_combine(depth)
    rhs = apply_block(diag_inverse, source)
    sideways = padded(start, (("gy", 1),), 1)
    ahead_plane = from_behind(start[:1], "gx", -1)
    ahead = jnp.concatenate([start[1:], ahead_plane], 0)
    lateral_start = (
        apply_block(side_blocks[0], sideways[:, :-2])
        + apply_block(side_blocks[1], sideways[:, 2:])
        + z_terms(side_blocks, start, depth)
    )
    drive_f = rhs - lateral_start - apply_block(x_upper, ahead)
    prefix = prefix_2(
        compose_planes(drive_f, x_lower, depth, upward),
        "gx",
        combine,
        neutral_map(rows, depth, species),
        False,
    )
    entering = prefix[1]
    forward = run_planes(drive_f, x_lower, entering, upward)
    widened = padded(forward, (("gy", 1),), 1)
    lateral_forward = (
        apply_block(side_blocks[0], widened[:, :-2])
        + apply_block(side_blocks[1], widened[:, 2:])
        + z_terms(side_blocks, forward, depth)
    )
    behind = jnp.concatenate([entering[None], forward[:-1]], 0)
    drive_b = rhs - lateral_forward - apply_block(x_lower, behind)
    suffix = prefix_2(
        compose_planes(drive_b, x_upper, depth, downward),
        "gx",
        combine,
        neutral_map(rows, depth, species),
        True,
    )
    arriving = suffix[1]
    result = run_planes(drive_b, x_upper, arriving, downward)
    return (forward, result)


def solution(mesh):
    return jax.shard_map(
        local,
        mesh=mesh,
        in_specs=(
            P("gx", "gy", None),
            P("gx", "gy", None),
            P("gx", "gy", None, None),
            P("gx", "gy", None, None),
            P("gx", "gy", None, None),
            P(None, "gx", "gy", None, None),
        ),
        out_specs=(P("gx", "gy", None), P("gx", "gy", None)),
        check_vma=False,
    )
```

profile of v0, /device:TPU:0, one launch (start us, length us, event | category | flops | bytes accessed | tf_op | source)
XLA Modules:
  0.0 128.5 jit_solution(14116739516541403468)
XLA Ops:
  7.2 1.0 fusion.4
  10.0 4.9 %collective-permute-start = (f32[2,1,1024]{2,1,0:T(1,128)S(1)}, f32[2,1,1024]{2,1,0:T(1,128)S(1)}, u32[]{:S(2)}, u32[]{:S(2)}) collective-permute-start(f32[2,1,1024]{2,1,0:T(1,128)S(1)} %copy-done.6), channel_id=1, source_target_pairs={{0,1},{1,2},{2,3},{4,5},{5,6},{6,7},{8,9},{9,10},{10,11},{12,13},{... | collective-permute-start | bytes 24584 | tf_op jit(solution)/shard_map/ppermute | solution.py:12
  14.9 1.3 %collective-permute-start.1 = (f32[2,1,1024]{2,1,0:T(1,128)S(1)}, f32[2,1,1024]{2,1,0:T(1,128)S(1)}, u32[]{:S(2)}, u32[]{:S(2)}) collective-permute-start(f32[2,1,1024]{2,1,0:T(1,128)S(1)} %copy-done.6), channel_id=1, source_target_pairs={{1,0},{2,1},{3,2},{5,4},{6,5},{7,6},{9,8},{10,9},{11,10},{13,12},{... | collective-permute-start | bytes 24584 | tf_op jit(solution)/shard_map/ppermute | solution.py:15
  16.2 1.3 %collective-permute-start.2 = (f32[1,1,1024]{2,1,0:T(1,128)S(1)}, f32[1,1,1024]{2,1,0:T(1,128)S(1)}, u32[]{:S(2)}, u32[]{:S(2)}) collective-permute-start(f32[1,1,1024]{2,1,0:T(1,128)S(1)} %get-tuple-element.173), channel_id=1, source_target_pairs={{4,0},{8,4},{12,8},{16,12},{20,16},{24,20},{28,24},{5,1},{9,5},{13... | collective-permute-start | bytes 12296 | tf_op jit(solution)/shard_map/ppermute | solution.py:23
  20.0 1.3 %reshape.541 = bf16[2,16,64,64]{3,2,1,0:T(8,128)(2,1)} reshape(bf16[1,2,1,16,4096]{4,3,2,1,0:T(8,128)(2,1)S(1)} %get-tuple-element.158) | data formatting | bytes 524288 | tf_op jit(solution)/shard_map/reshape.26
  21.3 1.5 %reshape.531 = bf16[2,16,64,64]{3,2,1,0:T(8,128)(2,1)S(1)} reshape(bf16[2,1,16,4096]{3,2,1,0:T(8,128)(2,1)} %param.12) | data formatting | bytes 524288 | tf_op jit(solution)/shard_map/reshape.6
  23.8 2.0 %fusion.16 = f32[2,16,1,64]{3,2,1,0:T(1,128)S(1)} fusion(f32[2,16,64,1]{2,3,1,0:T(1,128)S(1)} %bitcast.210, bf16[2,16,64,64]{3,2,1,0:T(8,128)(2,1)} %reshape.541), kind=kOutput, calls=%fused_computation.30 | convolution fusion | flops 1572864 | bytes 278528 | tf_op jit(solution)/shard_map/...zab,...zb->...za/dot_general | solution.py:48
  26.7 1.4 %reshape.543 = bf16[2,16,64,64]{3,2,1,0:T(8,128)(2,1)} reshape(bf16[2,1,16,4096]{3,2,1,0:T(8,128)(2,1)S(1)} %copy-done) | data formatting | bytes 524288 | tf_op jit(solution)/shard_map/reshape.36
  28.1 1.4 %reshape.556 = bf16[2,16,64,64]{3,2,1,0:T(8,128)(2,1)} reshape(bf16[2,1,16,4096]{3,2,1,0:T(8,128)(2,1)S(1)} %copy-done.1) | data formatting | bytes 524288 | tf_op jit(solution)/shard_map/reshape.137
  30.7 2.2 %fusion.17 = f32[2,16,1,64]{3,2,1,0:T(1,128)S(1)} fusion(f32[2,16,64,1]{2,3,1,0:T(1,128)S(1)} %bitcast.205, bf16[2,16,64,64]{3,2,1,0:T(8,128)(2,1)} %reshape.543), kind=kOutput, calls=%fused_computation.31 | convolution fusion | flops 1572864 | bytes 278528 | tf_op jit(solution)/shard_map/...zab,...zb->...za/dot_general | solution.py:48
  34.1 0.9 fusion.14
  35.8 10.1 %all_gather.14 = f32[8,1,1024]{2,1,0:T(1,128)S(1)} all-gather(f32[1,1,1024]{2,1,0:T(1,128)S(1)} %sub.104), channel_id=1, replica_groups=mesh['gx'=8,'gy'=4] {'gx'}, dimensions={0}, use_global_device_ids=true | all-gather | bytes 36864 | tf_op jit(solution)/shard_map/all_gather | solution.py:30
  49.1 1.3 %collective-permute-start.4 = (f32[2,1,1024]{2,1,0:T(1,128)S(1)}, f32[2,1,1024]{2,1,0:T(1,128)S(1)}, u32[]{:S(2)}, u32[]{:S(2)}) collective-permute-start(f32[2,1,1024]{2,1,0:T(1,128)S(1)} %pad_maximum_fusion.1), channel_id=1, source_target_pairs={{1,0},{2,1},{3,2},{5,4},{6,5},{7,6},{9,8},{10,9},{11,10},{13,12},{... | collective-permute-start | bytes 24584 | tf_op jit(solution)/shard_map/ppermute | solution.py:15
  50.4 5.1 %collective-permute-start.3 = (f32[2,1,1024]{2,1,0:T(1,128)S(1)}, f32[2,1,1024]{2,1,0:T(1,128)S(1)}, u32[]{:S(2)}, u32[]{:S(2)}) collective-permute-start(f32[2,1,1024]{2,1,0:T(1,128)S(1)} %pad_maximum_fusion.1), channel_id=1, source_target_pairs={{0,1},{1,2},{2,3},{4,5},{5,6},{6,7},{8,9},{9,10},{10,11},{12,13},{... | collective-permute-start | bytes 24584 | tf_op jit(solution)/shard_map/ppermute | solution.py:12
  55.8 0.9 fusion.25
  56.7 0.9 fusion.24
  57.6 1.9 %fusion.26 = f32[2,16,1,64]{3,2,1,0:T(1,128)S(1)} fusion(f32[2,16,64,1]{2,3,1,0:T(1,128)S(1)} %bitcast.206, bf16[2,16,64,64]{3,2,1,0:T(8,128)(2,1)} %reshape.556), kind=kOutput, calls=%fused_computation.40 | convolution fusion | flops 1572864 | bytes 278528 | tf_op jit(solution)/shard_map/...zab,...zb->...za/dot_general | solution.py:48
  60.8 0.9 fusion.22
  62.4 32.2 %all_gather.16 = f32[8,1,1024]{2,1,0:T(1,128)S(1)} all-gather(f32[1,1,1024]{2,1,0:T(1,128)S(1)} %sub.111), channel_id=1, replica_groups=mesh['gx'=8,'gy'=4] {'gx'}, dimensions={0}, use_global_device_ids=true | all-gather | bytes 36864 | tf_op jit(solution)/shard_map/all_gather | solution.py:30
  94.6 24.4 %while.27 = (s32[]{:T(128)}, f32[1,1024]{1,0:T(1,128)S(1)}, s32[]{:T(128)}, f32[8,1,1024]{2,1,0:T(1,128)S(1)}, f32[8,1,16,4096]{3,2,1,0:T(8,128)}, /*index=5*/s3...) while((s32[]{:T(128)}, f32[1,1024]{1,0:T(1,128)S(1)}, s32[]{:T(128)}, f32[8,1,1024]{2,1,0:T(1,128)S(1)}, ...), condition=%wide.region_3.4_spmd, body=%wide.region_2.3_spmd.sunk | while | flops 787462 | bytes 1355943 | solution.py:39
  94.6 1.0 constant_dynamic-slice_fusion.5
  97.1 0.9 fusion.84
  98.1 1.0 constant_dynamic-slice_fusion.5
  100.5 0.9 fusion.84
  101.6 1.0 constant_dynamic-slice_fusion.5
  104.0 0.9 fusion.84
  105.1 1.0 constant_dynamic-slice_fusion.5
  107.5 0.9 fusion.84
  108.5 1.0 constant_dynamic-slice_fusion.5
  111.0 0.9 fusion.84
  112.0 1.0 constant_dynamic-slice_fusion.5
  115.5 1.0 constant_dynamic-slice_fusion.5
  (154 shorter events, 29.7 us)
Async XLA Ops:
  7.2 2.8 %copy-start.6 = (f32[2,1,1024]{2,1,0:T(1,128)S(1)}, f32[2,1,1024]{2,1,0:T(1,128)}, u32[]{:S(2)}) copy-start(f32[2,1,1024]{2,1,0:T(1,128)} %param.10) | copy-start | bytes 24580
  7.2 10.3 %copy-start = (bf16[2,1,16,4096]{3,2,1,0:T(8,128)(2,1)S(1)}, bf16[2,1,16,4096]{3,2,1,0:T(8,128)(2,1)}, u32[]{:S(2)}) copy-start(bf16[2,1,16,4096]{3,2,1,0:T(8,128)(2,1)} %param.14) | copy-start | bytes 786436
  7.2 38.7 %all-gather.3.cloned.1.call-start = ((), (), s32[]{:S(2)}) async-start(), calls=%async_computation | async-start | bytes 2359296 | tf_op jit(solution)/shard_map/all_gather | solution.py:30
  9.0 10.2 %copy-start.2 = (bf16[4,2,1,16,4096]{4,3,2,1,0:T(8,128)(2,1)S(1)}, bf16[4,2,1,16,4096]{4,3,2,1,0:T(8,128)(2,1)}, u32[]{:S(2)}) copy-start(bf16[4,2,1,16,4096]{4,3,2,1,0:T(8,128)(2,1)} %param.15) | copy-start | bytes 3145732
  9.9 84.7 %all-gather.5.cloned.1.call-start = ((), (), s32[]{:S(2)}) async-start(), calls=%async_computation.1 | async-start | bytes 2359296 | tf_op jit(solution)/shard_map/all_gather | solution.py:30
  10.0 22.9 %collective-permute-start = (f32[2,1,1024]{2,1,0:T(1,128)S(1)}, f32[2,1,1024]{2,1,0:T(1,128)S(1)}, u32[]{:S(2)}, u32[]{:S(2)}) collective-permute-start(f32[2,1,1024]{2,1,0:T(1,128)S(1)} %copy-done.6), channel_id=1, source_target_pairs={{0,1},{1,2},{2,3},{4,5},{5,6},{6,7},{8,9},{9,10},{10,11},{12,13},{... | collective-permute-start | bytes 24584 | tf_op jit(solution)/shard_map/ppermute | solution.py:12
  14.9 18.1 %collective-permute-start.1 = (f32[2,1,1024]{2,1,0:T(1,128)S(1)}, f32[2,1,1024]{2,1,0:T(1,128)S(1)}, u32[]{:S(2)}, u32[]{:S(2)}) collective-permute-start(f32[2,1,1024]{2,1,0:T(1,128)S(1)} %copy-done.6), channel_id=1, source_target_pairs={{1,0},{2,1},{3,2},{5,4},{6,5},{7,6},{9,8},{10,9},{11,10},{13,12},{... | collective-permute-start | bytes 24584 | tf_op jit(solution)/shard_map/ppermute | solution.py:15
  16.2 14.4 %collective-permute-start.2 = (f32[1,1,1024]{2,1,0:T(1,128)S(1)}, f32[1,1,1024]{2,1,0:T(1,128)S(1)}, u32[]{:S(2)}, u32[]{:S(2)}) collective-permute-start(f32[1,1,1024]{2,1,0:T(1,128)S(1)} %get-tuple-element.173), channel_id=1, source_target_pairs={{4,0},{8,4},{12,8},{16,12},{20,16},{24,20},{28,24},{5,1},{9,5},{13... | collective-permute-start | bytes 12296 | tf_op jit(solution)/shard_map/ppermute | solution.py:23
  19.2 3.6 %copy-start.7 = (f32[2,1,1024]{2,1,0:T(1,128)S(1)}, f32[2,1,1024]{2,1,0:T(1,128)}, u32[]{:S(2)}) copy-start(f32[2,1,1024]{2,1,0:T(1,128)} %param.11) | copy-start | bytes 24580
  20.0 8.1 %copy-start.1 = (bf16[2,1,16,4096]{3,2,1,0:T(8,128)(2,1)S(1)}, bf16[2,1,16,4096]{3,2,1,0:T(8,128)(2,1)}, u32[]{:S(2)}) copy-start(bf16[2,1,16,4096]{3,2,1,0:T(8,128)(2,1)} %param.13) | copy-start | bytes 786436
  30.5 15.4 %copy-start.4 = (bf16[2,16,64,64]{3,2,1,0:T(8,128)(2,1)}, bf16[2,16,64,64]{3,2,1,0:T(8,128)(2,1)S(1)}, u32[]{:S(2)}) copy-start(bf16[2,16,64,64]{3,2,1,0:T(8,128)(2,1)S(1)} %reshape.535) | copy-start | bytes 786436
  45.9 9.9 %copy-start.3 = (bf16[2,16,64,64]{3,2,1,0:T(8,128)(2,1)S(1)}, bf16[2,16,64,64]{3,2,1,0:T(8,128)(2,1)}, u32[]{:S(2)}) copy-start(bf16[2,16,64,64]{3,2,1,0:T(8,128)(2,1)} %reshape.541) | copy-start | bytes 786436
  45.9 13.9 %copy-start.5 = (bf16[2,16,64,64]{3,2,1,0:T(8,128)(2,1)S(1)}, bf16[2,16,64,64]{3,2,1,0:T(8,128)(2,1)}, u32[]{:S(2)}) copy-start(bf16[2,16,64,64]{3,2,1,0:T(8,128)(2,1)} %copy-done.4) | copy-start | bytes 786436
  49.1 45.5 %copy-start.8 = (f32[2,1,1024]{2,1,0:T(1,128)}, f32[2,1,1024]{2,1,0:T(1,128)S(1)}, u32[]{:S(2)}) copy-start(f32[2,1,1024]{2,1,0:T(1,128)S(1)} %pad_maximum_fusion.1) | copy-start | bytes 24580
  49.1 10.5 %collective-permute-start.4 = (f32[2,1,1024]{2,1,0:T(1,128)S(1)}, f32[2,1,1024]{2,1,0:T(1,128)S(1)}, u32[]{:S(2)}, u32[]{:S(2)}) collective-permute-start(f32[2,1,1024]{2,1,0:T(1,128)S(1)} %pad_maximum_fusion.1), channel_id=1, source_target_pairs={{1,0},{2,1},{3,2},{5,4},{6,5},{7,6},{9,8},{10,9},{11,10},{13,12},{... | collective-permute-start | bytes 24584 | tf_op jit(solution)/shard_map/ppermute | solution.py:15
  50.4 9.3 %collective-permute-start.3 = (f32[2,1,1024]{2,1,0:T(1,128)S(1)}, f32[2,1,1024]{2,1,0:T(1,128)S(1)}, u32[]{:S(2)}, u32[]{:S(2)}) collective-permute-start(f32[2,1,1024]{2,1,0:T(1,128)S(1)} %pad_maximum_fusion.1), channel_id=1, source_target_pairs={{0,1},{1,2},{2,3},{4,5},{5,6},{6,7},{8,9},{9,10},{10,11},{12,13},{... | collective-permute-start | bytes 24584 | tf_op jit(solution)/shard_map/ppermute | solution.py:12
Sparse Core Ops, SparseCore 0:
  10.0 30.5 all-gather.2
  42.5 27.8 all-gather.4
where the time goes:
time: 129 us; the launch traced here: 128 us
  blocking collectives  42.3 us (33%)
  local copies, waits for them, and re-layouts  26.4 us (20%)
  matrix products  23.4 us (18%)
  between operations  14.5 us (11%)
  starting transfers between devices  14 us (11%)
  other arithmetic  7.51 us (6%)
    all_gather x2, blocking collectives, prefix_2(): gathered = jax.tree.map(lambda a: lax.all_gather(a, axis), part)  42.3 us
    dot_general x24, matrix products, apply_block(): jnp.einsum('...zab,...zb->...za', matrix, column, precision=lax.Precision...  23 us
    another operation x42, local copies, waits for them, and re-layouts  14.4 us
    ppermute x2, starting transfers between devices, padded(): lax.ppermute(lax.slice_in_dim(block, block.shape[dim] - width, None, axis...  10 us
    dynamic_slice x7, local copies, waits for them, and re-layouts, one(): lax.dynamic_index_in_dim(a, source, 0, False)  6.82 us
    another operation x7, other arithmetic  4.41 us
    ppermute x2, starting transfers between devices, padded(): lax.ppermute(lax.slice_in_dim(block, 0, width, axis=dim), axis, backward)  2.58 us
  transfers between devices with their start and end apart: 7, of which 0 were waited for; matrix products, arithmetic and copies ran while one was open for 22% of the time, Pallas kernels for 0%

commit v1 on v0

v1 whole, which is shorter than its diff:
```python
import functools

import jax
import jax.numpy as jnp
from jax import lax
from jax.experimental import pallas as pl
from jax.experimental.pallas import tpu as pltpu
from jax.sharding import PartitionSpec as P

LANES = 128
F32 = jnp.float32
BF16 = jnp.bfloat16


def lane_bit(shape, shift):
    return (lax.broadcasted_iota(jnp.int32, shape, len(shape) - 1) & shift) != 0


def segment_sums(leaf, tiles, rows):
    shape = (rows, LANES)

    def node(base, stride, shift):
        if stride == tiles:
            return leaf(base)
        low = node(base, stride * 2, shift * 2)
        high = node(base + stride, stride * 2, shift * 2)
        low = low + pltpu.roll(low, LANES - shift, 1)
        high = high + pltpu.roll(high, shift, 1)
        return jnp.where(lane_bit(shape, shift), high, low)

    part = node(0, 1, 2)
    odd = lane_bit(shape, 1)
    part = part + jnp.where(odd, pltpu.roll(part, 1, 1), pltpu.roll(part, LANES - 1, 1))
    upper = lane_bit(shape, LANES // 2)
    return jnp.where(upper == odd, part, pltpu.roll(part, LANES // 2, 1))


def apply(terms):
    rows = terms[0][1].shape[0]
    tiles = LANES // 4

    def leaf(t):
        return sum(read(t).astype(F32) * vector for read, vector in terms)

    return segment_sums(leaf, tiles, rows)


def reader(ref, *index):
    return lambda t: ref[(*index, slice(None), slice(t * LANES, (t + 1) * LANES))]


def spread(scratch, raw):
    upper = lane_bit(raw.shape, LANES // 2)
    other = pltpu.roll(raw, LANES // 2, 1)
    half = raw.shape[0]
    scratch[pl.ds(0, half, stride=2), :] = jnp.where(upper, other, raw)
    scratch[pl.ds(1, half, stride=2), :] = jnp.where(upper, raw, other)
    return scratch[...]


def gather_pairs(scratch, vector):
    scratch[...] = vector
    half = vector.shape[0] // 2
    even = scratch[pl.ds(0, half, stride=2), :]
    odd = scratch[pl.ds(1, half, stride=2), :]
    return jnp.where(lane_bit(even.shape, LANES // 2), odd, even)


def shifted(vector, down):
    rows = vector.shape[0]
    row = lax.broadcasted_iota(jnp.int32, vector.shape, 0)
    if down:
        return jnp.where(row == 0, 0.0, pltpu.roll(vector, 1, 0))
    return jnp.where(row == rows - 1, 0.0, pltpu.roll(vector, rows - 1, 0))


def to_rows(scratch, read, rows, species):
    for a in range(species):
        tile = read(a // 2).astype(F32)
        if a % 2:
            tile = pltpu.roll(tile, LANES // 2, 1)
        scratch[pl.ds(a, rows, stride=species), :] = tile


def from_rows(scratch, out, index, rows, species):
    upper = lane_bit((rows, LANES), LANES // 2)
    for t in range(species // 2):
        even = scratch[pl.ds(2 * t, rows, stride=species), :]
        odd = scratch[pl.ds(2 * t + 1, rows, stride=species), :]
        out[(*index, slice(None), slice(t * LANES, (t + 1) * LANES))] = jnp.where(upper, odd, even)


def twice(a):
    return jnp.concatenate([a, a], 1)


def halves(a):
    high = a.astype(BF16)
    return high, (a - high.astype(F32)).astype(BF16)


def dot(a, b):
    return jnp.dot(a, b, preferred_element_type=F32)


def prep_kernel(lower, upper, out, first, second):
    planes, _, rows, width = lower.shape
    species = LANES // 2
    for side, blocks, order in ((0, lower, range(planes)), (1, upper, range(planes)[::-1])):
        order = list(order)
        to_rows(first, reader(blocks, order[0], 0), rows, species)
        for plane in order[1:]:
            to_rows(second, reader(blocks, plane, 0), rows, species)
            for z in range(rows):
                at = pl.ds(z * species, species)
                left = second[at, : LANES // 2].astype(BF16)
                high, low = halves(first[at, : LANES // 2])
                if plane == order[1]:
                    product = dot(left, twice(high))
                else:
                    product = dot(left, twice(high)) + dot(left, twice(low))
                first[at, :] = product
        if planes % 2:
            first[...] = -first[...]
        from_rows(first, out, (side,), rows, species)


def join_kernel(level, axis, own, partner, out, first, second):
    rows, width = own.shape[1:]
    species = LANES // 2
    here = (lax.axis_index(axis) >> level) & 1
    for side in (0, 1):
        later = here == (1 if side == 0 else 0)
        a, b = reader(own, side), reader(partner, side)
        to_rows(first, lambda t: jnp.where(later, a(t), b(t)), rows, species)
        to_rows(second, lambda t: jnp.where(later, b(t), a(t)), rows, species)
        for z in range(rows):
            at = pl.ds(z * species, species)
            left_high, left_low = halves(first[at, : LANES // 2])
            high, low = halves(twice(second[at, : LANES // 2]))
            first[at, :] = dot(
                jnp.concatenate([left_high, left_low, left_high], 1),
                jnp.concatenate([high, high, low], 0),
            )
        from_rows(first, out, (side,), rows, species)


def base_kernel(start, source, diag, upper, side, rhs, base, scratch):
    planes = start.shape[0]
    vectors = [spread(scratch, start[p]) for p in range(planes)]
    for p in range(planes):
        own = apply([(reader(diag, p, 0), spread(scratch, source[p]))])
        rhs[p] = own
        terms = [
            (reader(side, 0, p, 0), shifted(vectors[p], True)),
            (reader(side, 1, p, 0), shifted(vectors[p], False)),
        ]
        if p + 1 < planes:
            terms.append((reader(upper, p, 0), vectors[p + 1]))
        base[p] = own - apply(terms)


def outgoing(offset, partners, here, sent):
    vector = offset
    for level in range(sent.shape[0]):
        sent[level] = vector
        if level + 1 < sent.shape[0]:
            passed = apply([(partners[level], vector)])
            vector = jnp.where((here >> level) & 1 == 0, passed, vector)


def incoming(gathered, partners, here, count, reverse):
    levels = gathered.shape[1]
    entering = None
    for level in range(levels)[::-1]:
        total = jnp.zeros(gathered.shape[2:], F32)
        for e in range(count):
            place = count - 1 - e if reverse else e
            total = total + jnp.where((place >> level) == (here >> level) - 1, gathered[e, level], 0.0)
        if entering is not None:
            total = total + apply([(partners[level], entering)])
        else:
            entering = jnp.zeros_like(total)
        entering = jnp.where((here >> level) & 1 == 1, total, entering)
    return entering


def forward_offset_kernel(axis, count, base, low, high, ahead, side, upper, lower, *rest):
    *partners, drive, sent, scratch = rest
    planes = base.shape[0]
    here = lax.axis_index(axis)
    previous = None
    for p in range(planes):
        terms = [
            (reader(side, 0, p, 0), spread(scratch, low[p])),
            (reader(side, 1, p, 0), spread(scratch, high[p])),
        ]
        if p + 1 == planes:
            terms.append((reader(upper, p, 0), spread(scratch, ahead[0])))
        fresh = base[p] - apply(terms)
        drive[p] = fresh
        if previous is not None:
            fresh = fresh - apply([(reader(lower, p, 0), previous)])
        previous = fresh
    outgoing(previous, [reader(ref, 0) for ref in partners], here, sent)


def forward_kernel(axis, count, gathered, drive, lower, rhs, *rest):
    *partners, out, vectors, base, scratch = rest
    planes = drive.shape[0]
    here = lax.axis_index(axis)
    previous = incoming(gathered, [reader(ref, 0) for ref in partners], here, count, False)
    for p in range(planes):
        term = apply([(reader(lower, p, 0), previous)])
        previous = drive[p] - term
        base[p] = rhs[p] - term
        vectors[p] = previous
        out[p] = gather_pairs(scratch, previous)


def side_kernel(base, vectors, side, out):
    for p in range(base.shape[0]):
        vector = vectors[p]
        out[p] = base[p] - apply(
            [
                (reader(side, 0, p, 0), shifted(vector, True)),
                (reader(side, 1, p, 0), shifted(vector, False)),
            ]
        )


def backward_offset_kernel(axis, count, base, low, high, side, upper, *rest):
    *partners, drive, sent, scratch = rest
    planes = base.shape[0]
    here = count - 1 - lax.axis_index(axis)
    previous = None
    for p in range(planes)[::-1]:
        fresh = base[p] - apply(
            [
                (reader(side, 0, p, 0), spread(scratch, low[p])),
                (reader(side, 1, p, 0), spread(scratch, high[p])),
            ]
        )
        drive[p] = fresh
        if previous is not None:
            fresh = fresh - apply([(reader(upper, p, 0), previous)])
        previous = fresh
    outgoing(previous, [reader(ref, 0) for ref in partners], here, sent)


def backward_kernel(axis, count, gathered, drive, upper, *rest):
    *partners, out, scratch = rest
    planes = drive.shape[0]
    here = count - 1 - lax.axis_index(axis)
    previous = incoming(gathered, [reader(ref, 0) for ref in partners], here, count, True)
    for p in range(planes)[::-1]:
        previous = drive[p] - apply([(reader(upper, p, 0), previous)])
        out[p] = gather_pairs(scratch, previous)


def call(kernel, operands, outs, scratch, flops=1 << 20):
    arrays = [o[0] if isinstance(o, tuple) else o for o in operands]
    parts = [(i, o[1], o[2]) for i, o in enumerate(operands) if isinstance(o, tuple)]
    buffers = [pltpu.VMEM((size,) + arrays[i].shape[1:], arrays[i].dtype) for i, _, size in parts]
    outs = [jax.ShapeDtypeStruct(shape, F32) for shape in outs]
    moved = sum(a.size * a.dtype.itemsize for a in arrays)

    def body(*refs):
        refs = list(refs)
        if parts:
            held, semaphores = refs[-len(parts) - 1 : -1], refs[-1]
            refs = refs[: -len(parts) - 1]
            copies = []
            for k, (i, first, size) in enumerate(parts):
                copies.append(
                    pltpu.make_async_copy(refs[i].at[pl.ds(first, size)], held[k], semaphores.at[k])
                )
                copies[-1].start()
                refs[i] = held[k]
            for copy in copies:
                copy.wait()
        kernel(*refs)

    inside = [pltpu.VMEM(shape, F32) for shape in scratch] + buffers
    if parts:
        inside.append(pltpu.SemaphoreType.DMA((len(parts),)))
    held = [i for i, _, _ in parts]
    return pl.pallas_call(
        body,
        out_shape=outs,
        in_specs=[
            pl.BlockSpec(memory_space=pl.ANY if i in held else pltpu.VMEM) for i in range(len(arrays))
        ],
        out_specs=[pl.BlockSpec(memory_space=pltpu.VMEM) for _ in outs],
        scratch_shapes=inside,
        compiler_params=pltpu.CompilerParams(vmem_limit_bytes=24 << 20),
        cost_estimate=pl.CostEstimate(flops=flops, bytes_accessed=moved, transcendentals=0),
    )(*arrays)


def neighbours(block, axis):
    count = lax.axis_size(axis)
    up = [(i, i + 1) for i in range(count - 1)]
    down = [(target, source) for source, target in up]
    return lax.ppermute(block, axis, up), lax.ppermute(block, axis, down)


def local(start, source, diag_inverse, x_lower, x_upper, side_blocks):
    planes, _, depth, width = x_lower.shape
    species = start.shape[2] // depth
    count = lax.axis_size("gx")
    levels = count.bit_length() - 1
    raw = (planes, depth * species // LANES, LANES)
    vec = (planes, depth, LANES)
    mat = (2, depth, width)
    rows = (depth * species, LANES)
    one = (depth, LANES)
    start = start.reshape(raw)
    source = source.reshape(raw)

    low, high = neighbours(start, "gy")
    ahead = lax.ppermute(start[:1], "gx", [(i + 1, i) for i in range(count - 1)])

    (maps,) = call(prep_kernel, [x_lower, x_upper], [mat], [rows, rows], 1 << 24)
    partners = []
    for level in range(levels - 1):
        got = lax.ppermute(maps, "gx", [(i, i ^ (1 << level)) for i in range(count)])
        partners.append(got)
        if level + 2 < levels:
            (maps,) = call(
                functools.partial(join_kernel, level, "gx"), [maps, got], [mat], [rows, rows], 1 << 25
            )
    forward_maps = [(a, 0, 1) for a in partners]
    backward_maps = [(a, 1, 1) for a in partners]

    near = (side_blocks, 0, 2)
    vertical = (side_blocks, 2, 2)
    rhs, base = call(base_kernel, [start, source, diag_inverse, x_upper, vertical], [vec, vec], [one])
    drive, sent = call(
        functools.partial(forward_offset_kernel, "gx", count),
        [base, low, high, ahead, near, x_upper, x_lower] + forward_maps,
        [vec, (levels,) + one],
        [one],
    )
    gathered = lax.all_gather(sent, "gx")
    forward, vectors, base = call(
        functools.partial(forward_kernel, "gx", count),
        [gathered, drive, x_lower, rhs] + forward_maps,
        [raw, vec, vec],
        [one],
    )
    low, high = neighbours(forward, "gy")
    (base,) = call(side_kernel, [base, vectors, vertical], [vec], [])
    drive, sent = call(
        functools.partial(backward_offset_kernel, "gx", count),
        [base, low, high, near, x_upper] + backward_maps,
        [vec, (levels,) + one],
        [one],
    )
    gathered = lax.all_gather(sent, "gx")
    (result,) = call(
        functools.partial(backward_kernel, "gx", count),
        [gathered, drive, x_upper] + backward_maps,
        [raw],
        [one],
    )
    shape = (planes, 1, depth * species)
    return forward.reshape(shape), result.reshape(shape)


def solution(mesh):
    return jax.shard_map(
        local,
        mesh=mesh,
        in_specs=(
            P("gx", "gy", None),
            P("gx", "gy", None),
            P("gx", "gy", None, None),
            P("gx", "gy", None, None),
            P("gx", "gy", None, None),
            P(None, "gx", "gy", None, None),
        ),
        out_specs=(P("gx", "gy", None), P("gx", "gy", None)),
        check_vma=False,
    )
```

time: 129 us -> 63.7 us (0.49)
  local copies, waits for them, and re-layouts: 26.4 us -> 1.93 us
  blocking collectives: 42.3 us -> 18.8 us
  matrix products: 23.4 us -> 0 us
  Pallas kernels: 0 us -> 17.7 us
  between operations: 14.5 us -> 0.83 us
  waiting for transfers between devices: 0.05 us -> 9.82 us
  other arithmetic: 7.51 us -> 0 us
    all_gather x2, blocking collectives: 42.3 us -> 18.8 us  [local(): gathered = lax.all_gather(sent, 'gx')]
    dot_general x26 -> x0, matrix products: 23.4 us -> none  [the longest x24 23 us: apply_block(): jnp.einsum('...zab,...zb->...za', matrix, column, precision=lax.Precision...]
    pallas_call x0 -> x8, Pallas kernels: none -> 17.7 us  [call(): pl.pallas_call(body, out_shape=outs, in_specs=[pl.BlockSpec(memory_space=...]
    another operation x47 -> x0, local copies, waits for them, and re-layouts: 16.3 us -> none
    ppermute x5 -> x7, waiting for transfers between devices: 0.01 us -> 9.82 us  [the longest x4 4.93 us: neighbours(): return (lax.ppermute(block, axis, up), lax.ppermute(block, axis, down))]
    dynamic_slice x7 -> x0, local copies, waits for them, and re-layouts: 6.82 us -> none  [one(): lax.dynamic_index_in_dim(a, source, 0, False)]
    another operation x9 -> x0, other arithmetic: 5.02 us -> none
    unnamed x19 -> x16, local copies, waits for them, and re-layouts: 0.05 us -> 1.93 us
  transfers between devices with their start and end apart: 7 -> 7, of which waited for: 0 -> 5; matrix products, arithmetic and copies ran while one was open for 22% -> 0% of each run, Pallas kernels for 0% -> 4%
where the time goes in v1:
time: 63.7 us; the launch traced here: 63.4 us
  blocking collectives  18.8 us (30%)
  Pallas kernels  17.7 us (28%)
  starting transfers between devices  14.3 us (22%)
  waiting for transfers between devices  9.82 us (15%)
  local copies, waits for them, and re-layouts  1.93 us (3%)
  between operations  0.83 us (1%)
    all_gather x2, blocking collectives, local(): gathered = lax.all_gather(sent, 'gx')  18.8 us
    pallas_call x8, Pallas kernels, call(): pl.pallas_call(body, out_shape=outs, in_specs=[pl.BlockSpec(memory_space=...  17.7 us
    ppermute x4, starting transfers between devices, neighbours(): return (lax.ppermute(block, axis, up), lax.ppermute(block, axis, down))  9.53 us
    ppermute x4, waiting for transfers between devices, neighbours(): return (lax.ppermute(block, axis, up), lax.ppermute(block, axis, down))  4.93 us
    ppermute x2, waiting for transfers between devices, local(): got = lax.ppermute(maps, 'gx', [(i, i ^ 1 << level) for i in range(count)])  4.74 us
    ppermute x2, starting transfers between devices, local(): got = lax.ppermute(maps, 'gx', [(i, i ^ 1 << level) for i in range(count)])  3.44 us
    unnamed x16, local copies, waits for them, and re-layouts  1.93 us
    ppermute x1, starting transfers between devices, local(): lax.ppermute(start[:1], 'gx', [(i + 1, i) for i in range(count - 1)])  1.29 us
  transfers between devices with their start and end apart: 7, of which 5 were waited for; matrix products, arithmetic and copies ran while one was open for 0% of the time, Pallas kernels for 4%

profile of v1, /device:TPU:0, one launch (start us, length us, event | category | flops | bytes accessed | tf_op | source)
XLA Modules:
  0.0 63.4 jit_solution(4790014130857878506)
XLA Ops:
  0.6 0.0 copy-start.1
  0.6 0.9 %copy-done.1 = bf16[2,1,16,4096]{3,2,1,0:T(8,128)(2,1)S(1)} copy-done((bf16[2,1,16,4096]{3,2,1,0:T(8,128)(2,1)S(1)}, bf16[2,1,16,4096]{3,2,1,0:T(8,128)(2,1)}, u32[]{:S(2)}) %copy-start.1) | copy-done | bytes 262168
  1.6 0.9 %copy-done.3 = bf16[2,1,16,4096]{3,2,1,0:T(8,128)(2,1)S(1)} copy-done((bf16[2,1,16,4096]{3,2,1,0:T(8,128)(2,1)S(1)}, bf16[2,1,16,4096]{3,2,1,0:T(8,128)(2,1)}, u32[]{:S(2)}) %copy-start.3) | copy-done | bytes 262168
  2.5 2.3 %shard_map.78.refs_0_ = f32[2,16,4096]{2,1,0:T(8,128)S(1)} custom-call(bf16[2,1,16,4096]{3,2,1,0:T(8,128)(2,1)S(1)} %copy-done.3, bf16[2,1,16,4096]{3,2,1,0:T(8,128)(2,1)S(1)} %copy-done.1), custom_call_target="tpu_custom_call" | custom-call | flops 16777216 | bytes 524288 | tf_op jit(solution)/shard_map/pallas_call | solution.py:288
  4.9 0.0 copy-start
  4.9 0.0 copy-start.2
  4.9 0.0 copy-start.5
  4.9 0.5 collective-permute-start.3
  5.4 1.5 %collective-permute-done.3.refs_1_.refs_7_.refs_4_.refs_5_.refs_3_ = f32[2,16,4096]{2,1,0:T(8,128)S(1)} collective-permute-done((f32[2,16,4096]{2,1,0:T(8,128)S(1)}, f32[2,16,4096]{2,1,0:T(8,128)S(1)}, u32[]{:S(2)}, u32[]{:S(2)}) %collective-permute-start.3) | collective-permute-done | bytes 524320 | tf_op jit(solution)/shard_map/ppermute | solution.py:327
  7.0 2.5 %shard_map.79 = f32[2,16,4096]{2,1,0:T(8,128)S(1)} custom-call(f32[2,16,4096]{2,1,0:T(8,128)S(1)} %shard_map.78.refs_0_, f32[2,16,4096]{2,1,0:T(8,128)S(1)} %collective-permute-done.3.refs_1_.refs_7_.refs_4_.refs_5_.refs_3_), custom_call_target="tpu_custom_call" | custom-call | flops 33554432 | bytes 1048576 | tf_op jit(solution)/shard_map/pallas_call | solution.py:288
  9.5 0.0 copy-start.7
  9.5 2.9 %collective-permute-start.4 = (f32[2,16,4096]{2,1,0:T(8,128)S(1)}, f32[2,16,4096]{2,1,0:T(8,128)S(1)}, u32[]{:S(2)}, u32[]{:S(2)}) collective-permute-start(f32[2,16,4096]{2,1,0:T(8,128)S(1)} %shard_map.79), channel_id=1, source_target_pairs={{0,8},{4,12},{8,0},{12,4},{16,24},{20,28},{24,16},{28,20},{1,9},{5... | collective-permute-start | bytes 1572872 | tf_op jit(solution)/shard_map/ppermute | solution.py:327
  12.5 3.5 %collective-permute-start = (f32[2,8,128]{2,1,0:T(8,128)S(1)}, f32[2,8,128]{2,1,0:T(8,128)S(1)}, u32[]{:S(2)}, u32[]{:S(2)}) collective-permute-start(f32[2,8,128]{2,1,0:T(8,128)S(1)} %bitcast.9), channel_id=1, source_target_pairs={{0,1},{1,2},{2,3},{4,5},{5,6},{6,7},{8,9},{9,10},{10,11},{12,13},{... | collective-permute-start | bytes 24584 | tf_op jit(solution)/shard_map/ppermute | solution.py:305
  15.9 1.3 %collective-permute-start.1 = (f32[2,8,128]{2,1,0:T(8,128)S(1)}, f32[2,8,128]{2,1,0:T(8,128)S(1)}, u32[]{:S(2)}, u32[]{:S(2)}) collective-permute-start(f32[2,8,128]{2,1,0:T(8,128)S(1)} %bitcast.10), channel_id=1, source_target_pairs={{1,0},{2,1},{3,2},{5,4},{6,5},{7,6},{9,8},{10,9},{11,10},{13,12},{... | collective-permute-start | bytes 24584 | tf_op jit(solution)/shard_map/ppermute | solution.py:305
  17.2 1.3 %collective-permute-start.2 = (f32[1,8,128]{2,1,0:T(8,128)S(1)}, f32[1,8,128]{2,1,0:T(8,128)S(1)}, u32[]{:S(2)}, u32[]{:S(2)}) collective-permute-start(f32[1,8,128]{2,1,0:T(8,128)S(1)} %bitcast.14), channel_id=1, source_target_pairs={{4,0},{8,4},{12,8},{16,12},{20,16},{24,20},{28,24},{5,1},{9,5},{13... | collective-permute-start | bytes 12296 | tf_op jit(solution)/shard_map/ppermute | solution.py:322
  18.6 0.0 copy-start.4
  18.6 1.5 %shard_map.77 = (f32[2,16,128]{2,1,0:T(8,128)S(1)}, f32[2,16,128]{2,1,0:T(8,128)S(1)}) custom-call(f32[2,8,128]{2,1,0:T(8,128)S(1)} %bitcast.11, f32[2,8,128]{2,1,0:T(8,128)S(1)} %bitcast.12, bf16[2,1,16,4096]{3,2,1,0:T(8,128)(2,1)S(1)} %copy-done.5, bf16[2,1,16,4096]{3,2,1,0:T(8,128)(2,1)S(1)} %copy-done.2, bf16[4,2,1,16,4096]{4,3,2,1,0:T(8,128)(2,1)S(1)} %copy-done), custom_call_target="tpu_custom_call" | custom-call | flops 1048576 | bytes 1589248 | tf_op jit(solution)/shard_map/pallas_call | solution.py:288
  20.1 0.2 collective-permute-done.2.refs_3_
  20.3 0.0 collective-permute-done.refs_1_
  20.3 1.2 %collective-permute-done.1.refs_2_ = f32[2,8,128]{2,1,0:T(8,128)S(1)} collective-permute-done((f32[2,8,128]{2,1,0:T(8,128)S(1)}, f32[2,8,128]{2,1,0:T(8,128)S(1)}, u32[]{:S(2)}, u32[]{:S(2)}) %collective-permute-start.1) | collective-permute-done | bytes 8224 | tf_op jit(solution)/shard_map/ppermute | solution.py:305
  21.5 3.2 %collective-permute-done.4.refs_8_.refs_5_.refs_6_.refs_4_ = f32[2,16,4096]{2,1,0:T(8,128)S(1)} collective-permute-done((f32[2,16,4096]{2,1,0:T(8,128)S(1)}, f32[2,16,4096]{2,1,0:T(8,128)S(1)}, u32[]{:S(2)}, u32[]{:S(2)}) %collective-permute-start.4) | collective-permute-done | bytes 524320 | tf_op jit(solution)/shard_map/ppermute | solution.py:327
  24.7 2.4 %shard_map.80 = (f32[2,16,128]{2,1,0:T(8,128)S(1)}, f32[3,16,128]{2,1,0:T(8,128)S(1)}) custom-call(f32[2,16,128]{2,1,0:T(8,128)S(1)} %get-tuple-element.11.refs_0_, f32[2,8,128]{2,1,0:T(8,128)S(1)} %collective-permute-done.refs_1_, f32[2,8,128]{2,1,0:T(8,128)S(1)} %collective-permute-done.1.refs_2_, f32[1,8,128]{2,1,0:T(8,128)S(1)} %collective-permute-done.2.refs_3_, ...), custom_call_target="tpu_custom_call" | custom-call | flops 1048576 | bytes 2658304 | tf_op jit(solution)/shard_map/pallas_call | solution.py:288
  27.1 9.5 %all-gather = f32[24,16,128]{2,1,0:T(8,128)S(1)} all-gather(f32[3,16,128]{2,1,0:T(8,128)S(1)} %get-tuple-element.12), channel_id=2, replica_groups=mesh['gx'=8,'gy'=4] {'gx'}, dimensions={0}, use_global_device_ids=true | all-gather | bytes 221184 | tf_op jit(solution)/shard_map/all_gather | solution.py:345
  36.7 2.9 %shard_map.81 = (f32[2,8,128]{2,1,0:T(8,128)}, f32[2,16,128]{2,1,0:T(8,128)S(1)}, f32[2,16,128]{2,1,0:T(8,128)S(1)}) custom-call(f32[8,3,16,128]{3,2,1,0:T(8,128)S(1)} %bitcast.7, f32[2,16,128]{2,1,0:T(8,128)S(1)} %get-tuple-element.13.refs_1_, bf16[2,1,16,4096]{3,2,1,0:T(8,128)(2,1)S(1)} %copy-done.4, f32[2,16,128]{2,1,0:T(8,128)S(1)} %get-tuple-element.14.refs_3_, ...), custom_call_target="tpu_custom_call" | custom-call | flops 1048576 | bytes 1540096 | tf_op jit(solution)/shard_map/pallas_call | solution.py:288
  39.5 3.5 %collective-permute-start.5 = (f32[2,8,128]{2,1,0:T(8,128)}, f32[2,8,128]{2,1,0:T(8,128)S(1)}, u32[]{:S(2)}, u32[]{:S(2)}) collective-permute-start(f32[2,8,128]{2,1,0:T(8,128)} %get-tuple-element.15), channel_id=1, source_target_pairs={{0,1},{1,2},{2,3},{4,5},{5,6},{6,7},{8,9},{9,10},{10,11},{12,13},{... | collective-permute-start | bytes 24584 | tf_op jit(solution)/shard_map/ppermute | solution.py:305
  43.0 1.3 %collective-permute-start.6 = (f32[2,8,128]{2,1,0:T(8,128)}, f32[2,8,128]{2,1,0:T(8,128)S(1)}, u32[]{:S(2)}, u32[]{:S(2)}) collective-permute-start(f32[2,8,128]{2,1,0:T(8,128)} %get-tuple-element.15), channel_id=1, source_target_pairs={{1,0},{2,1},{3,2},{5,4},{6,5},{7,6},{9,8},{10,9},{11,10},{13,12},{... | collective-permute-start | bytes 24584 | tf_op jit(solution)/shard_map/ppermute | solution.py:305
  44.3 0.7 %shard_map.82.refs_0_ = f32[2,16,128]{2,1,0:T(8,128)S(1)} custom-call(f32[2,16,128]{2,1,0:T(8,128)S(1)} %get-tuple-element.16.refs_0_, f32[2,16,128]{2,1,0:T(8,128)S(1)} %get-tuple-element.17.refs_1_, bf16[4,2,1,16,4096]{4,3,2,1,0:T(8,128)(2,1)S(1)} %copy-done), custom_call_target="tpu_custom_call" | custom-call | flops 1048576 | bytes 1081344 | tf_op jit(solution)/shard_map/pallas_call | solution.py:288
  45.0 0.0 collective-permute-done.5.refs_1_
  45.0 3.8 %collective-permute-done.6.refs_2_ = f32[2,8,128]{2,1,0:T(8,128)S(1)} collective-permute-done((f32[2,8,128]{2,1,0:T(8,128)}, f32[2,8,128]{2,1,0:T(8,128)S(1)}, u32[]{:S(2)}, u32[]{:S(2)}) %collective-permute-start.6) | collective-permute-done | bytes 8224 | tf_op jit(solution)/shard_map/ppermute | solution.py:305
  48.8 2.4 %shard_map.83 = (f32[2,16,128]{2,1,0:T(8,128)S(1)}, f32[3,16,128]{2,1,0:T(8,128)S(1)}) custom-call(f32[2,16,128]{2,1,0:T(8,128)S(1)} %shard_map.82.refs_0_, f32[2,8,128]{2,1,0:T(8,128)S(1)} %collective-permute-done.5.refs_1_, f32[2,8,128]{2,1,0:T(8,128)S(1)} %collective-permute-done.6.refs_2_, bf16[4,2,1,16,4096]{4,3,2,1,0:T(8,128)(2,1)S(1)} %copy-done, ...), custom_call_target="tpu_custom_call" | custom-call | flops 1048576 | bytes 2392064 | tf_op jit(solution)/shard_map/pallas_call | solution.py:288
  51.2 9.2 %all-gather.1 = f32[24,16,128]{2,1,0:T(8,128)S(1)} all-gather(f32[3,16,128]{2,1,0:T(8,128)S(1)} %get-tuple-element.18), channel_id=3, replica_groups=mesh['gx'=8,'gy'=4] {'gx'}, dimensions={0}, use_global_device_ids=true | all-gather | bytes 221184 | tf_op jit(solution)/shard_map/all_gather | solution.py:360
  60.5 2.9 %shard_map.84 = f32[2,8,128]{2,1,0:T(8,128)} custom-call(f32[8,3,16,128]{3,2,1,0:T(8,128)S(1)} %bitcast.8, f32[2,16,128]{2,1,0:T(8,128)S(1)} %get-tuple-element.19.refs_1_, bf16[2,1,16,4096]{3,2,1,0:T(8,128)(2,1)S(1)} %copy-done.2, f32[2,16,4096]{2,1,0:T(8,128)S(1)} %collective-permute-done.3.refs_1_.refs_7_.refs_4_.refs_5_.refs_3_, ...), custom_call_target="tpu_custom_call" | custom-call | flops 1048576 | bytes 1523712 | tf_op jit(solution)/shard_map/pallas_call | solution.py:288
  (9 shorter events, 0.0 us)
Async XLA Ops:
  0.6 1.0 %copy-start.1 = (bf16[2,1,16,4096]{3,2,1,0:T(8,128)(2,1)S(1)}, bf16[2,1,16,4096]{3,2,1,0:T(8,128)(2,1)}, u32[]{:S(2)}) copy-start(bf16[2,1,16,4096]{3,2,1,0:T(8,128)(2,1)} %refs_2_.7) | copy-start | bytes 786436
  1.6 0.9 %copy-start.3 = (bf16[2,1,16,4096]{3,2,1,0:T(8,128)(2,1)S(1)}, bf16[2,1,16,4096]{3,2,1,0:T(8,128)(2,1)}, u32[]{:S(2)}) copy-start(bf16[2,1,16,4096]{3,2,1,0:T(8,128)(2,1)} %refs_2_.5) | copy-start | bytes 786436
  2.5 9.9 %copy-start.6 = (f32[2,1,1024]{2,1,0:T(1,128)S(1)}, f32[2,1,1024]{2,1,0:T(1,128)}, u32[]{:S(2)}) copy-start(f32[2,1,1024]{2,1,0:T(1,128)} %param.6) | copy-start | bytes 24580
  4.9 13.7 %copy-start = (bf16[4,2,1,16,4096]{4,3,2,1,0:T(8,128)(2,1)S(1)}, bf16[4,2,1,16,4096]{4,3,2,1,0:T(8,128)(2,1)}, u32[]{:S(2)}) copy-start(bf16[4,2,1,16,4096]{4,3,2,1,0:T(8,128)(2,1)} %refs_3_.3) | copy-start | bytes 3145732
  4.9 13.7 %copy-start.2 = (bf16[2,1,16,4096]{3,2,1,0:T(8,128)(2,1)S(1)}, bf16[2,1,16,4096]{3,2,1,0:T(8,128)(2,1)}, u32[]{:S(2)}) copy-start(bf16[2,1,16,4096]{3,2,1,0:T(8,128)(2,1)} %refs_2_.7) | copy-start | bytes 786436
  4.9 13.7 %copy-start.5 = (bf16[2,1,16,4096]{3,2,1,0:T(8,128)(2,1)S(1)}, bf16[2,1,16,4096]{3,2,1,0:T(8,128)(2,1)}, u32[]{:S(2)}) copy-start(bf16[2,1,16,4096]{3,2,1,0:T(8,128)(2,1)} %refs_2_.4) | copy-start | bytes 786436
  4.9 2.1 %collective-permute-start.3 = (f32[2,16,4096]{2,1,0:T(8,128)S(1)}, f32[2,16,4096]{2,1,0:T(8,128)S(1)}, u32[]{:S(2)}, u32[]{:S(2)}) collective-permute-start(f32[2,16,4096]{2,1,0:T(8,128)S(1)} %shard_map.78.refs_0_), channel_id=1, source_target_pairs={{0,4},{4,0},{8,12},{12,8},{16,20},{20,16},{24,28},{28,24},{1,5},{5... | collective-permute-start | bytes 1572872 | tf_op jit(solution)/shard_map/ppermute | solution.py:327
  9.5 9.1 %copy-start.7 = (f32[2,1,1024]{2,1,0:T(1,128)S(1)}, f32[2,1,1024]{2,1,0:T(1,128)}, u32[]{:S(2)}) copy-start(f32[2,1,1024]{2,1,0:T(1,128)} %param.7) | copy-start | bytes 24580
  9.5 15.1 %collective-permute-start.4 = (f32[2,16,4096]{2,1,0:T(8,128)S(1)}, f32[2,16,4096]{2,1,0:T(8,128)S(1)}, u32[]{:S(2)}, u32[]{:S(2)}) collective-permute-start(f32[2,16,4096]{2,1,0:T(8,128)S(1)} %shard_map.79), channel_id=1, source_target_pairs={{0,8},{4,12},{8,0},{12,4},{16,24},{20,28},{24,16},{28,20},{1,9},{5... | collective-permute-start | bytes 1572872 | tf_op jit(solution)/shard_map/ppermute | solution.py:327
  12.5 7.9 %collective-permute-start = (f32[2,8,128]{2,1,0:T(8,128)S(1)}, f32[2,8,128]{2,1,0:T(8,128)S(1)}, u32[]{:S(2)}, u32[]{:S(2)}) collective-permute-start(f32[2,8,128]{2,1,0:T(8,128)S(1)} %bitcast.9), channel_id=1, source_target_pairs={{0,1},{1,2},{2,3},{4,5},{5,6},{6,7},{8,9},{9,10},{10,11},{12,13},{... | collective-permute-start | bytes 24584 | tf_op jit(solution)/shard_map/ppermute | solution.py:305
  15.9 5.5 %collective-permute-start.1 = (f32[2,8,128]{2,1,0:T(8,128)S(1)}, f32[2,8,128]{2,1,0:T(8,128)S(1)}, u32[]{:S(2)}, u32[]{:S(2)}) collective-permute-start(f32[2,8,128]{2,1,0:T(8,128)S(1)} %bitcast.10), channel_id=1, source_target_pairs={{1,0},{2,1},{3,2},{5,4},{6,5},{7,6},{9,8},{10,9},{11,10},{13,12},{... | collective-permute-start | bytes 24584 | tf_op jit(solution)/shard_map/ppermute | solution.py:305
  17.2 3.1 %collective-permute-start.2 = (f32[1,8,128]{2,1,0:T(8,128)S(1)}, f32[1,8,128]{2,1,0:T(8,128)S(1)}, u32[]{:S(2)}, u32[]{:S(2)}) collective-permute-start(f32[1,8,128]{2,1,0:T(8,128)S(1)} %bitcast.14), channel_id=1, source_target_pairs={{4,0},{8,4},{12,8},{16,12},{20,16},{24,20},{28,24},{5,1},{9,5},{13... | collective-permute-start | bytes 12296 | tf_op jit(solution)/shard_map/ppermute | solution.py:322
  18.6 6.1 %copy-start.4 = (bf16[2,1,16,4096]{3,2,1,0:T(8,128)(2,1)S(1)}, bf16[2,1,16,4096]{3,2,1,0:T(8,128)(2,1)}, u32[]{:S(2)}) copy-start(bf16[2,1,16,4096]{3,2,1,0:T(8,128)(2,1)} %refs_2_.5) | copy-start | bytes 786436
  39.5 5.5 %collective-permute-start.5 = (f32[2,8,128]{2,1,0:T(8,128)}, f32[2,8,128]{2,1,0:T(8,128)S(1)}, u32[]{:S(2)}, u32[]{:S(2)}) collective-permute-start(f32[2,8,128]{2,1,0:T(8,128)} %get-tuple-element.15), channel_id=1, source_target_pairs={{0,1},{1,2},{2,3},{4,5},{5,6},{6,7},{8,9},{9,10},{10,11},{12,13},{... | collective-permute-start | bytes 24584 | tf_op jit(solution)/shard_map/ppermute | solution.py:305
  43.0 5.8 %collective-permute-start.6 = (f32[2,8,128]{2,1,0:T(8,128)}, f32[2,8,128]{2,1,0:T(8,128)S(1)}, u32[]{:S(2)}, u32[]{:S(2)}) collective-permute-start(f32[2,8,128]{2,1,0:T(8,128)} %get-tuple-element.15), channel_id=1, source_target_pairs={{1,0},{2,1},{3,2},{5,4},{6,5},{7,6},{9,8},{10,9},{11,10},{13,12},{... | collective-permute-start | bytes 24584 | tf_op jit(solution)/shard_map/ppermute | solution.py:305

commit v2 on v1

--- a/solution.py
+++ b/solution.py
@@ -103,10 +103,10 @@
     return jnp.dot(a, b, preferred_element_type=F32)
 
 
-def prep_kernel(lower, upper, out, first, second):
+def prep_kernel(lower, upper, lower_map, upper_map, first, second):
     planes, _, rows, width = lower.shape
     species = LANES // 2
-    for side, blocks, order in ((0, lower, range(planes)), (1, upper, range(planes)[::-1])):
+    for out, blocks, order in ((lower_map, lower, range(planes)), (upper_map, upper, range(planes)[::-1])):
         order = list(order)
         to_rows(first, reader(blocks, order[0], 0), rows, species)
         for plane in order[1:]:
@@ -122,16 +122,18 @@
                 first[at, :] = product
         if planes % 2:
             first[...] = -first[...]
-        from_rows(first, out, (side,), rows, species)
-
-
-def join_kernel(level, axis, own, partner, out, first, second):
-    rows, width = own.shape[1:]
+        from_rows(first, out, (), rows, species)
+
+
+def join_kernel(level, axis, *refs):
+    *refs, first, second = refs
+    rows = refs[0].shape[0]
     species = LANES // 2
     here = (lax.axis_index(axis) >> level) & 1
     for side in (0, 1):
         later = here == (1 if side == 0 else 0)
-        a, b = reader(own, side), reader(partner, side)
+        own, partner, out = refs[side::2]
+        a, b = reader(own), reader(partner)
         to_rows(first, lambda t: jnp.where(later, a(t), b(t)), rows, species)
         to_rows(second, lambda t: jnp.where(later, b(t), a(t)), rows, species)
         for z in range(rows):
@@ -142,7 +144,7 @@
                 jnp.concatenate([left_high, left_low, left_high], 1),
                 jnp.concatenate([high, high, low], 0),
             )
-        from_rows(first, out, (side,), rows, species)
+        from_rows(first, out, (), rows, species)
 
 
 def base_kernel(start, source, diag, upper, side, rhs, base, scratch):
@@ -162,21 +164,17 @@
 
 def outgoing(offset, partners, here, sent):
     vector = offset
-    for level in range(sent.shape[0]):
-        sent[level] = vector
-        if level + 1 < sent.shape[0]:
+    for level, out in enumerate(sent):
+        out[...] = vector
+        if level + 1 < len(sent):
             passed = apply([(partners[level], vector)])
             vector = jnp.where((here >> level) & 1 == 0, passed, vector)
 
 
-def incoming(gathered, partners, here, count, reverse):
-    levels = gathered.shape[1]
+def incoming(received, partners, here):
     entering = None
-    for level in range(levels)[::-1]:
-        total = jnp.zeros(gathered.shape[2:], F32)
-        for e in range(count):
-            place = count - 1 - e if reverse else e
-            total = total + jnp.where((place >> level) == (here >> level) - 1, gathered[e, level], 0.0)
+    for level in range(len(partners) + 1)[::-1]:
+        total = sum(ref[...] for ref in received[(1 << level) - 1 : (2 << level) - 1])
         if entering is not None:
             total = total + apply([(partners[level], entering)])
         else:
@@ -185,31 +183,44 @@
     return entering
 
 
-def forward_offset_kernel(axis, count, base, low, high, ahead, side, upper, lower, *rest):
-    *partners, drive, sent, scratch = rest
+def beside(axis, paired, other):
+    place, count = lax.axis_index(axis), lax.axis_size(axis)
+    odd = place & 1 == 1
+    low = jnp.where(odd, paired, other)
+    high = jnp.where(odd, other, paired)
+    return jnp.where(place == 0, 0.0, low), jnp.where(place == count - 1, 0.0, high)
+
+
+def forward_offset_kernel(levels, base, paired, other, ahead, side, upper, lower, *rest):
+    partners, drive = rest[: levels - 1], rest[levels - 1]
+    sent, scratch = rest[levels:-1], rest[-1]
     planes = base.shape[0]
-    here = lax.axis_index(axis)
+    here = lax.axis_index("gx")
+    last = here == lax.axis_size("gx") - 1
     previous = None
     for p in range(planes):
+        low, high = beside("gy", paired[p], other[p])
         terms = [
-            (reader(side, 0, p, 0), spread(scratch, low[p])),
-            (reader(side, 1, p, 0), spread(scratch, high[p])),
+            (reader(side, 0, p, 0), spread(scratch, low)),
+            (reader(side, 1, p, 0), spread(scratch, high)),
         ]
         if p + 1 == planes:
-            terms.append((reader(upper, p, 0), spread(scratch, ahead[0])))
+            beyond = jnp.where(last, 0.0, ahead[0])
+            terms.append((reader(upper, p, 0), spread(scratch, beyond)))
         fresh = base[p] - apply(terms)
         drive[p] = fresh
         if previous is not None:
             fresh = fresh - apply([(reader(lower, p, 0), previous)])
         previous = fresh
-    outgoing(previous, [reader(ref, 0) for ref in partners], here, sent)
-
-
-def forward_kernel(axis, count, gathered, drive, lower, rhs, *rest):
-    *partners, out, vectors, base, scratch = rest
+    outgoing(previous, [reader(ref) for ref in partners], here, sent)
+
+
+def forward_kernel(drive, lower, rhs, *rest):
+    *rest, out, vectors, base, scratch = rest
     planes = drive.shape[0]
-    here = lax.axis_index(axis)
-    previous = incoming(gathered, [reader(ref, 0) for ref in partners], here, count, False)
+    here, count = lax.axis_index("gx"), lax.axis_size("gx")
+    received, partners = rest[: count - 1], rest[count - 1 :]
+    previous = incoming(received, [reader(ref) for ref in partners], here)
     for p in range(planes):
         term = apply([(reader(lower, p, 0), previous)])
         previous = drive[p] - term
@@ -229,30 +240,34 @@
         )
 
 
-def backward_offset_kernel(axis, count, base, low, high, side, upper, *rest):
-    *partners, drive, sent, scratch = rest
+def backward_offset_kernel(levels, base, paired, other, side, upper, *rest):
+    partners, drive = rest[: levels - 1], rest[levels - 1]
+    sent, scratch = rest[levels:-1], rest[-1]
     planes = base.shape[0]
-    here = count - 1 - lax.axis_index(axis)
+    here = lax.axis_size("gx") - 1 - lax.axis_index("gx")
     previous = None
     for p in range(planes)[::-1]:
+        low, high = beside("gy", paired[p], other[p])
         fresh = base[p] - apply(
             [
-                (reader(side, 0, p, 0), spread(scratch, low[p])),
-                (reader(side, 1, p, 0), spread(scratch, high[p])),
+                (reader(side, 0, p, 0), spread(scratch, low)),
+                (reader(side, 1, p, 0), spread(scratch, high)),
             ]
         )
         drive[p] = fresh
         if previous is not None:
             fresh = fresh - apply([(reader(upper, p, 0), previous)])
         previous = fresh
-    outgoing(previous, [reader(ref, 0) for ref in partners], here, sent)
-
-
-def backward_kernel(axis, count, gathered, drive, upper, *rest):
-    *partners, out, scratch = rest
+    outgoing(previous, [reader(ref) for ref in partners], here, sent)
+
+
+def backward_kernel(drive, upper, *rest):
+    *rest, out, scratch = rest
     planes = drive.shape[0]
-    here = count - 1 - lax.axis_index(axis)
-    previous = incoming(gathered, [reader(ref, 0) for ref in partners], here, count, True)
+    count = lax.axis_size("gx")
+    here = count - 1 - lax.axis_index("gx")
+    received, partners = rest[: count - 1], rest[count - 1 :]
+    previous = incoming(received, [reader(ref) for ref in partners], here)
     for p in range(planes)[::-1]:
         previous = drive[p] - apply([(reader(upper, p, 0), previous)])
         out[p] = gather_pairs(scratch, previous)
@@ -298,11 +313,16 @@
     )(*arrays)
 
 
-def neighbours(block, axis):
+def swaps(block, axis):
     count = lax.axis_size(axis)
-    up = [(i, i + 1) for i in range(count - 1)]
-    down = [(target, source) for source, target in up]
-    return lax.ppermute(block, axis, up), lax.ppermute(block, axis, down)
+    other = [(i, (i + 1 if i & 1 else i - 1)) for i in range(1, count - 1)]
+    other += [(0, 0), (count - 1, count - 1)]
+    paired = lax.ppermute(block, axis, [(i, i ^ 1) for i in range(count)])
+    return paired, lax.ppermute(block, axis, other)
+
+
+def crossed(block, axis, distance):
+    return lax.ppermute(block, axis, [(i, i ^ distance) for i in range(lax.axis_size(axis))])
 
 
 def local(start, source, diag_inverse, x_lower, x_upper, side_blocks):
@@ -312,55 +332,60 @@
     levels = count.bit_length() - 1
     raw = (planes, depth * species // LANES, LANES)
     vec = (planes, depth, LANES)
-    mat = (2, depth, width)
+    mat = (depth, width)
     rows = (depth * species, LANES)
     one = (depth, LANES)
     start = start.reshape(raw)
     source = source.reshape(raw)
 
-    low, high = neighbours(start, "gy")
-    ahead = lax.ppermute(start[:1], "gx", [(i + 1, i) for i in range(count - 1)])
-
-    (maps,) = call(prep_kernel, [x_lower, x_upper], [mat], [rows, rows], 1 << 24)
+    paired, other = swaps(start, "gy")
+    ahead = lax.ppermute(start[:1], "gx", [(i, (i - 1) % count) for i in range(count)])
+
+    maps = call(prep_kernel, [x_lower, x_upper], [mat, mat], [rows, rows], 1 << 24)
     partners = []
     for level in range(levels - 1):
-        got = lax.ppermute(maps, "gx", [(i, i ^ (1 << level)) for i in range(count)])
-        partners.append(got)
+        partners.append([crossed(a, "gx", 1 << level) for a in maps])
         if level + 2 < levels:
-            (maps,) = call(
-                functools.partial(join_kernel, level, "gx"), [maps, got], [mat], [rows, rows], 1 << 25
+            maps = call(
+                functools.partial(join_kernel, level, "gx"),
+                [*maps, *partners[-1]],
+                [mat, mat],
+                [rows, rows],
+                1 << 25,
             )
-    forward_maps = [(a, 0, 1) for a in partners]
-    backward_maps = [(a, 1, 1) for a in partners]
+    forward_maps = [a for a, _ in partners]
+    backward_maps = [a for _, a in partners]
+    pack = [one] * levels
+
+    def exchange(sent):
+        return [crossed(sent[m.bit_length() - 1], "gx", m) for m in range(1, count)]
 
     near = (side_blocks, 0, 2)
     vertical = (side_blocks, 2, 2)
     rhs, base = call(base_kernel, [start, source, diag_inverse, x_upper, vertical], [vec, vec], [one])
-    drive, sent = call(
-        functools.partial(forward_offset_kernel, "gx", count),
-        [base, low, high, ahead, near, x_upper, x_lower] + forward_maps,
-        [vec, (levels,) + one],
+    drive, *sent = call(
+        functools.partial(forward_offset_kernel, levels),
+        [base, paired, other, ahead, near, x_upper, x_lower] + forward_maps,
+        [vec] + pack,
         [one],
     )
-    gathered = lax.all_gather(sent, "gx")
     forward, vectors, base = call(
-        functools.partial(forward_kernel, "gx", count),
-        [gathered, drive, x_lower, rhs] + forward_maps,
+        forward_kernel,
+        [drive, x_lower, rhs] + exchange(sent) + forward_maps,
         [raw, vec, vec],
         [one],
     )
-    low, high = neighbours(forward, "gy")
+    paired, other = swaps(forward, "gy")
     (base,) = call(side_kernel, [base, vectors, vertical], [vec], [])
-    drive, sent = call(
-        functools.partial(backward_offset_kernel, "gx", count),
-        [base, low, high, near, x_upper] + backward_maps,
-        [vec, (levels,) + one],
+    drive, *sent = call(
+        functools.partial(backward_offset_kernel, levels),
+        [base, paired, other, near, x_upper] + backward_maps,
+        [vec] + pack,
         [one],
     )
-    gathered = lax.all_gather(sent, "gx")
     (result,) = call(
-        functools.partial(backward_kernel, "gx", count),
-        [gathered, drive, x_upper] + backward_maps,
+        backward_kernel,
+        [drive, x_upper] + exchange(sent) + backward_maps,
         [raw],
         [one],
     )

time: 63.7 us -> 60.6 us (0.951)
  the two profiles are of different devices: /device:TPU:0 before, /device:TPU:17 now
where the time goes in v2:
time: 60.6 us; the launch traced here: 60.3 us
  starting transfers between devices  25.3 us (42%)
  Pallas kernels  17.5 us (29%)
  waiting for transfers between devices  14.7 us (24%)
  local copies, waits for them, and re-layouts  2.01 us (3%)
  between operations  0.79 us (1%)
    ppermute x18, starting transfers between devices, crossed(): lax.ppermute(block, axis, [(i, i ^ distance) for i in range(lax.axis_size...  17.7 us
    pallas_call x8, Pallas kernels, call(): pl.pallas_call(body, out_shape=outs, in_specs=[pl.BlockSpec(memory_space=...  17.5 us
    ppermute x1, waiting for transfers between devices, local(): lax.ppermute(start[:1], 'gx', [(i, (i - 1) % count) for i in range(count)])  6.41 us
    ppermute x18, waiting for transfers between devices, crossed(): lax.ppermute(block, axis, [(i, i ^ distance) for i in range(lax.axis_size...  6.31 us
    ppermute x2, starting transfers between devices, swaps(): return (paired, lax.ppermute(block, axis, other))  3.82 us
    ppermute x2, starting transfers between devices, swaps(): paired = lax.ppermute(block, axis, [(i, i ^ 1) for i in range(count)])  2.59 us
    unnamed x16, local copies, waits for them, and re-layouts  2.01 us
    ppermute x2, waiting for transfers between devices, swaps(): return (paired, lax.ppermute(block, axis, other))  1.97 us
  transfers between devices with their start and end apart: 23, of which 7 were waited for; matrix products, arithmetic and copies ran while one was open for 0% of the time, Pallas kernels for 12%

profile of v2, /device:TPU:17, one launch (start us, length us, event | category | flops | bytes accessed | tf_op | source)
XLA Modules:
  0.0 60.3 jit_solution(16883289007614005450)
XLA Ops:
  0.7 1.0 %copy-done.1 = bf16[2,1,16,4096]{3,2,1,0:T(8,128)(2,1)S(1)} copy-done((bf16[2,1,16,4096]{3,2,1,0:T(8,128)(2,1)S(1)}, bf16[2,1,16,4096]{3,2,1,0:T(8,128)(2,1)}, u32[]{:S(2)}) %copy-start.1) | copy-done | bytes 262168
  1.7 0.9 %copy-done.3 = bf16[2,1,16,4096]{3,2,1,0:T(8,128)(2,1)S(1)} copy-done((bf16[2,1,16,4096]{3,2,1,0:T(8,128)(2,1)S(1)}, bf16[2,1,16,4096]{3,2,1,0:T(8,128)(2,1)}, u32[]{:S(2)}) %copy-start.3) | copy-done | bytes 262168
  2.6 2.3 %shard_map.78 = (f32[16,4096]{1,0:T(8,128)S(1)}, f32[16,4096]{1,0:T(8,128)S(1)}) custom-call(bf16[2,1,16,4096]{3,2,1,0:T(8,128)(2,1)S(1)} %copy-done.3, bf16[2,1,16,4096]{3,2,1,0:T(8,128)(2,1)S(1)} %copy-done.1), custom_call_target="tpu_custom_call" | custom-call | flops 16777216 | bytes 524288 | tf_op jit(solution)/shard_map/pallas_call | solution.py:303
  5.0 0.7 %collective-permute-start.3 = (f32[16,4096]{1,0:T(8,128)S(1)}, f32[16,4096]{1,0:T(8,128)S(1)}, u32[]{:S(2)}, u32[]{:S(2)}) collective-permute-start(f32[16,4096]{1,0:T(8,128)S(1)} %get-tuple-element.20.refs_0_), channel_id=1, source_target_pairs={{0,4},{4,0},{8,12},{12,8},{16,20},{20,16},{24,28},{28,24},{1,5},{5... | collective-permute-start | bytes 786440 | tf_op jit(solution)/shard_map/ppermute | solution.py:325
  5.8 1.0 %collective-permute-done.3.refs_2_.refs_7_.refs_10_ = f32[16,4096]{1,0:T(8,128)S(1)} collective-permute-done((f32[16,4096]{1,0:T(8,128)S(1)}, f32[16,4096]{1,0:T(8,128)S(1)}, u32[]{:S(2)}, u32[]{:S(2)}) %collective-permute-start.3) | collective-permute-done | bytes 262176 | tf_op jit(solution)/shard_map/ppermute | solution.py:325
  7.3 2.5 %shard_map.79 = (f32[16,4096]{1,0:T(8,128)S(1)}, f32[16,4096]{1,0:T(8,128)S(1)}) custom-call(f32[16,4096]{1,0:T(8,128)S(1)} %get-tuple-element.20.refs_0_, f32[16,4096]{1,0:T(8,128)S(1)} %get-tuple-element.21.refs_1_, f32[16,4096]{1,0:T(8,128)S(1)} %collective-permute-done.3.refs_2_.refs_7_.refs_10_, ...), custom_call_target="tpu_custom_call" | custom-call | flops 33554432 | bytes 1048576 | tf_op jit(solution)/shard_map/pallas_call | solution.py:303
  9.8 1.3 %collective-permute-start.5 = (f32[16,4096]{1,0:T(8,128)S(1)}, f32[16,4096]{1,0:T(8,128)S(1)}, u32[]{:S(2)}, u32[]{:S(2)}) collective-permute-start(f32[16,4096]{1,0:T(8,128)S(1)} %get-tuple-element.22), channel_id=1, source_target_pairs={{0,8},{4,12},{8,0},{12,4},{16,24},{20,28},{24,16},{28,20},{1,9},{5... | collective-permute-start | bytes 786440 | tf_op jit(solution)/shard_map/ppermute | solution.py:325
  11.4 1.3 %collective-permute-start = (f32[2,8,128]{2,1,0:T(8,128)S(1)}, f32[2,8,128]{2,1,0:T(8,128)S(1)}, u32[]{:S(2)}, u32[]{:S(2)}) collective-permute-start(f32[2,8,128]{2,1,0:T(8,128)S(1)} %bitcast.5), channel_id=1, source_target_pairs={{0,1},{1,0},{2,3},{3,2},{4,5},{5,4},{6,7},{7,6},{8,9},{9,8},{10,11... | collective-permute-start | bytes 24584 | tf_op jit(solution)/shard_map/ppermute | solution.py:320
  12.7 1.9 %collective-permute-start.1 = (f32[2,8,128]{2,1,0:T(8,128)S(1)}, f32[2,8,128]{2,1,0:T(8,128)S(1)}, u32[]{:S(2)}, u32[]{:S(2)}) collective-permute-start(f32[2,8,128]{2,1,0:T(8,128)S(1)} %bitcast.6), channel_id=1, source_target_pairs={{1,2},{2,1},{0,0},{3,3},{5,6},{6,5},{4,4},{7,7},{9,10},{10,9},{8,8... | collective-permute-start | bytes 24584 | tf_op jit(solution)/shard_map/ppermute | solution.py:321
  14.6 1.2 %collective-permute-start.2 = (f32[1,8,128]{2,1,0:T(8,128)S(1)}, f32[1,8,128]{2,1,0:T(8,128)S(1)}, u32[]{:S(2)}, u32[]{:S(2)}) collective-permute-start(f32[1,8,128]{2,1,0:T(8,128)S(1)} %bitcast.10), channel_id=1, source_target_pairs={{0,28},{4,0},{8,4},{12,8},{16,12},{20,16},{24,20},{28,24},{1,29},{... | collective-permute-start | bytes 12296 | tf_op jit(solution)/shard_map/ppermute | solution.py:342
  15.9 1.5 %shard_map.77 = (f32[2,16,128]{2,1,0:T(8,128)S(1)}, f32[2,16,128]{2,1,0:T(8,128)S(1)}) custom-call(f32[2,8,128]{2,1,0:T(8,128)S(1)} %bitcast.7, f32[2,8,128]{2,1,0:T(8,128)S(1)} %bitcast.8, bf16[2,1,16,4096]{3,2,1,0:T(8,128)(2,1)S(1)} %copy-done.5, bf16[2,1,16,4096]{3,2,1,0:T(8,128)(2,1)S(1)} %copy-done.2, bf16[4,2,1,16,4096]{4,3,2,1,0:T(8,128)(2,1)S(1)} %copy-done), custom_call_target="tpu_custom_call" | custom-call | flops 1048576 | bytes 1589248 | tf_op jit(solution)/shard_map/pallas_call | solution.py:303
  17.4 6.4 %collective-permute-done.2.refs_3_ = f32[1,8,128]{2,1,0:T(8,128)S(1)} collective-permute-done((f32[1,8,128]{2,1,0:T(8,128)S(1)}, f32[1,8,128]{2,1,0:T(8,128)S(1)}, u32[]{:S(2)}, u32[]{:S(2)}) %collective-permute-start.2) | collective-permute-done | bytes 4128 | tf_op jit(solution)/shard_map/ppermute | solution.py:342
  23.8 2.4 %shard_map.80 = (f32[2,16,128]{2,1,0:T(8,128)S(1)}, f32[16,128]{1,0:T(8,128)S(1)}, f32[16,128]{1,0:T(8,128)S(1)}, f32[16,128]{1,0:T(8,128)S(1)}) custom-call(f32[2,16,128]{2,1,0:T(8,128)S(1)} %get-tuple-element.19.refs_0_, f32[2,8,128]{2,1,0:T(8,128)S(1)} %collective-permute-done.refs_1_, f32[2,8,128]{2,1,0:T(8,128)S(1)} %collective-permute-done.1.refs_2_, ...), custom_call_target="tpu_custom_call" | custom-call | flops 1048576 | bytes 2134016 | tf_op jit(solution)/shard_map/pallas_call | solution.py:303
  26.9 1.4 %collective-permute-start.11 = (f32[16,128]{1,0:T(8,128)S(1)}, f32[16,128]{1,0:T(8,128)S(1)}, u32[]{:S(2)}, u32[]{:S(2)}) collective-permute-start(f32[16,128]{1,0:T(8,128)S(1)} %get-tuple-element.27), channel_id=1, source_target_pairs={{0,24},{4,28},{8,16},{12,20},{16,8},{20,12},{24,0},{28,4},{1,25},{... | collective-permute-start | bytes 24584 | tf_op jit(solution)/shard_map/ppermute | solution.py:325
  28.3 2.2 %collective-permute-start.12 = (f32[16,128]{1,0:T(8,128)S(1)}, f32[16,128]{1,0:T(8,128)S(1)}, u32[]{:S(2)}, u32[]{:S(2)}) collective-permute-start(f32[16,128]{1,0:T(8,128)S(1)} %get-tuple-element.27), channel_id=1, source_target_pairs={{0,28},{4,24},{8,20},{12,16},{16,12},{20,8},{24,4},{28,0},{1,29},{... | collective-permute-start | bytes 24584 | tf_op jit(solution)/shard_map/ppermute | solution.py:325
  30.7 1.9 %collective-permute-start.7 = (f32[16,128]{1,0:T(8,128)S(1)}, f32[16,128]{1,0:T(8,128)S(1)}, u32[]{:S(2)}, u32[]{:S(2)}) collective-permute-start(f32[16,128]{1,0:T(8,128)S(1)} %get-tuple-element.26), channel_id=1, source_target_pairs={{0,8},{4,12},{8,0},{12,4},{16,24},{20,28},{24,16},{28,20},{1,9},{5... | collective-permute-start | bytes 24584 | tf_op jit(solution)/shard_map/ppermute | solution.py:325
  33.3 0.8 %collective-permute-start.6 = (f32[16,128]{1,0:T(8,128)S(1)}, f32[16,128]{1,0:T(8,128)S(1)}, u32[]{:S(2)}, u32[]{:S(2)}) collective-permute-start(f32[16,128]{1,0:T(8,128)S(1)} %get-tuple-element.25), channel_id=1, source_target_pairs={{0,4},{4,0},{8,12},{12,8},{16,20},{20,16},{24,28},{28,24},{1,5},{5... | collective-permute-start | bytes 24584 | tf_op jit(solution)/shard_map/ppermute | solution.py:325
  34.1 1.6 %collective-permute-done.8.refs_5_ = f32[16,128]{1,0:T(8,128)S(1)} collective-permute-done((f32[16,128]{1,0:T(8,128)S(1)}, f32[16,128]{1,0:T(8,128)S(1)}, u32[]{:S(2)}, u32[]{:S(2)}) %collective-permute-start.8) | collective-permute-done | bytes 8224 | tf_op jit(solution)/shard_map/ppermute | solution.py:325
  35.7 2.8 %shard_map.81 = (f32[2,8,128]{2,1,0:T(8,128)}, f32[2,16,128]{2,1,0:T(8,128)S(1)}, f32[2,16,128]{2,1,0:T(8,128)S(1)}) custom-call(f32[2,16,128]{2,1,0:T(8,128)S(1)} %get-tuple-element.23.refs_0_, bf16[2,1,16,4096]{3,2,1,0:T(8,128)(2,1)S(1)} %copy-done.4, f32[2,16,128]{2,1,0:T(8,128)S(1)} %get-tuple-element.24.refs_2_, ...), custom_call_target="tpu_custom_call" | custom-call | flops 1048576 | bytes 876544 | tf_op jit(solution)/shard_map/pallas_call | solution.py:303
  38.5 1.3 %collective-permute-start.13 = (f32[2,8,128]{2,1,0:T(8,128)}, f32[2,8,128]{2,1,0:T(8,128)S(1)}, u32[]{:S(2)}, u32[]{:S(2)}) collective-permute-start(f32[2,8,128]{2,1,0:T(8,128)} %get-tuple-element.28), channel_id=1, source_target_pairs={{0,1},{1,0},{2,3},{3,2},{4,5},{5,4},{6,7},{7,6},{8,9},{9,8},{10,11... | collective-permute-start | bytes 24584 | tf_op jit(solution)/shard_map/ppermute | solution.py:320
  39.8 1.9 %collective-permute-start.14 = (f32[2,8,128]{2,1,0:T(8,128)}, f32[2,8,128]{2,1,0:T(8,128)S(1)}, u32[]{:S(2)}, u32[]{:S(2)}) collective-permute-start(f32[2,8,128]{2,1,0:T(8,128)} %get-tuple-element.28), channel_id=1, source_target_pairs={{1,2},{2,1},{0,0},{3,3},{5,6},{6,5},{4,4},{7,7},{9,10},{10,9},{8,8... | collective-permute-start | bytes 24584 | tf_op jit(solution)/shard_map/ppermute | solution.py:321
  42.5 2.0 %collective-permute-done.14.refs_2_ = f32[2,8,128]{2,1,0:T(8,128)S(1)} collective-permute-done((f32[2,8,128]{2,1,0:T(8,128)}, f32[2,8,128]{2,1,0:T(8,128)S(1)}, u32[]{:S(2)}, u32[]{:S(2)}) %collective-permute-start.14) | collective-permute-done | bytes 8224 | tf_op jit(solution)/shard_map/ppermute | solution.py:321
  44.4 2.4 %shard_map.83 = (f32[2,16,128]{2,1,0:T(8,128)S(1)}, f32[16,128]{1,0:T(8,128)S(1)}, f32[16,128]{1,0:T(8,128)S(1)}, f32[16,128]{1,0:T(8,128)S(1)}) custom-call(f32[2,16,128]{2,1,0:T(8,128)S(1)} %shard_map.82.refs_0_, f32[2,8,128]{2,1,0:T(8,128)S(1)} %collective-permute-done.13.refs_1_, f32[2,8,128]{2,1,0:T(8,128)S(1)} %collective-permute-done.14.refs_2_, ...), custom_call_target="tpu_custom_call" | custom-call | flops 1048576 | bytes 1867776 | tf_op jit(solution)/shard_map/pallas_call | solution.py:303
  46.8 1.4 %collective-permute-start.16 = (f32[16,128]{1,0:T(8,128)S(1)}, f32[16,128]{1,0:T(8,128)S(1)}, u32[]{:S(2)}, u32[]{:S(2)}) collective-permute-start(f32[16,128]{1,0:T(8,128)S(1)} %get-tuple-element.33), channel_id=1, source_target_pairs={{0,4},{4,0},{8,12},{12,8},{16,20},{20,16},{24,28},{28,24},{1,5},{5... | collective-permute-start | bytes 24584 | tf_op jit(solution)/shard_map/ppermute | solution.py:325
  48.2 1.0 %collective-permute-start.17 = (f32[16,128]{1,0:T(8,128)S(1)}, f32[16,128]{1,0:T(8,128)S(1)}, u32[]{:S(2)}, u32[]{:S(2)}) collective-permute-start(f32[16,128]{1,0:T(8,128)S(1)} %get-tuple-element.34), channel_id=1, source_target_pairs={{0,8},{4,12},{8,0},{12,4},{16,24},{20,28},{24,16},{28,20},{1,9},{5... | collective-permute-start | bytes 24584 | tf_op jit(solution)/shard_map/ppermute | solution.py:325
  49.2 0.7 %collective-permute-start.18 = (f32[16,128]{1,0:T(8,128)S(1)}, f32[16,128]{1,0:T(8,128)S(1)}, u32[]{:S(2)}, u32[]{:S(2)}) collective-permute-start(f32[16,128]{1,0:T(8,128)S(1)} %get-tuple-element.34), channel_id=1, source_target_pairs={{0,12},{4,8},{8,4},{12,0},{16,28},{20,24},{24,20},{28,16},{1,13},{... | collective-permute-start | bytes 24584 | tf_op jit(solution)/shard_map/ppermute | solution.py:325
  50.5 1.2 %collective-permute-start.20 = (f32[16,128]{1,0:T(8,128)S(1)}, f32[16,128]{1,0:T(8,128)S(1)}, u32[]{:S(2)}, u32[]{:S(2)}) collective-permute-start(f32[16,128]{1,0:T(8,128)S(1)} %get-tuple-element.35), channel_id=1, source_target_pairs={{0,20},{4,16},{8,28},{12,24},{16,4},{20,0},{24,12},{28,8},{1,21},{... | collective-permute-start | bytes 24584 | tf_op jit(solution)/shard_map/ppermute | solution.py:325
  51.7 1.8 %collective-permute-start.21 = (f32[16,128]{1,0:T(8,128)S(1)}, f32[16,128]{1,0:T(8,128)S(1)}, u32[]{:S(2)}, u32[]{:S(2)}) collective-permute-start(f32[16,128]{1,0:T(8,128)S(1)} %get-tuple-element.35), channel_id=1, source_target_pairs={{0,24},{4,28},{8,16},{12,20},{16,8},{20,12},{24,0},{28,4},{1,25},{... | collective-permute-start | bytes 24584 | tf_op jit(solution)/shard_map/ppermute | solution.py:325
  53.5 0.7 %collective-permute-start.22 = (f32[16,128]{1,0:T(8,128)S(1)}, f32[16,128]{1,0:T(8,128)S(1)}, u32[]{:S(2)}, u32[]{:S(2)}) collective-permute-start(f32[16,128]{1,0:T(8,128)S(1)} %get-tuple-element.35), channel_id=1, source_target_pairs={{0,28},{4,24},{8,20},{12,16},{16,12},{20,8},{24,4},{28,0},{1,29},{... | collective-permute-start | bytes 24584 | tf_op jit(solution)/shard_map/ppermute | solution.py:325
  54.3 0.8 %collective-permute-done.21.refs_7_ = f32[16,128]{1,0:T(8,128)S(1)} collective-permute-done((f32[16,128]{1,0:T(8,128)S(1)}, f32[16,128]{1,0:T(8,128)S(1)}, u32[]{:S(2)}, u32[]{:S(2)}) %collective-permute-start.21) | collective-permute-done | bytes 8224 | tf_op jit(solution)/shard_map/ppermute | solution.py:325
  55.1 2.4 %collective-permute-done.22.refs_8_ = f32[16,128]{1,0:T(8,128)S(1)} collective-permute-done((f32[16,128]{1,0:T(8,128)S(1)}, f32[16,128]{1,0:T(8,128)S(1)}, u32[]{:S(2)}, u32[]{:S(2)}) %collective-permute-start.22) | collective-permute-done | bytes 8224 | tf_op jit(solution)/shard_map/ppermute | solution.py:325
  57.5 2.8 %shard_map.84 = f32[2,8,128]{2,1,0:T(8,128)} custom-call(f32[2,16,128]{2,1,0:T(8,128)S(1)} %get-tuple-element.32.refs_0_, bf16[2,1,16,4096]{3,2,1,0:T(8,128)(2,1)S(1)} %copy-done.2, f32[16,128]{1,0:T(8,128)S(1)} %collective-permute-done.16.refs_2_, f32[16,128]{1,0:T(8,128)S(1)} %collective-permute-done.17.refs_3_, ...), custom_call_target="tpu_custom_call" | custom-call | flops 1048576 | bytes 860160 | tf_op jit(solution)/shard_map/pallas_call | solution.py:303
  (39 shorter events, 3.6 us)
Async XLA Ops:
  0.6 15.2 %copy-start = (bf16[4,2,1,16,4096]{4,3,2,1,0:T(8,128)(2,1)S(1)}, bf16[4,2,1,16,4096]{4,3,2,1,0:T(8,128)(2,1)}, u32[]{:S(2)}) copy-start(bf16[4,2,1,16,4096]{4,3,2,1,0:T(8,128)(2,1)} %refs_3_.3) | copy-start | bytes 3145732
  0.6 1.0 %copy-start.1 = (bf16[2,1,16,4096]{3,2,1,0:T(8,128)(2,1)S(1)}, bf16[2,1,16,4096]{3,2,1,0:T(8,128)(2,1)}, u32[]{:S(2)}) copy-start(bf16[2,1,16,4096]{3,2,1,0:T(8,128)(2,1)} %refs_1_.5) | copy-start | bytes 786436
  1.7 0.9 %copy-start.3 = (bf16[2,1,16,4096]{3,2,1,0:T(8,128)(2,1)S(1)}, bf16[2,1,16,4096]{3,2,1,0:T(8,128)(2,1)}, u32[]{:S(2)}) copy-start(bf16[2,1,16,4096]{3,2,1,0:T(8,128)(2,1)} %refs_1_.4) | copy-start | bytes 786436
  5.0 1.9 %collective-permute-start.3 = (f32[16,4096]{1,0:T(8,128)S(1)}, f32[16,4096]{1,0:T(8,128)S(1)}, u32[]{:S(2)}, u32[]{:S(2)}) collective-permute-start(f32[16,4096]{1,0:T(8,128)S(1)} %get-tuple-element.20.refs_0_), channel_id=1, source_target_pairs={{0,4},{4,0},{8,12},{12,8},{16,20},{20,16},{24,28},{28,24},{1,5},{5... | collective-permute-start | bytes 786440 | tf_op jit(solution)/shard_map/ppermute | solution.py:325
  5.7 5.7 %copy-start.6 = (f32[2,1,1024]{2,1,0:T(1,128)S(1)}, f32[2,1,1024]{2,1,0:T(1,128)}, u32[]{:S(2)}) copy-start(f32[2,1,1024]{2,1,0:T(1,128)} %param.6) | copy-start | bytes 24580
  5.7 10.1 %copy-start.2 = (bf16[2,1,16,4096]{3,2,1,0:T(8,128)(2,1)S(1)}, bf16[2,1,16,4096]{3,2,1,0:T(8,128)(2,1)}, u32[]{:S(2)}) copy-start(bf16[2,1,16,4096]{3,2,1,0:T(8,128)(2,1)} %refs_1_.5) | copy-start | bytes 786436
  5.7 10.1 %copy-start.5 = (bf16[2,1,16,4096]{3,2,1,0:T(8,128)(2,1)S(1)}, bf16[2,1,16,4096]{3,2,1,0:T(8,128)(2,1)}, u32[]{:S(2)}) copy-start(bf16[2,1,16,4096]{3,2,1,0:T(8,128)(2,1)} %refs_2_.2) | copy-start | bytes 786436
  5.7 1.5 %collective-permute-start.4 = (f32[16,4096]{1,0:T(8,128)S(1)}, f32[16,4096]{1,0:T(8,128)S(1)}, u32[]{:S(2)}, u32[]{:S(2)}) collective-permute-start(f32[16,4096]{1,0:T(8,128)S(1)} %get-tuple-element.21.refs_1_), channel_id=1, source_target_pairs={{0,4},{4,0},{8,12},{12,8},{16,20},{20,16},{24,28},{28,24},{1,5},{5... | collective-permute-start | bytes 786440 | tf_op jit(solution)/shard_map/ppermute | solution.py:325
  9.8 6.0 %copy-start.7 = (f32[2,1,1024]{2,1,0:T(1,128)S(1)}, f32[2,1,1024]{2,1,0:T(1,128)}, u32[]{:S(2)}) copy-start(f32[2,1,1024]{2,1,0:T(1,128)} %param.7) | copy-start | bytes 24580
  9.8 14.0 %collective-permute-start.5 = (f32[16,4096]{1,0:T(8,128)S(1)}, f32[16,4096]{1,0:T(8,128)S(1)}, u32[]{:S(2)}, u32[]{:S(2)}) collective-permute-start(f32[16,4096]{1,0:T(8,128)S(1)} %get-tuple-element.22), channel_id=1, source_target_pairs={{0,8},{4,12},{8,0},{12,4},{16,24},{20,28},{24,16},{28,20},{1,9},{5... | collective-permute-start | bytes 786440 | tf_op jit(solution)/shard_map/ppermute | solution.py:325
  11.1 31.3 %collective-permute-start.15 = (f32[16,4096]{1,0:T(8,128)S(1)}, f32[16,4096]{1,0:T(8,128)S(1)}, u32[]{:S(2)}, u32[]{:S(2)}) collective-permute-start(f32[16,4096]{1,0:T(8,128)S(1)} %get-tuple-element.31), channel_id=1, source_target_pairs={{0,8},{4,12},{8,0},{12,4},{16,24},{20,28},{24,16},{28,20},{1,9},{5... | collective-permute-start | bytes 786440 | tf_op jit(solution)/shard_map/ppermute | solution.py:325
  11.4 12.4 %collective-permute-start = (f32[2,8,128]{2,1,0:T(8,128)S(1)}, f32[2,8,128]{2,1,0:T(8,128)S(1)}, u32[]{:S(2)}, u32[]{:S(2)}) collective-permute-start(f32[2,8,128]{2,1,0:T(8,128)S(1)} %bitcast.5), channel_id=1, source_target_pairs={{0,1},{1,0},{2,3},{3,2},{4,5},{5,4},{6,7},{7,6},{8,9},{9,8},{10,11... | collective-permute-start | bytes 24584 | tf_op jit(solution)/shard_map/ppermute | solution.py:320
  12.7 11.2 %collective-permute-start.1 = (f32[2,8,128]{2,1,0:T(8,128)S(1)}, f32[2,8,128]{2,1,0:T(8,128)S(1)}, u32[]{:S(2)}, u32[]{:S(2)}) collective-permute-start(f32[2,8,128]{2,1,0:T(8,128)S(1)} %bitcast.6), channel_id=1, source_target_pairs={{1,2},{2,1},{0,0},{3,3},{5,6},{6,5},{4,4},{7,7},{9,10},{10,9},{8,8... | collective-permute-start | bytes 24584 | tf_op jit(solution)/shard_map/ppermute | solution.py:321
  14.6 9.2 %collective-permute-start.2 = (f32[1,8,128]{2,1,0:T(8,128)S(1)}, f32[1,8,128]{2,1,0:T(8,128)S(1)}, u32[]{:S(2)}, u32[]{:S(2)}) collective-permute-start(f32[1,8,128]{2,1,0:T(8,128)S(1)} %bitcast.10), channel_id=1, source_target_pairs={{0,28},{4,0},{8,4},{12,8},{16,12},{20,16},{24,20},{28,24},{1,29},{... | collective-permute-start | bytes 12296 | tf_op jit(solution)/shard_map/ppermute | solution.py:342
  15.9 8.0 %copy-start.4 = (bf16[2,1,16,4096]{3,2,1,0:T(8,128)(2,1)S(1)}, bf16[2,1,16,4096]{3,2,1,0:T(8,128)(2,1)}, u32[]{:S(2)}) copy-start(bf16[2,1,16,4096]{3,2,1,0:T(8,128)(2,1)} %refs_1_.4) | copy-start | bytes 786436
  26.2 4.5 %collective-permute-start.10 = (f32[16,128]{1,0:T(8,128)S(1)}, f32[16,128]{1,0:T(8,128)S(1)}, u32[]{:S(2)}, u32[]{:S(2)}) collective-permute-start(f32[16,128]{1,0:T(8,128)S(1)} %get-tuple-element.27), channel_id=1, source_target_pairs={{0,20},{4,16},{8,28},{12,24},{16,4},{20,0},{24,12},{28,8},{1,21},{... | collective-permute-start | bytes 24584 | tf_op jit(solution)/shard_map/ppermute | solution.py:325
  26.9 5.7 %collective-permute-start.11 = (f32[16,128]{1,0:T(8,128)S(1)}, f32[16,128]{1,0:T(8,128)S(1)}, u32[]{:S(2)}, u32[]{:S(2)}) collective-permute-start(f32[16,128]{1,0:T(8,128)S(1)} %get-tuple-element.27), channel_id=1, source_target_pairs={{0,24},{4,28},{8,16},{12,20},{16,8},{20,12},{24,0},{28,4},{1,25},{... | collective-permute-start | bytes 24584 | tf_op jit(solution)/shard_map/ppermute | solution.py:325
  28.3 5.0 %collective-permute-start.12 = (f32[16,128]{1,0:T(8,128)S(1)}, f32[16,128]{1,0:T(8,128)S(1)}, u32[]{:S(2)}, u32[]{:S(2)}) collective-permute-start(f32[16,128]{1,0:T(8,128)S(1)} %get-tuple-element.27), channel_id=1, source_target_pairs={{0,28},{4,24},{8,20},{12,16},{16,12},{20,8},{24,4},{28,0},{1,29},{... | collective-permute-start | bytes 24584 | tf_op jit(solution)/shard_map/ppermute | solution.py:325
  30.5 3.6 %collective-permute-start.9 = (f32[16,128]{1,0:T(8,128)S(1)}, f32[16,128]{1,0:T(8,128)S(1)}, u32[]{:S(2)}, u32[]{:S(2)}) collective-permute-start(f32[16,128]{1,0:T(8,128)S(1)} %get-tuple-element.27), channel_id=1, source_target_pairs={{0,16},{4,20},{8,24},{12,28},{16,0},{20,4},{24,8},{28,12},{1,17},{... | collective-permute-start | bytes 24584 | tf_op jit(solution)/shard_map/ppermute | solution.py:325
  30.7 3.4 %collective-permute-start.7 = (f32[16,128]{1,0:T(8,128)S(1)}, f32[16,128]{1,0:T(8,128)S(1)}, u32[]{:S(2)}, u32[]{:S(2)}) collective-permute-start(f32[16,128]{1,0:T(8,128)S(1)} %get-tuple-element.26), channel_id=1, source_target_pairs={{0,8},{4,12},{8,0},{12,4},{16,24},{20,28},{24,16},{28,20},{1,9},{5... | collective-permute-start | bytes 24584 | tf_op jit(solution)/shard_map/ppermute | solution.py:325
  32.6 3.1 %collective-permute-start.8 = (f32[16,128]{1,0:T(8,128)S(1)}, f32[16,128]{1,0:T(8,128)S(1)}, u32[]{:S(2)}, u32[]{:S(2)}) collective-permute-start(f32[16,128]{1,0:T(8,128)S(1)} %get-tuple-element.26), channel_id=1, source_target_pairs={{0,12},{4,8},{8,4},{12,0},{16,28},{20,24},{24,20},{28,16},{1,13},{... | collective-permute-start | bytes 24584 | tf_op jit(solution)/shard_map/ppermute | solution.py:325
  33.3 2.4 %collective-permute-start.6 = (f32[16,128]{1,0:T(8,128)S(1)}, f32[16,128]{1,0:T(8,128)S(1)}, u32[]{:S(2)}, u32[]{:S(2)}) collective-permute-start(f32[16,128]{1,0:T(8,128)S(1)} %get-tuple-element.25), channel_id=1, source_target_pairs={{0,4},{4,0},{8,12},{12,8},{16,20},{20,16},{24,28},{28,24},{1,5},{5... | collective-permute-start | bytes 24584 | tf_op jit(solution)/shard_map/ppermute | solution.py:325
  38.5 3.9 %collective-permute-start.13 = (f32[2,8,128]{2,1,0:T(8,128)}, f32[2,8,128]{2,1,0:T(8,128)S(1)}, u32[]{:S(2)}, u32[]{:S(2)}) collective-permute-start(f32[2,8,128]{2,1,0:T(8,128)} %get-tuple-element.28), channel_id=1, source_target_pairs={{0,1},{1,0},{2,3},{3,2},{4,5},{5,4},{6,7},{7,6},{8,9},{9,8},{10,11... | collective-permute-start | bytes 24584 | tf_op jit(solution)/shard_map/ppermute | solution.py:320
  39.8 4.6 %collective-permute-start.14 = (f32[2,8,128]{2,1,0:T(8,128)}, f32[2,8,128]{2,1,0:T(8,128)S(1)}, u32[]{:S(2)}, u32[]{:S(2)}) collective-permute-start(f32[2,8,128]{2,1,0:T(8,128)} %get-tuple-element.28), channel_id=1, source_target_pairs={{1,2},{2,1},{0,0},{3,3},{5,6},{6,5},{4,4},{7,7},{9,10},{10,9},{8,8... | collective-permute-start | bytes 24584 | tf_op jit(solution)/shard_map/ppermute | solution.py:321
  46.8 4.9 %collective-permute-start.16 = (f32[16,128]{1,0:T(8,128)S(1)}, f32[16,128]{1,0:T(8,128)S(1)}, u32[]{:S(2)}, u32[]{:S(2)}) collective-permute-start(f32[16,128]{1,0:T(8,128)S(1)} %get-tuple-element.33), channel_id=1, source_target_pairs={{0,4},{4,0},{8,12},{12,8},{16,20},{20,16},{24,28},{28,24},{1,5},{5... | collective-permute-start | bytes 24584 | tf_op jit(solution)/shard_map/ppermute | solution.py:325
  48.2 5.4 %collective-permute-start.17 = (f32[16,128]{1,0:T(8,128)S(1)}, f32[16,128]{1,0:T(8,128)S(1)}, u32[]{:S(2)}, u32[]{:S(2)}) collective-permute-start(f32[16,128]{1,0:T(8,128)S(1)} %get-tuple-element.34), channel_id=1, source_target_pairs={{0,8},{4,12},{8,0},{12,4},{16,24},{20,28},{24,16},{28,20},{1,9},{5... | collective-permute-start | bytes 24584 | tf_op jit(solution)/shard_map/ppermute | solution.py:325
  49.2 5.1 %collective-permute-start.18 = (f32[16,128]{1,0:T(8,128)S(1)}, f32[16,128]{1,0:T(8,128)S(1)}, u32[]{:S(2)}, u32[]{:S(2)}) collective-permute-start(f32[16,128]{1,0:T(8,128)S(1)} %get-tuple-element.34), channel_id=1, source_target_pairs={{0,12},{4,8},{8,4},{12,0},{16,28},{20,24},{24,20},{28,16},{1,13},{... | collective-permute-start | bytes 24584 | tf_op jit(solution)/shard_map/ppermute | solution.py:325
  49.9 4.4 %collective-permute-start.19 = (f32[16,128]{1,0:T(8,128)S(1)}, f32[16,128]{1,0:T(8,128)S(1)}, u32[]{:S(2)}, u32[]{:S(2)}) collective-permute-start(f32[16,128]{1,0:T(8,128)S(1)} %get-tuple-element.35), channel_id=1, source_target_pairs={{0,16},{4,20},{8,24},{12,28},{16,0},{20,4},{24,8},{28,12},{1,17},{... | collective-permute-start | bytes 24584 | tf_op jit(solution)/shard_map/ppermute | solution.py:325
  50.5 3.8 %collective-permute-start.20 = (f32[16,128]{1,0:T(8,128)S(1)}, f32[16,128]{1,0:T(8,128)S(1)}, u32[]{:S(2)}, u32[]{:S(2)}) collective-permute-start(f32[16,128]{1,0:T(8,128)S(1)} %get-tuple-element.35), channel_id=1, source_target_pairs={{0,20},{4,16},{8,28},{12,24},{16,4},{20,0},{24,12},{28,8},{1,21},{... | collective-permute-start | bytes 24584 | tf_op jit(solution)/shard_map/ppermute | solution.py:325
  51.7 3.4 %collective-permute-start.21 = (f32[16,128]{1,0:T(8,128)S(1)}, f32[16,128]{1,0:T(8,128)S(1)}, u32[]{:S(2)}, u32[]{:S(2)}) collective-permute-start(f32[16,128]{1,0:T(8,128)S(1)} %get-tuple-element.35), channel_id=1, source_target_pairs={{0,24},{4,28},{8,16},{12,20},{16,8},{20,12},{24,0},{28,4},{1,25},{... | collective-permute-start | bytes 24584 | tf_op jit(solution)/shard_map/ppermute | solution.py:325
  53.5 4.0 %collective-permute-start.22 = (f32[16,128]{1,0:T(8,128)S(1)}, f32[16,128]{1,0:T(8,128)S(1)}, u32[]{:S(2)}, u32[]{:S(2)}) collective-permute-start(f32[16,128]{1,0:T(8,128)S(1)} %get-tuple-element.35), channel_id=1, source_target_pairs={{0,28},{4,24},{8,20},{12,16},{16,12},{20,8},{24,4},{28,0},{1,29},{... | collective-permute-start | bytes 24584 | tf_op jit(solution)/shard_map/ppermute | solution.py:325

commit v3 on v2

v3 whole, which is shorter than its diff:
```python
import functools

import jax
import jax.numpy as jnp
from jax import lax
from jax.experimental import pallas as pl
from jax.experimental.pallas import tpu as pltpu
from jax.sharding import PartitionSpec as P

LANES = 128
F32 = jnp.float32
BF16 = jnp.bfloat16


def lane_bit(shape, shift):
    return (lax.broadcasted_iota(jnp.int32, shape, len(shape) - 1) & shift) != 0


def segment_sums(leaf, tiles, rows):
    shape = (rows, LANES)

    def node(base, stride, shift):
        if stride == tiles:
            return leaf(base)
        low = node(base, stride * 2, shift * 2)
        high = node(base + stride, stride * 2, shift * 2)
        low = low + pltpu.roll(low, LANES - shift, 1)
        high = high + pltpu.roll(high, shift, 1)
        return jnp.where(lane_bit(shape, shift), high, low)

    part = node(0, 1, 2)
    odd = lane_bit(shape, 1)
    part = part + jnp.where(odd, pltpu.roll(part, 1, 1), pltpu.roll(part, LANES - 1, 1))
    upper = lane_bit(shape, LANES // 2)
    return jnp.where(upper == odd, part, pltpu.roll(part, LANES // 2, 1))


def apply(terms):
    rows = terms[0][1].shape[0]
    tiles = LANES // 4

    def leaf(t):
        return sum(read(t).astype(F32) * vector for read, vector in terms)

    return segment_sums(leaf, tiles, rows)


def reader(ref, *index):
    return lambda t: ref[(*index, slice(None), slice(t * LANES, (t + 1) * LANES))]


def spread(scratch, raw):
    upper = lane_bit(raw.shape, LANES // 2)
    other = pltpu.roll(raw, LANES // 2, 1)
    half = raw.shape[0]
    scratch[pl.ds(0, half, stride=2), :] = jnp.where(upper, other, raw)
    scratch[pl.ds(1, half, stride=2), :] = jnp.where(upper, raw, other)
    return scratch[...]


def gather_pairs(scratch, vector):
    scratch[...] = vector
    half = vector.shape[0] // 2
    even = scratch[pl.ds(0, half, stride=2), :]
    odd = scratch[pl.ds(1, half, stride=2), :]
    return jnp.where(lane_bit(even.shape, LANES // 2), odd, even)


def shifted(vector, down):
    rows = vector.shape[0]
    row = lax.broadcasted_iota(jnp.int32, vector.shape, 0)
    if down:
        return jnp.where(row == 0, 0.0, pltpu.roll(vector, 1, 0))
    return jnp.where(row == rows - 1, 0.0, pltpu.roll(vector, rows - 1, 0))


def to_rows(scratch, read, rows, species):
    for a in range(species):
        tile = read(a // 2).astype(F32)
        if a % 2:
            tile = pltpu.roll(tile, LANES // 2, 1)
        scratch[pl.ds(a, rows, stride=species), :] = tile


def halves(a):
    high = a.astype(BF16)
    return high, (a - high.astype(F32)).astype(BF16)


def dot(a, b, dims=((1,), (0,))):
    return lax.dot_general(a, b, (dims, ((), ())), preferred_element_type=F32)


def turn(scratch, out, first, pairs, species):
    unit = (
        lax.broadcasted_iota(jnp.int32, (species, species), 0)
        == lax.broadcasted_iota(jnp.int32, (species, species), 1)
    ).astype(F32).astype(BF16)
    for pair in range(pairs):
        block = scratch[pair * LANES : (pair + 1) * LANES, :species].astype(BF16)
        out[pl.ds(first + pair, species, stride=pairs), :] = dot(unit, block, ((1,), (1,)))


def both(block):
    upper = lane_bit(block.shape, LANES // 2)
    zero = jnp.zeros_like(block)
    return jnp.concatenate([jnp.where(upper, zero, block), jnp.where(upper, block, zero)], 0)


def multiply(earlier, later, exact):
    if exact:
        return dot(earlier.astype(BF16), both(later).astype(BF16))
    earlier_high, earlier_low = halves(earlier)
    high, low = halves(both(later))
    return dot(earlier_high, high) + (dot(earlier_low, high) + dot(earlier_high, low))


def turned(ref, vector, first=0, swapped=None):
    pairs = vector.shape[0]
    lane = lax.broadcasted_iota(jnp.int32, vector.shape, 1)
    side = lane & (LANES // 2)
    refs = [(ref, first)] if swapped is None else [(ref, 0), (swapped, 0)]
    sums = [None] * 4
    total = LANES // 2
    share = total // len(refs)
    for b in range(total):
        held, at = refs[b // share]
        row = at + (b % share) * pairs
        term = held[row : row + pairs, :] * jnp.take_along_axis(vector, side + b, 1)
        sums[b % 4] = term if sums[b % 4] is None else sums[b % 4] + term
    return (sums[0] + sums[1]) + (sums[2] + sums[3])


def prep_kernel(lower, upper, lower_turned, upper_turned, lower_products, upper_products, rows_scratch):
    planes, _, rows, width = lower.shape
    species = LANES // 2
    pairs = rows // 2
    size = species * pairs
    for blocks, maps, products, order in (
        (lower, lower_turned, lower_products, list(range(planes))),
        (upper, upper_turned, upper_products, list(range(planes))[::-1]),
    ):
        for plane in order:
            to_rows(rows_scratch, reader(blocks, plane, 0), rows, species)
            turn(rows_scratch, maps, plane * size, pairs, species)
        for step, plane in enumerate(order):
            at = pl.ds(plane * size, size)
            if step == 0:
                products[at, :] = -maps[at, :]
                continue
            for pair in range(pairs):
                here = pl.ds(plane * size + pair, species, stride=pairs)
                before = pl.ds(order[step - 1] * size + pair, species, stride=pairs)
                later = -maps[here, :]
                if step == 1:
                    products[here, :] = multiply(products[before, :], later, True)
                else:
                    products[here, :] = multiply(products[before, :], later, False)


def join_kernel(level, full, pairs, own_planes, *refs):
    here = (lax.axis_index("gx") >> level) & 1
    core = lax.axis_index("gx") & 1
    species = LANES // 2
    size = species * pairs
    half = size // 2
    inputs, outputs = refs[: len(own_planes)], refs[len(own_planes) :]
    each = len(inputs) // 2
    for side in (0, 1):
        later_is_own = here == (1 if side == 0 else 0)
        own, *partner = inputs[side * each : (side + 1) * each]
        first = own_planes[side * each] * size
        outs = outputs[side * (len(outputs) // 2) : (side + 1) * (len(outputs) // 2)]
        for pair in range(pairs):
            mine = own[pl.ds(first + pair, species, stride=pairs), :]
            if len(partner) == 1:
                theirs = partner[0][pl.ds(pair, species, stride=pairs), :]
            else:
                near = partner[0][pl.ds(pair, species // 2, stride=pairs), :]
                far = partner[1][pl.ds(pair, species // 2, stride=pairs), :]
                theirs = jnp.where(
                    core == 0, jnp.concatenate([near, far], 0), jnp.concatenate([far, near], 0)
                )
            earlier = jnp.where(later_is_own, theirs, mine)
            later = jnp.where(later_is_own, mine, theirs)
            kept = jnp.where(core == 0, earlier[: species // 2], earlier[species // 2 :])
            if full:
                product = multiply(earlier, later, False)
                outs[0][pl.ds(pair, species, stride=pairs), :] = product
                kept = jnp.where(core == 0, product[: species // 2], product[species // 2 :])
            else:
                kept = multiply(kept, later, False)
            outs[-1][pl.ds(pair, species // 2, stride=pairs), :] = kept


def base_kernel(start, source, diag, upper, side, rhs, base, scratch):
    planes = start.shape[0]
    vectors = [spread(scratch, start[p]) for p in range(planes)]
    for p in range(planes):
        own = apply([(reader(diag, p, 0), spread(scratch, source[p]))])
        terms = [
            (reader(side, 0, p, 0), shifted(vectors[p], True)),
            (reader(side, 1, p, 0), shifted(vectors[p], False)),
        ]
        if p + 1 < planes:
            terms.append((reader(upper, p, 0), vectors[p + 1]))
        around = apply(terms)
        rhs[p] = gather_pairs(scratch, own)
        base[p] = gather_pairs(scratch, own - around)


def partner_map(refs, vector):
    if len(refs) == 1:
        return turned(refs[0], vector)
    core = lax.axis_index("gx") & 1
    quarter = LANES // 4
    inner = lane_bit(vector.shape, quarter)
    crossed_over = jnp.where(
        inner, pltpu.roll(vector, quarter, 1), pltpu.roll(vector, LANES - quarter, 1)
    )
    return turned(refs[0], jnp.where(core == 0, vector, crossed_over), 0, refs[1])


def outgoing(offset, partners, here, slots):
    vectors = [offset]
    for level, refs in enumerate(partners):
        passed = partner_map(refs, vectors[-1])
        vectors.append(jnp.where((here >> level) & 1 == 0, passed, vectors[-1]))
    place = lax.axis_index("gx")
    for target in range(slots.shape[0]):
        apart = place ^ target
        value = vectors[0]
        for level in range(1, len(vectors)):
            value = jnp.where(apart >= 1 << level, vectors[level], value)
        slots[target] = value


def incoming(got, partners, here, reverse):
    count = got.shape[0]
    entering = None
    for level in range(len(partners) + 1)[::-1]:
        total = None
        for source in range(count):
            place = count - 1 - source if reverse else source
            term = jnp.where((place >> level) == (here >> level) - 1, got[source], 0.0)
            total = term if total is None else total + term
        if entering is not None:
            total = total + partner_map(partners[level], entering)
        before = jnp.zeros_like(total) if entering is None else entering
        entering = jnp.where((here >> level) & 1 == 1, total, before)
    return entering


def grouped(refs, levels):
    return [list(refs[:1])] + [list(refs[i : i + 2]) for i in range(1, 2 * levels - 3, 2)]


def beside(axis, paired, other):
    place, count = lax.axis_index(axis), lax.axis_size(axis)
    odd = place & 1 == 1
    low = jnp.where(odd, paired, other)
    high = jnp.where(odd, other, paired)
    return jnp.where(place == 0, 0.0, low), jnp.where(place == count - 1, 0.0, high)


def forward_offset_kernel(levels, base, paired, other, ahead, side, upper, lower, *rest):
    *partners, drive, offsets, slots, scratch = rest
    planes = base.shape[0]
    size = base.shape[1] * LANES // 2
    here = lax.axis_index("gx")
    last = here == lax.axis_size("gx") - 1
    previous = None
    for p in range(planes):
        low, high = beside("gy", paired[p], other[p])
        terms = [
            (reader(side, 0, p, 0), spread(scratch, low)),
            (reader(side, 1, p, 0), spread(scratch, high)),
        ]
        if p + 1 == planes:
            beyond = jnp.where(last, 0.0, ahead[0])
            terms.append((reader(upper, p, 0), spread(scratch, beyond)))
        fresh = base[p] - gather_pairs(scratch, apply(terms))
        drive[p] = fresh
        if previous is not None:
            fresh = fresh - turned(lower, previous, p * size)
        offsets[p] = fresh
        previous = fresh
    outgoing(previous, grouped(partners, levels), here, slots)


def forward_kernel(levels, got, drive, offsets, rhs, products, *rest):
    *partners, out, copies, base = rest
    planes = drive.shape[0]
    size = drive.shape[1] * LANES // 2
    entering = incoming(got, grouped(partners, levels), lax.axis_index("gx"), False)
    for p in range(planes):
        value = offsets[p] + turned(products, entering, p * size)
        base[p] = rhs[p] - (drive[p] - value)
        out[p] = value
        for target in range(copies.shape[0]):
            copies[target, p] = value


def side_kernel(base, vectors, side, out, scratch):
    for p in range(base.shape[0]):
        vector = spread(scratch, vectors[p])
        around = apply(
            [
                (reader(side, 0, p, 0), shifted(vector, True)),
                (reader(side, 1, p, 0), shifted(vector, False)),
            ]
        )
        out[p] = base[p] - gather_pairs(scratch, around)


def backward_offset_kernel(levels, base, got, side, upper, *rest):
    *partners, offsets, slots, scratch = rest
    planes = base.shape[0]
    size = base.shape[1] * LANES // 2
    row, rows = lax.axis_index("gy"), lax.axis_size("gy")
    here = lax.axis_size("gx") - 1 - lax.axis_index("gx")
    previous = None
    for p in range(planes)[::-1]:
        low = jnp.where(row == 0, 0.0, got[jnp.maximum(row - 1, 0), p])
        high = jnp.where(row == rows - 1, 0.0, got[jnp.minimum(row + 1, rows - 1), p])
        around = apply(
            [
                (reader(side, 0, p, 0), spread(scratch, low)),
                (reader(side, 1, p, 0), spread(scratch, high)),
            ]
        )
        fresh = base[p] - gather_pairs(scratch, around)
        if previous is not None:
            fresh = fresh - turned(upper, previous, p * size)
        offsets[p] = fresh
        previous = fresh
    outgoing(previous, grouped(partners, levels), here, slots)


def backward_kernel(levels, got, offsets, products, *rest):
    *partners, out = rest
    size = offsets.shape[1] * LANES // 2
    here = lax.axis_size("gx") - 1 - lax.axis_index("gx")
    entering = incoming(got, grouped(partners, levels), here, True)
    for p in range(offsets.shape[0]):
        out[p] = offsets[p] + turned(products, entering, p * size)


def call(kernel, operands, outs, scratch, micros):
    arrays = [o[0] if isinstance(o, tuple) else o for o in operands]
    parts = [(i, o[1], o[2]) for i, o in enumerate(operands) if isinstance(o, tuple)]
    buffers = [pltpu.VMEM((size,) + arrays[i].shape[1:], arrays[i].dtype) for i, _, size in parts]
    outs = [jax.ShapeDtypeStruct(shape, F32) for shape in outs]
    moved = sum(a.size * a.dtype.itemsize for a in arrays)

    def body(*refs):
        refs = list(refs)
        if parts:
            held, semaphores = refs[-len(parts) - 1 : -1], refs[-1]
            refs = refs[: -len(parts) - 1]
            copies = []
            for k, (i, first, size) in enumerate(parts):
                copies.append(
                    pltpu.make_async_copy(refs[i].at[pl.ds(first, size)], held[k], semaphores.at[k])
                )
                copies[-1].start()
                refs[i] = held[k]
            for copy in copies:
                copy.wait()
        kernel(*refs)

    inside = [pltpu.VMEM(shape, F32) for shape in scratch] + buffers
    if parts:
        inside.append(pltpu.SemaphoreType.DMA((len(parts),)))
    held = [i for i, _, _ in parts]
    return pl.pallas_call(
        body,
        out_shape=outs,
        in_specs=[
            pl.BlockSpec(memory_space=pl.ANY if i in held else pltpu.VMEM) for i in range(len(arrays))
        ],
        out_specs=[pl.BlockSpec(memory_space=pltpu.VMEM) for _ in outs],
        scratch_shapes=inside,
        compiler_params=pltpu.CompilerParams(vmem_limit_bytes=24 << 20),
        cost_estimate=pl.CostEstimate(flops=int(micros * 1.15e9), bytes_accessed=moved, transcendentals=0),
    )(*arrays)


def swaps(block, axis):
    count = lax.axis_size(axis)
    other = [(i, (i + 1 if i & 1 else i - 1)) for i in range(1, count - 1)]
    other += [(0, 0), (count - 1, count - 1)]
    paired = lax.ppermute(block, axis, [(i, i ^ 1) for i in range(count)])
    return paired, lax.ppermute(block, axis, other)


def crossed(block, axis, distance):
    return lax.ppermute(block, axis, [(i, i ^ distance) for i in range(lax.axis_size(axis))])


def exchange(slots, axis):
    return lax.all_to_all(slots, axis, 0, 0)


def local(start, source, diag_inverse, x_lower, x_upper, side_blocks):
    planes, _, depth, width = x_lower.shape
    species = start.shape[2] // depth
    pairs = depth // 2
    count, rows = lax.axis_size("gx"), lax.axis_size("gy")
    levels = count.bit_length() - 1
    size = species * pairs
    one = (pairs, LANES)
    vec = (planes,) + one
    maps = (planes * size, LANES)
    whole, half = (size, LANES), (size // 2, LANES)
    dup = (depth, LANES)
    slots = (count,) + one
    start = start.reshape(vec)
    source = source.reshape(vec)

    paired, other = swaps(start, "gy")
    ahead = lax.ppermute(start[:1], "gx", [(i, (i - 1) % count) for i in range(count)])

    lower, upper, lower_products, upper_products = call(
        prep_kernel, [x_lower, x_upper], [maps] * 4, [(depth * species, LANES)], 2.0
    )
    owns = [(lower_products, planes - 1), (upper_products, 0)]
    partners = [[], []]
    for level in range(levels - 1):
        got = []
        for side, (own, plane) in enumerate(owns):
            if level == 0:
                got.append([crossed(own[plane * size : (plane + 1) * size], "gx", 1)])
            else:
                mine = crossed(kept[side], "gx", 1 << level)
                got.append([mine, crossed(mine, "gx", 1)])
            partners[side] += got[side]
        if level + 2 < levels:
            full = level + 3 < levels
            operands, places = [], []
            for (own, plane), parts in zip(owns, got):
                operands += [own] + parts
                places += [plane] + [0] * len(parts)
            outs = call(
                functools.partial(join_kernel, level, full, pairs, places),
                operands,
                ([whole, half] if full else [half]) * 2,
                [],
                1.5,
            )
            kept = [outs[1], outs[3]] if full else outs
            owns = [(outs[0], 0), (outs[2 if full else 1], 0)]

    near = (side_blocks, 0, 2)
    vertical = (side_blocks, 2, 2)
    rhs, base = call(
        base_kernel, [start, source, diag_inverse, x_upper, vertical], [vec, vec], [dup], 1.5
    )
    drive, offsets, sent = call(
        functools.partial(forward_offset_kernel, levels),
        [base, paired, other, ahead, near, x_upper, lower] + partners[0],
        [vec, vec, slots],
        [dup],
        1.5,
    )
    forward, copies, base = call(
        functools.partial(forward_kernel, levels),
        [exchange(sent, "gx"), drive, offsets, rhs, lower_products] + partners[0],
        [vec, (rows,) + vec, vec],
        [],
        1.0,
    )
    beyond = exchange(copies, "gy")
    (base,) = call(side_kernel, [base, forward, vertical], [vec], [dup], 0.7)
    offsets, sent = call(
        functools.partial(backward_offset_kernel, levels),
        [base, beyond, near, upper] + partners[1],
        [vec, slots],
        [dup],
        1.5,
    )
    (result,) = call(
        functools.partial(backward_kernel, levels),
        [exchange(sent, "gx"), offsets, upper_products] + partners[1],
        [vec],
        [],
        1.0,
    )
    shape = (planes, 1, depth * species)
    return forward.reshape(shape), result.reshape(shape)


def solution(mesh):
    return jax.shard_map(
        local,
        mesh=mesh,
        in_specs=(
            P("gx", "gy", None),
            P("gx", "gy", None),
            P("gx", "gy", None, None),
            P("gx", "gy", None, None),
            P("gx", "gy", None, None),
            P(None, "gx", "gy", None, None),
        ),
        out_specs=(P("gx", "gy", None), P("gx", "gy", None)),
        check_vma=False,
    )
```

time: 60.6 us -> 51.4 us (0.85)
  the two profiles are of different devices: /device:TPU:17 before, /device:TPU:0 now
where the time goes in v3:
time: 51.4 us; the launch traced here: 51 us
  starting transfers between devices  18.4 us (36%)
  Pallas kernels  12.5 us (24%)
  waiting for transfers between devices  9.89 us (19%)
  blocking collectives  7.22 us (14%)
  local copies, waits for them, and re-layouts  2.22 us (4%)
  between operations  0.78 us (2%)
    pallas_call x8, Pallas kernels, call(): pl.pallas_call(body, out_shape=outs, in_specs=[pl.BlockSpec(memory_space=...  12.5 us
    all_to_all x2, waiting for transfers between devices, exchange(): return lax.all_to_all(slots, axis, 0, 0)  8.71 us
    all_to_all x2, starting transfers between devices, exchange(): return lax.all_to_all(slots, axis, 0, 0)  7.63 us
    all_to_all x1, blocking collectives, exchange(): return lax.all_to_all(slots, axis, 0, 0)  7.22 us
    ppermute x6, starting transfers between devices, crossed(): lax.ppermute(block, axis, [(i, i ^ distance) for i in range(lax.axis_size...  5.22 us
    ppermute x1, starting transfers between devices, swaps(): paired = lax.ppermute(block, axis, [(i, i ^ 1) for i in range(count)])  4.46 us
    unnamed x20, local copies, waits for them, and re-layouts  2.18 us
    ppermute x6, waiting for transfers between devices, crossed(): lax.ppermute(block, axis, [(i, i ^ distance) for i in range(lax.axis_size...  1.17 us
  transfers between devices with their start and end apart: 11, of which 4 were waited for; matrix products, arithmetic and copies ran while one was open for 0% of the time, Pallas kernels for 13%

profile of v3, /device:TPU:0, one launch (start us, length us, event | category | flops | bytes accessed | tf_op | source)
XLA Modules:
  0.0 51.0 jit_solution(2286069782673859980)
XLA Ops:
  0.6 0.9 %copy-done.2 = bf16[2,1,16,4096]{3,2,1,0:T(8,128)(2,1)S(1)} copy-done((bf16[2,1,16,4096]{3,2,1,0:T(8,128)(2,1)S(1)}, bf16[2,1,16,4096]{3,2,1,0:T(8,128)(2,1)}, u32[]{:S(2)}) %copy-start.2) | copy-done | bytes 262168
  1.6 0.9 %copy-done.4 = bf16[2,1,16,4096]{3,2,1,0:T(8,128)(2,1)S(1)} copy-done((bf16[2,1,16,4096]{3,2,1,0:T(8,128)(2,1)S(1)}, bf16[2,1,16,4096]{3,2,1,0:T(8,128)(2,1)}, u32[]{:S(2)}) %copy-start.4) | copy-done | bytes 262168
  2.5 2.2 %shard_map.78 = (f32[1024,128]{1,0:T(8,128)S(1)}, f32[1024,128]{1,0:T(8,128)S(1)}, f32[1024,128]{1,0:T(8,128)S(1)}, f32[1024,128]{1,0:T(8,128)S(1)}) custom-call(bf16[2,1,16,4096]{3,2,1,0:T(8,128)(2,1)S(1)} %copy-done.2, bf16[2,1,16,4096]{3,2,1,0:T(8,128)(2,1)S(1)} %copy-done.4), custom_call_target="tpu_custom_call" | custom-call | flops 2300000000 | bytes 524288 | tf_op jit(solution)/shard_map/pallas_call | solution.py:376
  4.7 0.5 %collective-permute-start.4 = (f32[512,128]{1,0:T(8,128)S(1)}, f32[512,128]{1,0:T(8,128)S(1)}, u32[]{:S(2)}, u32[]{:S(2)}) collective-permute-start(f32[512,128]{1,0:T(8,128)S(1)} %slice.15), channel_id=1, source_target_pairs={{0,4},{4,0},{8,12},{12,8},{16,20},{20,16},{24,28},{28,24},{1,5},{5... | collective-permute-start | bytes 786440 | tf_op jit(solution)/shard_map/ppermute | solution.py:398
  5.3 0.3 copy-done.8
  5.5 0.0 copy-start
  5.6 0.0 copy-start.1
  5.6 0.0 copy-start.3
  5.6 0.0 copy-start.5
  5.6 0.5 %collective-permute-start.3 = (f32[512,128]{1,0:T(8,128)S(1)}, f32[512,128]{1,0:T(8,128)S(1)}, u32[]{:S(2)}, u32[]{:S(2)}) collective-permute-start(f32[512,128]{1,0:T(8,128)S(1)} %slice.14), channel_id=1, source_target_pairs={{0,4},{4,0},{8,12},{12,8},{16,20},{20,16},{24,28},{28,24},{1,5},{5... | collective-permute-start | bytes 786440 | tf_op jit(solution)/shard_map/ppermute | solution.py:398
  6.1 0.3 collective-permute-done.4.refs_3_.refs_4_
  6.4 0.8 %collective-permute-done.3.refs_1_.refs_7_.refs_5_ = f32[512,128]{1,0:T(8,128)S(1)} collective-permute-done((f32[512,128]{1,0:T(8,128)S(1)}, f32[512,128]{1,0:T(8,128)S(1)}, u32[]{:S(2)}, u32[]{:S(2)}) %collective-permute-start.3) | collective-permute-done | bytes 262176 | tf_op jit(solution)/shard_map/ppermute | solution.py:398
  7.3 0.5 %shard_map.79 = (f32[256,128]{1,0:T(8,128)S(1)}, f32[256,128]{1,0:T(8,128)S(1)}) custom-call(f32[1024,128]{1,0:T(8,128)S(1)} %get-tuple-element.20.refs_0_.refs_4_, f32[512,128]{1,0:T(8,128)S(1)} %collective-permute-done.3.refs_1_.refs_7_.refs_5_, f32[1024,128]{1,0:T(8,128)S(1)} %get-tuple-element.21.refs_2_, ...), custom_call_target="tpu_custom_call" | custom-call | flops 1724999936 | bytes 1572864 | tf_op jit(solution)/shard_map/pallas_call | solution.py:376
  7.8 2.9 %collective-permute-start.5 = (f32[256,128]{1,0:T(8,128)S(1)}, f32[256,128]{1,0:T(8,128)S(1)}, u32[]{:S(2)}, u32[]{:S(2)}) collective-permute-start(f32[256,128]{1,0:T(8,128)S(1)} %get-tuple-element.22), channel_id=1, source_target_pairs={{0,8},{4,12},{8,0},{12,4},{16,24},{20,28},{24,16},{28,20},{1,9},{5... | collective-permute-start | bytes 393224 | tf_op jit(solution)/shard_map/ppermute | solution.py:398
  10.8 0.7 %collective-permute-start.1 = (f32[2,8,128]{2,1,0:T(8,128)S(1)}, f32[2,8,128]{2,1,0:T(8,128)S(1)}, u32[]{:S(2)}, u32[]{:S(2)}) collective-permute-start(f32[2,8,128]{2,1,0:T(8,128)S(1)} %bitcast.5), channel_id=1, source_target_pairs={{1,2},{2,1},{0,0},{3,3},{5,6},{6,5},{4,4},{7,7},{9,10},{10,9},{8,8... | collective-permute-start | bytes 24584 | tf_op jit(solution)/shard_map/ppermute | solution.py:394
  11.4 4.5 %collective-permute-start = (f32[2,8,128]{2,1,0:T(8,128)S(1)}, f32[2,8,128]{2,1,0:T(8,128)S(1)}, u32[]{:S(2)}, u32[]{:S(2)}) collective-permute-start(f32[2,8,128]{2,1,0:T(8,128)S(1)} %bitcast.6), channel_id=1, source_target_pairs={{0,1},{1,0},{2,3},{3,2},{4,5},{5,4},{6,7},{7,6},{8,9},{9,8},{10,11... | collective-permute-start | bytes 24584 | tf_op jit(solution)/shard_map/ppermute | solution.py:393
  15.9 0.4 collective-permute-start.2
  16.3 0.1 collective-permute-start.6
  16.4 1.4 %shard_map.77 = (f32[2,8,128]{2,1,0:T(8,128)S(1)}, f32[2,8,128]{2,1,0:T(8,128)S(1)}) custom-call(f32[2,8,128]{2,1,0:T(8,128)S(1)} %bitcast.7, f32[2,8,128]{2,1,0:T(8,128)S(1)} %bitcast.8, bf16[2,1,16,4096]{3,2,1,0:T(8,128)(2,1)S(1)} %copy-done.3, bf16[2,1,16,4096]{3,2,1,0:T(8,128)(2,1)S(1)} %copy-done.5, bf16[4,2,1,16,4096]{4,3,2,1,0:T(8,128)(2,1)S(1)} %copy-done.1), custom_call_target="tpu_custom_call" | custom-call | flops 1724999936 | bytes 1589248 | tf_op jit(solution)/shard_map/pallas_call | solution.py:376
  17.8 0.6 %collective-permute-start.7 = (f32[256,128]{1,0:T(8,128)S(1)}, f32[256,128]{1,0:T(8,128)S(1)}, u32[]{:S(2)}, u32[]{:S(2)}) collective-permute-start(f32[256,128]{1,0:T(8,128)S(1)} %get-tuple-element.31), channel_id=1, source_target_pairs={{0,8},{4,12},{8,0},{12,4},{16,24},{20,28},{24,16},{28,20},{1,9},{5... | collective-permute-start | bytes 393224 | tf_op jit(solution)/shard_map/ppermute | solution.py:398
  18.4 0.0 collective-permute-done.2.refs_3_
  18.4 2.5 %shard_map.80 = (f32[2,8,128]{2,1,0:T(8,128)S(1)}, f32[2,8,128]{2,1,0:T(8,128)S(1)}, f32[8,8,128]{2,1,0:T(8,128)}) custom-call(f32[2,8,128]{2,1,0:T(8,128)S(1)} %get-tuple-element.18.refs_0_, f32[2,8,128]{2,1,0:T(8,128)S(1)} %collective-permute-done.refs_1_, f32[2,8,128]{2,1,0:T(8,128)S(1)} %collective-permute-done.1.refs_2_, ...), custom_call_target="tpu_custom_call" | custom-call | flops 1724999936 | bytes 2387968 | tf_op jit(solution)/shard_map/pallas_call | solution.py:376
  20.9 3.7 %all-to-all-start = ((f32[8,8,128]{2,1,0:T(8,128)}), f32[8,8,128]{2,1,0:T(8,128)S(1)}, u32[]{:S(2)}, u32[]{:S(2)}) async-start(f32[8,8,128]{2,1,0:T(8,128)} %get-tuple-element.23), calls=%async_computation | async-start | bytes 65536 | tf_op jit(solution)/shard_map/all_to_all | solution.py:402
  24.6 0.5 collective-permute-start.8
  25.1 4.3 %all-to-all-done.refs_0_ = f32[8,8,128]{2,1,0:T(8,128)S(1)} async-done(((f32[8,8,128]{2,1,0:T(8,128)}), f32[8,8,128]{2,1,0:T(8,128)S(1)}, u32[]{:S(2)}, u32[]{:S(2)}) %all-to-all-start) | async-done | bytes 32800 | tf_op jit(solution)/shard_map/all_to_all | solution.py:402
  29.4 1.4 %shard_map.81 = (f32[2,8,128]{2,1,0:T(8,128)}, f32[4,2,8,128]{3,2,1,0:T(8,128)}, f32[2,8,128]{2,1,0:T(8,128)S(1)}) custom-call(f32[8,8,128]{2,1,0:T(8,128)S(1)} %all-to-all-done.refs_0_, f32[2,8,128]{2,1,0:T(8,128)S(1)} %get-tuple-element.24.refs_1_, f32[2,8,128]{2,1,0:T(8,128)S(1)} %get-tuple-element.25.refs_2_, ...), custom_call_target="tpu_custom_call" | custom-call | flops 1150000000 | bytes 1105920 | tf_op jit(solution)/shard_map/pallas_call | solution.py:376
  30.9 3.9 %all-to-all-start.1 = ((f32[4,2,8,128]{3,2,1,0:T(8,128)}), f32[4,2,8,128]{3,2,1,0:T(8,128)S(1)}, u32[]{:S(2)}, u32[]{:S(2)}) async-start(f32[4,2,8,128]{3,2,1,0:T(8,128)} %get-tuple-element.29), calls=%async_computation.1 | async-start | bytes 65536 | tf_op jit(solution)/shard_map/all_to_all | solution.py:402
  34.8 1.3 %shard_map.82.refs_0_ = f32[2,8,128]{2,1,0:T(8,128)S(1)} custom-call(f32[2,8,128]{2,1,0:T(8,128)S(1)} %get-tuple-element.28.refs_0_, f32[2,8,128]{2,1,0:T(8,128)S(1)} %copy-done.7, bf16[4,2,1,16,4096]{4,3,2,1,0:T(8,128)(2,1)S(1)} %copy-done.1), custom_call_target="tpu_custom_call" | custom-call | flops 805000000 | bytes 1064960 | tf_op jit(solution)/shard_map/pallas_call | solution.py:376
  36.1 4.4 %all-to-all-done.1.refs_1_ = f32[4,2,8,128]{3,2,1,0:T(8,128)S(1)} async-done(((f32[4,2,8,128]{3,2,1,0:T(8,128)}), f32[4,2,8,128]{3,2,1,0:T(8,128)S(1)}, u32[]{:S(2)}, u32[]{:S(2)}) %all-to-all-start.1) | async-done | bytes 32800 | tf_op jit(solution)/shard_map/all_to_all | solution.py:402
  40.5 1.9 %shard_map.83 = (f32[2,8,128]{2,1,0:T(8,128)S(1)}, f32[8,8,128]{2,1,0:T(8,128)S(1)}) custom-call(f32[2,8,128]{2,1,0:T(8,128)S(1)} %shard_map.82.refs_0_, f32[4,2,8,128]{3,2,1,0:T(8,128)S(1)} %all-to-all-done.1.refs_1_, bf16[4,2,1,16,4096]{4,3,2,1,0:T(8,128)(2,1)S(1)} %copy-done.1, f32[1024,128]{1,0:T(8,128)S(1)} %copy-done.9, ...), custom_call_target="tpu_custom_call" | custom-call | flops 1724999936 | bytes 2138112 | tf_op jit(solution)/shard_map/pallas_call | solution.py:376
  42.3 7.2 %all_to_all.15.refs_0_ = f32[8,8,128]{2,1,0:T(8,128)S(1)} all-to-all(f32[8,8,128]{2,1,0:T(8,128)S(1)} %get-tuple-element.32), channel_id=1, replica_groups=mesh['gx'=8,'gy'=4] {'gx'}, dimensions={0} | all-to-all | bytes 65536 | tf_op jit(solution)/shard_map/all_to_all | solution.py:402
  49.6 1.4 %shard_map.84 = f32[2,8,128]{2,1,0:T(8,128)} custom-call(f32[8,8,128]{2,1,0:T(8,128)S(1)} %all_to_all.15.refs_0_, f32[2,8,128]{2,1,0:T(8,128)S(1)} %get-tuple-element.33.refs_1_, f32[1024,128]{1,0:T(8,128)S(1)} %get-tuple-element.21.refs_2_, f32[512,128]{1,0:T(8,128)S(1)} %collective-permute-done.4.refs_3_.refs_4_, ...), custom_call_target="tpu_custom_call" | custom-call | flops 1150000000 | bytes 1089536 | tf_op jit(solution)/shard_map/pallas_call | solution.py:376
  (22 shorter events, 0.1 us)
Async XLA Ops:
  0.6 1.0 %copy-start.2 = (bf16[2,1,16,4096]{3,2,1,0:T(8,128)(2,1)S(1)}, bf16[2,1,16,4096]{3,2,1,0:T(8,128)(2,1)}, u32[]{:S(2)}) copy-start(bf16[2,1,16,4096]{3,2,1,0:T(8,128)(2,1)} %refs_0_.1) | copy-start | bytes 786436
  1.6 0.9 %copy-start.4 = (bf16[2,1,16,4096]{3,2,1,0:T(8,128)(2,1)S(1)}, bf16[2,1,16,4096]{3,2,1,0:T(8,128)(2,1)}, u32[]{:S(2)}) copy-start(bf16[2,1,16,4096]{3,2,1,0:T(8,128)(2,1)} %refs_5_.1) | copy-start | bytes 786436
  4.7 0.8 %copy-start.8 = (f32[1024,128]{1,0:T(8,128)}, f32[1024,128]{1,0:T(8,128)S(1)}, u32[]{:S(2)}) copy-start(f32[1024,128]{1,0:T(8,128)S(1)} %get-tuple-element.30.refs_3_) | copy-start | bytes 1572868
  4.7 1.7 %collective-permute-start.4 = (f32[512,128]{1,0:T(8,128)S(1)}, f32[512,128]{1,0:T(8,128)S(1)}, u32[]{:S(2)}, u32[]{:S(2)}) collective-permute-start(f32[512,128]{1,0:T(8,128)S(1)} %slice.15), channel_id=1, source_target_pairs={{0,4},{4,0},{8,12},{12,8},{16,20},{20,16},{24,28},{28,24},{1,5},{5... | collective-permute-start | bytes 786440 | tf_op jit(solution)/shard_map/ppermute | solution.py:398
  5.5 5.2 %copy-start = (f32[2,1,1024]{2,1,0:T(1,128)S(1)}, f32[2,1,1024]{2,1,0:T(1,128)}, u32[]{:S(2)}) copy-start(f32[2,1,1024]{2,1,0:T(1,128)} %param.6) | copy-start | bytes 24580
  5.6 10.8 %copy-start.1 = (bf16[4,2,1,16,4096]{4,3,2,1,0:T(8,128)(2,1)S(1)}, bf16[4,2,1,16,4096]{4,3,2,1,0:T(8,128)(2,1)}, u32[]{:S(2)}) copy-start(bf16[4,2,1,16,4096]{4,3,2,1,0:T(8,128)(2,1)} %refs_2_.5) | copy-start | bytes 3145732
  5.6 10.8 %copy-start.3 = (bf16[2,1,16,4096]{3,2,1,0:T(8,128)(2,1)S(1)}, bf16[2,1,16,4096]{3,2,1,0:T(8,128)(2,1)}, u32[]{:S(2)}) copy-start(bf16[2,1,16,4096]{3,2,1,0:T(8,128)(2,1)} %refs_2_.3) | copy-start | bytes 786436
  5.6 10.8 %copy-start.5 = (bf16[2,1,16,4096]{3,2,1,0:T(8,128)(2,1)S(1)}, bf16[2,1,16,4096]{3,2,1,0:T(8,128)(2,1)}, u32[]{:S(2)}) copy-start(bf16[2,1,16,4096]{3,2,1,0:T(8,128)(2,1)} %refs_5_.1) | copy-start | bytes 786436
  5.6 1.7 %collective-permute-start.3 = (f32[512,128]{1,0:T(8,128)S(1)}, f32[512,128]{1,0:T(8,128)S(1)}, u32[]{:S(2)}, u32[]{:S(2)}) collective-permute-start(f32[512,128]{1,0:T(8,128)S(1)} %slice.14), channel_id=1, source_target_pairs={{0,4},{4,0},{8,12},{12,8},{16,20},{20,16},{24,28},{28,24},{1,5},{5... | collective-permute-start | bytes 786440 | tf_op jit(solution)/shard_map/ppermute | solution.py:398
  7.8 8.6 %copy-start.6 = (f32[2,1,1024]{2,1,0:T(1,128)S(1)}, f32[2,1,1024]{2,1,0:T(1,128)}, u32[]{:S(2)}) copy-start(f32[2,1,1024]{2,1,0:T(1,128)} %param.7) | copy-start | bytes 24580
  7.8 8.4 %collective-permute-start.5 = (f32[256,128]{1,0:T(8,128)S(1)}, f32[256,128]{1,0:T(8,128)S(1)}, u32[]{:S(2)}, u32[]{:S(2)}) collective-permute-start(f32[256,128]{1,0:T(8,128)S(1)} %get-tuple-element.22), channel_id=1, source_target_pairs={{0,8},{4,12},{8,0},{12,4},{16,24},{20,28},{24,16},{28,20},{1,9},{5... | collective-permute-start | bytes 393224 | tf_op jit(solution)/shard_map/ppermute | solution.py:398
  10.8 7.7 %collective-permute-start.1 = (f32[2,8,128]{2,1,0:T(8,128)S(1)}, f32[2,8,128]{2,1,0:T(8,128)S(1)}, u32[]{:S(2)}, u32[]{:S(2)}) collective-permute-start(f32[2,8,128]{2,1,0:T(8,128)S(1)} %bitcast.5), channel_id=1, source_target_pairs={{1,2},{2,1},{0,0},{3,3},{5,6},{6,5},{4,4},{7,7},{9,10},{10,9},{8,8... | collective-permute-start | bytes 24584 | tf_op jit(solution)/shard_map/ppermute | solution.py:394
  11.4 7.0 %collective-permute-start = (f32[2,8,128]{2,1,0:T(8,128)S(1)}, f32[2,8,128]{2,1,0:T(8,128)S(1)}, u32[]{:S(2)}, u32[]{:S(2)}) collective-permute-start(f32[2,8,128]{2,1,0:T(8,128)S(1)} %bitcast.6), channel_id=1, source_target_pairs={{0,1},{1,0},{2,3},{3,2},{4,5},{5,4},{6,7},{7,6},{8,9},{9,8},{10,11... | collective-permute-start | bytes 24584 | tf_op jit(solution)/shard_map/ppermute | solution.py:393
  15.9 2.5 %collective-permute-start.2 = (f32[1,8,128]{2,1,0:T(8,128)S(1)}, f32[1,8,128]{2,1,0:T(8,128)S(1)}, u32[]{:S(2)}, u32[]{:S(2)}) collective-permute-start(f32[1,8,128]{2,1,0:T(8,128)S(1)} %bitcast.10), channel_id=1, source_target_pairs={{0,28},{4,0},{8,4},{12,8},{16,12},{20,16},{24,20},{28,24},{1,29},{... | collective-permute-start | bytes 12296 | tf_op jit(solution)/shard_map/ppermute | solution.py:422
  16.3 2.1 %collective-permute-start.6 = (f32[256,128]{1,0:T(8,128)S(1)}, f32[256,128]{1,0:T(8,128)S(1)}, u32[]{:S(2)}, u32[]{:S(2)}) collective-permute-start(f32[256,128]{1,0:T(8,128)S(1)} %collective-permute-done.5.refs_8_.refs_6_), channel_id=1, source_target_pairs={{0,4},{4,0},{8,12},{12,8},{16,20},{20,16},{24,28},{28,24},{1,5},{5... | collective-permute-start | bytes 393224 | tf_op jit(solution)/shard_map/ppermute | solution.py:398
  17.8 6.8 %collective-permute-start.7 = (f32[256,128]{1,0:T(8,128)S(1)}, f32[256,128]{1,0:T(8,128)S(1)}, u32[]{:S(2)}, u32[]{:S(2)}) collective-permute-start(f32[256,128]{1,0:T(8,128)S(1)} %get-tuple-element.31), channel_id=1, source_target_pairs={{0,8},{4,12},{8,0},{12,4},{16,24},{20,28},{24,16},{28,20},{1,9},{5... | collective-permute-start | bytes 393224 | tf_op jit(solution)/shard_map/ppermute | solution.py:398
  20.9 8.5 %all-to-all-start = ((f32[8,8,128]{2,1,0:T(8,128)}), f32[8,8,128]{2,1,0:T(8,128)S(1)}, u32[]{:S(2)}, u32[]{:S(2)}) async-start(f32[8,8,128]{2,1,0:T(8,128)} %get-tuple-element.23), calls=%async_computation | async-start | bytes 65536 | tf_op jit(solution)/shard_map/all_to_all | solution.py:402
  24.6 11.5 %collective-permute-start.8 = (f32[256,128]{1,0:T(8,128)S(1)}, f32[256,128]{1,0:T(8,128)S(1)}, u32[]{:S(2)}, u32[]{:S(2)}) collective-permute-start(f32[256,128]{1,0:T(8,128)S(1)} %collective-permute-done.7.refs_5_.refs_4_), channel_id=1, source_target_pairs={{0,4},{4,0},{8,12},{12,8},{16,20},{20,16},{24,28},{28,24},{1,5},{5... | collective-permute-start | bytes 393224 | tf_op jit(solution)/shard_map/ppermute | solution.py:398
  30.9 3.9 %copy-start.7 = (f32[2,8,128]{2,1,0:T(8,128)S(1)}, f32[2,8,128]{2,1,0:T(8,128)}, u32[]{:S(2)}) copy-start(f32[2,8,128]{2,1,0:T(8,128)} %get-tuple-element.27.refs_1_) | copy-start | bytes 24580
  30.9 9.6 %all-to-all-start.1 = ((f32[4,2,8,128]{3,2,1,0:T(8,128)}), f32[4,2,8,128]{3,2,1,0:T(8,128)S(1)}, u32[]{:S(2)}, u32[]{:S(2)}) async-start(f32[4,2,8,128]{3,2,1,0:T(8,128)} %get-tuple-element.29), calls=%async_computation.1 | async-start | bytes 65536 | tf_op jit(solution)/shard_map/all_to_all | solution.py:402
  34.8 5.7 %copy-start.9 = (f32[1024,128]{1,0:T(8,128)S(1)}, f32[1024,128]{1,0:T(8,128)}, u32[]{:S(2)}) copy-start(f32[1024,128]{1,0:T(8,128)} %copy-done.8) | copy-start | bytes 1572868

commit v4 on v3

--- a/solution.py
+++ b/solution.py
@@ -131,66 +131,55 @@
     return (sums[0] + sums[1]) + (sums[2] + sums[3])
 
 
-def prep_kernel(lower, upper, lower_turned, upper_turned, lower_products, upper_products, rows_scratch):
-    planes, _, rows, width = lower.shape
+def prep_kernel(reverse, blocks, *refs):
+    maps, products, own, rows_scratch = refs[-4:]
+    planes, _, rows, width = blocks.shape
     species = LANES // 2
     pairs = rows // 2
     size = species * pairs
-    for blocks, maps, products, order in (
-        (lower, lower_turned, lower_products, list(range(planes))),
-        (upper, upper_turned, upper_products, list(range(planes))[::-1]),
-    ):
-        for plane in order:
-            to_rows(rows_scratch, reader(blocks, plane, 0), rows, species)
-            turn(rows_scratch, maps, plane * size, pairs, species)
-        for step, plane in enumerate(order):
-            at = pl.ds(plane * size, size)
-            if step == 0:
-                products[at, :] = -maps[at, :]
-                continue
-            for pair in range(pairs):
-                here = pl.ds(plane * size + pair, species, stride=pairs)
-                before = pl.ds(order[step - 1] * size + pair, species, stride=pairs)
-                later = -maps[here, :]
-                if step == 1:
-                    products[here, :] = multiply(products[before, :], later, True)
-                else:
-                    products[here, :] = multiply(products[before, :], later, False)
-
-
-def join_kernel(level, full, pairs, own_planes, *refs):
+    order = list(range(planes))[::-1] if reverse else list(range(planes))
+    for plane in order:
+        to_rows(rows_scratch, reader(blocks, plane, 0), rows, species)
+        turn(rows_scratch, maps, plane * size, pairs, species)
+    for step, plane in enumerate(order):
+        at = pl.ds(plane * size, size)
+        if step == 0:
+            products[at, :] = -maps[at, :]
+            continue
+        for pair in range(pairs):
+            here = pl.ds(plane * size + pair, species, stride=pairs)
+            before = pl.ds(order[step - 1] * size + pair, species, stride=pairs)
+            products[here, :] = multiply(products[before, :], -maps[here, :], step == 1)
+    own[...] = products[pl.ds(order[-1] * size, size), :]
+
+
+def join_kernel(level, reverse, full, pairs, own, *refs):
     here = (lax.axis_index("gx") >> level) & 1
     core = lax.axis_index("gx") & 1
     species = LANES // 2
-    size = species * pairs
-    half = size // 2
-    inputs, outputs = refs[: len(own_planes)], refs[len(own_planes) :]
-    each = len(inputs) // 2
-    for side in (0, 1):
-        later_is_own = here == (1 if side == 0 else 0)
-        own, *partner = inputs[side * each : (side + 1) * each]
-        first = own_planes[side * each] * size
-        outs = outputs[side * (len(outputs) // 2) : (side + 1) * (len(outputs) // 2)]
-        for pair in range(pairs):
-            mine = own[pl.ds(first + pair, species, stride=pairs), :]
-            if len(partner) == 1:
-                theirs = partner[0][pl.ds(pair, species, stride=pairs), :]
-            else:
-                near = partner[0][pl.ds(pair, species // 2, stride=pairs), :]
-                far = partner[1][pl.ds(pair, species // 2, stride=pairs), :]
-                theirs = jnp.where(
-                    core == 0, jnp.concatenate([near, far], 0), jnp.concatenate([far, near], 0)
-                )
-            earlier = jnp.where(later_is_own, theirs, mine)
-            later = jnp.where(later_is_own, mine, theirs)
+    outs = refs[-2:] if full else refs[-1:]
+    partner = refs[: len(refs) - len(outs)]
+    later_is_own = here == (0 if reverse else 1)
+    for pair in range(pairs):
+        mine = own[pl.ds(pair, species, stride=pairs), :]
+        if len(partner) == 1:
+            theirs = partner[0][pl.ds(pair, species, stride=pairs), :]
+        else:
+            close = partner[0][pl.ds(pair, species // 2, stride=pairs), :]
+            far = partner[1][pl.ds(pair, species // 2, stride=pairs), :]
+            theirs = jnp.where(
+                core == 0, jnp.concatenate([close, far], 0), jnp.concatenate([far, close], 0)
+            )
+        earlier = jnp.where(later_is_own, theirs, mine)
+        later = jnp.where(later_is_own, mine, theirs)
+        if full:
+            kept = multiply(earlier, later, False)
+            outs[0][pl.ds(pair, species, stride=pairs), :] = kept
+            kept = jnp.where(core == 0, kept[: species // 2], kept[species // 2 :])
+        else:
             kept = jnp.where(core == 0, earlier[: species // 2], earlier[species // 2 :])
-            if full:
-                product = multiply(earlier, later, False)
-                outs[0][pl.ds(pair, species, stride=pairs), :] = product
-                kept = jnp.where(core == 0, product[: species // 2], product[species // 2 :])
-            else:
-                kept = multiply(kept, later, False)
-            outs[-1][pl.ds(pair, species // 2, stride=pairs), :] = kept
+            kept = multiply(kept, later, False)
+        outs[-1][pl.ds(pair, species // 2, stride=pairs), :] = kept
 
 
 def base_kernel(start, source, diag, upper, side, rhs, base, scratch):
@@ -199,8 +188,8 @@
     for p in range(planes):
         own = apply([(reader(diag, p, 0), spread(scratch, source[p]))])
         terms = [
-            (reader(side, 0, p, 0), shifted(vectors[p], True)),
-            (reader(side, 1, p, 0), shifted(vectors[p], False)),
+            (reader(side, 2, p, 0), shifted(vectors[p], True)),
+            (reader(side, 3, p, 0), shifted(vectors[p], False)),
         ]
         if p + 1 < planes:
             terms.append((reader(upper, p, 0), vectors[p + 1]))
@@ -289,7 +278,7 @@
 
 
 def forward_kernel(levels, got, drive, offsets, rhs, products, *rest):
-    *partners, out, copies, base = rest
+    *partners, out, copy, base = rest
     planes = drive.shape[0]
     size = drive.shape[1] * LANES // 2
     entering = incoming(got, grouped(partners, levels), lax.axis_index("gx"), False)
@@ -297,8 +286,7 @@
         value = offsets[p] + turned(products, entering, p * size)
         base[p] = rhs[p] - (drive[p] - value)
         out[p] = value
-        for target in range(copies.shape[0]):
-            copies[target, p] = value
+        copy[p] = value
 
 
 def side_kernel(base, vectors, side, out, scratch):
@@ -306,23 +294,21 @@
         vector = spread(scratch, vectors[p])
         around = apply(
             [
-                (reader(side, 0, p, 0), shifted(vector, True)),
-                (reader(side, 1, p, 0), shifted(vector, False)),
+                (reader(side, 2, p, 0), shifted(vector, True)),
+                (reader(side, 3, p, 0), shifted(vector, False)),
             ]
         )
         out[p] = base[p] - gather_pairs(scratch, around)
 
 
-def backward_offset_kernel(levels, base, got, side, upper, *rest):
+def backward_offset_kernel(levels, base, paired, other, side, upper, *rest):
     *partners, offsets, slots, scratch = rest
     planes = base.shape[0]
     size = base.shape[1] * LANES // 2
-    row, rows = lax.axis_index("gy"), lax.axis_size("gy")
     here = lax.axis_size("gx") - 1 - lax.axis_index("gx")
     previous = None
     for p in range(planes)[::-1]:
-        low = jnp.where(row == 0, 0.0, got[jnp.maximum(row - 1, 0), p])
-        high = jnp.where(row == rows - 1, 0.0, got[jnp.minimum(row + 1, rows - 1), p])
+        low, high = beside("gy", paired[p], other[p])
         around = apply(
             [
                 (reader(side, 0, p, 0), spread(scratch, low)),
@@ -348,39 +334,18 @@
 
 def call(kernel, operands, outs, scratch, micros):
     arrays = [o[0] if isinstance(o, tuple) else o for o in operands]
-    parts = [(i, o[1], o[2]) for i, o in enumerate(operands) if isinstance(o, tuple)]
-    buffers = [pltpu.VMEM((size,) + arrays[i].shape[1:], arrays[i].dtype) for i, _, size in parts]
+    held = [i for i, o in enumerate(operands) if isinstance(o, tuple)]
     outs = [jax.ShapeDtypeStruct(shape, F32) for shape in outs]
     moved = sum(a.size * a.dtype.itemsize for a in arrays)
 
-    def body(*refs):
-        refs = list(refs)
-        if parts:
-            held, semaphores = refs[-len(parts) - 1 : -1], refs[-1]
-            refs = refs[: -len(parts) - 1]
-            copies = []
-            for k, (i, first, size) in enumerate(parts):
-                copies.append(
-                    pltpu.make_async_copy(refs[i].at[pl.ds(first, size)], held[k], semaphores.at[k])
-                )
-                copies[-1].start()
-                refs[i] = held[k]
-            for copy in copies:
-                copy.wait()
-        kernel(*refs)
-
-    inside = [pltpu.VMEM(shape, F32) for shape in scratch] + buffers
-    if parts:
-        inside.append(pltpu.SemaphoreType.DMA((len(parts),)))
-    held = [i for i, _, _ in parts]
     return pl.pallas_call(
-        body,
+        kernel,
         out_shape=outs,
         in_specs=[
             pl.BlockSpec(memory_space=pl.ANY if i in held else pltpu.VMEM) for i in range(len(arrays))
         ],
         out_specs=[pl.BlockSpec(memory_space=pltpu.VMEM) for _ in outs],
-        scratch_shapes=inside,
+        scratch_shapes=[pltpu.VMEM(shape, F32) for shape in scratch],
         compiler_params=pltpu.CompilerParams(vmem_limit_bytes=24 << 20),
         cost_estimate=pl.CostEstimate(flops=int(micros * 1.15e9), bytes_accessed=moved, transcendentals=0),
     )(*arrays)
@@ -388,10 +353,8 @@
 
 def swaps(block, axis):
     count = lax.axis_size(axis)
-    other = [(i, (i + 1 if i & 1 else i - 1)) for i in range(1, count - 1)]
-    other += [(0, 0), (count - 1, count - 1)]
-    paired = lax.ppermute(block, axis, [(i, i ^ 1) for i in range(count)])
-    return paired, lax.ppermute(block, axis, other)
+    other = [(i, (i + 1 if i & 1 else i - 1) % count) for i in range(count)]
+    return crossed(block, axis, 1), lax.ppermute(block, axis, other)
 
 
 def crossed(block, axis, distance):
@@ -406,7 +369,7 @@
     planes, _, depth, width = x_lower.shape
     species = start.shape[2] // depth
     pairs = depth // 2
-    count, rows = lax.axis_size("gx"), lax.axis_size("gy")
+    count = lax.axis_size("gx")
     levels = count.bit_length() - 1
     size = species * pairs
     one = (pairs, LANES)
@@ -421,67 +384,65 @@
     paired, other = swaps(start, "gy")
     ahead = lax.ppermute(start[:1], "gx", [(i, (i - 1) % count) for i in range(count)])
 
-    lower, upper, lower_products, upper_products = call(
-        prep_kernel, [x_lower, x_upper], [maps] * 4, [(depth * species, LANES)], 2.0
-    )
-    owns = [(lower_products, planes - 1), (upper_products, 0)]
-    partners = [[], []]
-    for level in range(levels - 1):
-        got = []
-        for side, (own, plane) in enumerate(owns):
+    def prepare(reverse, blocks, after):
+        turned_blocks, products, own = call(
+            functools.partial(prep_kernel, reverse),
+            [blocks] + [(a, None) for a in after],
+            [maps, maps, whole],
+            [(depth * species, LANES)],
+            1.0,
+        )
+        partners, kept = [], None
+        for level in range(levels - 1):
             if level == 0:
-                got.append([crossed(own[plane * size : (plane + 1) * size], "gx", 1)])
+                got = [crossed(own, "gx", 1)]
             else:
-                mine = crossed(kept[side], "gx", 1 << level)
-                got.append([mine, crossed(mine, "gx", 1)])
-            partners[side] += got[side]
-        if level + 2 < levels:
-            full = level + 3 < levels
-            operands, places = [], []
-            for (own, plane), parts in zip(owns, got):
-                operands += [own] + parts
-                places += [plane] + [0] * len(parts)
-            outs = call(
-                functools.partial(join_kernel, level, full, pairs, places),
-                operands,
-                ([whole, half] if full else [half]) * 2,
-                [],
-                1.5,
-            )
-            kept = [outs[1], outs[3]] if full else outs
-            owns = [(outs[0], 0), (outs[2 if full else 1], 0)]
-
-    near = (side_blocks, 0, 2)
-    vertical = (side_blocks, 2, 2)
+                mine = crossed(kept, "gx", 1 << level)
+                got = [mine, crossed(mine, "gx", 1)]
+            partners += got
+            if level + 2 < levels:
+                full = level + 3 < levels
+                outs = call(
+                    functools.partial(join_kernel, level, reverse, full, pairs),
+                    [own] + got,
+                    [whole, half] if full else [half],
+                    [],
+                    0.4,
+                )
+                own, kept = outs[0], outs[-1]
+        return turned_blocks, products, partners
+
+    lower, lower_products, lower_partners = prepare(False, x_lower, [])
+    upper, upper_products, upper_partners = prepare(True, x_upper, [lower_products])
     rhs, base = call(
-        base_kernel, [start, source, diag_inverse, x_upper, vertical], [vec, vec], [dup], 1.5
+        base_kernel, [start, source, diag_inverse, x_upper, side_blocks], [vec, vec], [dup], 1.5
     )
     drive, offsets, sent = call(
         functools.partial(forward_offset_kernel, levels),
-        [base, paired, other, ahead, near, x_upper, lower] + partners[0],
+        [base, paired, other, ahead, side_blocks, x_upper, lower] + lower_partners,
         [vec, vec, slots],
         [dup],
         1.5,
     )
-    forward, copies, base = call(
+    forward, copy, base = call(
         functools.partial(forward_kernel, levels),
-        [exchange(sent, "gx"), drive, offsets, rhs, lower_products] + partners[0],
-        [vec, (rows,) + vec, vec],
+        [exchange(sent, "gx"), drive, offsets, rhs, lower_products] + lower_partners,
+        [vec, vec, vec],
         [],
         1.0,
     )
-    beyond = exchange(copies, "gy")
-    (base,) = call(side_kernel, [base, forward, vertical], [vec], [dup], 0.7)
+    paired, other = swaps(copy, "gy")
+    (base,) = call(side_kernel, [base, copy, side_blocks], [vec], [dup], 0.7)
     offsets, sent = call(
         functools.partial(backward_offset_kernel, levels),
-        [base, beyond, near, upper] + partners[1],
+        [base, paired, other, side_blocks, upper] + upper_partners,
         [vec, slots],
         [dup],
         1.5,
     )
     (result,) = call(
         functools.partial(backward_kernel, levels),
-        [exchange(sent, "gx"), offsets, upper_products] + partners[1],
+        [exchange(sent, "gx"), offsets, upper_products] + upper_partners,
         [vec],
         [],
         1.0,

time: 51.4 us -> 45.2 us (0.88)
  starting transfers between devices: 18.4 us -> 14.4 us
  waiting for transfers between devices: 9.89 us -> 8.16 us
    all_to_all x2 -> x1, waiting for transfers between devices: 8.71 us -> 4.36 us  [exchange(): return lax.all_to_all(slots, axis, 0, 0)]
    all_to_all x2 -> x1, starting transfers between devices: 7.63 us -> 3.32 us  [exchange(): return lax.all_to_all(slots, axis, 0, 0)]
    ppermute x2, waiting for transfers between devices: 0.01 us -> 2.43 us  [swaps(): return (crossed(block, axis, 1), lax.ppermute(block, axis, other))]
    ppermute x1, starting transfers between devices: 0.39 us -> 1.26 us  [local(): lax.ppermute(start[:1], 'gx', [(i, (i - 1) % count) for i in range(count)])]
    ppermute x6 -> x8, starting transfers between devices: 5.22 us -> 4.38 us  [crossed(): lax.ppermute(block, axis, [(i, i ^ distance) for i in range(lax.axis_size...]
    unnamed x20 -> x16, local copies, waits for them, and re-layouts: 2.18 us -> 1.76 us
    ppermute x6 -> x8, waiting for transfers between devices: 1.17 us -> 1.36 us  [crossed(): lax.ppermute(block, axis, [(i, i ^ distance) for i in range(lax.axis_size...]
    pallas_call x8 -> x10, Pallas kernels: 12.5 us -> 12.6 us  [call(): pl.pallas_call(kernel, out_shape=outs, in_specs=[pl.BlockSpec(memory_spac...]
  transfers between devices with their start and end apart: 11 -> 12, of which waited for: 4 -> 5; matrix products, arithmetic and copies ran while one was open for 0% -> 0% of each run, Pallas kernels for 13% -> 18%
where the time goes in v4:
time: 45.2 us; the launch traced here: 44.9 us
  starting transfers between devices  14.4 us (32%)
  Pallas kernels  12.6 us (28%)
  waiting for transfers between devices  8.16 us (18%)
  blocking collectives  7.22 us (16%)
  local copies, waits for them, and re-layouts  1.76 us (4%)
  between operations  0.73 us (2%)
    pallas_call x10, Pallas kernels, call(): pl.pallas_call(kernel, out_shape=outs, in_specs=[pl.BlockSpec(memory_spac...  12.6 us
    all_to_all x1, blocking collectives, exchange(): return lax.all_to_all(slots, axis, 0, 0)  7.22 us
    ppermute x2, starting transfers between devices, swaps(): return (crossed(block, axis, 1), lax.ppermute(block, axis, other))  5.46 us
    ppermute x8, starting transfers between devices, crossed(): lax.ppermute(block, axis, [(i, i ^ distance) for i in range(lax.axis_size...  4.38 us
    all_to_all x1, waiting for transfers between devices, exchange(): return lax.all_to_all(slots, axis, 0, 0)  4.36 us
    all_to_all x1, starting transfers between devices, exchange(): return lax.all_to_all(slots, axis, 0, 0)  3.32 us
    ppermute x2, waiting for transfers between devices, swaps(): return (crossed(block, axis, 1), lax.ppermute(block, axis, other))  2.43 us
    unnamed x16, local copies, waits for them, and re-layouts  1.76 us
  transfers between devices with their start and end apart: 12, of which 5 were waited for; matrix products, arithmetic and copies ran while one was open for 0% of the time, Pallas kernels for 18%

profile of v4, /device:TPU:0, one launch (start us, length us, event | category | flops | bytes accessed | tf_op | source)
XLA Modules:
  0.0 44.9 jit_solution(17141519280295321262)
XLA Ops:
  0.6 0.9 %copy-done.2 = bf16[2,1,16,4096]{3,2,1,0:T(8,128)(2,1)S(1)} copy-done((bf16[2,1,16,4096]{3,2,1,0:T(8,128)(2,1)S(1)}, bf16[2,1,16,4096]{3,2,1,0:T(8,128)(2,1)}, u32[]{:S(2)}) %copy-start.2) | copy-done | bytes 262168
  1.6 1.2 %shard_map.78 = (f32[1024,128]{1,0:T(8,128)S(1)}, f32[1024,128]{1,0:T(8,128)S(1)}, f32[512,128]{1,0:T(8,128)S(1)}) custom-call(bf16[2,1,16,4096]{3,2,1,0:T(8,128)(2,1)S(1)} %copy-done.2), custom_call_target="tpu_custom_call" | custom-call | flops 1150000000 | bytes 262144 | tf_op jit(solution)/shard_map/pallas_call | solution.py:341
  2.7 0.0 copy-start.4
  2.8 0.5 %collective-permute-start.3 = (f32[512,128]{1,0:T(8,128)S(1)}, f32[512,128]{1,0:T(8,128)S(1)}, u32[]{:S(2)}, u32[]{:S(2)}) collective-permute-start(f32[512,128]{1,0:T(8,128)S(1)} %get-tuple-element.20.own), channel_id=1, source_target_pairs={{0,4},{4,0},{8,12},{12,8},{16,20},{20,16},{24,28},{28,24},{1,5},{5... | collective-permute-start | bytes 786440 | tf_op jit(solution)/shard_map/ppermute | solution.py:361
  3.3 1.2 %collective-permute-done.3.refs_0_.rest_0_ = f32[512,128]{1,0:T(8,128)S(1)} collective-permute-done((f32[512,128]{1,0:T(8,128)S(1)}, f32[512,128]{1,0:T(8,128)S(1)}, u32[]{:S(2)}, u32[]{:S(2)}) %collective-permute-start.3) | collective-permute-done | bytes 262176 | tf_op jit(solution)/shard_map/ppermute | solution.py:361
  4.4 0.3 shard_map.79
  4.8 2.9 %collective-permute-start.4 = (f32[256,128]{1,0:T(8,128)S(1)}, f32[256,128]{1,0:T(8,128)S(1)}, u32[]{:S(2)}, u32[]{:S(2)}) collective-permute-start(f32[256,128]{1,0:T(8,128)S(1)} %shard_map.79), channel_id=1, source_target_pairs={{0,8},{4,12},{8,0},{12,4},{16,24},{20,28},{24,16},{28,20},{1,9},{5... | collective-permute-start | bytes 393224 | tf_op jit(solution)/shard_map/ppermute | solution.py:361
  7.7 1.2 %shard_map.83 = (f32[1024,128]{1,0:T(8,128)S(1)}, f32[1024,128]{1,0:T(8,128)S(1)}, f32[512,128]{1,0:T(8,128)S(1)}) custom-call(bf16[2,1,16,4096]{3,2,1,0:T(8,128)(2,1)S(1)} %copy-done.4, f32[1024,128]{1,0:T(8,128)S(1)} %get-tuple-element.25.products.refs_0_), custom_call_target="tpu_custom_call" | custom-call | flops 1150000000 | bytes 786432 | tf_op jit(solution)/shard_map/pallas_call | solution.py:341
  8.9 0.8 %copy-done.6 = f32[1024,128]{1,0:T(8,128)} copy-done((f32[1024,128]{1,0:T(8,128)}, f32[1024,128]{1,0:T(8,128)S(1)}, u32[]{:S(2)}) %copy-start.6) | copy-done | bytes 524312
  9.7 0.0 collective-permute-start.8
  9.7 3.7 %collective-permute-start.1 = (f32[2,8,128]{2,1,0:T(8,128)S(1)}, f32[2,8,128]{2,1,0:T(8,128)S(1)}, u32[]{:S(2)}, u32[]{:S(2)}) collective-permute-start(f32[2,8,128]{2,1,0:T(8,128)S(1)} %bitcast.5), channel_id=1, source_target_pairs={{0,3},{1,2},{2,1},{3,0},{4,7},{5,6},{6,5},{7,4},{8,11},{9,10},{10,... | collective-permute-start | bytes 24584 | tf_op jit(solution)/shard_map/ppermute | solution.py:357
  13.3 0.0 collective-permute-start
  13.3 1.3 %collective-permute-start.2 = (f32[1,8,128]{2,1,0:T(8,128)S(1)}, f32[1,8,128]{2,1,0:T(8,128)S(1)}, u32[]{:S(2)}, u32[]{:S(2)}) collective-permute-start(f32[1,8,128]{2,1,0:T(8,128)S(1)} %bitcast.9), channel_id=1, source_target_pairs={{0,28},{4,0},{8,4},{12,8},{16,12},{20,16},{24,20},{28,24},{1,29},{... | collective-permute-start | bytes 12296 | tf_op jit(solution)/shard_map/ppermute | solution.py:385
  14.6 0.0 collective-permute-done.4.rest_1_
  14.6 0.0 collective-permute-start.5
  14.6 1.3 %shard_map.77 = (f32[2,8,128]{2,1,0:T(8,128)S(1)}, f32[2,8,128]{2,1,0:T(8,128)S(1)}) custom-call(f32[2,8,128]{2,1,0:T(8,128)S(1)} %bitcast.7, f32[2,8,128]{2,1,0:T(8,128)S(1)} %bitcast.8, bf16[2,1,16,4096]{3,2,1,0:T(8,128)(2,1)S(1)} %copy-done.3, bf16[2,1,16,4096]{3,2,1,0:T(8,128)(2,1)S(1)} %copy-done.4, bf16[4,2,1,16,4096]{4,3,2,1,0:T(8,128)(2,1)S(1)} %copy-done.1), custom_call_target="tpu_custom_call" | custom-call | flops 1724999936 | bytes 1589248 | tf_op jit(solution)/shard_map/pallas_call | solution.py:341
  15.9 0.4 shard_map.84
  16.3 0.6 %collective-permute-start.9 = (f32[256,128]{1,0:T(8,128)S(1)}, f32[256,128]{1,0:T(8,128)S(1)}, u32[]{:S(2)}, u32[]{:S(2)}) collective-permute-start(f32[256,128]{1,0:T(8,128)S(1)} %shard_map.84), channel_id=1, source_target_pairs={{0,8},{4,12},{8,0},{12,4},{16,24},{20,28},{24,16},{28,20},{1,9},{5... | collective-permute-start | bytes 393224 | tf_op jit(solution)/shard_map/ppermute | solution.py:361
  16.9 0.0 collective-permute-done.2.ahead
  16.9 0.1 collective-permute-done.paired
  17.0 2.4 %shard_map.80 = (f32[2,8,128]{2,1,0:T(8,128)S(1)}, f32[2,8,128]{2,1,0:T(8,128)S(1)}, f32[8,8,128]{2,1,0:T(8,128)}) custom-call(f32[2,8,128]{2,1,0:T(8,128)S(1)} %get-tuple-element.18.base, f32[2,8,128]{2,1,0:T(8,128)S(1)} %collective-permute-done.paired, f32[2,8,128]{2,1,0:T(8,128)S(1)} %collective-permute-done.1.other, ...), custom_call_target="tpu_custom_call" | custom-call | flops 1724999936 | bytes 2387968 | tf_op jit(solution)/shard_map/pallas_call | solution.py:341
  19.4 3.3 %all-to-all-start = ((f32[8,8,128]{2,1,0:T(8,128)}), f32[8,8,128]{2,1,0:T(8,128)S(1)}, u32[]{:S(2)}, u32[]{:S(2)}) async-start(f32[8,8,128]{2,1,0:T(8,128)} %get-tuple-element.21), calls=%async_computation | async-start | bytes 65536 | tf_op jit(solution)/shard_map/all_to_all | solution.py:365
  22.7 0.4 collective-permute-start.10
  23.1 4.4 %all-to-all-done.got = f32[8,8,128]{2,1,0:T(8,128)S(1)} async-done(((f32[8,8,128]{2,1,0:T(8,128)}), f32[8,8,128]{2,1,0:T(8,128)S(1)}, u32[]{:S(2)}, u32[]{:S(2)}) %all-to-all-start) | async-done | bytes 32800 | tf_op jit(solution)/shard_map/all_to_all | solution.py:365
  27.5 1.4 %shard_map.81 = (f32[2,8,128]{2,1,0:T(8,128)}, f32[2,8,128]{2,1,0:T(8,128)S(1)}, f32[2,8,128]{2,1,0:T(8,128)S(1)}) custom-call(f32[8,8,128]{2,1,0:T(8,128)S(1)} %all-to-all-done.got, f32[2,8,128]{2,1,0:T(8,128)S(1)} %get-tuple-element.22.drive, f32[2,8,128]{2,1,0:T(8,128)S(1)} %get-tuple-element.23.offsets, f32[2,8,128]{2,1,0:T(8,128)S(1)} %get-tuple-element.24.rhs, ...), custom_call_target="tpu_custom_call" | custom-call | flops 1150000000 | bytes 1105920 | tf_op jit(solution)/shard_map/pallas_call | solution.py:341
  28.9 1.8 %collective-permute-start.7 = (f32[2,8,128]{2,1,0:T(8,128)S(1)}, f32[2,8,128]{2,1,0:T(8,128)S(1)}, u32[]{:S(2)}, u32[]{:S(2)}) collective-permute-start(f32[2,8,128]{2,1,0:T(8,128)S(1)} %get-tuple-element.28.vectors), channel_id=1, source_target_pairs={{0,3},{1,2},{2,1},{3,0},{4,7},{5,6},{6,5},{7,4},{8,11},{9,10},{10,... | collective-permute-start | bytes 24584 | tf_op jit(solution)/shard_map/ppermute | solution.py:357
  30.7 1.2 %shard_map.82.base = f32[2,8,128]{2,1,0:T(8,128)S(1)} custom-call(f32[2,8,128]{2,1,0:T(8,128)S(1)} %get-tuple-element.27.base, f32[2,8,128]{2,1,0:T(8,128)S(1)} %get-tuple-element.28.vectors, bf16[4,2,1,16,4096]{4,3,2,1,0:T(8,128)(2,1)S(1)} %copy-done.1), custom_call_target="tpu_custom_call" | custom-call | flops 805000000 | bytes 1064960 | tf_op jit(solution)/shard_map/pallas_call | solution.py:341
  32.0 2.4 %collective-permute-done.7.other = f32[2,8,128]{2,1,0:T(8,128)S(1)} collective-permute-done((f32[2,8,128]{2,1,0:T(8,128)S(1)}, f32[2,8,128]{2,1,0:T(8,128)S(1)}, u32[]{:S(2)}, u32[]{:S(2)}) %collective-permute-start.7) | collective-permute-done | bytes 8224 | tf_op jit(solution)/shard_map/ppermute | solution.py:357
  34.4 0.1 collective-permute-done.6.paired
  34.5 1.8 %shard_map.85 = (f32[2,8,128]{2,1,0:T(8,128)S(1)}, f32[8,8,128]{2,1,0:T(8,128)S(1)}) custom-call(f32[2,8,128]{2,1,0:T(8,128)S(1)} %shard_map.82.base, f32[2,8,128]{2,1,0:T(8,128)S(1)} %collective-permute-done.6.paired, f32[2,8,128]{2,1,0:T(8,128)S(1)} %collective-permute-done.7.other, bf16[4,2,1,16,4096]{4,3,2,1,0:T(8,128)(2,1)S(1)} %copy-done.1, ...), custom_call_target="tpu_custom_call" | custom-call | flops 1724999936 | bytes 2121728 | tf_op jit(solution)/shard_map/pallas_call | solution.py:341
  36.3 7.2 %all_to_all.10.got = f32[8,8,128]{2,1,0:T(8,128)S(1)} all-to-all(f32[8,8,128]{2,1,0:T(8,128)S(1)} %get-tuple-element.31), channel_id=1, replica_groups=mesh['gx'=8,'gy'=4] {'gx'}, dimensions={0} | all-to-all | bytes 65536 | tf_op jit(solution)/shard_map/all_to_all | solution.py:365
  43.5 1.4 %shard_map.86 = f32[2,8,128]{2,1,0:T(8,128)} custom-call(f32[8,8,128]{2,1,0:T(8,128)S(1)} %all_to_all.10.got, f32[2,8,128]{2,1,0:T(8,128)S(1)} %get-tuple-element.32.offsets, f32[1024,128]{1,0:T(8,128)S(1)} %get-tuple-element.33.products, f32[512,128]{1,0:T(8,128)S(1)} %collective-permute-done.8.refs_0_.rest_0_, ...), custom_call_target="tpu_custom_call" | custom-call | flops 1150000000 | bytes 1089536 | tf_op jit(solution)/shard_map/pallas_call | solution.py:341
  (20 shorter events, 0.0 us)
Async XLA Ops:
  0.6 1.0 %copy-start.2 = (bf16[2,1,16,4096]{3,2,1,0:T(8,128)(2,1)S(1)}, bf16[2,1,16,4096]{3,2,1,0:T(8,128)(2,1)}, u32[]{:S(2)}) copy-start(bf16[2,1,16,4096]{3,2,1,0:T(8,128)(2,1)} %blocks.2) | copy-start | bytes 786436
  2.7 4.9 %copy-start.4 = (bf16[2,1,16,4096]{3,2,1,0:T(8,128)(2,1)S(1)}, bf16[2,1,16,4096]{3,2,1,0:T(8,128)(2,1)}, u32[]{:S(2)}) copy-start(bf16[2,1,16,4096]{3,2,1,0:T(8,128)(2,1)} %blocks.3) | copy-start | bytes 786436
  2.8 1.7 %collective-permute-start.3 = (f32[512,128]{1,0:T(8,128)S(1)}, f32[512,128]{1,0:T(8,128)S(1)}, u32[]{:S(2)}, u32[]{:S(2)}) collective-permute-start(f32[512,128]{1,0:T(8,128)S(1)} %get-tuple-element.20.own), channel_id=1, source_target_pairs={{0,4},{4,0},{8,12},{12,8},{16,20},{20,16},{24,28},{28,24},{1,5},{5... | collective-permute-start | bytes 786440 | tf_op jit(solution)/shard_map/ppermute | solution.py:361
  4.8 9.8 %collective-permute-start.4 = (f32[256,128]{1,0:T(8,128)S(1)}, f32[256,128]{1,0:T(8,128)S(1)}, u32[]{:S(2)}, u32[]{:S(2)}) collective-permute-start(f32[256,128]{1,0:T(8,128)S(1)} %shard_map.79), channel_id=1, source_target_pairs={{0,8},{4,12},{8,0},{12,4},{16,24},{20,28},{24,16},{28,20},{1,9},{5... | collective-permute-start | bytes 393224 | tf_op jit(solution)/shard_map/ppermute | solution.py:361
  7.7 2.0 %copy-start = (f32[2,1,1024]{2,1,0:T(1,128)S(1)}, f32[2,1,1024]{2,1,0:T(1,128)}, u32[]{:S(2)}) copy-start(f32[2,1,1024]{2,1,0:T(1,128)} %param.6) | copy-start | bytes 24580
  7.7 6.9 %copy-start.1 = (bf16[4,2,1,16,4096]{4,3,2,1,0:T(8,128)(2,1)S(1)}, bf16[4,2,1,16,4096]{4,3,2,1,0:T(8,128)(2,1)}, u32[]{:S(2)}) copy-start(bf16[4,2,1,16,4096]{4,3,2,1,0:T(8,128)(2,1)} %side.7) | copy-start | bytes 3145732
  7.7 6.9 %copy-start.3 = (bf16[2,1,16,4096]{3,2,1,0:T(8,128)(2,1)S(1)}, bf16[2,1,16,4096]{3,2,1,0:T(8,128)(2,1)}, u32[]{:S(2)}) copy-start(bf16[2,1,16,4096]{3,2,1,0:T(8,128)(2,1)} %diag.1) | copy-start | bytes 786436
  8.9 0.8 %copy-start.6 = (f32[1024,128]{1,0:T(8,128)}, f32[1024,128]{1,0:T(8,128)S(1)}, u32[]{:S(2)}) copy-start(f32[1024,128]{1,0:T(8,128)S(1)} %get-tuple-element.29.upper) | copy-start | bytes 1572868
  9.7 5.0 %copy-start.5 = (f32[2,1,1024]{2,1,0:T(1,128)S(1)}, f32[2,1,1024]{2,1,0:T(1,128)}, u32[]{:S(2)}) copy-start(f32[2,1,1024]{2,1,0:T(1,128)} %param.7) | copy-start | bytes 24580
  9.7 6.3 %collective-permute-start.8 = (f32[512,128]{1,0:T(8,128)S(1)}, f32[512,128]{1,0:T(8,128)S(1)}, u32[]{:S(2)}, u32[]{:S(2)}) collective-permute-start(f32[512,128]{1,0:T(8,128)S(1)} %get-tuple-element.30.own), channel_id=1, source_target_pairs={{0,4},{4,0},{8,12},{12,8},{16,20},{20,16},{24,28},{28,24},{1,5},{5... | collective-permute-start | bytes 786440 | tf_op jit(solution)/shard_map/ppermute | solution.py:361
  9.7 7.2 %collective-permute-start.1 = (f32[2,8,128]{2,1,0:T(8,128)S(1)}, f32[2,8,128]{2,1,0:T(8,128)S(1)}, u32[]{:S(2)}, u32[]{:S(2)}) collective-permute-start(f32[2,8,128]{2,1,0:T(8,128)S(1)} %bitcast.5), channel_id=1, source_target_pairs={{0,3},{1,2},{2,1},{3,0},{4,7},{5,6},{6,5},{7,4},{8,11},{9,10},{10,... | collective-permute-start | bytes 24584 | tf_op jit(solution)/shard_map/ppermute | solution.py:357
  13.3 3.7 %collective-permute-start = (f32[2,8,128]{2,1,0:T(8,128)S(1)}, f32[2,8,128]{2,1,0:T(8,128)S(1)}, u32[]{:S(2)}, u32[]{:S(2)}) collective-permute-start(f32[2,8,128]{2,1,0:T(8,128)S(1)} %bitcast.6), channel_id=1, source_target_pairs={{0,1},{1,0},{2,3},{3,2},{4,5},{5,4},{6,7},{7,6},{8,9},{9,8},{10,11... | collective-permute-start | bytes 24584 | tf_op jit(solution)/shard_map/ppermute | solution.py:361
  13.3 3.5 %collective-permute-start.2 = (f32[1,8,128]{2,1,0:T(8,128)S(1)}, f32[1,8,128]{2,1,0:T(8,128)S(1)}, u32[]{:S(2)}, u32[]{:S(2)}) collective-permute-start(f32[1,8,128]{2,1,0:T(8,128)S(1)} %bitcast.9), channel_id=1, source_target_pairs={{0,28},{4,0},{8,4},{12,8},{16,12},{20,16},{24,20},{28,24},{1,29},{... | collective-permute-start | bytes 12296 | tf_op jit(solution)/shard_map/ppermute | solution.py:385
  14.6 2.4 %collective-permute-start.5 = (f32[256,128]{1,0:T(8,128)S(1)}, f32[256,128]{1,0:T(8,128)S(1)}, u32[]{:S(2)}, u32[]{:S(2)}) collective-permute-start(f32[256,128]{1,0:T(8,128)S(1)} %collective-permute-done.4.rest_1_), channel_id=1, source_target_pairs={{0,4},{4,0},{8,12},{12,8},{16,20},{20,16},{24,28},{28,24},{1,5},{5... | collective-permute-start | bytes 393224 | tf_op jit(solution)/shard_map/ppermute | solution.py:361
  16.3 6.4 %collective-permute-start.9 = (f32[256,128]{1,0:T(8,128)S(1)}, f32[256,128]{1,0:T(8,128)S(1)}, u32[]{:S(2)}, u32[]{:S(2)}) collective-permute-start(f32[256,128]{1,0:T(8,128)S(1)} %shard_map.84), channel_id=1, source_target_pairs={{0,8},{4,12},{8,0},{12,4},{16,24},{20,28},{24,16},{28,20},{1,9},{5... | collective-permute-start | bytes 393224 | tf_op jit(solution)/shard_map/ppermute | solution.py:361
  19.4 8.1 %all-to-all-start = ((f32[8,8,128]{2,1,0:T(8,128)}), f32[8,8,128]{2,1,0:T(8,128)S(1)}, u32[]{:S(2)}, u32[]{:S(2)}) async-start(f32[8,8,128]{2,1,0:T(8,128)} %get-tuple-element.21), calls=%async_computation | async-start | bytes 65536 | tf_op jit(solution)/shard_map/all_to_all | solution.py:365
  22.7 9.2 %collective-permute-start.10 = (f32[256,128]{1,0:T(8,128)S(1)}, f32[256,128]{1,0:T(8,128)S(1)}, u32[]{:S(2)}, u32[]{:S(2)}) collective-permute-start(f32[256,128]{1,0:T(8,128)S(1)} %collective-permute-done.9.rest_1_), channel_id=1, source_target_pairs={{0,4},{4,0},{8,12},{12,8},{16,20},{20,16},{24,28},{28,24},{1,5},{5... | collective-permute-start | bytes 393224 | tf_op jit(solution)/shard_map/ppermute | solution.py:361
  28.9 5.5 %collective-permute-start.7 = (f32[2,8,128]{2,1,0:T(8,128)S(1)}, f32[2,8,128]{2,1,0:T(8,128)S(1)}, u32[]{:S(2)}, u32[]{:S(2)}) collective-permute-start(f32[2,8,128]{2,1,0:T(8,128)S(1)} %get-tuple-element.28.vectors), channel_id=1, source_target_pairs={{0,3},{1,2},{2,1},{3,0},{4,7},{5,6},{6,5},{7,4},{8,11},{9,10},{10,... | collective-permute-start | bytes 24584 | tf_op jit(solution)/shard_map/ppermute | solution.py:357
  30.7 3.7 %collective-permute-start.6 = (f32[2,8,128]{2,1,0:T(8,128)S(1)}, f32[2,8,128]{2,1,0:T(8,128)S(1)}, u32[]{:S(2)}, u32[]{:S(2)}) collective-permute-start(f32[2,8,128]{2,1,0:T(8,128)S(1)} %get-tuple-element.28.vectors), channel_id=1, source_target_pairs={{0,1},{1,0},{2,3},{3,2},{4,5},{5,4},{6,7},{7,6},{8,9},{9,8},{10,11... | collective-permute-start | bytes 24584 | tf_op jit(solution)/shard_map/ppermute | solution.py:361
  30.7 3.7 %copy-start.7 = (f32[1024,128]{1,0:T(8,128)S(1)}, f32[1024,128]{1,0:T(8,128)}, u32[]{:S(2)}) copy-start(f32[1024,128]{1,0:T(8,128)} %copy-done.6) | copy-start | bytes 1572868

commit v5 on v4

--- a/solution.py
+++ b/solution.py
@@ -49,21 +49,27 @@
     return lambda t: ref[(*index, slice(None), slice(t * LANES, (t + 1) * LANES))]
 
 
-def spread(scratch, raw):
-    upper = lane_bit(raw.shape, LANES // 2)
-    other = pltpu.roll(raw, LANES // 2, 1)
+def spread(raw):
     half = raw.shape[0]
-    scratch[pl.ds(0, half, stride=2), :] = jnp.where(upper, other, raw)
-    scratch[pl.ds(1, half, stride=2), :] = jnp.where(upper, raw, other)
-    return scratch[...]
-
-
-def gather_pairs(scratch, vector):
-    scratch[...] = vector
+    row = lax.broadcasted_iota(jnp.int32, raw.shape, 0)
+    same = (row & 1 == 1) == lane_bit(raw.shape, LANES // 2)
+    parts = []
+    for first in (0, half // 2):
+        block = jnp.take_along_axis(raw, first + row // 2, 0)
+        parts.append(jnp.where(same, block, pltpu.roll(block, LANES // 2, 1)))
+    return jnp.concatenate(parts, 0)
+
+
+def gather_pairs(vector):
     half = vector.shape[0] // 2
-    even = scratch[pl.ds(0, half, stride=2), :]
-    odd = scratch[pl.ds(1, half, stride=2), :]
-    return jnp.where(lane_bit(even.shape, LANES // 2), odd, even)
+    shape = (half, LANES)
+    row = lax.broadcasted_iota(jnp.int32, shape, 0)
+    upper = lane_bit(shape, LANES // 2)
+    parts = []
+    for block in (vector[:half], vector[half:]):
+        block = jnp.where(upper, pltpu.roll(block, half - 1, 0), block)
+        parts.append(jnp.take_along_axis(block, 2 * row & half - 1, 0))
+    return jnp.where(row < half // 2, parts[0], parts[1])
 
 
 def shifted(vector, down):
@@ -131,7 +137,9 @@
     return (sums[0] + sums[1]) + (sums[2] + sums[3])
 
 
-def prep_kernel(reverse, blocks, *refs):
+def prep_kernel(reverse, blocks, beside_it, *refs):
+    if not reverse:
+        refs[0][...] = beside_it[...]
     maps, products, own, rows_scratch = refs[-4:]
     planes, _, rows, width = blocks.shape
     species = LANES // 2
@@ -182,11 +190,11 @@
         outs[-1][pl.ds(pair, species // 2, stride=pairs), :] = kept
 
 
-def base_kernel(start, source, diag, upper, side, rhs, base, scratch):
+def base_kernel(start, source, diag, upper, side, rhs, base):
     planes = start.shape[0]
-    vectors = [spread(scratch, start[p]) for p in range(planes)]
+    vectors = [spread(start[p]) for p in range(planes)]
     for p in range(planes):
-        own = apply([(reader(diag, p, 0), spread(scratch, source[p]))])
+        own = apply([(reader(diag, p, 0), spread(source[p]))])
         terms = [
             (reader(side, 2, p, 0), shifted(vectors[p], True)),
             (reader(side, 3, p, 0), shifted(vectors[p], False)),
@@ -194,8 +202,8 @@
         if p + 1 < planes:
             terms.append((reader(upper, p, 0), vectors[p + 1]))
         around = apply(terms)
-        rhs[p] = gather_pairs(scratch, own)
-        base[p] = gather_pairs(scratch, own - around)
+        rhs[p] = gather_pairs(own)
+        base[p] = gather_pairs(own - around)
 
 
 def partner_map(refs, vector):
@@ -253,7 +261,7 @@
 
 
 def forward_offset_kernel(levels, base, paired, other, ahead, side, upper, lower, *rest):
-    *partners, drive, offsets, slots, scratch = rest
+    *partners, drive, offsets, slots = rest
     planes = base.shape[0]
     size = base.shape[1] * LANES // 2
     here = lax.axis_index("gx")
@@ -262,13 +270,13 @@
     for p in range(planes):
         low, high = beside("gy", paired[p], other[p])
         terms = [
-            (reader(side, 0, p, 0), spread(scratch, low)),
-            (reader(side, 1, p, 0), spread(scratch, high)),
+            (reader(side, 0, p, 0), spread(low)),
+            (reader(side, 1, p, 0), spread(high)),
         ]
         if p + 1 == planes:
             beyond = jnp.where(last, 0.0, ahead[0])
-            terms.append((reader(upper, p, 0), spread(scratch, beyond)))
-        fresh = base[p] - gather_pairs(scratch, apply(terms))
+            terms.append((reader(upper, p, 0), spread(beyond)))
+        fresh = base[p] - gather_pairs(apply(terms))
         drive[p] = fresh
         if previous is not None:
             fresh = fresh - turned(lower, previous, p * size)
@@ -289,20 +297,20 @@
         copy[p] = value
 
 
-def side_kernel(base, vectors, side, out, scratch):
+def side_kernel(base, vectors, side, out):
     for p in range(base.shape[0]):
-        vector = spread(scratch, vectors[p])
+        vector = spread(vectors[p])
         around = apply(
             [
                 (reader(side, 2, p, 0), shifted(vector, True)),
                 (reader(side, 3, p, 0), shifted(vector, False)),
             ]
         )
-        out[p] = base[p] - gather_pairs(scratch, around)
+        out[p] = base[p] - gather_pairs(around)
 
 
 def backward_offset_kernel(levels, base, paired, other, side, upper, *rest):
-    *partners, offsets, slots, scratch = rest
+    *partners, offsets, slots = rest
     planes = base.shape[0]
     size = base.shape[1] * LANES // 2
     here = lax.axis_size("gx") - 1 - lax.axis_index("gx")
@@ -311,11 +319,11 @@
         low, high = beside("gy", paired[p], other[p])
         around = apply(
             [
-                (reader(side, 0, p, 0), spread(scratch, low)),
-                (reader(side, 1, p, 0), spread(scratch, high)),
+                (reader(side, 0, p, 0), spread(low)),
+                (reader(side, 1, p, 0), spread(high)),
             ]
         )
-        fresh = base[p] - gather_pairs(scratch, around)
+        fresh = base[p] - gather_pairs(around)
         if previous is not None:
             fresh = fresh - turned(upper, previous, p * size)
         offsets[p] = fresh
@@ -351,10 +359,15 @@
     )(*arrays)
 
 
-def swaps(block, axis):
-    count = lax.axis_size(axis)
-    other = [(i, (i + 1 if i & 1 else i - 1) % count) for i in range(count)]
-    return crossed(block, axis, 1), lax.ppermute(block, axis, other)
+def swaps(block):
+    count, rows = lax.axis_size("gx"), lax.axis_size("gy")
+    route = []
+    for place in range(count):
+        for row in range(rows):
+            target = row + 1 if row & 1 else row - 1
+            to = place * rows + target if 0 <= target < rows else (place ^ 1) * rows + row
+            route.append((place * rows + row, to))
+    return crossed(block, "gy", 1), lax.ppermute(block, ("gx", "gy"), route)
 
 
 def crossed(block, axis, distance):
@@ -376,19 +389,15 @@
     vec = (planes,) + one
     maps = (planes * size, LANES)
     whole, half = (size, LANES), (size // 2, LANES)
-    dup = (depth, LANES)
     slots = (count,) + one
     start = start.reshape(vec)
     source = source.reshape(vec)
 
-    paired, other = swaps(start, "gy")
-    ahead = lax.ppermute(start[:1], "gx", [(i, (i - 1) % count) for i in range(count)])
-
-    def prepare(reverse, blocks, after):
-        turned_blocks, products, own = call(
+    def prepare(reverse, blocks, other):
+        *passed, turned_blocks, products, own = call(
             functools.partial(prep_kernel, reverse),
-            [blocks] + [(a, None) for a in after],
-            [maps, maps, whole],
+            [blocks, (other, None) if reverse else other],
+            ([] if reverse else [vec]) + [maps, maps, whole],
             [(depth * species, LANES)],
             1.0,
         )
@@ -410,20 +419,22 @@
                     0.4,
                 )
                 own, kept = outs[0], outs[-1]
-        return turned_blocks, products, partners
-
-    lower, lower_products, lower_partners = prepare(False, x_lower, [])
-    upper, upper_products, upper_partners = prepare(True, x_upper, [lower_products])
+        return turned_blocks, products, partners, passed
+
+    lower, lower_products, lower_partners, (start,) = prepare(False, x_lower, start)
+    paired, other = swaps(start)
+    ahead = lax.ppermute(start[:1], "gx", [(i, (i - 1) % count) for i in range(count)])
     rhs, base = call(
-        base_kernel, [start, source, diag_inverse, x_upper, side_blocks], [vec, vec], [dup], 1.5
+        base_kernel, [start, source, diag_inverse, x_upper, side_blocks], [vec, vec], [], 1.0
     )
     drive, offsets, sent = call(
         functools.partial(forward_offset_kernel, levels),
         [base, paired, other, ahead, side_blocks, x_upper, lower] + lower_partners,
         [vec, vec, slots],
-        [dup],
+        [],
         1.5,
     )
+    upper, upper_products, upper_partners, _ = prepare(True, x_upper, offsets)
     forward, copy, base = call(
         functools.partial(forward_kernel, levels),
         [exchange(sent, "gx"), drive, offsets, rhs, lower_products] + lower_partners,
@@ -431,13 +442,13 @@
         [],
         1.0,
     )
-    paired, other = swaps(copy, "gy")
-    (base,) = call(side_kernel, [base, copy, side_blocks], [vec], [dup], 0.7)
+    paired, other = swaps(copy)
+    (base,) = call(side_kernel, [base, copy, side_blocks], [vec], [], 0.7)
     offsets, sent = call(
         functools.partial(backward_offset_kernel, levels),
         [base, paired, other, side_blocks, upper] + upper_partners,
         [vec, slots],
-        [dup],
+        [],
         1.5,
     )
     (result,) = call(

time: 45.2 us -> 50.3 us (1.11)
  waiting for transfers between devices: 8.16 us -> 12.4 us
  starting transfers between devices: 14.4 us -> 15.7 us
    ppermute x8, waiting for transfers between devices: 1.36 us -> 8.26 us  [crossed(): lax.ppermute(block, axis, [(i, i ^ distance) for i in range(lax.axis_size...]
    ppermute x8, starting transfers between devices: 4.38 us -> 9.85 us  [crossed(): lax.ppermute(block, axis, [(i, i ^ distance) for i in range(lax.axis_size...]
    ppermute x2, starting transfers between devices: 5.46 us -> 0.51 us  [swaps(): return (crossed(block, 'gy', 1), lax.ppermute(block, ('gx', 'gy'), route))]
    ppermute x2, waiting for transfers between devices: 2.43 us -> 0.01 us  [swaps(): return (crossed(block, 'gy', 1), lax.ppermute(block, ('gx', 'gy'), route))]
    ppermute x1, starting transfers between devices: 1.26 us -> 2 us  [local(): lax.ppermute(start[:1], 'gx', [(i, (i - 1) % count) for i in range(count)])]
  transfers between devices with their start and end apart: 12 -> 12, of which waited for: 5 -> 6; matrix products, arithmetic and copies ran while one was open for 0% -> 0% of each run, Pallas kernels for 18% -> 7%
where the time goes in v5:
time: 50.3 us; the launch traced here: 50 us
  starting transfers between devices  15.7 us (31%)
  waiting for transfers between devices  12.4 us (25%)
  Pallas kernels  12.3 us (24%)
  blocking collectives  7.22 us (14%)
  local copies, waits for them, and re-layouts  1.67 us (3%)
  between operations  0.76 us (2%)
    pallas_call x10, Pallas kernels, call(): pl.pallas_call(kernel, out_shape=outs, in_specs=[pl.BlockSpec(memory_spac...  12.3 us
    ppermute x8, starting transfers between devices, crossed(): lax.ppermute(block, axis, [(i, i ^ distance) for i in range(lax.axis_size...  9.85 us
    ppermute x8, waiting for transfers between devices, crossed(): lax.ppermute(block, axis, [(i, i ^ distance) for i in range(lax.axis_size...  8.26 us
    all_to_all x1, blocking collectives, exchange(): return lax.all_to_all(slots, axis, 0, 0)  7.22 us
    all_to_all x1, waiting for transfers between devices, exchange(): return lax.all_to_all(slots, axis, 0, 0)  4.08 us
    all_to_all x1, starting transfers between devices, exchange(): return lax.all_to_all(slots, axis, 0, 0)  3.32 us
    ppermute x1, starting transfers between devices, local(): lax.ppermute(start[:1], 'gx', [(i, (i - 1) % count) for i in range(count)])  2 us
    unnamed x16, local copies, waits for them, and re-layouts  1.67 us
  transfers between devices with their start and end apart: 12, of which 6 were waited for; matrix products, arithmetic and copies ran while one was open for 0% of the time, Pallas kernels for 7%

profile of v5, /device:TPU:0, one launch (start us, length us, event | category | flops | bytes accessed | tf_op | source)
XLA Modules:
  0.0 50.0 jit_solution(11177486767668617146)
XLA Ops:
  0.6 0.9 %copy-done.1 = bf16[2,1,16,4096]{3,2,1,0:T(8,128)(2,1)S(1)} copy-done((bf16[2,1,16,4096]{3,2,1,0:T(8,128)(2,1)S(1)}, bf16[2,1,16,4096]{3,2,1,0:T(8,128)(2,1)}, u32[]{:S(2)}) %copy-start.1) | copy-done | bytes 262168
  1.6 0.7 %copy-done.4 = f32[2,1,1024]{2,1,0:T(1,128)S(1)} copy-done((f32[2,1,1024]{2,1,0:T(1,128)S(1)}, f32[2,1,1024]{2,1,0:T(1,128)}, u32[]{:S(2)}) %copy-start.4) | copy-done | bytes 8216
  2.3 1.2 %shard_map.77 = (f32[2,8,128]{2,1,0:T(8,128)S(1)}, f32[1024,128]{1,0:T(8,128)S(1)}, f32[1024,128]{1,0:T(8,128)S(1)}, f32[512,128]{1,0:T(8,128)S(1)}) custom-call(bf16[2,1,16,4096]{3,2,1,0:T(8,128)(2,1)S(1)} %copy-done.1, f32[2,8,128]{2,1,0:T(8,128)S(1)} %bitcast.4), custom_call_target="tpu_custom_call" | custom-call | flops 1150000000 | bytes 270336 | tf_op jit(solution)/shard_map/pallas_call | solution.py:349
  3.4 0.0 copy-start
  3.5 0.0 copy-start.2
  3.5 0.0 copy-start.3
  3.5 0.5 %collective-permute-start.3 = (f32[512,128]{1,0:T(8,128)S(1)}, f32[512,128]{1,0:T(8,128)S(1)}, u32[]{:S(2)}, u32[]{:S(2)}) collective-permute-start(f32[512,128]{1,0:T(8,128)S(1)} %get-tuple-element.22.own), channel_id=1, source_target_pairs={{0,4},{4,0},{8,12},{12,8},{16,20},{20,16},{24,28},{28,24},{1,5},{5... | collective-permute-start | bytes 786440 | tf_op jit(solution)/shard_map/ppermute | solution.py:374
  4.0 1.2 %collective-permute-done.3.refs_0_.rest_0_ = f32[512,128]{1,0:T(8,128)S(1)} collective-permute-done((f32[512,128]{1,0:T(8,128)S(1)}, f32[512,128]{1,0:T(8,128)S(1)}, u32[]{:S(2)}, u32[]{:S(2)}) %collective-permute-start.3) | collective-permute-done | bytes 262176 | tf_op jit(solution)/shard_map/ppermute | solution.py:374
  5.2 0.3 shard_map.79
  5.5 2.9 %collective-permute-start.4 = (f32[256,128]{1,0:T(8,128)S(1)}, f32[256,128]{1,0:T(8,128)S(1)}, u32[]{:S(2)}, u32[]{:S(2)}) collective-permute-start(f32[256,128]{1,0:T(8,128)S(1)} %shard_map.79), channel_id=1, source_target_pairs={{0,8},{4,12},{8,0},{12,4},{16,24},{20,28},{24,16},{28,20},{1,9},{5... | collective-permute-start | bytes 393224 | tf_op jit(solution)/shard_map/ppermute | solution.py:374
  8.4 3.8 %collective-permute-done.4.rest_1_ = f32[256,128]{1,0:T(8,128)S(1)} collective-permute-done((f32[256,128]{1,0:T(8,128)S(1)}, f32[256,128]{1,0:T(8,128)S(1)}, u32[]{:S(2)}, u32[]{:S(2)}) %collective-permute-start.4) | collective-permute-done | bytes 131104 | tf_op jit(solution)/shard_map/ppermute | solution.py:374
  12.2 0.5 %collective-permute-start.1 = (f32[2,8,128]{2,1,0:T(8,128)S(1)}, f32[2,8,128]{2,1,0:T(8,128)S(1)}, u32[]{:S(2)}, u32[]{:S(2)}) collective-permute-start(f32[2,8,128]{2,1,0:T(8,128)S(1)} %get-tuple-element.19.start), channel_id=1, source_target_pairs={{0,4},{1,2},{2,1},{3,7},{4,0},{5,6},{6,5},{7,3},{8,12},{9,10},{10,... | collective-permute-start | bytes 24584 | tf_op jit(solution)/shard_map/ppermute | solution.py:370
  12.7 2.9 %collective-permute-start = (f32[2,8,128]{2,1,0:T(8,128)S(1)}, f32[2,8,128]{2,1,0:T(8,128)S(1)}, u32[]{:S(2)}, u32[]{:S(2)}) collective-permute-start(f32[2,8,128]{2,1,0:T(8,128)S(1)} %get-tuple-element.19.start), channel_id=1, source_target_pairs={{0,1},{1,0},{2,3},{3,2},{4,5},{5,4},{6,7},{7,6},{8,9},{9,8},{10,11... | collective-permute-start | bytes 24584 | tf_op jit(solution)/shard_map/ppermute | solution.py:374
  15.6 2.0 %collective-permute-start.2 = (f32[1,8,128]{2,1,0:T(8,128)S(1)}, f32[1,8,128]{2,1,0:T(8,128)S(1)}, u32[]{:S(2)}, u32[]{:S(2)}) collective-permute-start(f32[1,8,128]{2,1,0:T(8,128)S(1)} %slice.3), channel_id=1, source_target_pairs={{0,28},{4,0},{8,4},{12,8},{16,12},{20,16},{24,20},{28,24},{1,29},{... | collective-permute-start | bytes 12296 | tf_op jit(solution)/shard_map/ppermute | solution.py:426
  17.6 1.4 %shard_map.78 = (f32[2,8,128]{2,1,0:T(8,128)S(1)}, f32[2,8,128]{2,1,0:T(8,128)S(1)}) custom-call(f32[2,8,128]{2,1,0:T(8,128)S(1)} %get-tuple-element.19.start, f32[2,8,128]{2,1,0:T(8,128)S(1)} %bitcast.5, bf16[2,1,16,4096]{3,2,1,0:T(8,128)(2,1)S(1)} %copy-done.2, bf16[2,1,16,4096]{3,2,1,0:T(8,128)(2,1)S(1)} %copy-done.3, bf16[4,2,1,16,4096]{4,3,2,1,0:T(8,128)(2,1)S(1)} %copy-done), custom_call_target="tpu_custom_call" | custom-call | flops 1150000000 | bytes 1589248 | tf_op jit(solution)/shard_map/pallas_call | solution.py:349
  19.1 0.0 collective-permute-done.2.ahead
  19.1 2.4 %shard_map.80 = (f32[2,8,128]{2,1,0:T(8,128)S(1)}, f32[2,8,128]{2,1,0:T(8,128)S(1)}, f32[8,8,128]{2,1,0:T(8,128)}) custom-call(f32[2,8,128]{2,1,0:T(8,128)S(1)} %get-tuple-element.20.base, f32[2,8,128]{2,1,0:T(8,128)S(1)} %collective-permute-done.paired, f32[2,8,128]{2,1,0:T(8,128)S(1)} %collective-permute-done.1.other, ...), custom_call_target="tpu_custom_call" | custom-call | flops 1724999936 | bytes 2387968 | tf_op jit(solution)/shard_map/pallas_call | solution.py:349
  21.6 1.2 %shard_map.83 = (f32[1024,128]{1,0:T(8,128)S(1)}, f32[1024,128]{1,0:T(8,128)S(1)}, f32[512,128]{1,0:T(8,128)S(1)}) custom-call(bf16[2,1,16,4096]{3,2,1,0:T(8,128)(2,1)S(1)} %copy-done.3, f32[2,8,128]{2,1,0:T(8,128)S(1)} %get-tuple-element.25.offsets.beside_it), custom_call_target="tpu_custom_call" | custom-call | flops 1150000000 | bytes 270336 | tf_op jit(solution)/shard_map/pallas_call | solution.py:349
  22.7 0.1 collective-permute-start.8
  22.8 1.5 %collective-permute-done.8.refs_0_.rest_0_ = f32[512,128]{1,0:T(8,128)S(1)} collective-permute-done((f32[512,128]{1,0:T(8,128)S(1)}, f32[512,128]{1,0:T(8,128)S(1)}, u32[]{:S(2)}, u32[]{:S(2)}) %collective-permute-start.8) | collective-permute-done | bytes 262176 | tf_op jit(solution)/shard_map/ppermute | solution.py:374
  24.3 0.3 shard_map.84
  24.7 1.6 %collective-permute-start.9 = (f32[256,128]{1,0:T(8,128)S(1)}, f32[256,128]{1,0:T(8,128)S(1)}, u32[]{:S(2)}, u32[]{:S(2)}) collective-permute-start(f32[256,128]{1,0:T(8,128)S(1)} %shard_map.84), channel_id=1, source_target_pairs={{0,8},{4,12},{8,0},{12,4},{16,24},{20,28},{24,16},{28,20},{1,9},{5... | collective-permute-start | bytes 393224 | tf_op jit(solution)/shard_map/ppermute | solution.py:374
  26.3 3.3 %all-to-all-start = ((f32[8,8,128]{2,1,0:T(8,128)}), f32[8,8,128]{2,1,0:T(8,128)S(1)}, u32[]{:S(2)}, u32[]{:S(2)}) async-start(f32[8,8,128]{2,1,0:T(8,128)} %get-tuple-element.23), calls=%async_computation | async-start | bytes 65536 | tf_op jit(solution)/shard_map/all_to_all | solution.py:378
  29.6 0.7 %collective-permute-done.9.rest_1_ = f32[256,128]{1,0:T(8,128)S(1)} collective-permute-done((f32[256,128]{1,0:T(8,128)S(1)}, f32[256,128]{1,0:T(8,128)S(1)}, u32[]{:S(2)}, u32[]{:S(2)}) %collective-permute-start.9) | collective-permute-done | bytes 131104 | tf_op jit(solution)/shard_map/ppermute | solution.py:374
  30.3 4.1 %all-to-all-done.got = f32[8,8,128]{2,1,0:T(8,128)S(1)} async-done(((f32[8,8,128]{2,1,0:T(8,128)}), f32[8,8,128]{2,1,0:T(8,128)S(1)}, u32[]{:S(2)}, u32[]{:S(2)}) %all-to-all-start) | async-done | bytes 32800 | tf_op jit(solution)/shard_map/all_to_all | solution.py:378
  34.4 1.4 %shard_map.81 = (f32[2,8,128]{2,1,0:T(8,128)}, f32[2,8,128]{2,1,0:T(8,128)S(1)}, f32[2,8,128]{2,1,0:T(8,128)S(1)}) custom-call(f32[8,8,128]{2,1,0:T(8,128)S(1)} %all-to-all-done.got, f32[2,8,128]{2,1,0:T(8,128)S(1)} %get-tuple-element.24.drive, f32[2,8,128]{2,1,0:T(8,128)S(1)} %get-tuple-element.25.offsets.beside_it, ...), custom_call_target="tpu_custom_call" | custom-call | flops 1150000000 | bytes 1105920 | tf_op jit(solution)/shard_map/pallas_call | solution.py:349
  35.8 1.9 %collective-permute-start.6 = (f32[2,8,128]{2,1,0:T(8,128)S(1)}, f32[2,8,128]{2,1,0:T(8,128)S(1)}, u32[]{:S(2)}, u32[]{:S(2)}) collective-permute-start(f32[2,8,128]{2,1,0:T(8,128)S(1)} %get-tuple-element.30.vectors), channel_id=1, source_target_pairs={{0,1},{1,0},{2,3},{3,2},{4,5},{5,4},{6,7},{7,6},{8,9},{9,8},{10,11... | collective-permute-start | bytes 24584 | tf_op jit(solution)/shard_map/ppermute | solution.py:374
  37.7 0.7 %shard_map.82.base = f32[2,8,128]{2,1,0:T(8,128)S(1)} custom-call(f32[2,8,128]{2,1,0:T(8,128)S(1)} %get-tuple-element.29.base, f32[2,8,128]{2,1,0:T(8,128)S(1)} %get-tuple-element.30.vectors, bf16[4,2,1,16,4096]{4,3,2,1,0:T(8,128)(2,1)S(1)} %copy-done), custom_call_target="tpu_custom_call" | custom-call | flops 805000000 | bytes 1064960 | tf_op jit(solution)/shard_map/pallas_call | solution.py:349
  38.4 1.1 %collective-permute-done.6.paired = f32[2,8,128]{2,1,0:T(8,128)S(1)} collective-permute-done((f32[2,8,128]{2,1,0:T(8,128)S(1)}, f32[2,8,128]{2,1,0:T(8,128)S(1)}, u32[]{:S(2)}, u32[]{:S(2)}) %collective-permute-start.6) | collective-permute-done | bytes 8224 | tf_op jit(solution)/shard_map/ppermute | solution.py:374
  39.5 1.9 %shard_map.85 = (f32[2,8,128]{2,1,0:T(8,128)S(1)}, f32[8,8,128]{2,1,0:T(8,128)S(1)}) custom-call(f32[2,8,128]{2,1,0:T(8,128)S(1)} %shard_map.82.base, f32[2,8,128]{2,1,0:T(8,128)S(1)} %collective-permute-done.6.paired, f32[2,8,128]{2,1,0:T(8,128)S(1)} %collective-permute-done.7.other, bf16[4,2,1,16,4096]{4,3,2,1,0:T(8,128)(2,1)S(1)} %copy-done, ...), custom_call_target="tpu_custom_call" | custom-call | flops 1724999936 | bytes 2121728 | tf_op jit(solution)/shard_map/pallas_call | solution.py:349
  41.3 7.2 %all_to_all.10.got = f32[8,8,128]{2,1,0:T(8,128)S(1)} all-to-all(f32[8,8,128]{2,1,0:T(8,128)S(1)} %get-tuple-element.33), channel_id=1, replica_groups=mesh['gx'=8,'gy'=4] {'gx'}, dimensions={0} | all-to-all | bytes 65536 | tf_op jit(solution)/shard_map/all_to_all | solution.py:378
  48.6 1.4 %shard_map.86 = f32[2,8,128]{2,1,0:T(8,128)} custom-call(f32[8,8,128]{2,1,0:T(8,128)S(1)} %all_to_all.10.got, f32[2,8,128]{2,1,0:T(8,128)S(1)} %get-tuple-element.34.offsets, f32[1024,128]{1,0:T(8,128)S(1)} %get-tuple-element.35.products, f32[512,128]{1,0:T(8,128)S(1)} %collective-permute-done.8.refs_0_.rest_0_, ...), custom_call_target="tpu_custom_call" | custom-call | flops 1150000000 | bytes 1089536 | tf_op jit(solution)/shard_map/pallas_call | solution.py:349
  (20 shorter events, 0.0 us)
Async XLA Ops:
  0.6 1.0 %copy-start.1 = (bf16[2,1,16,4096]{3,2,1,0:T(8,128)(2,1)S(1)}, bf16[2,1,16,4096]{3,2,1,0:T(8,128)(2,1)}, u32[]{:S(2)}) copy-start(bf16[2,1,16,4096]{3,2,1,0:T(8,128)(2,1)} %blocks.2) | copy-start | bytes 786436
  1.6 0.7 %copy-start.4 = (f32[2,1,1024]{2,1,0:T(1,128)S(1)}, f32[2,1,1024]{2,1,0:T(1,128)}, u32[]{:S(2)}) copy-start(f32[2,1,1024]{2,1,0:T(1,128)} %param.6) | copy-start | bytes 24580
  3.4 14.2 %copy-start = (bf16[4,2,1,16,4096]{4,3,2,1,0:T(8,128)(2,1)S(1)}, bf16[4,2,1,16,4096]{4,3,2,1,0:T(8,128)(2,1)}, u32[]{:S(2)}) copy-start(bf16[4,2,1,16,4096]{4,3,2,1,0:T(8,128)(2,1)} %side.7) | copy-start | bytes 3145732
  3.5 14.2 %copy-start.2 = (bf16[2,1,16,4096]{3,2,1,0:T(8,128)(2,1)S(1)}, bf16[2,1,16,4096]{3,2,1,0:T(8,128)(2,1)}, u32[]{:S(2)}) copy-start(bf16[2,1,16,4096]{3,2,1,0:T(8,128)(2,1)} %diag.1) | copy-start | bytes 786436
  3.5 14.2 %copy-start.3 = (bf16[2,1,16,4096]{3,2,1,0:T(8,128)(2,1)S(1)}, bf16[2,1,16,4096]{3,2,1,0:T(8,128)(2,1)}, u32[]{:S(2)}) copy-start(bf16[2,1,16,4096]{3,2,1,0:T(8,128)(2,1)} %blocks.3) | copy-start | bytes 786436
  3.5 1.7 %collective-permute-start.3 = (f32[512,128]{1,0:T(8,128)S(1)}, f32[512,128]{1,0:T(8,128)S(1)}, u32[]{:S(2)}, u32[]{:S(2)}) collective-permute-start(f32[512,128]{1,0:T(8,128)S(1)} %get-tuple-element.22.own), channel_id=1, source_target_pairs={{0,4},{4,0},{8,12},{12,8},{16,20},{20,16},{24,28},{28,24},{1,5},{5... | collective-permute-start | bytes 786440 | tf_op jit(solution)/shard_map/ppermute | solution.py:374
  5.5 12.1 %copy-start.5 = (f32[2,1,1024]{2,1,0:T(1,128)S(1)}, f32[2,1,1024]{2,1,0:T(1,128)}, u32[]{:S(2)}) copy-start(f32[2,1,1024]{2,1,0:T(1,128)} %param.7) | copy-start | bytes 24580
  5.5 6.7 %collective-permute-start.4 = (f32[256,128]{1,0:T(8,128)S(1)}, f32[256,128]{1,0:T(8,128)S(1)}, u32[]{:S(2)}, u32[]{:S(2)}) collective-permute-start(f32[256,128]{1,0:T(8,128)S(1)} %shard_map.79), channel_id=1, source_target_pairs={{0,8},{4,12},{8,0},{12,4},{16,24},{20,28},{24,16},{28,20},{1,9},{5... | collective-permute-start | bytes 393224 | tf_op jit(solution)/shard_map/ppermute | solution.py:374
  12.2 6.9 %collective-permute-start.5 = (f32[256,128]{1,0:T(8,128)S(1)}, f32[256,128]{1,0:T(8,128)S(1)}, u32[]{:S(2)}, u32[]{:S(2)}) collective-permute-start(f32[256,128]{1,0:T(8,128)S(1)} %collective-permute-done.4.rest_1_), channel_id=1, source_target_pairs={{0,4},{4,0},{8,12},{12,8},{16,20},{20,16},{24,28},{28,24},{1,5},{5... | collective-permute-start | bytes 393224 | tf_op jit(solution)/shard_map/ppermute | solution.py:374
  12.2 6.9 %collective-permute-start.1 = (f32[2,8,128]{2,1,0:T(8,128)S(1)}, f32[2,8,128]{2,1,0:T(8,128)S(1)}, u32[]{:S(2)}, u32[]{:S(2)}) collective-permute-start(f32[2,8,128]{2,1,0:T(8,128)S(1)} %get-tuple-element.19.start), channel_id=1, source_target_pairs={{0,4},{1,2},{2,1},{3,7},{4,0},{5,6},{6,5},{7,3},{8,12},{9,10},{10,... | collective-permute-start | bytes 24584 | tf_op jit(solution)/shard_map/ppermute | solution.py:370
  12.7 6.4 %collective-permute-start = (f32[2,8,128]{2,1,0:T(8,128)S(1)}, f32[2,8,128]{2,1,0:T(8,128)S(1)}, u32[]{:S(2)}, u32[]{:S(2)}) collective-permute-start(f32[2,8,128]{2,1,0:T(8,128)S(1)} %get-tuple-element.19.start), channel_id=1, source_target_pairs={{0,1},{1,0},{2,3},{3,2},{4,5},{5,4},{6,7},{7,6},{8,9},{9,8},{10,11... | collective-permute-start | bytes 24584 | tf_op jit(solution)/shard_map/ppermute | solution.py:374
  15.6 3.5 %collective-permute-start.2 = (f32[1,8,128]{2,1,0:T(8,128)S(1)}, f32[1,8,128]{2,1,0:T(8,128)S(1)}, u32[]{:S(2)}, u32[]{:S(2)}) collective-permute-start(f32[1,8,128]{2,1,0:T(8,128)S(1)} %slice.3), channel_id=1, source_target_pairs={{0,28},{4,0},{8,4},{12,8},{16,12},{20,16},{24,20},{28,24},{1,29},{... | collective-permute-start | bytes 12296 | tf_op jit(solution)/shard_map/ppermute | solution.py:426
  22.7 1.9 %copy-start.6 = (f32[1024,128]{1,0:T(8,128)}, f32[1024,128]{1,0:T(8,128)S(1)}, u32[]{:S(2)}) copy-start(f32[1024,128]{1,0:T(8,128)S(1)} %get-tuple-element.31.upper) | copy-start | bytes 1572868
  22.7 1.6 %collective-permute-start.8 = (f32[512,128]{1,0:T(8,128)S(1)}, f32[512,128]{1,0:T(8,128)S(1)}, u32[]{:S(2)}, u32[]{:S(2)}) collective-permute-start(f32[512,128]{1,0:T(8,128)S(1)} %get-tuple-element.32.own), channel_id=1, source_target_pairs={{0,4},{4,0},{8,12},{12,8},{16,20},{20,16},{24,28},{28,24},{1,5},{5... | collective-permute-start | bytes 786440 | tf_op jit(solution)/shard_map/ppermute | solution.py:374
  24.7 5.6 %collective-permute-start.9 = (f32[256,128]{1,0:T(8,128)S(1)}, f32[256,128]{1,0:T(8,128)S(1)}, u32[]{:S(2)}, u32[]{:S(2)}) collective-permute-start(f32[256,128]{1,0:T(8,128)S(1)} %shard_map.84), channel_id=1, source_target_pairs={{0,8},{4,12},{8,0},{12,4},{16,24},{20,28},{24,16},{28,20},{1,9},{5... | collective-permute-start | bytes 393224 | tf_op jit(solution)/shard_map/ppermute | solution.py:374
  26.3 8.1 %all-to-all-start = ((f32[8,8,128]{2,1,0:T(8,128)}), f32[8,8,128]{2,1,0:T(8,128)S(1)}, u32[]{:S(2)}, u32[]{:S(2)}) async-start(f32[8,8,128]{2,1,0:T(8,128)} %get-tuple-element.23), calls=%async_computation | async-start | bytes 65536 | tf_op jit(solution)/shard_map/all_to_all | solution.py:378
  30.3 9.2 %collective-permute-start.10 = (f32[256,128]{1,0:T(8,128)S(1)}, f32[256,128]{1,0:T(8,128)S(1)}, u32[]{:S(2)}, u32[]{:S(2)}) collective-permute-start(f32[256,128]{1,0:T(8,128)S(1)} %collective-permute-done.9.rest_1_), channel_id=1, source_target_pairs={{0,4},{4,0},{8,12},{12,8},{16,20},{20,16},{24,28},{28,24},{1,5},{5... | collective-permute-start | bytes 393224 | tf_op jit(solution)/shard_map/ppermute | solution.py:374
  35.8 2.6 %collective-permute-start.7 = (f32[2,8,128]{2,1,0:T(8,128)S(1)}, f32[2,8,128]{2,1,0:T(8,128)S(1)}, u32[]{:S(2)}, u32[]{:S(2)}) collective-permute-start(f32[2,8,128]{2,1,0:T(8,128)S(1)} %get-tuple-element.30.vectors), channel_id=1, source_target_pairs={{0,4},{1,2},{2,1},{3,7},{4,0},{5,6},{6,5},{7,3},{8,12},{9,10},{10,... | collective-permute-start | bytes 24584 | tf_op jit(solution)/shard_map/ppermute | solution.py:370
  35.8 3.7 %collective-permute-start.6 = (f32[2,8,128]{2,1,0:T(8,128)S(1)}, f32[2,8,128]{2,1,0:T(8,128)S(1)}, u32[]{:S(2)}, u32[]{:S(2)}) collective-permute-start(f32[2,8,128]{2,1,0:T(8,128)S(1)} %get-tuple-element.30.vectors), channel_id=1, source_target_pairs={{0,1},{1,0},{2,3},{3,2},{4,5},{5,4},{6,7},{7,6},{8,9},{9,8},{10,11... | collective-permute-start | bytes 24584 | tf_op jit(solution)/shard_map/ppermute | solution.py:374
  37.7 1.8 %copy-start.7 = (f32[1024,128]{1,0:T(8,128)S(1)}, f32[1024,128]{1,0:T(8,128)}, u32[]{:S(2)}) copy-start(f32[1024,128]{1,0:T(8,128)} %copy-done.6) | copy-start | bytes 1572868

commit v6 on v5

--- a/solution.py
+++ b/solution.py
@@ -422,10 +422,11 @@
         return turned_blocks, products, partners, passed
 
     lower, lower_products, lower_partners, (start,) = prepare(False, x_lower, start)
+    upper, upper_products, upper_partners, _ = prepare(True, x_upper, lower_products)
     paired, other = swaps(start)
     ahead = lax.ppermute(start[:1], "gx", [(i, (i - 1) % count) for i in range(count)])
     rhs, base = call(
-        base_kernel, [start, source, diag_inverse, x_upper, side_blocks], [vec, vec], [], 1.0
+        base_kernel, [start, source, diag_inverse, x_upper, side_blocks], [vec, vec], [], 5.0
     )
     drive, offsets, sent = call(
         functools.partial(forward_offset_kernel, levels),
@@ -434,7 +435,6 @@
         [],
         1.5,
     )
-    upper, upper_products, upper_partners, _ = prepare(True, x_upper, offsets)
     forward, copy, base = call(
         functools.partial(forward_kernel, levels),
         [exchange(sent, "gx"), drive, offsets, rhs, lower_products] + lower_partners,

time: 50.3 us -> 43.4 us (0.86)
  waiting for transfers between devices: 12.4 us -> 6.42 us
  starting transfers between devices: 15.7 us -> 14.7 us
    ppermute x8, waiting for transfers between devices: 8.26 us -> 2.08 us  [crossed(): lax.ppermute(block, axis, [(i, i ^ distance) for i in range(lax.axis_size...]
    ppermute x1, starting transfers between devices: 2 us -> 0.39 us  [local(): lax.ppermute(start[:1], 'gx', [(i, (i - 1) % count) for i in range(count)])]
    ppermute x8, starting transfers between devices: 9.85 us -> 10.9 us  [crossed(): lax.ppermute(block, axis, [(i, i ^ distance) for i in range(lax.axis_size...]
    ppermute x2, starting transfers between devices: 0.51 us -> 0.01 us  [swaps(): return (crossed(block, 'gy', 1), lax.ppermute(block, ('gx', 'gy'), route))]
  transfers between devices with their start and end apart: 12 -> 12, of which waited for: 6 -> 3; matrix products, arithmetic and copies ran while one was open for 0% -> 0% of each run, Pallas kernels for 7% -> 17%
where the time goes in v6:
time: 43.4 us; the launch traced here: 43.1 us
  starting transfers between devices  14.7 us (34%)
  Pallas kernels  12.3 us (28%)
  blocking collectives  7.22 us (17%)
  waiting for transfers between devices  6.42 us (15%)
  local copies, waits for them, and re-layouts  1.67 us (4%)
  between operations  0.73 us (2%)
    pallas_call x10, Pallas kernels, call(): pl.pallas_call(kernel, out_shape=outs, in_specs=[pl.BlockSpec(memory_spac...  12.3 us
    ppermute x8, starting transfers between devices, crossed(): lax.ppermute(block, axis, [(i, i ^ distance) for i in range(lax.axis_size...  10.9 us
    all_to_all x1, blocking collectives, exchange(): return lax.all_to_all(slots, axis, 0, 0)  7.22 us
    all_to_all x1, waiting for transfers between devices, exchange(): return lax.all_to_all(slots, axis, 0, 0)  4.33 us
    all_to_all x1, starting transfers between devices, exchange(): return lax.all_to_all(slots, axis, 0, 0)  3.42 us
    ppermute x8, waiting for transfers between devices, crossed(): lax.ppermute(block, axis, [(i, i ^ distance) for i in range(lax.axis_size...  2.08 us
    unnamed x16, local copies, waits for them, and re-layouts  1.66 us
  transfers between devices with their start and end apart: 12, of which 3 were waited for; matrix products, arithmetic and copies ran while one was open for 0% of the time, Pallas kernels for 17%

profile of v6, /device:TPU:0, one launch (start us, length us, event | category | flops | bytes accessed | tf_op | source)
XLA Modules:
  0.0 43.1 jit_solution(13386931471324890459)
XLA Ops:
  0.6 0.9 %copy-done.1 = bf16[2,1,16,4096]{3,2,1,0:T(8,128)(2,1)S(1)} copy-done((bf16[2,1,16,4096]{3,2,1,0:T(8,128)(2,1)S(1)}, bf16[2,1,16,4096]{3,2,1,0:T(8,128)(2,1)}, u32[]{:S(2)}) %copy-start.1) | copy-done | bytes 262168
  1.6 0.7 %copy-done.4 = f32[2,1,1024]{2,1,0:T(1,128)S(1)} copy-done((f32[2,1,1024]{2,1,0:T(1,128)S(1)}, f32[2,1,1024]{2,1,0:T(1,128)}, u32[]{:S(2)}) %copy-start.4) | copy-done | bytes 8216
  2.3 1.2 %shard_map.77 = (f32[2,8,128]{2,1,0:T(8,128)S(1)}, f32[1024,128]{1,0:T(8,128)S(1)}, f32[1024,128]{1,0:T(8,128)S(1)}, f32[512,128]{1,0:T(8,128)S(1)}) custom-call(bf16[2,1,16,4096]{3,2,1,0:T(8,128)(2,1)S(1)} %copy-done.1, f32[2,8,128]{2,1,0:T(8,128)S(1)} %bitcast.4), custom_call_target="tpu_custom_call" | custom-call | flops 1150000000 | bytes 270336 | tf_op jit(solution)/shard_map/pallas_call | solution.py:349
  3.4 0.0 copy-start.3
  3.5 0.5 %collective-permute-start.3 = (f32[512,128]{1,0:T(8,128)S(1)}, f32[512,128]{1,0:T(8,128)S(1)}, u32[]{:S(2)}, u32[]{:S(2)}) collective-permute-start(f32[512,128]{1,0:T(8,128)S(1)} %get-tuple-element.22.own), channel_id=1, source_target_pairs={{0,4},{4,0},{8,12},{12,8},{16,20},{20,16},{24,28},{28,24},{1,5},{5... | collective-permute-start | bytes 786440 | tf_op jit(solution)/shard_map/ppermute | solution.py:374
  4.0 1.2 %collective-permute-done.3.refs_0_.rest_0_ = f32[512,128]{1,0:T(8,128)S(1)} collective-permute-done((f32[512,128]{1,0:T(8,128)S(1)}, f32[512,128]{1,0:T(8,128)S(1)}, u32[]{:S(2)}, u32[]{:S(2)}) %collective-permute-start.3) | collective-permute-done | bytes 262176 | tf_op jit(solution)/shard_map/ppermute | solution.py:374
  5.1 0.3 shard_map.79
  5.5 2.9 %collective-permute-start.4 = (f32[256,128]{1,0:T(8,128)S(1)}, f32[256,128]{1,0:T(8,128)S(1)}, u32[]{:S(2)}, u32[]{:S(2)}) collective-permute-start(f32[256,128]{1,0:T(8,128)S(1)} %shard_map.79), channel_id=1, source_target_pairs={{0,8},{4,12},{8,0},{12,4},{16,24},{20,28},{24,16},{28,20},{1,9},{5... | collective-permute-start | bytes 393224 | tf_op jit(solution)/shard_map/ppermute | solution.py:374
  8.4 3.2 %collective-permute-start = (f32[2,8,128]{2,1,0:T(8,128)S(1)}, f32[2,8,128]{2,1,0:T(8,128)S(1)}, u32[]{:S(2)}, u32[]{:S(2)}) collective-permute-start(f32[2,8,128]{2,1,0:T(8,128)S(1)} %get-tuple-element.19.start), channel_id=1, source_target_pairs={{0,1},{1,0},{2,3},{3,2},{4,5},{5,4},{6,7},{7,6},{8,9},{9,8},{10,11... | collective-permute-start | bytes 24584 | tf_op jit(solution)/shard_map/ppermute | solution.py:374
  11.5 0.4 collective-permute-start.2
  11.9 1.2 %shard_map.83 = (f32[1024,128]{1,0:T(8,128)S(1)}, f32[1024,128]{1,0:T(8,128)S(1)}, f32[512,128]{1,0:T(8,128)S(1)}) custom-call(bf16[2,1,16,4096]{3,2,1,0:T(8,128)(2,1)S(1)} %copy-done.3, f32[1024,128]{1,0:T(8,128)S(1)} %get-tuple-element.27.products.beside_it), custom_call_target="tpu_custom_call" | custom-call | flops 1150000000 | bytes 786432 | tf_op jit(solution)/shard_map/pallas_call | solution.py:349
  13.1 0.2 collective-permute-start.8
  13.3 0.0 collective-permute-done.4.rest_1_
  13.3 0.4 collective-permute-start.5
  13.7 1.4 %shard_map.78 = (f32[2,8,128]{2,1,0:T(8,128)S(1)}, f32[2,8,128]{2,1,0:T(8,128)S(1)}) custom-call(f32[2,8,128]{2,1,0:T(8,128)S(1)} %get-tuple-element.19.start, f32[2,8,128]{2,1,0:T(8,128)S(1)} %bitcast.5, bf16[2,1,16,4096]{3,2,1,0:T(8,128)(2,1)S(1)} %copy-done.2, bf16[2,1,16,4096]{3,2,1,0:T(8,128)(2,1)S(1)} %copy-done.3, bf16[4,2,1,16,4096]{4,3,2,1,0:T(8,128)(2,1)S(1)} %copy-done), custom_call_target="tpu_custom_call" | custom-call | flops 5750000128 | bytes 1589248 | tf_op jit(solution)/shard_map/pallas_call | solution.py:349
  15.1 0.0 collective-permute-done.8.refs_0_.rest_0_
  15.2 0.3 shard_map.84
  15.5 0.6 %collective-permute-start.9 = (f32[256,128]{1,0:T(8,128)S(1)}, f32[256,128]{1,0:T(8,128)S(1)}, u32[]{:S(2)}, u32[]{:S(2)}) collective-permute-start(f32[256,128]{1,0:T(8,128)S(1)} %shard_map.84), channel_id=1, source_target_pairs={{0,8},{4,12},{8,0},{12,4},{16,24},{20,28},{24,16},{28,20},{1,9},{5... | collective-permute-start | bytes 393224 | tf_op jit(solution)/shard_map/ppermute | solution.py:374
  16.1 0.0 collective-permute-done.2.ahead
  16.1 0.0 collective-permute-done.5.rest_2_
  16.1 2.4 %shard_map.80 = (f32[2,8,128]{2,1,0:T(8,128)S(1)}, f32[2,8,128]{2,1,0:T(8,128)S(1)}, f32[8,8,128]{2,1,0:T(8,128)}) custom-call(f32[2,8,128]{2,1,0:T(8,128)S(1)} %get-tuple-element.20.base, f32[2,8,128]{2,1,0:T(8,128)S(1)} %collective-permute-done.paired, f32[2,8,128]{2,1,0:T(8,128)S(1)} %collective-permute-done.1.other, ...), custom_call_target="tpu_custom_call" | custom-call | flops 1724999936 | bytes 2387968 | tf_op jit(solution)/shard_map/pallas_call | solution.py:349
  18.5 3.4 %all-to-all-start = ((f32[8,8,128]{2,1,0:T(8,128)}), f32[8,8,128]{2,1,0:T(8,128)S(1)}, u32[]{:S(2)}, u32[]{:S(2)}) async-start(f32[8,8,128]{2,1,0:T(8,128)} %get-tuple-element.23), calls=%async_computation | async-start | bytes 65536 | tf_op jit(solution)/shard_map/all_to_all | solution.py:378
  21.9 0.5 %collective-permute-start.10 = (f32[256,128]{1,0:T(8,128)S(1)}, f32[256,128]{1,0:T(8,128)S(1)}, u32[]{:S(2)}, u32[]{:S(2)}) collective-permute-start(f32[256,128]{1,0:T(8,128)S(1)} %collective-permute-done.9.rest_1_), channel_id=1, source_target_pairs={{0,4},{4,0},{8,12},{12,8},{16,20},{20,16},{24,28},{28,24},{1,5},{5... | collective-permute-start | bytes 393224 | tf_op jit(solution)/shard_map/ppermute | solution.py:374
  22.4 4.3 %all-to-all-done.got = f32[8,8,128]{2,1,0:T(8,128)S(1)} async-done(((f32[8,8,128]{2,1,0:T(8,128)}), f32[8,8,128]{2,1,0:T(8,128)S(1)}, u32[]{:S(2)}, u32[]{:S(2)}) %all-to-all-start) | async-done | bytes 32800 | tf_op jit(solution)/shard_map/all_to_all | solution.py:378
  26.8 1.4 %shard_map.81 = (f32[2,8,128]{2,1,0:T(8,128)}, f32[2,8,128]{2,1,0:T(8,128)S(1)}, f32[2,8,128]{2,1,0:T(8,128)S(1)}) custom-call(f32[8,8,128]{2,1,0:T(8,128)S(1)} %all-to-all-done.got, f32[2,8,128]{2,1,0:T(8,128)S(1)} %get-tuple-element.24.drive, f32[2,8,128]{2,1,0:T(8,128)S(1)} %get-tuple-element.25.offsets, f32[2,8,128]{2,1,0:T(8,128)S(1)} %get-tuple-element.26.rhs, ...), custom_call_target="tpu_custom_call" | custom-call | flops 1150000000 | bytes 1105920 | tf_op jit(solution)/shard_map/pallas_call | solution.py:349
  28.2 2.7 %collective-permute-start.6 = (f32[2,8,128]{2,1,0:T(8,128)S(1)}, f32[2,8,128]{2,1,0:T(8,128)S(1)}, u32[]{:S(2)}, u32[]{:S(2)}) collective-permute-start(f32[2,8,128]{2,1,0:T(8,128)S(1)} %get-tuple-element.30.vectors), channel_id=1, source_target_pairs={{0,1},{1,0},{2,3},{3,2},{4,5},{5,4},{6,7},{7,6},{8,9},{9,8},{10,11... | collective-permute-start | bytes 24584 | tf_op jit(solution)/shard_map/ppermute | solution.py:374
  30.9 0.7 %shard_map.82.base = f32[2,8,128]{2,1,0:T(8,128)S(1)} custom-call(f32[2,8,128]{2,1,0:T(8,128)S(1)} %get-tuple-element.29.base, f32[2,8,128]{2,1,0:T(8,128)S(1)} %get-tuple-element.30.vectors, bf16[4,2,1,16,4096]{4,3,2,1,0:T(8,128)(2,1)S(1)} %copy-done), custom_call_target="tpu_custom_call" | custom-call | flops 805000000 | bytes 1064960 | tf_op jit(solution)/shard_map/pallas_call | solution.py:349
  31.6 0.0 collective-permute-done.7.other
  31.6 0.9 %collective-permute-done.6.paired = f32[2,8,128]{2,1,0:T(8,128)S(1)} collective-permute-done((f32[2,8,128]{2,1,0:T(8,128)S(1)}, f32[2,8,128]{2,1,0:T(8,128)S(1)}, u32[]{:S(2)}, u32[]{:S(2)}) %collective-permute-start.6) | collective-permute-done | bytes 8224 | tf_op jit(solution)/shard_map/ppermute | solution.py:374
  32.5 1.9 %shard_map.85 = (f32[2,8,128]{2,1,0:T(8,128)S(1)}, f32[8,8,128]{2,1,0:T(8,128)S(1)}) custom-call(f32[2,8,128]{2,1,0:T(8,128)S(1)} %shard_map.82.base, f32[2,8,128]{2,1,0:T(8,128)S(1)} %collective-permute-done.6.paired, f32[2,8,128]{2,1,0:T(8,128)S(1)} %collective-permute-done.7.other, bf16[4,2,1,16,4096]{4,3,2,1,0:T(8,128)(2,1)S(1)} %copy-done, ...), custom_call_target="tpu_custom_call" | custom-call | flops 1724999936 | bytes 2121728 | tf_op jit(solution)/shard_map/pallas_call | solution.py:349
  34.4 7.2 %all_to_all.10.got = f32[8,8,128]{2,1,0:T(8,128)S(1)} all-to-all(f32[8,8,128]{2,1,0:T(8,128)S(1)} %get-tuple-element.33), channel_id=1, replica_groups=mesh['gx'=8,'gy'=4] {'gx'}, dimensions={0} | all-to-all | bytes 65536 | tf_op jit(solution)/shard_map/all_to_all | solution.py:378
  41.6 1.4 %shard_map.86 = f32[2,8,128]{2,1,0:T(8,128)} custom-call(f32[8,8,128]{2,1,0:T(8,128)S(1)} %all_to_all.10.got, f32[2,8,128]{2,1,0:T(8,128)S(1)} %get-tuple-element.34.offsets, f32[1024,128]{1,0:T(8,128)S(1)} %get-tuple-element.35.products, f32[512,128]{1,0:T(8,128)S(1)} %collective-permute-done.8.refs_0_.rest_0_, ...), custom_call_target="tpu_custom_call" | custom-call | flops 1150000000 | bytes 1089536 | tf_op jit(solution)/shard_map/pallas_call | solution.py:349
  (20 shorter events, 0.0 us)
Async XLA Ops:
  0.6 1.0 %copy-start.1 = (bf16[2,1,16,4096]{3,2,1,0:T(8,128)(2,1)S(1)}, bf16[2,1,16,4096]{3,2,1,0:T(8,128)(2,1)}, u32[]{:S(2)}) copy-start(bf16[2,1,16,4096]{3,2,1,0:T(8,128)(2,1)} %blocks.2) | copy-start | bytes 786436
  1.6 0.7 %copy-start.4 = (f32[2,1,1024]{2,1,0:T(1,128)S(1)}, f32[2,1,1024]{2,1,0:T(1,128)}, u32[]{:S(2)}) copy-start(f32[2,1,1024]{2,1,0:T(1,128)} %param.6) | copy-start | bytes 24580
  3.4 8.5 %copy-start.3 = (bf16[2,1,16,4096]{3,2,1,0:T(8,128)(2,1)S(1)}, bf16[2,1,16,4096]{3,2,1,0:T(8,128)(2,1)}, u32[]{:S(2)}) copy-start(bf16[2,1,16,4096]{3,2,1,0:T(8,128)(2,1)} %blocks.3) | copy-start | bytes 786436
  3.5 1.7 %collective-permute-start.3 = (f32[512,128]{1,0:T(8,128)S(1)}, f32[512,128]{1,0:T(8,128)S(1)}, u32[]{:S(2)}, u32[]{:S(2)}) collective-permute-start(f32[512,128]{1,0:T(8,128)S(1)} %get-tuple-element.22.own), channel_id=1, source_target_pairs={{0,4},{4,0},{8,12},{12,8},{16,20},{20,16},{24,28},{28,24},{1,5},{5... | collective-permute-start | bytes 786440 | tf_op jit(solution)/shard_map/ppermute | solution.py:374
  5.5 7.8 %collective-permute-start.4 = (f32[256,128]{1,0:T(8,128)S(1)}, f32[256,128]{1,0:T(8,128)S(1)}, u32[]{:S(2)}, u32[]{:S(2)}) collective-permute-start(f32[256,128]{1,0:T(8,128)S(1)} %shard_map.79), channel_id=1, source_target_pairs={{0,8},{4,12},{8,0},{12,4},{16,24},{20,28},{24,16},{28,20},{1,9},{5... | collective-permute-start | bytes 393224 | tf_op jit(solution)/shard_map/ppermute | solution.py:374
  8.4 7.7 %collective-permute-start.1 = (f32[2,8,128]{2,1,0:T(8,128)S(1)}, f32[2,8,128]{2,1,0:T(8,128)S(1)}, u32[]{:S(2)}, u32[]{:S(2)}) collective-permute-start(f32[2,8,128]{2,1,0:T(8,128)S(1)} %get-tuple-element.19.start), channel_id=1, source_target_pairs={{0,4},{1,2},{2,1},{3,7},{4,0},{5,6},{6,5},{7,3},{8,12},{9,10},{10,... | collective-permute-start | bytes 24584 | tf_op jit(solution)/shard_map/ppermute | solution.py:370
  8.4 7.7 %collective-permute-start = (f32[2,8,128]{2,1,0:T(8,128)S(1)}, f32[2,8,128]{2,1,0:T(8,128)S(1)}, u32[]{:S(2)}, u32[]{:S(2)}) collective-permute-start(f32[2,8,128]{2,1,0:T(8,128)S(1)} %get-tuple-element.19.start), channel_id=1, source_target_pairs={{0,1},{1,0},{2,3},{3,2},{4,5},{5,4},{6,7},{7,6},{8,9},{9,8},{10,11... | collective-permute-start | bytes 24584 | tf_op jit(solution)/shard_map/ppermute | solution.py:374
  11.5 4.5 %collective-permute-start.2 = (f32[1,8,128]{2,1,0:T(8,128)S(1)}, f32[1,8,128]{2,1,0:T(8,128)S(1)}, u32[]{:S(2)}, u32[]{:S(2)}) collective-permute-start(f32[1,8,128]{2,1,0:T(8,128)S(1)} %slice.3), channel_id=1, source_target_pairs={{0,28},{4,0},{8,4},{12,8},{16,12},{20,16},{24,20},{28,24},{1,29},{... | collective-permute-start | bytes 12296 | tf_op jit(solution)/shard_map/ppermute | solution.py:427
  11.9 1.8 %copy-start = (bf16[4,2,1,16,4096]{4,3,2,1,0:T(8,128)(2,1)S(1)}, bf16[4,2,1,16,4096]{4,3,2,1,0:T(8,128)(2,1)}, u32[]{:S(2)}) copy-start(bf16[4,2,1,16,4096]{4,3,2,1,0:T(8,128)(2,1)} %side.7) | copy-start | bytes 3145732
  11.9 1.8 %copy-start.2 = (bf16[2,1,16,4096]{3,2,1,0:T(8,128)(2,1)S(1)}, bf16[2,1,16,4096]{3,2,1,0:T(8,128)(2,1)}, u32[]{:S(2)}) copy-start(bf16[2,1,16,4096]{3,2,1,0:T(8,128)(2,1)} %diag.1) | copy-start | bytes 786436
  11.9 1.8 %copy-start.5 = (f32[2,1,1024]{2,1,0:T(1,128)S(1)}, f32[2,1,1024]{2,1,0:T(1,128)}, u32[]{:S(2)}) copy-start(f32[2,1,1024]{2,1,0:T(1,128)} %param.7) | copy-start | bytes 24580
  13.1 2.0 %copy-start.6 = (f32[1024,128]{1,0:T(8,128)}, f32[1024,128]{1,0:T(8,128)S(1)}, u32[]{:S(2)}) copy-start(f32[1024,128]{1,0:T(8,128)S(1)} %get-tuple-element.31.upper) | copy-start | bytes 1572868
  13.1 2.0 %collective-permute-start.8 = (f32[512,128]{1,0:T(8,128)S(1)}, f32[512,128]{1,0:T(8,128)S(1)}, u32[]{:S(2)}, u32[]{:S(2)}) collective-permute-start(f32[512,128]{1,0:T(8,128)S(1)} %get-tuple-element.32.own), channel_id=1, source_target_pairs={{0,4},{4,0},{8,12},{12,8},{16,20},{20,16},{24,28},{28,24},{1,5},{5... | collective-permute-start | bytes 786440 | tf_op jit(solution)/shard_map/ppermute | solution.py:374
  13.3 2.8 %collective-permute-start.5 = (f32[256,128]{1,0:T(8,128)S(1)}, f32[256,128]{1,0:T(8,128)S(1)}, u32[]{:S(2)}, u32[]{:S(2)}) collective-permute-start(f32[256,128]{1,0:T(8,128)S(1)} %collective-permute-done.4.rest_1_), channel_id=1, source_target_pairs={{0,4},{4,0},{8,12},{12,8},{16,20},{20,16},{24,28},{28,24},{1,5},{5... | collective-permute-start | bytes 393224 | tf_op jit(solution)/shard_map/ppermute | solution.py:374
  15.5 6.4 %collective-permute-start.9 = (f32[256,128]{1,0:T(8,128)S(1)}, f32[256,128]{1,0:T(8,128)S(1)}, u32[]{:S(2)}, u32[]{:S(2)}) collective-permute-start(f32[256,128]{1,0:T(8,128)S(1)} %shard_map.84), channel_id=1, source_target_pairs={{0,8},{4,12},{8,0},{12,4},{16,24},{20,28},{24,16},{28,20},{1,9},{5... | collective-permute-start | bytes 393224 | tf_op jit(solution)/shard_map/ppermute | solution.py:374
  18.5 8.3 %all-to-all-start = ((f32[8,8,128]{2,1,0:T(8,128)}), f32[8,8,128]{2,1,0:T(8,128)S(1)}, u32[]{:S(2)}, u32[]{:S(2)}) async-start(f32[8,8,128]{2,1,0:T(8,128)} %get-tuple-element.23), calls=%async_computation | async-start | bytes 65536 | tf_op jit(solution)/shard_map/all_to_all | solution.py:378
  21.9 9.7 %collective-permute-start.10 = (f32[256,128]{1,0:T(8,128)S(1)}, f32[256,128]{1,0:T(8,128)S(1)}, u32[]{:S(2)}, u32[]{:S(2)}) collective-permute-start(f32[256,128]{1,0:T(8,128)S(1)} %collective-permute-done.9.rest_1_), channel_id=1, source_target_pairs={{0,4},{4,0},{8,12},{12,8},{16,20},{20,16},{24,28},{28,24},{1,5},{5... | collective-permute-start | bytes 393224 | tf_op jit(solution)/shard_map/ppermute | solution.py:374
  28.2 3.4 %collective-permute-start.7 = (f32[2,8,128]{2,1,0:T(8,128)S(1)}, f32[2,8,128]{2,1,0:T(8,128)S(1)}, u32[]{:S(2)}, u32[]{:S(2)}) collective-permute-start(f32[2,8,128]{2,1,0:T(8,128)S(1)} %get-tuple-element.30.vectors), channel_id=1, source_target_pairs={{0,4},{1,2},{2,1},{3,7},{4,0},{5,6},{6,5},{7,3},{8,12},{9,10},{10,... | collective-permute-start | bytes 24584 | tf_op jit(solution)/shard_map/ppermute | solution.py:370
  28.2 4.3 %collective-permute-start.6 = (f32[2,8,128]{2,1,0:T(8,128)S(1)}, f32[2,8,128]{2,1,0:T(8,128)S(1)}, u32[]{:S(2)}, u32[]{:S(2)}) collective-permute-start(f32[2,8,128]{2,1,0:T(8,128)S(1)} %get-tuple-element.30.vectors), channel_id=1, source_target_pairs={{0,1},{1,0},{2,3},{3,2},{4,5},{5,4},{6,7},{7,6},{8,9},{9,8},{10,11... | collective-permute-start | bytes 24584 | tf_op jit(solution)/shard_map/ppermute | solution.py:374
  30.9 1.6 %copy-start.7 = (f32[1024,128]{1,0:T(8,128)S(1)}, f32[1024,128]{1,0:T(8,128)}, u32[]{:S(2)}) copy-start(f32[1024,128]{1,0:T(8,128)} %copy-done.6) | copy-start | bytes 1572868

commit v7 on v6

v7 whole, which is shorter than its diff:
```python
import functools

import jax
import jax.numpy as jnp
from jax import lax
from jax.experimental import pallas as pl
from jax.experimental.pallas import tpu as pltpu
from jax.sharding import PartitionSpec as P

LANES = 128
F32 = jnp.float32
BF16 = jnp.bfloat16


def lane_bit(shape, shift):
    return (lax.broadcasted_iota(jnp.int32, shape, len(shape) - 1) & shift) != 0


def segment_sums(leaf, tiles, rows):
    shape = (rows, LANES)

    def node(base, stride, shift):
        if stride == tiles:
            return leaf(base)
        low = node(base, stride * 2, shift * 2)
        high = node(base + stride, stride * 2, shift * 2)
        low = low + pltpu.roll(low, LANES - shift, 1)
        high = high + pltpu.roll(high, shift, 1)
        return jnp.where(lane_bit(shape, shift), high, low)

    part = node(0, 1, 2)
    odd = lane_bit(shape, 1)
    part = part + jnp.where(odd, pltpu.roll(part, 1, 1), pltpu.roll(part, LANES - 1, 1))
    upper = lane_bit(shape, LANES // 2)
    return jnp.where(upper == odd, part, pltpu.roll(part, LANES // 2, 1))


def apply(terms):
    rows = terms[0][1].shape[0]
    tiles = LANES // 4

    def leaf(t):
        return sum(read(t).astype(F32) * vector for read, vector in terms)

    return segment_sums(leaf, tiles, rows)


def reader(ref, *index):
    return lambda t: ref[(*index, slice(None), slice(t * LANES, (t + 1) * LANES))]


def lanes(shape):
    return lax.broadcasted_iota(jnp.int32, shape, 1)


def woven(raw):
    lane = lanes(raw.shape)
    return jnp.take_along_axis(raw, (lane >> 1) + (lane & 1) * (LANES // 2), 1)


def unwoven(vector):
    lane = lanes(vector.shape)
    return jnp.take_along_axis(vector, (lane & LANES // 2 - 1) * 2 + lane // (LANES // 2), 1)


def spread(vector):
    half = vector.shape[0]
    row = lax.broadcasted_iota(jnp.int32, vector.shape, 0)
    place = (lanes(vector.shape) & LANES // 2 - 1) * 2 + (row & 1)
    parts = []
    for first in (0, half // 2):
        block = jnp.take_along_axis(vector, first + row // 2, 0)
        parts.append(jnp.take_along_axis(block, place, 1))
    return jnp.concatenate(parts, 0)


def gather_pairs(vector):
    half = vector.shape[0] // 2
    shape = (half, LANES)
    row = lax.broadcasted_iota(jnp.int32, shape, 0)
    odd = lane_bit(shape, 1)
    parts = []
    for block in (vector[:half], vector[half:]):
        block = jnp.take_along_axis(block, lanes(shape) >> 1, 1)
        block = jnp.where(odd, pltpu.roll(block, half - 1, 0), block)
        parts.append(jnp.take_along_axis(block, 2 * row & half - 1, 0))
    return jnp.where(row < half // 2, parts[0], parts[1])


def shifted(vector, down):
    rows = vector.shape[0]
    row = lax.broadcasted_iota(jnp.int32, vector.shape, 0)
    if down:
        return jnp.where(row == 0, 0.0, pltpu.roll(vector, 1, 0))
    return jnp.where(row == rows - 1, 0.0, pltpu.roll(vector, rows - 1, 0))


def to_rows(scratch, native, read, rows, species):
    pairs = rows // 2
    for t in range(species // 2):
        native[t * rows : (t + 1) * rows, :] = read(t).astype(F32)
    for t in range(species // 2):
        for inner in (0, 1):
            tile = native[pl.ds(t * rows + inner, pairs, stride=2), :]
            other = pltpu.roll(tile, LANES // 2, 1)
            scratch[pl.ds(4 * t + inner, pairs, stride=LANES), :] = tile
            scratch[pl.ds(4 * t + 2 + inner, pairs, stride=LANES), :] = other


def halves(a):
    high = a.astype(BF16)
    return high, (a - high.astype(F32)).astype(BF16)


def dot(a, b, dims=((1,), (0,))):
    return lax.dot_general(a, b, (dims, ((), ())), preferred_element_type=F32)


def turn(scratch, out, first, pairs, species):
    unit = (
        lax.broadcasted_iota(jnp.int32, (species, species), 0)
        == lax.broadcasted_iota(jnp.int32, (species, species), 1)
    ).astype(F32).astype(BF16)
    for pair in range(pairs):
        block = scratch[pair * LANES : (pair + 1) * LANES, :species].astype(BF16)
        out[pl.ds(first + pair, species, stride=pairs), :] = dot(unit, block, ((1,), (1,)))


def both(scratch, pair, block):
    odd = lane_bit(block.shape, 1)
    zero = jnp.zeros_like(block)
    scratch[pl.ds(pair * LANES, block.shape[0], stride=2), :] = jnp.where(odd, zero, block)
    scratch[pl.ds(pair * LANES + 1, block.shape[0], stride=2), :] = jnp.where(odd, block, zero)
    return scratch[pair * LANES : (pair + 1) * LANES, :]


def multiply(scratch, pair, earlier, later, exact):
    later = both(scratch, pair, later)
    if exact:
        return dot(earlier.astype(BF16), later.astype(BF16))
    earlier_high, earlier_low = halves(earlier)
    high, low = halves(later)
    return dot(earlier_high, high) + (dot(earlier_low, high) + dot(earlier_high, low))


STEP = 8


def diagonals(tiles, out, first):
    count = len(tiles)
    shape = tiles[0].shape
    shift = 1
    while shift < count:
        here = lane_bit(shape, 2 * shift)
        tiles = [jnp.where(here, tiles[(j + shift) % count], tiles[j]) for j in range(count)]
        shift *= 2
    for j, tile in enumerate(tiles):
        turn_by = j // STEP * STEP * 2
        at = first + j * shape[0]
        out[at : at + shape[0], :] = pltpu.roll(tile, turn_by, 1) if turn_by else tile


def whole_tiles(ref, first, pairs, count=LANES // 2):
    return [ref[first + b * pairs : first + (b + 1) * pairs, :] for b in range(count)]


def part_tiles(mine, other, pairs):
    first_core = lax.axis_index("gx") & 1 == 0
    halves_of = [whole_tiles(ref, 0, pairs, LANES // 4) for ref in (mine, other)]
    low = [jnp.where(first_core, a, b) for a, b in zip(*halves_of)]
    high = [jnp.where(first_core, b, a) for a, b in zip(*halves_of)]
    return low + high


def mapped(ref, vector, first=0):
    pairs = vector.shape[0]
    turns = [vector] + [pltpu.roll(vector, LANES - 2 * j, 1) for j in range(1, STEP)]
    total = None
    for giant in range(LANES // 2 // STEP):
        terms = []
        for j in range(STEP):
            at = first + (giant * STEP + j) * pairs
            terms.append(ref[at : at + pairs, :] * turns[j])
        while len(terms) > 1:
            terms = [a + b for a, b in zip(terms[::2], terms[1::2])]
        part = pltpu.roll(terms[0], LANES - 2 * STEP * giant, 1) if giant else terms[0]
        total = part if total is None else total + part
    return total


def prep_kernel(reverse, blocks, beside_it, *refs):
    *passed, maps, products, own, held, held_start, native, rows_scratch, semaphores = refs
    planes, _, rows, width = blocks.shape
    species = LANES // 2
    pairs = rows // 2
    size = species * pairs
    order = list(range(planes))[::-1] if reverse else list(range(planes))
    copies = [
        pltpu.make_async_copy(blocks.at[p], held.at[p], semaphores.at[p]) for p in range(planes)
    ]
    for plane in order:
        copies[plane].start()
    if passed:
        copy = pltpu.make_async_copy(beside_it, held_start, semaphores.at[planes])
        copy.start()
        copy.wait()
        for p in range(planes):
            passed[0][p] = woven(held_start[p])
    for plane in order:
        copies[plane].wait()
        to_rows(rows_scratch, native, reader(held, plane, 0), rows, species)
        turn(rows_scratch, maps, plane * size, pairs, species)
    for step, plane in enumerate(order):
        at = pl.ds(plane * size, size)
        if step == 0:
            products[at, :] = -maps[at, :]
            continue
        for pair in range(pairs):
            here = pl.ds(plane * size + pair, species, stride=pairs)
            before = pl.ds(order[step - 1] * size + pair, species, stride=pairs)
            products[here, :] = multiply(
                rows_scratch, pair, products[before, :], -maps[here, :], step == 1
            )
    own[...] = products[pl.ds(order[-1] * size, size), :]


def join_kernel(level, reverse, full, pairs, own, *refs):
    here = (lax.axis_index("gx") >> level) & 1
    core = lax.axis_index("gx") & 1
    species = LANES // 2
    *refs, scratch = refs
    outs = refs[-2:] if full else refs[-1:]
    partner = refs[: len(refs) - len(outs)]
    later_is_own = here == (0 if reverse else 1)
    for pair in range(pairs):
        mine = own[pl.ds(pair, species, stride=pairs), :]
        if len(partner) == 1:
            theirs = partner[0][pl.ds(pair, species, stride=pairs), :]
        else:
            close = partner[0][pl.ds(pair, species // 2, stride=pairs), :]
            far = partner[1][pl.ds(pair, species // 2, stride=pairs), :]
            theirs = jnp.where(
                core == 0, jnp.concatenate([close, far], 0), jnp.concatenate([far, close], 0)
            )
        earlier = jnp.where(later_is_own, theirs, mine)
        later = jnp.where(later_is_own, mine, theirs)
        if full:
            kept = multiply(scratch, pair, earlier, later, False)
            outs[0][pl.ds(pair, species, stride=pairs), :] = kept
            kept = jnp.where(core == 0, kept[: species // 2], kept[species // 2 :])
        else:
            kept = jnp.where(core == 0, earlier[: species // 2], earlier[species // 2 :])
            kept = multiply(scratch, pair, kept, later, False)
        outs[-1][pl.ds(pair, species // 2, stride=pairs), :] = kept


def base_kernel(start, source, diag, upper, side, maps, products, partner, *outs):
    rhs, base, step_maps, entry_maps, near_map = outs
    planes, pairs = start.shape[:2]
    size = pairs * LANES // 2
    vectors = [spread(start[p]) for p in range(planes)]
    for p in range(planes):
        own = apply([(reader(diag, p, 0), spread(woven(source[p])))])
        terms = [
            (reader(side, 2, p, 0), shifted(vectors[p], True)),
            (reader(side, 3, p, 0), shifted(vectors[p], False)),
        ]
        if p + 1 < planes:
            terms.append((reader(upper, p, 0), vectors[p + 1]))
        around = apply(terms)
        rhs[p] = gather_pairs(own)
        base[p] = gather_pairs(own - around)
    for p in range(planes):
        if p:
            diagonals(whole_tiles(maps, p * size, pairs), step_maps, p * size)
        diagonals(whole_tiles(products, p * size, pairs), entry_maps, p * size)
    diagonals(whole_tiles(partner, 0, pairs), near_map, 0)


def outgoing(offset, partners, here, slots):
    vectors = [offset]
    for level, ref in enumerate(partners):
        passed = mapped(ref, vectors[-1])
        vectors.append(jnp.where((here >> level) & 1 == 0, passed, vectors[-1]))
    place = lax.axis_index("gx")
    for target in range(slots.shape[0]):
        apart = place ^ target
        value = vectors[0]
        for level in range(1, len(vectors)):
            value = jnp.where(apart >= 1 << level, vectors[level], value)
        slots[target] = value


def incoming(got, partners, here, reverse):
    count = got.shape[0]
    entering = None
    for level in range(len(partners) + 1)[::-1]:
        total = None
        for source in range(count):
            place = count - 1 - source if reverse else source
            term = jnp.where((place >> level) == (here >> level) - 1, got[source], 0.0)
            total = term if total is None else total + term
        if entering is not None:
            total = total + mapped(partners[level], entering)
        before = jnp.zeros_like(total) if entering is None else entering
        entering = jnp.where((here >> level) & 1 == 1, total, before)
    return entering


def beside(axis, paired, other):
    place, count = lax.axis_index(axis), lax.axis_size(axis)
    odd = place & 1 == 1
    low = jnp.where(odd, paired, other)
    high = jnp.where(odd, other, paired)
    return jnp.where(place == 0, 0.0, low), jnp.where(place == count - 1, 0.0, high)


def forward_offset_kernel(levels, base, paired, other, ahead, side, upper, step_maps, near, *rest):
    parts, (drive, offsets, slots, *far) = rest[: 2 * (levels - 2)], rest[2 * (levels - 2) :]
    planes, pairs = base.shape[:2]
    size = pairs * LANES // 2
    here = lax.axis_index("gx")
    last = here == lax.axis_size("gx") - 1
    for level, ref in enumerate(far):
        diagonals(part_tiles(*parts[2 * level : 2 * level + 2], pairs), ref, 0)
    previous = None
    for p in range(planes):
        low, high = beside("gy", paired[p], other[p])
        terms = [(reader(side, 0, p, 0), spread(low)), (reader(side, 1, p, 0), spread(high))]
        if p + 1 == planes:
            beyond = jnp.where(last, 0.0, ahead[0])
            terms.append((reader(upper, p, 0), spread(beyond)))
        fresh = base[p] - gather_pairs(apply(terms))
        drive[p] = fresh
        if previous is not None:
            fresh = fresh - mapped(step_maps, previous, p * size)
        offsets[p] = fresh
        previous = fresh
    outgoing(previous, [near, *far], here, slots)


def forward_kernel(got, drive, offsets, rhs, entry_maps, *rest):
    *partners, out, copy, base = rest
    planes = drive.shape[0]
    size = drive.shape[1] * LANES // 2
    entering = incoming(got, partners, lax.axis_index("gx"), False)
    for p in range(planes):
        value = offsets[p] + mapped(entry_maps, entering, p * size)
        base[p] = rhs[p] - (drive[p] - value)
        out[p] = unwoven(value)
        copy[p] = value


def side_kernel(levels, base, vectors, side, maps, products, partner, *rest):
    parts = rest[: 2 * (levels - 2)]
    out, step_maps, entry_maps, near, *far = rest[2 * (levels - 2) :]
    planes, pairs = base.shape[:2]
    size = pairs * LANES // 2
    for p in range(planes):
        vector = spread(vectors[p])
        around = apply(
            [
                (reader(side, 2, p, 0), shifted(vector, True)),
                (reader(side, 3, p, 0), shifted(vector, False)),
            ]
        )
        out[p] = base[p] - gather_pairs(around)
        if p + 1 < planes:
            diagonals(whole_tiles(maps, p * size, pairs), step_maps, p * size)
        diagonals(whole_tiles(products, p * size, pairs), entry_maps, p * size)
    diagonals(whole_tiles(partner, 0, pairs), near, 0)
    for level, ref in enumerate(far):
        diagonals(part_tiles(*parts[2 * level : 2 * level + 2], pairs), ref, 0)


def backward_offset_kernel(base, paired, other, side, step_maps, *rest):
    *partners, offsets, slots = rest
    planes = base.shape[0]
    size = base.shape[1] * LANES // 2
    here = lax.axis_size("gx") - 1 - lax.axis_index("gx")
    previous = None
    for p in range(planes)[::-1]:
        low, high = beside("gy", paired[p], other[p])
        around = apply([(reader(side, 0, p, 0), spread(low)), (reader(side, 1, p, 0), spread(high))])
        fresh = base[p] - gather_pairs(around)
        if previous is not None:
            fresh = fresh - mapped(step_maps, previous, p * size)
        offsets[p] = fresh
        previous = fresh
    outgoing(previous, partners, here, slots)


def backward_kernel(got, offsets, entry_maps, *rest):
    *partners, out = rest
    size = offsets.shape[1] * LANES // 2
    here = lax.axis_size("gx") - 1 - lax.axis_index("gx")
    entering = incoming(got, partners, here, True)
    for p in range(offsets.shape[0]):
        out[p] = unwoven(offsets[p] + mapped(entry_maps, entering, p * size))


def call(kernel, operands, outs, scratch, micros):
    arrays = [o[0] if isinstance(o, tuple) else o for o in operands]
    held = [i for i, o in enumerate(operands) if isinstance(o, tuple)]
    outs = [jax.ShapeDtypeStruct(shape, F32) for shape in outs]
    moved = sum(a.size * a.dtype.itemsize for a in arrays)
    return pl.pallas_call(
        kernel,
        out_shape=outs,
        in_specs=[
            pl.BlockSpec(memory_space=pltpu.HBM if i in held else pltpu.VMEM) for i in range(len(arrays))
        ],
        out_specs=[pl.BlockSpec(memory_space=pltpu.VMEM) for _ in outs],
        scratch_shapes=[pltpu.VMEM(s, F32) if isinstance(s, tuple) else s for s in scratch],
        compiler_params=pltpu.CompilerParams(vmem_limit_bytes=24 << 20),
        cost_estimate=pl.CostEstimate(
            flops=int(micros * 1.15e9), bytes_accessed=moved, transcendentals=0
        ),
    )(*arrays)


def swaps(block):
    count, rows = lax.axis_size("gx"), lax.axis_size("gy")
    route = []
    for place in range(count):
        for row in range(rows):
            target = row + 1 if row & 1 else row - 1
            to = place * rows + target if 0 <= target < rows else (place ^ 1) * rows + row
            route.append((place * rows + row, to))
    return crossed(block, "gy", 1), lax.ppermute(block, ("gx", "gy"), route)


def crossed(block, axis, distance):
    return lax.ppermute(block, axis, [(i, i ^ distance) for i in range(lax.axis_size(axis))])


def exchange(slots, axis):
    return lax.all_to_all(slots, axis, 0, 0)


def local(start, source, diag_inverse, x_lower, x_upper, side_blocks):
    planes, _, depth, width = x_lower.shape
    species = start.shape[2] // depth
    pairs = depth // 2
    count = lax.axis_size("gx")
    levels = count.bit_length() - 1
    size = species * pairs
    one = (pairs, LANES)
    vec = (planes,) + one
    maps = (planes * size, LANES)
    whole, half = (size, LANES), (size // 2, LANES)
    slots = (count,) + one
    start = start.reshape(vec)
    source = source.reshape(vec)

    def prepare(reverse, blocks, other):
        *passed, maps_of, products, own = call(
            functools.partial(prep_kernel, reverse),
            [(blocks, None), other if reverse else (other, None)],
            ([] if reverse else [vec]) + [maps, maps, whole],
            [
                pltpu.VMEM(blocks.shape, blocks.dtype),
                vec,
                (depth * species // 2, LANES),
                (depth * species, LANES),
                pltpu.SemaphoreType.DMA((planes + 1,)),
            ],
            1.0,
        )
        partners, kept = [], None
        for level in range(levels - 1):
            if level == 0:
                got = [crossed(own, "gx", 1)]
            else:
                mine = crossed(kept, "gx", 1 << level)
                got = [mine, crossed(mine, "gx", 1)]
            partners += got
            if level + 2 < levels:
                full = level + 3 < levels
                outs = call(
                    functools.partial(join_kernel, level, reverse, full, pairs),
                    [own] + got,
                    [whole, half] if full else [half],
                    [(depth * species, LANES)],
                    0.4,
                )
                own, kept = outs[0], outs[-1]
        return [maps_of, products, *partners], passed

    lower, (start,) = prepare(False, x_lower, start)
    upper, _ = prepare(True, x_upper, lower[1])
    paired, other = swaps(start)
    ahead = lax.ppermute(start[:1], "gx", [(i, (i - 1) % count) for i in range(count)])

    far = [whole] * (levels - 2)
    rhs, base, step_maps, entry_maps, near = call(
        base_kernel,
        [start, source, diag_inverse, x_upper, side_blocks] + lower[:3],
        [vec, vec, maps, maps, whole],
        [],
        5.0,
    )
    drive, offsets, sent, *partners = call(
        functools.partial(forward_offset_kernel, levels),
        [base, paired, other, ahead, side_blocks, x_upper, step_maps, near] + lower[3:],
        [vec, vec, slots] + far,
        [],
        1.5,
    )
    forward, copy, base = call(
        forward_kernel,
        [exchange(sent, "gx"), drive, offsets, rhs, entry_maps, near] + partners,
        [vec, vec, vec],
        [],
        1.0,
    )
    paired, other = swaps(copy)
    base, step_maps, entry_maps, *partners = call(
        functools.partial(side_kernel, levels),
        [base, copy, side_blocks] + upper,
        [vec, maps, maps, whole] + far,
        [],
        0.7,
    )
    offsets, sent = call(
        backward_offset_kernel,
        [base, paired, other, side_blocks, step_maps] + partners,
        [vec, slots],
        [],
        1.5,
    )
    (result,) = call(
        backward_kernel, [exchange(sent, "gx"), offsets, entry_maps] + partners, [vec], [], 1.0
    )
    shape = (planes, 1, depth * species)
    return forward.reshape(shape), result.reshape(shape)


def solution(mesh):
    return jax.shard_map(
        local,
        mesh=mesh,
        in_specs=(
            P("gx", "gy", None),
            P("gx", "gy", None),
            P("gx", "gy", None, None),
            P("gx", "gy", None, None),
            P("gx", "gy", None, None),
            P(None, "gx", "gy", None, None),
        ),
        out_specs=(P("gx", "gy", None), P("gx", "gy", None)),
        check_vma=False,
    )
```

time: 43.4 us -> 45 us (1.037)
  the two profiles are of different devices: /device:TPU:0 before, /device:TPU:16 now
where the time goes in v7:
time: 45 us; the launch traced here: 44.7 us
  Pallas kernels  14.3 us (32%)
  starting transfers between devices  11.7 us (26%)
  waiting for transfers between devices  7.44 us (17%)
  blocking collectives  7.21 us (16%)
  local copies, waits for them, and re-layouts  3.3 us (7%)
  between operations  0.75 us (2%)
    pallas_call x10, Pallas kernels, call(): pl.pallas_call(kernel, out_shape=outs, in_specs=[pl.BlockSpec(memory_spac...  14.3 us
    ppermute x8, starting transfers between devices, crossed(): lax.ppermute(block, axis, [(i, i ^ distance) for i in range(lax.axis_size...  7.28 us
    all_to_all x1, blocking collectives, exchange(): return lax.all_to_all(slots, axis, 0, 0)  7.21 us
    all_to_all x1, waiting for transfers between devices, exchange(): return lax.all_to_all(slots, axis, 0, 0)  4.33 us
    all_to_all x1, starting transfers between devices, exchange(): return lax.all_to_all(slots, axis, 0, 0)  3.83 us
    unnamed x16, local copies, waits for them, and re-layouts  3.3 us
    ppermute x2, waiting for transfers between devices, swaps(): return (crossed(block, 'gy', 1), lax.ppermute(block, ('gx', 'gy'), route))  2.03 us
    ppermute x8, waiting for transfers between devices, crossed(): lax.ppermute(block, axis, [(i, i ^ distance) for i in range(lax.axis_size...  1.08 us
  transfers between devices with their start and end apart: 12, of which 4 were waited for; matrix products, arithmetic and copies ran while one was open for 0% of the time, Pallas kernels for 22%

profile of v7, /device:TPU:16, one launch (start us, length us, event | category | flops | bytes accessed | tf_op | source)
XLA Modules:
  0.0 44.7 jit_solution(15064283767186386548)
XLA Ops:
  0.6 0.9 %copy-done.1 = bf16[2,1,16,4096]{3,2,1,0:T(8,128)(2,1)S(1)} copy-done((bf16[2,1,16,4096]{3,2,1,0:T(8,128)(2,1)S(1)}, bf16[2,1,16,4096]{3,2,1,0:T(8,128)(2,1)}, u32[]{:S(2)}) %copy-start.1) | copy-done | bytes 262168
  1.6 0.7 %copy-done.4 = f32[2,1,1024]{2,1,0:T(1,128)S(1)} copy-done((f32[2,1,1024]{2,1,0:T(1,128)S(1)}, f32[2,1,1024]{2,1,0:T(1,128)}, u32[]{:S(2)}) %copy-start.4) | copy-done | bytes 8216
  2.3 1.9 %shard_map.77 = (f32[2,8,128]{2,1,0:T(8,128)S(1)}, f32[1024,128]{1,0:T(8,128)S(1)}, f32[1024,128]{1,0:T(8,128)S(1)}, f32[512,128]{1,0:T(8,128)S(1)}) custom-call(bf16[2,1,16,4096]{3,2,1,0:T(8,128)(2,1)S(1)} %copy-done.1, f32[2,8,128]{2,1,0:T(8,128)S(1)} %bitcast.4), custom_call_target="tpu_custom_call" | custom-call | flops 1150000000 | bytes 270336 | tf_op jit(solution)/shard_map/pallas_call | solution.py:407
  4.2 0.1 collective-permute-start
  4.3 1.8 %shard_map.82 = (f32[1024,128]{1,0:T(8,128)S(1)}, f32[1024,128]{1,0:T(8,128)S(1)}, f32[512,128]{1,0:T(8,128)S(1)}) custom-call(bf16[2,1,16,4096]{3,2,1,0:T(8,128)(2,1)S(1)} %copy-done.3, f32[1024,128]{1,0:T(8,128)S(1)} %get-tuple-element.30.products.beside_it), custom_call_target="tpu_custom_call" | custom-call | flops 1150000000 | bytes 786432 | tf_op jit(solution)/shard_map/pallas_call | solution.py:407
  6.1 0.5 %collective-permute-start.6 = (f32[512,128]{1,0:T(8,128)S(1)}, f32[512,128]{1,0:T(8,128)S(1)}, u32[]{:S(2)}, u32[]{:S(2)}) collective-permute-start(f32[512,128]{1,0:T(8,128)S(1)} %get-tuple-element.46.own), channel_id=1, source_target_pairs={{0,4},{4,0},{8,12},{12,8},{16,20},{20,16},{24,28},{28,24},{1,5},{5... | collective-permute-start | bytes 786440 | tf_op jit(solution)/shard_map/ppermute | solution.py:434
  6.6 0.0 collective-permute-done.partner.refs_0_
  6.6 0.4 shard_map.79
  7.0 1.6 %collective-permute-start.4 = (f32[256,128]{1,0:T(8,128)S(1)}, f32[256,128]{1,0:T(8,128)S(1)}, u32[]{:S(2)}, u32[]{:S(2)}) collective-permute-start(f32[256,128]{1,0:T(8,128)S(1)} %shard_map.79), channel_id=1, source_target_pairs={{0,8},{4,12},{8,0},{12,4},{16,24},{20,28},{24,16},{28,20},{1,9},{5... | collective-permute-start | bytes 393224 | tf_op jit(solution)/shard_map/ppermute | solution.py:434
  8.5 1.6 %collective-permute-start.1 = (f32[2,8,128]{2,1,0:T(8,128)S(1)}, f32[2,8,128]{2,1,0:T(8,128)S(1)}, u32[]{:S(2)}, u32[]{:S(2)}) collective-permute-start(f32[2,8,128]{2,1,0:T(8,128)S(1)} %get-tuple-element.28.start), channel_id=1, source_target_pairs={{0,1},{1,0},{2,3},{3,2},{4,5},{5,4},{6,7},{7,6},{8,9},{9,8},{10,11... | collective-permute-start | bytes 24584 | tf_op jit(solution)/shard_map/ppermute | solution.py:434
  10.1 0.0 collective-permute-start.2
  10.1 0.6 %collective-permute-start.3 = (f32[1,8,128]{2,1,0:T(8,128)S(1)}, f32[1,8,128]{2,1,0:T(8,128)S(1)}, u32[]{:S(2)}, u32[]{:S(2)}) collective-permute-start(f32[1,8,128]{2,1,0:T(8,128)S(1)} %slice.3), channel_id=1, source_target_pairs={{0,28},{4,0},{8,4},{12,8},{16,12},{20,16},{24,20},{28,24},{1,29},{... | collective-permute-start | bytes 12296 | tf_op jit(solution)/shard_map/ppermute | solution.py:493
  10.7 0.4 shard_map.83
  11.1 0.6 %collective-permute-start.7 = (f32[256,128]{1,0:T(8,128)S(1)}, f32[256,128]{1,0:T(8,128)S(1)}, u32[]{:S(2)}, u32[]{:S(2)}) collective-permute-start(f32[256,128]{1,0:T(8,128)S(1)} %shard_map.83), channel_id=1, source_target_pairs={{0,8},{4,12},{8,0},{12,4},{16,24},{20,28},{24,16},{28,20},{1,9},{5... | collective-permute-start | bytes 393224 | tf_op jit(solution)/shard_map/ppermute | solution.py:434
  11.7 0.8 %collective-permute-done.4.rest_0_ = f32[256,128]{1,0:T(8,128)S(1)} collective-permute-done((f32[256,128]{1,0:T(8,128)S(1)}, f32[256,128]{1,0:T(8,128)S(1)}, u32[]{:S(2)}, u32[]{:S(2)}) %collective-permute-start.4) | collective-permute-done | bytes 131104 | tf_op jit(solution)/shard_map/ppermute | solution.py:434
  12.5 3.2 %shard_map.78 = (f32[2,8,128]{2,1,0:T(8,128)S(1)}, f32[2,8,128]{2,1,0:T(8,128)S(1)}, f32[1024,128]{1,0:T(8,128)S(1)}, f32[1024,128]{1,0:T(8,128)S(1)}, f32[512,128]{1,0:T(8,128)S(1)}) custom-call(f32[2,8,128]{2,1,0:T(8,128)S(1)} %get-tuple-element.28.start, f32[2,8,128]{2,1,0:T(8,128)S(1)} %bitcast.5, bf16[2,1,16,4096]{3,2,1,0:T(8,128)(2,1)S(1)} %copy-done.2, ...), custom_call_target="tpu_custom_call" | custom-call | flops 5750000128 | bytes 2899968 | tf_op jit(solution)/shard_map/pallas_call | solution.py:407
  15.7 0.0 collective-permute-done.3.ahead
  15.7 0.0 collective-permute-done.1.paired
  15.8 1.8 %shard_map.80 = (f32[2,8,128]{2,1,0:T(8,128)S(1)}, f32[2,8,128]{2,1,0:T(8,128)S(1)}, f32[8,8,128]{2,1,0:T(8,128)}, f32[512,128]{1,0:T(8,128)S(1)}) custom-call(f32[2,8,128]{2,1,0:T(8,128)S(1)} %get-tuple-element.32.base, f32[2,8,128]{2,1,0:T(8,128)S(1)} %collective-permute-done.1.paired, f32[2,8,128]{2,1,0:T(8,128)S(1)} %collective-permute-done.2.other, ...), custom_call_target="tpu_custom_call" | custom-call | flops 1724999936 | bytes 2387968 | tf_op jit(solution)/shard_map/pallas_call | solution.py:407
  17.6 0.7 %copy-done.6 = f32[512,128]{1,0:T(8,128)} copy-done((f32[512,128]{1,0:T(8,128)}, f32[512,128]{1,0:T(8,128)S(1)}, u32[]{:S(2)}) %copy-start.6) | copy-done | bytes 262168
  18.3 3.8 %all-to-all-start = ((f32[8,8,128]{2,1,0:T(8,128)}), f32[8,8,128]{2,1,0:T(8,128)S(1)}, u32[]{:S(2)}, u32[]{:S(2)}) async-start(f32[8,8,128]{2,1,0:T(8,128)} %get-tuple-element.35), calls=%async_computation | async-start | bytes 65536 | tf_op jit(solution)/shard_map/all_to_all | solution.py:438
  22.1 0.5 %collective-permute-start.8 = (f32[256,128]{1,0:T(8,128)S(1)}, f32[256,128]{1,0:T(8,128)S(1)}, u32[]{:S(2)}, u32[]{:S(2)}) collective-permute-start(f32[256,128]{1,0:T(8,128)S(1)} %collective-permute-done.7.rest_0_), channel_id=1, source_target_pairs={{0,4},{4,0},{8,12},{12,8},{16,20},{20,16},{24,28},{28,24},{1,5},{5... | collective-permute-start | bytes 393224 | tf_op jit(solution)/shard_map/ppermute | solution.py:434
  22.6 4.3 %all-to-all-done.got = f32[8,8,128]{2,1,0:T(8,128)S(1)} async-done(((f32[8,8,128]{2,1,0:T(8,128)}), f32[8,8,128]{2,1,0:T(8,128)S(1)}, u32[]{:S(2)}, u32[]{:S(2)}) %all-to-all-start) | async-done | bytes 32800 | tf_op jit(solution)/shard_map/all_to_all | solution.py:438
  26.9 0.9 %copy-done.7 = f32[512,128]{1,0:T(8,128)S(1)} copy-done((f32[512,128]{1,0:T(8,128)S(1)}, f32[512,128]{1,0:T(8,128)}, u32[]{:S(2)}) %copy-start.7) | copy-done | bytes 262168
  27.9 1.2 %shard_map.81 = (f32[2,8,128]{2,1,0:T(8,128)}, f32[2,8,128]{2,1,0:T(8,128)S(1)}, f32[2,8,128]{2,1,0:T(8,128)S(1)}) custom-call(f32[8,8,128]{2,1,0:T(8,128)S(1)} %all-to-all-done.got, f32[2,8,128]{2,1,0:T(8,128)S(1)} %get-tuple-element.36.drive, f32[2,8,128]{2,1,0:T(8,128)S(1)} %get-tuple-element.37.offsets, f32[2,8,128]{2,1,0:T(8,128)S(1)} %get-tuple-element.38.rhs, ...), custom_call_target="tpu_custom_call" | custom-call | flops 1150000000 | bytes 1105920 | tf_op jit(solution)/shard_map/pallas_call | solution.py:407
  29.0 2.5 %collective-permute-start.9 = (f32[2,8,128]{2,1,0:T(8,128)S(1)}, f32[2,8,128]{2,1,0:T(8,128)S(1)}, u32[]{:S(2)}, u32[]{:S(2)}) collective-permute-start(f32[2,8,128]{2,1,0:T(8,128)S(1)} %get-tuple-element.43.vectors), channel_id=1, source_target_pairs={{0,1},{1,0},{2,3},{3,2},{4,5},{5,4},{6,7},{7,6},{8,9},{9,8},{10,11... | collective-permute-start | bytes 24584 | tf_op jit(solution)/shard_map/ppermute | solution.py:434
  31.5 1.3 %shard_map.84 = (f32[2,8,128]{2,1,0:T(8,128)S(1)}, f32[1024,128]{1,0:T(8,128)S(1)}, f32[1024,128]{1,0:T(8,128)S(1)}, f32[512,128]{1,0:T(8,128)S(1)}, f32[512,128]{1,0:T(8,128)S(1)}) custom-call(f32[2,8,128]{2,1,0:T(8,128)S(1)} %get-tuple-element.42.base, f32[2,8,128]{2,1,0:T(8,128)S(1)} %get-tuple-element.43.vectors, ...), custom_call_target="tpu_custom_call" | custom-call | flops 805000000 | bytes 2637824 | tf_op jit(solution)/shard_map/pallas_call | solution.py:407
  32.9 0.3 collective-permute-done.9.paired
  33.1 2.0 %collective-permute-done.10.other = f32[2,8,128]{2,1,0:T(8,128)S(1)} collective-permute-done((f32[2,8,128]{2,1,0:T(8,128)S(1)}, f32[2,8,128]{2,1,0:T(8,128)S(1)}, u32[]{:S(2)}, u32[]{:S(2)}) %collective-permute-start.10) | collective-permute-done | bytes 8224 | tf_op jit(solution)/shard_map/ppermute | solution.py:430
  35.2 1.2 %shard_map.85 = (f32[2,8,128]{2,1,0:T(8,128)S(1)}, f32[8,8,128]{2,1,0:T(8,128)S(1)}) custom-call(f32[2,8,128]{2,1,0:T(8,128)S(1)} %get-tuple-element.47.base, f32[2,8,128]{2,1,0:T(8,128)S(1)} %collective-permute-done.9.paired, f32[2,8,128]{2,1,0:T(8,128)S(1)} %collective-permute-done.10.other, bf16[4,2,1,16,4096]{4,3,2,1,0:T(8,128)(2,1)S(1)} %copy-done, ...), custom_call_target="tpu_custom_call" | custom-call | flops 1724999936 | bytes 2121728 | tf_op jit(solution)/shard_map/pallas_call | solution.py:407
  36.3 7.2 %all_to_all.10.got = f32[8,8,128]{2,1,0:T(8,128)S(1)} all-to-all(f32[8,8,128]{2,1,0:T(8,128)S(1)} %get-tuple-element.51), channel_id=1, replica_groups=mesh['gx'=8,'gy'=4] {'gx'}, dimensions={0} | all-to-all | bytes 65536 | tf_op jit(solution)/shard_map/all_to_all | solution.py:438
  43.5 1.2 %shard_map.86 = f32[2,8,128]{2,1,0:T(8,128)} custom-call(f32[8,8,128]{2,1,0:T(8,128)S(1)} %all_to_all.10.got, f32[2,8,128]{2,1,0:T(8,128)S(1)} %get-tuple-element.52.offsets, f32[1024,128]{1,0:T(8,128)S(1)} %get-tuple-element.53.entry_maps, f32[512,128]{1,0:T(8,128)S(1)} %get-tuple-element.49.rest_0_, f32[512,128]{1,0:T(8,128)S(1)} %get-tuple-element.50.rest_1_), custom_call_target="tpu_custom_call" | custom-call | flops 1150000000 | bytes 1089536 | tf_op jit(solution)/shard_map/pallas_call | solution.py:407
  (20 shorter events, 0.0 us)
Async XLA Ops:
  0.6 1.0 %copy-start.1 = (bf16[2,1,16,4096]{3,2,1,0:T(8,128)(2,1)S(1)}, bf16[2,1,16,4096]{3,2,1,0:T(8,128)(2,1)}, u32[]{:S(2)}) copy-start(bf16[2,1,16,4096]{3,2,1,0:T(8,128)(2,1)} %blocks.2) | copy-start | bytes 786436
  1.6 0.7 %copy-start.4 = (f32[2,1,1024]{2,1,0:T(1,128)S(1)}, f32[2,1,1024]{2,1,0:T(1,128)}, u32[]{:S(2)}) copy-start(f32[2,1,1024]{2,1,0:T(1,128)} %param.6) | copy-start | bytes 24580
  2.3 2.0 %copy-start.3 = (bf16[2,1,16,4096]{3,2,1,0:T(8,128)(2,1)S(1)}, bf16[2,1,16,4096]{3,2,1,0:T(8,128)(2,1)}, u32[]{:S(2)}) copy-start(bf16[2,1,16,4096]{3,2,1,0:T(8,128)(2,1)} %blocks.3) | copy-start | bytes 786436
  4.2 2.4 %collective-permute-start = (f32[512,128]{1,0:T(8,128)S(1)}, f32[512,128]{1,0:T(8,128)S(1)}, u32[]{:S(2)}, u32[]{:S(2)}) collective-permute-start(f32[512,128]{1,0:T(8,128)S(1)} %get-tuple-element.31.own), channel_id=1, source_target_pairs={{0,4},{4,0},{8,12},{12,8},{16,20},{20,16},{24,28},{28,24},{1,5},{5... | collective-permute-start | bytes 786440 | tf_op jit(solution)/shard_map/ppermute | solution.py:434
  6.1 4.7 %collective-permute-start.6 = (f32[512,128]{1,0:T(8,128)S(1)}, f32[512,128]{1,0:T(8,128)S(1)}, u32[]{:S(2)}, u32[]{:S(2)}) collective-permute-start(f32[512,128]{1,0:T(8,128)S(1)} %get-tuple-element.46.own), channel_id=1, source_target_pairs={{0,4},{4,0},{8,12},{12,8},{16,20},{20,16},{24,28},{28,24},{1,5},{5... | collective-permute-start | bytes 786440 | tf_op jit(solution)/shard_map/ppermute | solution.py:434
  7.0 5.5 %copy-start = (bf16[4,2,1,16,4096]{4,3,2,1,0:T(8,128)(2,1)S(1)}, bf16[4,2,1,16,4096]{4,3,2,1,0:T(8,128)(2,1)}, u32[]{:S(2)}) copy-start(bf16[4,2,1,16,4096]{4,3,2,1,0:T(8,128)(2,1)} %side.7) | copy-start | bytes 3145732
  7.0 5.5 %collective-permute-start.4 = (f32[256,128]{1,0:T(8,128)S(1)}, f32[256,128]{1,0:T(8,128)S(1)}, u32[]{:S(2)}, u32[]{:S(2)}) collective-permute-start(f32[256,128]{1,0:T(8,128)S(1)} %shard_map.79), channel_id=1, source_target_pairs={{0,8},{4,12},{8,0},{12,4},{16,24},{20,28},{24,16},{28,20},{1,9},{5... | collective-permute-start | bytes 393224 | tf_op jit(solution)/shard_map/ppermute | solution.py:434
  8.5 7.2 %collective-permute-start.1 = (f32[2,8,128]{2,1,0:T(8,128)S(1)}, f32[2,8,128]{2,1,0:T(8,128)S(1)}, u32[]{:S(2)}, u32[]{:S(2)}) collective-permute-start(f32[2,8,128]{2,1,0:T(8,128)S(1)} %get-tuple-element.28.start), channel_id=1, source_target_pairs={{0,1},{1,0},{2,3},{3,2},{4,5},{5,4},{6,7},{7,6},{8,9},{9,8},{10,11... | collective-permute-start | bytes 24584 | tf_op jit(solution)/shard_map/ppermute | solution.py:434
  10.1 5.6 %collective-permute-start.2 = (f32[2,8,128]{2,1,0:T(8,128)S(1)}, f32[2,8,128]{2,1,0:T(8,128)S(1)}, u32[]{:S(2)}, u32[]{:S(2)}) collective-permute-start(f32[2,8,128]{2,1,0:T(8,128)S(1)} %get-tuple-element.28.start), channel_id=1, source_target_pairs={{0,4},{1,2},{2,1},{3,7},{4,0},{5,6},{6,5},{7,3},{8,12},{9,10},{10,... | collective-permute-start | bytes 24584 | tf_op jit(solution)/shard_map/ppermute | solution.py:430
  10.1 2.4 %copy-start.2 = (bf16[2,1,16,4096]{3,2,1,0:T(8,128)(2,1)S(1)}, bf16[2,1,16,4096]{3,2,1,0:T(8,128)(2,1)}, u32[]{:S(2)}) copy-start(bf16[2,1,16,4096]{3,2,1,0:T(8,128)(2,1)} %diag.1) | copy-start | bytes 786436
  10.1 2.4 %copy-start.5 = (f32[2,1,1024]{2,1,0:T(1,128)S(1)}, f32[2,1,1024]{2,1,0:T(1,128)}, u32[]{:S(2)}) copy-start(f32[2,1,1024]{2,1,0:T(1,128)} %param.7) | copy-start | bytes 24580
  10.1 5.6 %collective-permute-start.3 = (f32[1,8,128]{2,1,0:T(8,128)S(1)}, f32[1,8,128]{2,1,0:T(8,128)S(1)}, u32[]{:S(2)}, u32[]{:S(2)}) collective-permute-start(f32[1,8,128]{2,1,0:T(8,128)S(1)} %slice.3), channel_id=1, source_target_pairs={{0,28},{4,0},{8,4},{12,8},{16,12},{20,16},{24,20},{28,24},{1,29},{... | collective-permute-start | bytes 12296 | tf_op jit(solution)/shard_map/ppermute | solution.py:493
  11.1 11.0 %collective-permute-start.7 = (f32[256,128]{1,0:T(8,128)S(1)}, f32[256,128]{1,0:T(8,128)S(1)}, u32[]{:S(2)}, u32[]{:S(2)}) collective-permute-start(f32[256,128]{1,0:T(8,128)S(1)} %shard_map.83), channel_id=1, source_target_pairs={{0,8},{4,12},{8,0},{12,4},{16,24},{20,28},{24,16},{28,20},{1,9},{5... | collective-permute-start | bytes 393224 | tf_op jit(solution)/shard_map/ppermute | solution.py:434
  12.5 3.3 %collective-permute-start.5 = (f32[256,128]{1,0:T(8,128)S(1)}, f32[256,128]{1,0:T(8,128)S(1)}, u32[]{:S(2)}, u32[]{:S(2)}) collective-permute-start(f32[256,128]{1,0:T(8,128)S(1)} %collective-permute-done.4.rest_0_), channel_id=1, source_target_pairs={{0,4},{4,0},{8,12},{12,8},{16,20},{20,16},{24,28},{28,24},{1,5},{5... | collective-permute-start | bytes 393224 | tf_op jit(solution)/shard_map/ppermute | solution.py:434
  17.6 0.7 %copy-start.6 = (f32[512,128]{1,0:T(8,128)}, f32[512,128]{1,0:T(8,128)S(1)}, u32[]{:S(2)}) copy-start(f32[512,128]{1,0:T(8,128)S(1)} %get-tuple-element.40.rest_1_) | copy-start | bytes 786436
  18.3 8.7 %all-to-all-start = ((f32[8,8,128]{2,1,0:T(8,128)}), f32[8,8,128]{2,1,0:T(8,128)S(1)}, u32[]{:S(2)}, u32[]{:S(2)}) async-start(f32[8,8,128]{2,1,0:T(8,128)} %get-tuple-element.35), calls=%async_computation | async-start | bytes 65536 | tf_op jit(solution)/shard_map/all_to_all | solution.py:438
  22.1 9.4 %collective-permute-start.8 = (f32[256,128]{1,0:T(8,128)S(1)}, f32[256,128]{1,0:T(8,128)S(1)}, u32[]{:S(2)}, u32[]{:S(2)}) collective-permute-start(f32[256,128]{1,0:T(8,128)S(1)} %collective-permute-done.7.rest_0_), channel_id=1, source_target_pairs={{0,4},{4,0},{8,12},{12,8},{16,20},{20,16},{24,28},{28,24},{1,5},{5... | collective-permute-start | bytes 393224 | tf_op jit(solution)/shard_map/ppermute | solution.py:434
  26.9 1.0 %copy-start.7 = (f32[512,128]{1,0:T(8,128)S(1)}, f32[512,128]{1,0:T(8,128)}, u32[]{:S(2)}) copy-start(f32[512,128]{1,0:T(8,128)} %copy-done.6) | copy-start | bytes 786436
  29.0 4.1 %collective-permute-start.9 = (f32[2,8,128]{2,1,0:T(8,128)S(1)}, f32[2,8,128]{2,1,0:T(8,128)S(1)}, u32[]{:S(2)}, u32[]{:S(2)}) collective-permute-start(f32[2,8,128]{2,1,0:T(8,128)S(1)} %get-tuple-element.43.vectors), channel_id=1, source_target_pairs={{0,1},{1,0},{2,3},{3,2},{4,5},{5,4},{6,7},{7,6},{8,9},{9,8},{10,11... | collective-permute-start | bytes 24584 | tf_op jit(solution)/shard_map/ppermute | solution.py:434
  31.5 3.7 %collective-permute-start.10 = (f32[2,8,128]{2,1,0:T(8,128)S(1)}, f32[2,8,128]{2,1,0:T(8,128)S(1)}, u32[]{:S(2)}, u32[]{:S(2)}) collective-permute-start(f32[2,8,128]{2,1,0:T(8,128)S(1)} %get-tuple-element.43.vectors), channel_id=1, source_target_pairs={{0,4},{1,2},{2,1},{3,7},{4,0},{5,6},{6,5},{7,3},{8,12},{9,10},{10,... | collective-permute-start | bytes 24584 | tf_op jit(solution)/shard_map/ppermute | solution.py:430

commit v8 on v7

--- a/solution.py
+++ b/solution.py
@@ -146,30 +146,52 @@
 STEP = 8
 
 
-def diagonals(tiles, out, first):
-    count = len(tiles)
-    shape = tiles[0].shape
-    shift = 1
-    while shift < count:
-        here = lane_bit(shape, 2 * shift)
-        tiles = [jnp.where(here, tiles[(j + shift) % count], tiles[j]) for j in range(count)]
-        shift *= 2
-    for j, tile in enumerate(tiles):
-        turn_by = j // STEP * STEP * 2
-        at = first + j * shape[0]
-        out[at : at + shape[0], :] = pltpu.roll(tile, turn_by, 1) if turn_by else tile
-
-
-def whole_tiles(ref, first, pairs, count=LANES // 2):
-    return [ref[first + b * pairs : first + (b + 1) * pairs, :] for b in range(count)]
+def diagonals(load, out, first, scratch, pairs):
+    count = LANES // 2
+    shape = (pairs, LANES)
+    giants = count // STEP
+
+    def slid(tiles, shift, mask):
+        here = lane_bit(shape, mask)
+        return [jnp.where(here, b, a) for a, b in zip(tiles, tiles[shift:] + tiles[:shift])]
+
+    for small in range(STEP):
+        tiles = [load(small + STEP * giant) for giant in range(giants)]
+        shift = 1
+        while shift < giants:
+            tiles = slid(tiles, shift, 2 * STEP * shift)
+            shift *= 2
+        for giant, tile in enumerate(tiles):
+            at = (small + STEP * giant) * pairs
+            scratch[at : at + pairs, :] = tile
+    for giant in range(giants):
+        tiles = []
+        for j in range(2 * STEP - 1):
+            at = (giant * STEP + j) % count * pairs
+            tiles.append(scratch[at : at + pairs, :])
+        shift = 1
+        while shift < STEP:
+            tiles = slid(tiles, shift, 2 * shift)[:-shift]
+            shift *= 2
+        for j, tile in enumerate(tiles):
+            at = first + (giant * STEP + j) * pairs
+            turn_by = 2 * STEP * giant
+            out[at : at + pairs, :] = pltpu.roll(tile, turn_by, 1) if giant else tile
+
+
+def whole_tiles(ref, first, pairs):
+    return lambda b: ref[first + b * pairs : first + (b + 1) * pairs, :]
 
 
 def part_tiles(mine, other, pairs):
     first_core = lax.axis_index("gx") & 1 == 0
-    halves_of = [whole_tiles(ref, 0, pairs, LANES // 4) for ref in (mine, other)]
-    low = [jnp.where(first_core, a, b) for a, b in zip(*halves_of)]
-    high = [jnp.where(first_core, b, a) for a, b in zip(*halves_of)]
-    return low + high
+
+    def load(b):
+        low, at = b < LANES // 4, b % (LANES // 4) * pairs
+        own, far = mine[at : at + pairs, :], other[at : at + pairs, :]
+        return jnp.where(first_core, own if low else far, far if low else own)
+
+    return load
 
 
 def mapped(ref, vector, first=0):
@@ -189,26 +211,17 @@
 
 
 def prep_kernel(reverse, blocks, beside_it, *refs):
-    *passed, maps, products, own, held, held_start, native, rows_scratch, semaphores = refs
+    *passed, maps, products, own, native, rows_scratch = refs
     planes, _, rows, width = blocks.shape
     species = LANES // 2
     pairs = rows // 2
     size = species * pairs
     order = list(range(planes))[::-1] if reverse else list(range(planes))
-    copies = [
-        pltpu.make_async_copy(blocks.at[p], held.at[p], semaphores.at[p]) for p in range(planes)
-    ]
+    if passed:
+        for p in range(planes):
+            passed[0][p] = woven(beside_it[p])
     for plane in order:
-        copies[plane].start()
-    if passed:
-        copy = pltpu.make_async_copy(beside_it, held_start, semaphores.at[planes])
-        copy.start()
-        copy.wait()
-        for p in range(planes):
-            passed[0][p] = woven(held_start[p])
-    for plane in order:
-        copies[plane].wait()
-        to_rows(rows_scratch, native, reader(held, plane, 0), rows, species)
+        to_rows(rows_scratch, native, reader(blocks, plane, 0), rows, species)
         turn(rows_scratch, maps, plane * size, pairs, species)
     for step, plane in enumerate(order):
         at = pl.ds(plane * size, size)
@@ -255,7 +268,7 @@
 
 
 def base_kernel(start, source, diag, upper, side, maps, products, partner, *outs):
-    rhs, base, step_maps, entry_maps, near_map = outs
+    rhs, base, step_maps, entry_maps, near_map, scratch = outs
     planes, pairs = start.shape[:2]
     size = pairs * LANES // 2
     vectors = [spread(start[p]) for p in range(planes)]
@@ -272,9 +285,13 @@
         base[p] = gather_pairs(own - around)
     for p in range(planes):
         if p:
-            diagonals(whole_tiles(maps, p * size, pairs), step_maps, p * size)
-        diagonals(whole_tiles(products, p * size, pairs), entry_maps, p * size)
-    diagonals(whole_tiles(partner, 0, pairs), near_map, 0)
+            diagonals(whole_tiles(maps, p * size, pairs), step_maps, p * size, scratch.at[0], pairs)
+        diagonals(whole_tiles(products, p * size, pairs), entry_maps, p * size, scratch.at[1], pairs)
+    diagonals(whole_tiles(partner, 0, pairs), near_map, 0, scratch.at[2], pairs)
+
+
+def far_kernel(pairs, mine, other, out, scratch):
+    diagonals(part_tiles(mine, other, pairs), out, 0, scratch, pairs)
 
 
 def outgoing(offset, partners, here, slots):
@@ -315,14 +332,12 @@
     return jnp.where(place == 0, 0.0, low), jnp.where(place == count - 1, 0.0, high)
 
 
-def forward_offset_kernel(levels, base, paired, other, ahead, side, upper, step_maps, near, *rest):
-    parts, (drive, offsets, slots, *far) = rest[: 2 * (levels - 2)], rest[2 * (levels - 2) :]
+def forward_offset_kernel(base, other, paired, ahead, side, upper, step_maps, *rest):
+    *partners, drive, offsets, slots = rest
     planes, pairs = base.shape[:2]
     size = pairs * LANES // 2
     here = lax.axis_index("gx")
     last = here == lax.axis_size("gx") - 1
-    for level, ref in enumerate(far):
-        diagonals(part_tiles(*parts[2 * level : 2 * level + 2], pairs), ref, 0)
     previous = None
     for p in range(planes):
         low, high = beside("gy", paired[p], other[p])
@@ -336,7 +351,7 @@
             fresh = fresh - mapped(step_maps, previous, p * size)
         offsets[p] = fresh
         previous = fresh
-    outgoing(previous, [near, *far], here, slots)
+    outgoing(previous, partners, here, slots)
 
 
 def forward_kernel(got, drive, offsets, rhs, entry_maps, *rest):
@@ -353,7 +368,7 @@
 
 def side_kernel(levels, base, vectors, side, maps, products, partner, *rest):
     parts = rest[: 2 * (levels - 2)]
-    out, step_maps, entry_maps, near, *far = rest[2 * (levels - 2) :]
+    out, step_maps, entry_maps, near, *far, scratch = rest[2 * (levels - 2) :]
     planes, pairs = base.shape[:2]
     size = pairs * LANES // 2
     for p in range(planes):
@@ -366,14 +381,14 @@
         )
         out[p] = base[p] - gather_pairs(around)
         if p + 1 < planes:
-            diagonals(whole_tiles(maps, p * size, pairs), step_maps, p * size)
-        diagonals(whole_tiles(products, p * size, pairs), entry_maps, p * size)
-    diagonals(whole_tiles(partner, 0, pairs), near, 0)
+            diagonals(whole_tiles(maps, p * size, pairs), step_maps, p * size, scratch.at[0], pairs)
+        diagonals(whole_tiles(products, p * size, pairs), entry_maps, p * size, scratch.at[1], pairs)
+    diagonals(whole_tiles(partner, 0, pairs), near, 0, scratch.at[2], pairs)
     for level, ref in enumerate(far):
-        diagonals(part_tiles(*parts[2 * level : 2 * level + 2], pairs), ref, 0)
-
-
-def backward_offset_kernel(base, paired, other, side, step_maps, *rest):
+        diagonals(part_tiles(*parts[2 * level : 2 * level + 2], pairs), ref, 0, scratch.at[3], pairs)
+
+
+def backward_offset_kernel(base, other, paired, side, step_maps, *rest):
     *partners, offsets, slots = rest
     planes = base.shape[0]
     size = base.shape[1] * LANES // 2
@@ -408,11 +423,11 @@
         kernel,
         out_shape=outs,
         in_specs=[
-            pl.BlockSpec(memory_space=pltpu.HBM if i in held else pltpu.VMEM) for i in range(len(arrays))
+            pl.BlockSpec(memory_space=pl.ANY if i in held else pltpu.VMEM) for i in range(len(arrays))
         ],
         out_specs=[pl.BlockSpec(memory_space=pltpu.VMEM) for _ in outs],
-        scratch_shapes=[pltpu.VMEM(s, F32) if isinstance(s, tuple) else s for s in scratch],
-        compiler_params=pltpu.CompilerParams(vmem_limit_bytes=24 << 20),
+        scratch_shapes=[pltpu.VMEM(shape, F32) for shape in scratch],
+        compiler_params=pltpu.CompilerParams(vmem_limit_bytes=12 << 20),
         cost_estimate=pl.CostEstimate(
             flops=int(micros * 1.15e9), bytes_accessed=moved, transcendentals=0
         ),
@@ -456,15 +471,9 @@
     def prepare(reverse, blocks, other):
         *passed, maps_of, products, own = call(
             functools.partial(prep_kernel, reverse),
-            [(blocks, None), other if reverse else (other, None)],
+            [blocks, (other, None) if reverse else other],
             ([] if reverse else [vec]) + [maps, maps, whole],
-            [
-                pltpu.VMEM(blocks.shape, blocks.dtype),
-                vec,
-                (depth * species // 2, LANES),
-                (depth * species, LANES),
-                pltpu.SemaphoreType.DMA((planes + 1,)),
-            ],
+            [(depth * species // 2, LANES), (depth * species, LANES)],
             1.0,
         )
         partners, kept = [], None
@@ -492,24 +501,32 @@
     paired, other = swaps(start)
     ahead = lax.ppermute(start[:1], "gx", [(i, (i - 1) % count) for i in range(count)])
 
-    far = [whole] * (levels - 2)
     rhs, base, step_maps, entry_maps, near = call(
         base_kernel,
         [start, source, diag_inverse, x_upper, side_blocks] + lower[:3],
         [vec, vec, maps, maps, whole],
-        [],
+        [(3,) + whole],
         5.0,
     )
-    drive, offsets, sent, *partners = call(
-        functools.partial(forward_offset_kernel, levels),
-        [base, paired, other, ahead, side_blocks, x_upper, step_maps, near] + lower[3:],
-        [vec, vec, slots] + far,
+    partners = [near]
+    for level in range(levels - 2):
+        partners += call(
+            functools.partial(far_kernel, pairs),
+            lower[3 + 2 * level : 5 + 2 * level],
+            [whole],
+            [whole],
+            0.3,
+        )
+    drive, offsets, sent = call(
+        forward_offset_kernel,
+        [base, other, paired, ahead, side_blocks, x_upper, step_maps] + partners,
+        [vec, vec, slots],
         [],
         1.5,
     )
     forward, copy, base = call(
         forward_kernel,
-        [exchange(sent, "gx"), drive, offsets, rhs, entry_maps, near] + partners,
+        [exchange(sent, "gx"), drive, offsets, rhs, entry_maps] + partners,
         [vec, vec, vec],
         [],
         1.0,
@@ -518,13 +535,13 @@
     base, step_maps, entry_maps, *partners = call(
         functools.partial(side_kernel, levels),
         [base, copy, side_blocks] + upper,
-        [vec, maps, maps, whole] + far,
-        [],
+        [vec, maps, maps, whole] + [whole] * (levels - 2),
+        [(4,) + whole],
         0.7,
     )
     offsets, sent = call(
         backward_offset_kernel,
-        [base, paired, other, side_blocks, step_maps] + partners,
+        [base, other, paired, side_blocks, step_maps] + partners,
         [vec, slots],
         [],
         1.5,

time: 45 us -> 43.9 us (0.976)
  the two profiles are of different devices: /device:TPU:16 before, /device:TPU:0 now
where the time goes in v8:
time: 43.9 us; the launch traced here: 43.6 us
  starting transfers between devices  14.7 us (33%)
  Pallas kernels  13.2 us (30%)
  blocking collectives  7.21 us (16%)
  waiting for transfers between devices  4.67 us (11%)
  local copies, waits for them, and re-layouts  3.08 us (7%)
  between operations  0.76 us (2%)
    pallas_call x11, Pallas kernels, call(): pl.pallas_call(kernel, out_shape=outs, in_specs=[pl.BlockSpec(memory_spac...  13.2 us
    ppermute x8, starting transfers between devices, crossed(): lax.ppermute(block, axis, [(i, i ^ distance) for i in range(lax.axis_size...  10.7 us
    all_to_all x1, blocking collectives, exchange(): return lax.all_to_all(slots, axis, 0, 0)  7.21 us
    all_to_all x1, waiting for transfers between devices, exchange(): return lax.all_to_all(slots, axis, 0, 0)  4.33 us
    all_to_all x1, starting transfers between devices, exchange(): return lax.all_to_all(slots, axis, 0, 0)  3.65 us
    unnamed x16, local copies, waits for them, and re-layouts  3.08 us
  transfers between devices with their start and end apart: 12, of which 2 were waited for; matrix products, arithmetic and copies ran while one was open for 0% of the time, Pallas kernels for 22%

profile of v8, /device:TPU:0, one launch (start us, length us, event | category | flops | bytes accessed | tf_op | source)
XLA Modules:
  0.0 43.6 jit_solution(10447280958184156198)
XLA Ops:
  0.6 0.9 %copy-done.1 = bf16[2,1,16,4096]{3,2,1,0:T(8,128)(2,1)S(1)} copy-done((bf16[2,1,16,4096]{3,2,1,0:T(8,128)(2,1)S(1)}, bf16[2,1,16,4096]{3,2,1,0:T(8,128)(2,1)}, u32[]{:S(2)}) %copy-start.1) | copy-done | bytes 262168
  1.6 0.7 %copy-done.4 = f32[2,1,1024]{2,1,0:T(1,128)S(1)} copy-done((f32[2,1,1024]{2,1,0:T(1,128)S(1)}, f32[2,1,1024]{2,1,0:T(1,128)}, u32[]{:S(2)}) %copy-start.4) | copy-done | bytes 8216
  2.3 1.3 %shard_map.77 = (f32[2,8,128]{2,1,0:T(8,128)S(1)}, f32[1024,128]{1,0:T(8,128)S(1)}, f32[1024,128]{1,0:T(8,128)S(1)}, f32[512,128]{1,0:T(8,128)S(1)}) custom-call(bf16[2,1,16,4096]{3,2,1,0:T(8,128)(2,1)S(1)} %copy-done.1, f32[2,8,128]{2,1,0:T(8,128)S(1)} %bitcast.4), custom_call_target="tpu_custom_call" | custom-call | flops 1150000000 | bytes 270336 | tf_op jit(solution)/shard_map/pallas_call | solution.py:422
  3.6 0.5 %collective-permute-start = (f32[512,128]{1,0:T(8,128)S(1)}, f32[512,128]{1,0:T(8,128)S(1)}, u32[]{:S(2)}, u32[]{:S(2)}) collective-permute-start(f32[512,128]{1,0:T(8,128)S(1)} %get-tuple-element.30.own), channel_id=1, source_target_pairs={{0,4},{4,0},{8,12},{12,8},{16,20},{20,16},{24,28},{28,24},{1,5},{5... | collective-permute-start | bytes 786440 | tf_op jit(solution)/shard_map/ppermute | solution.py:449
  4.1 1.3 %shard_map.83 = (f32[1024,128]{1,0:T(8,128)S(1)}, f32[1024,128]{1,0:T(8,128)S(1)}, f32[512,128]{1,0:T(8,128)S(1)}) custom-call(bf16[2,1,16,4096]{3,2,1,0:T(8,128)(2,1)S(1)} %copy-done.3, f32[1024,128]{1,0:T(8,128)S(1)} %get-tuple-element.29.products.beside_it), custom_call_target="tpu_custom_call" | custom-call | flops 1150000000 | bytes 786432 | tf_op jit(solution)/shard_map/pallas_call | solution.py:422
  5.4 0.1 collective-permute-start.6
  5.5 0.4 shard_map.79
  5.9 3.0 %collective-permute-start.4 = (f32[256,128]{1,0:T(8,128)S(1)}, f32[256,128]{1,0:T(8,128)S(1)}, u32[]{:S(2)}, u32[]{:S(2)}) collective-permute-start(f32[256,128]{1,0:T(8,128)S(1)} %shard_map.79), channel_id=1, source_target_pairs={{0,8},{4,12},{8,0},{12,4},{16,24},{20,28},{24,16},{28,20},{1,9},{5... | collective-permute-start | bytes 393224 | tf_op jit(solution)/shard_map/ppermute | solution.py:449
  8.9 0.0 collective-permute-start.1
  8.9 3.1 %collective-permute-start.2 = (f32[2,8,128]{2,1,0:T(8,128)S(1)}, f32[2,8,128]{2,1,0:T(8,128)S(1)}, u32[]{:S(2)}, u32[]{:S(2)}) collective-permute-start(f32[2,8,128]{2,1,0:T(8,128)S(1)} %get-tuple-element.27.start), channel_id=1, source_target_pairs={{0,1},{1,0},{2,3},{3,2},{4,5},{5,4},{6,7},{7,6},{8,9},{9,8},{10,11... | collective-permute-start | bytes 24584 | tf_op jit(solution)/shard_map/ppermute | solution.py:449
  12.0 0.3 collective-permute-start.3
  12.3 0.0 collective-permute-done.6.refs_0_.partner
  12.3 0.4 shard_map.84
  12.7 0.6 %collective-permute-start.7 = (f32[256,128]{1,0:T(8,128)S(1)}, f32[256,128]{1,0:T(8,128)S(1)}, u32[]{:S(2)}, u32[]{:S(2)}) collective-permute-start(f32[256,128]{1,0:T(8,128)S(1)} %shard_map.84), channel_id=1, source_target_pairs={{0,8},{4,12},{8,0},{12,4},{16,24},{20,28},{24,16},{28,20},{1,9},{5... | collective-permute-start | bytes 393224 | tf_op jit(solution)/shard_map/ppermute | solution.py:449
  13.3 0.0 collective-permute-start.5
  13.3 3.2 %shard_map.78 = (f32[2,8,128]{2,1,0:T(8,128)S(1)}, f32[2,8,128]{2,1,0:T(8,128)S(1)}, f32[1024,128]{1,0:T(8,128)S(1)}, f32[1024,128]{1,0:T(8,128)S(1)}, f32[512,128]{1,0:T(8,128)S(1)}) custom-call(f32[2,8,128]{2,1,0:T(8,128)S(1)} %get-tuple-element.27.start, f32[2,8,128]{2,1,0:T(8,128)S(1)} %bitcast.5, bf16[2,1,16,4096]{3,2,1,0:T(8,128)(2,1)S(1)} %copy-done.2, ...), custom_call_target="tpu_custom_call" | custom-call | flops 5750000128 | bytes 2899968 | tf_op jit(solution)/shard_map/pallas_call | solution.py:422
  16.5 0.2 shard_map.80.rest_1_
  16.6 0.0 collective-permute-done.3.ahead
  16.7 0.5 %copy-done.6 = f32[512,128]{1,0:T(8,128)} copy-done((f32[512,128]{1,0:T(8,128)}, f32[512,128]{1,0:T(8,128)S(1)}, u32[]{:S(2)}) %copy-start.6) | copy-done | bytes 262168
  17.2 1.8 %shard_map.81 = (f32[2,8,128]{2,1,0:T(8,128)S(1)}, f32[2,8,128]{2,1,0:T(8,128)S(1)}, f32[8,8,128]{2,1,0:T(8,128)}) custom-call(f32[2,8,128]{2,1,0:T(8,128)S(1)} %get-tuple-element.31.base, f32[2,8,128]{2,1,0:T(8,128)S(1)} %collective-permute-done.1.other, f32[2,8,128]{2,1,0:T(8,128)S(1)} %collective-permute-done.2.paired, ...), custom_call_target="tpu_custom_call" | custom-call | flops 1724999936 | bytes 2387968 | tf_op jit(solution)/shard_map/pallas_call | solution.py:422
  18.9 3.7 %all-to-all-start = ((f32[8,8,128]{2,1,0:T(8,128)}), f32[8,8,128]{2,1,0:T(8,128)S(1)}, u32[]{:S(2)}, u32[]{:S(2)}) async-start(f32[8,8,128]{2,1,0:T(8,128)} %get-tuple-element.34), calls=%async_computation | async-start | bytes 65536 | tf_op jit(solution)/shard_map/all_to_all | solution.py:453
  22.6 0.5 %collective-permute-start.8 = (f32[256,128]{1,0:T(8,128)S(1)}, f32[256,128]{1,0:T(8,128)S(1)}, u32[]{:S(2)}, u32[]{:S(2)}) collective-permute-start(f32[256,128]{1,0:T(8,128)S(1)} %collective-permute-done.7.rest_0_), channel_id=1, source_target_pairs={{0,4},{4,0},{8,12},{12,8},{16,20},{20,16},{24,28},{28,24},{1,5},{5... | collective-permute-start | bytes 393224 | tf_op jit(solution)/shard_map/ppermute | solution.py:449
  23.1 4.3 %all-to-all-done.got = f32[8,8,128]{2,1,0:T(8,128)S(1)} async-done(((f32[8,8,128]{2,1,0:T(8,128)}), f32[8,8,128]{2,1,0:T(8,128)S(1)}, u32[]{:S(2)}, u32[]{:S(2)}) %all-to-all-start) | async-done | bytes 32800 | tf_op jit(solution)/shard_map/all_to_all | solution.py:453
  27.4 0.9 %copy-done.7 = f32[512,128]{1,0:T(8,128)S(1)} copy-done((f32[512,128]{1,0:T(8,128)S(1)}, f32[512,128]{1,0:T(8,128)}, u32[]{:S(2)}) %copy-start.7) | copy-done | bytes 262168
  28.4 1.2 %shard_map.82 = (f32[2,8,128]{2,1,0:T(8,128)}, f32[2,8,128]{2,1,0:T(8,128)S(1)}, f32[2,8,128]{2,1,0:T(8,128)S(1)}) custom-call(f32[8,8,128]{2,1,0:T(8,128)S(1)} %all-to-all-done.got, f32[2,8,128]{2,1,0:T(8,128)S(1)} %get-tuple-element.35.drive, f32[2,8,128]{2,1,0:T(8,128)S(1)} %get-tuple-element.36.offsets, f32[2,8,128]{2,1,0:T(8,128)S(1)} %get-tuple-element.37.rhs, ...), custom_call_target="tpu_custom_call" | custom-call | flops 1150000000 | bytes 1105920 | tf_op jit(solution)/shard_map/pallas_call | solution.py:422
  29.5 0.0 collective-permute-start.9
  29.5 2.9 %collective-permute-start.10 = (f32[2,8,128]{2,1,0:T(8,128)S(1)}, f32[2,8,128]{2,1,0:T(8,128)S(1)}, u32[]{:S(2)}, u32[]{:S(2)}) collective-permute-start(f32[2,8,128]{2,1,0:T(8,128)S(1)} %get-tuple-element.41.vectors), channel_id=1, source_target_pairs={{0,1},{1,0},{2,3},{3,2},{4,5},{5,4},{6,7},{7,6},{8,9},{9,8},{10,11... | collective-permute-start | bytes 24584 | tf_op jit(solution)/shard_map/ppermute | solution.py:449
  32.4 1.3 %shard_map.85 = (f32[2,8,128]{2,1,0:T(8,128)S(1)}, f32[1024,128]{1,0:T(8,128)S(1)}, f32[1024,128]{1,0:T(8,128)S(1)}, f32[512,128]{1,0:T(8,128)S(1)}, f32[512,128]{1,0:T(8,128)S(1)}) custom-call(f32[2,8,128]{2,1,0:T(8,128)S(1)} %get-tuple-element.40.base, f32[2,8,128]{2,1,0:T(8,128)S(1)} %get-tuple-element.41.vectors, ...), custom_call_target="tpu_custom_call" | custom-call | flops 805000000 | bytes 2637824 | tf_op jit(solution)/shard_map/pallas_call | solution.py:422
  33.7 0.3 collective-permute-done.10.paired
  34.0 1.2 %shard_map.86 = (f32[2,8,128]{2,1,0:T(8,128)S(1)}, f32[8,8,128]{2,1,0:T(8,128)S(1)}) custom-call(f32[2,8,128]{2,1,0:T(8,128)S(1)} %get-tuple-element.45.base, f32[2,8,128]{2,1,0:T(8,128)S(1)} %collective-permute-done.9.other, f32[2,8,128]{2,1,0:T(8,128)S(1)} %collective-permute-done.10.paired, bf16[4,2,1,16,4096]{4,3,2,1,0:T(8,128)(2,1)S(1)} %copy-done, ...), custom_call_target="tpu_custom_call" | custom-call | flops 1724999936 | bytes 2121728 | tf_op jit(solution)/shard_map/pallas_call | solution.py:422
  35.2 7.2 %all_to_all.10.got = f32[8,8,128]{2,1,0:T(8,128)S(1)} all-to-all(f32[8,8,128]{2,1,0:T(8,128)S(1)} %get-tuple-element.49), channel_id=1, replica_groups=mesh['gx'=8,'gy'=4] {'gx'}, dimensions={0} | all-to-all | bytes 65536 | tf_op jit(solution)/shard_map/all_to_all | solution.py:453
  42.4 1.2 %shard_map.87 = f32[2,8,128]{2,1,0:T(8,128)} custom-call(f32[8,8,128]{2,1,0:T(8,128)S(1)} %all_to_all.10.got, f32[2,8,128]{2,1,0:T(8,128)S(1)} %get-tuple-element.50.offsets, f32[1024,128]{1,0:T(8,128)S(1)} %get-tuple-element.51.entry_maps, f32[512,128]{1,0:T(8,128)S(1)} %get-tuple-element.47.rest_0_, f32[512,128]{1,0:T(8,128)S(1)} %get-tuple-element.48.rest_1_), custom_call_target="tpu_custom_call" | custom-call | flops 1150000000 | bytes 1089536 | tf_op jit(solution)/shard_map/pallas_call | solution.py:422
  (21 shorter events, 0.0 us)
Async XLA Ops:
  0.6 1.0 %copy-start.1 = (bf16[2,1,16,4096]{3,2,1,0:T(8,128)(2,1)S(1)}, bf16[2,1,16,4096]{3,2,1,0:T(8,128)(2,1)}, u32[]{:S(2)}) copy-start(bf16[2,1,16,4096]{3,2,1,0:T(8,128)(2,1)} %blocks.2) | copy-start | bytes 786436
  1.6 0.7 %copy-start.4 = (f32[2,1,1024]{2,1,0:T(1,128)S(1)}, f32[2,1,1024]{2,1,0:T(1,128)}, u32[]{:S(2)}) copy-start(f32[2,1,1024]{2,1,0:T(1,128)} %param.6) | copy-start | bytes 24580
  2.3 1.8 %copy-start.3 = (bf16[2,1,16,4096]{3,2,1,0:T(8,128)(2,1)S(1)}, bf16[2,1,16,4096]{3,2,1,0:T(8,128)(2,1)}, u32[]{:S(2)}) copy-start(bf16[2,1,16,4096]{3,2,1,0:T(8,128)(2,1)} %blocks.3) | copy-start | bytes 786436
  3.6 1.9 %collective-permute-start = (f32[512,128]{1,0:T(8,128)S(1)}, f32[512,128]{1,0:T(8,128)S(1)}, u32[]{:S(2)}, u32[]{:S(2)}) collective-permute-start(f32[512,128]{1,0:T(8,128)S(1)} %get-tuple-element.30.own), channel_id=1, source_target_pairs={{0,4},{4,0},{8,12},{12,8},{16,20},{20,16},{24,28},{28,24},{1,5},{5... | collective-permute-start | bytes 786440 | tf_op jit(solution)/shard_map/ppermute | solution.py:449
  5.4 6.9 %collective-permute-start.6 = (f32[512,128]{1,0:T(8,128)S(1)}, f32[512,128]{1,0:T(8,128)S(1)}, u32[]{:S(2)}, u32[]{:S(2)}) collective-permute-start(f32[512,128]{1,0:T(8,128)S(1)} %get-tuple-element.44.own), channel_id=1, source_target_pairs={{0,4},{4,0},{8,12},{12,8},{16,20},{20,16},{24,28},{28,24},{1,5},{5... | collective-permute-start | bytes 786440 | tf_op jit(solution)/shard_map/ppermute | solution.py:449
  5.9 7.4 %copy-start = (bf16[4,2,1,16,4096]{4,3,2,1,0:T(8,128)(2,1)S(1)}, bf16[4,2,1,16,4096]{4,3,2,1,0:T(8,128)(2,1)}, u32[]{:S(2)}) copy-start(bf16[4,2,1,16,4096]{4,3,2,1,0:T(8,128)(2,1)} %side.7) | copy-start | bytes 3145732
  5.9 7.4 %collective-permute-start.4 = (f32[256,128]{1,0:T(8,128)S(1)}, f32[256,128]{1,0:T(8,128)S(1)}, u32[]{:S(2)}, u32[]{:S(2)}) collective-permute-start(f32[256,128]{1,0:T(8,128)S(1)} %shard_map.79), channel_id=1, source_target_pairs={{0,8},{4,12},{8,0},{12,4},{16,24},{20,28},{24,16},{28,20},{1,9},{5... | collective-permute-start | bytes 393224 | tf_op jit(solution)/shard_map/ppermute | solution.py:449
  8.9 7.8 %collective-permute-start.1 = (f32[2,8,128]{2,1,0:T(8,128)S(1)}, f32[2,8,128]{2,1,0:T(8,128)S(1)}, u32[]{:S(2)}, u32[]{:S(2)}) collective-permute-start(f32[2,8,128]{2,1,0:T(8,128)S(1)} %get-tuple-element.27.start), channel_id=1, source_target_pairs={{0,4},{1,2},{2,1},{3,7},{4,0},{5,6},{6,5},{7,3},{8,12},{9,10},{10,... | collective-permute-start | bytes 24584 | tf_op jit(solution)/shard_map/ppermute | solution.py:445
  8.9 7.8 %collective-permute-start.2 = (f32[2,8,128]{2,1,0:T(8,128)S(1)}, f32[2,8,128]{2,1,0:T(8,128)S(1)}, u32[]{:S(2)}, u32[]{:S(2)}) collective-permute-start(f32[2,8,128]{2,1,0:T(8,128)S(1)} %get-tuple-element.27.start), channel_id=1, source_target_pairs={{0,1},{1,0},{2,3},{3,2},{4,5},{5,4},{6,7},{7,6},{8,9},{9,8},{10,11... | collective-permute-start | bytes 24584 | tf_op jit(solution)/shard_map/ppermute | solution.py:449
  12.0 1.2 %copy-start.2 = (bf16[2,1,16,4096]{3,2,1,0:T(8,128)(2,1)S(1)}, bf16[2,1,16,4096]{3,2,1,0:T(8,128)(2,1)}, u32[]{:S(2)}) copy-start(bf16[2,1,16,4096]{3,2,1,0:T(8,128)(2,1)} %diag.1) | copy-start | bytes 786436
  12.0 1.2 %copy-start.5 = (f32[2,1,1024]{2,1,0:T(1,128)S(1)}, f32[2,1,1024]{2,1,0:T(1,128)}, u32[]{:S(2)}) copy-start(f32[2,1,1024]{2,1,0:T(1,128)} %param.7) | copy-start | bytes 24580
  12.0 4.6 %collective-permute-start.3 = (f32[1,8,128]{2,1,0:T(8,128)S(1)}, f32[1,8,128]{2,1,0:T(8,128)S(1)}, u32[]{:S(2)}, u32[]{:S(2)}) collective-permute-start(f32[1,8,128]{2,1,0:T(8,128)S(1)} %slice.3), channel_id=1, source_target_pairs={{0,28},{4,0},{8,4},{12,8},{16,12},{20,16},{24,20},{28,24},{1,29},{... | collective-permute-start | bytes 12296 | tf_op jit(solution)/shard_map/ppermute | solution.py:502
  12.7 9.9 %collective-permute-start.7 = (f32[256,128]{1,0:T(8,128)S(1)}, f32[256,128]{1,0:T(8,128)S(1)}, u32[]{:S(2)}, u32[]{:S(2)}) collective-permute-start(f32[256,128]{1,0:T(8,128)S(1)} %shard_map.84), channel_id=1, source_target_pairs={{0,8},{4,12},{8,0},{12,4},{16,24},{20,28},{24,16},{28,20},{1,9},{5... | collective-permute-start | bytes 393224 | tf_op jit(solution)/shard_map/ppermute | solution.py:449
  13.3 3.2 %collective-permute-start.5 = (f32[256,128]{1,0:T(8,128)S(1)}, f32[256,128]{1,0:T(8,128)S(1)}, u32[]{:S(2)}, u32[]{:S(2)}) collective-permute-start(f32[256,128]{1,0:T(8,128)S(1)} %collective-permute-done.4.mine), channel_id=1, source_target_pairs={{0,4},{4,0},{8,12},{12,8},{16,20},{20,16},{24,28},{28,24},{1,5},{5... | collective-permute-start | bytes 393224 | tf_op jit(solution)/shard_map/ppermute | solution.py:449
  16.5 0.7 %copy-start.6 = (f32[512,128]{1,0:T(8,128)}, f32[512,128]{1,0:T(8,128)S(1)}, u32[]{:S(2)}) copy-start(f32[512,128]{1,0:T(8,128)S(1)} %get-tuple-element.33.rest_0_) | copy-start | bytes 786436
  18.9 8.5 %all-to-all-start = ((f32[8,8,128]{2,1,0:T(8,128)}), f32[8,8,128]{2,1,0:T(8,128)S(1)}, u32[]{:S(2)}, u32[]{:S(2)}) async-start(f32[8,8,128]{2,1,0:T(8,128)} %get-tuple-element.34), calls=%async_computation | async-start | bytes 65536 | tf_op jit(solution)/shard_map/all_to_all | solution.py:453
  22.6 9.8 %collective-permute-start.8 = (f32[256,128]{1,0:T(8,128)S(1)}, f32[256,128]{1,0:T(8,128)S(1)}, u32[]{:S(2)}, u32[]{:S(2)}) collective-permute-start(f32[256,128]{1,0:T(8,128)S(1)} %collective-permute-done.7.rest_0_), channel_id=1, source_target_pairs={{0,4},{4,0},{8,12},{12,8},{16,20},{20,16},{24,28},{28,24},{1,5},{5... | collective-permute-start | bytes 393224 | tf_op jit(solution)/shard_map/ppermute | solution.py:449
  27.4 1.0 %copy-start.7 = (f32[512,128]{1,0:T(8,128)S(1)}, f32[512,128]{1,0:T(8,128)}, u32[]{:S(2)}) copy-start(f32[512,128]{1,0:T(8,128)} %copy-done.6) | copy-start | bytes 786436
  29.5 4.2 %collective-permute-start.9 = (f32[2,8,128]{2,1,0:T(8,128)S(1)}, f32[2,8,128]{2,1,0:T(8,128)S(1)}, u32[]{:S(2)}, u32[]{:S(2)}) collective-permute-start(f32[2,8,128]{2,1,0:T(8,128)S(1)} %get-tuple-element.41.vectors), channel_id=1, source_target_pairs={{0,4},{1,2},{2,1},{3,7},{4,0},{5,6},{6,5},{7,3},{8,12},{9,10},{10,... | collective-permute-start | bytes 24584 | tf_op jit(solution)/shard_map/ppermute | solution.py:445
  29.5 4.5 %collective-permute-start.10 = (f32[2,8,128]{2,1,0:T(8,128)S(1)}, f32[2,8,128]{2,1,0:T(8,128)S(1)}, u32[]{:S(2)}, u32[]{:S(2)}) collective-permute-start(f32[2,8,128]{2,1,0:T(8,128)S(1)} %get-tuple-element.41.vectors), channel_id=1, source_target_pairs={{0,1},{1,0},{2,3},{3,2},{4,5},{5,4},{6,7},{7,6},{8,9},{9,8},{10,11... | collective-permute-start | bytes 24584 | tf_op jit(solution)/shard_map/ppermute | solution.py:449

commit v9 on v8

--- a/solution.py
+++ b/solution.py
@@ -71,6 +71,17 @@
     for first in (0, half // 2):
         block = jnp.take_along_axis(vector, first + row // 2, 0)
         parts.append(jnp.take_along_axis(block, place, 1))
+    return jnp.concatenate(parts, 0)
+
+
+def spread_raw(raw):
+    half = raw.shape[0]
+    row = lax.broadcasted_iota(jnp.int32, raw.shape, 0)
+    same = (row & 1 == 1) == lane_bit(raw.shape, LANES // 2)
+    parts = []
+    for first in (0, half // 2):
+        block = jnp.take_along_axis(raw, first + row // 2, 0)
+        parts.append(jnp.where(same, block, pltpu.roll(block, LANES // 2, 1)))
     return jnp.concatenate(parts, 0)
 
 
@@ -210,30 +221,30 @@
     return total
 
 
-def prep_kernel(reverse, blocks, beside_it, *refs):
-    *passed, maps, products, own, native, rows_scratch = refs
+def prep_kernel(reverse, blocks, *refs):
+    if reverse:
+        start, _, passed, *refs = refs
+        for p in range(start.shape[0]):
+            passed[p] = woven(start[p])
+    steps, products, own, maps, native, rows_scratch = refs
     planes, _, rows, width = blocks.shape
     species = LANES // 2
     pairs = rows // 2
     size = species * pairs
     order = list(range(planes))[::-1] if reverse else list(range(planes))
-    if passed:
-        for p in range(planes):
-            passed[0][p] = woven(beside_it[p])
-    for plane in order:
-        to_rows(rows_scratch, native, reader(blocks, plane, 0), rows, species)
-        turn(rows_scratch, maps, plane * size, pairs, species)
     for step, plane in enumerate(order):
         at = pl.ds(plane * size, size)
+        to_rows(rows_scratch, native, reader(blocks, plane, 0), rows, species)
+        turn(rows_scratch, maps, 0, pairs, species)
         if step == 0:
-            products[at, :] = -maps[at, :]
+            products[at, :] = -maps[...]
             continue
+        steps[pl.ds((step - 1) * size, size), :] = maps[...]
         for pair in range(pairs):
             here = pl.ds(plane * size + pair, species, stride=pairs)
             before = pl.ds(order[step - 1] * size + pair, species, stride=pairs)
-            products[here, :] = multiply(
-                rows_scratch, pair, products[before, :], -maps[here, :], step == 1
-            )
+            later = -maps[pl.ds(pair, species, stride=pairs), :]
+            products[here, :] = multiply(rows_scratch, pair, products[before, :], later, step == 1)
     own[...] = products[pl.ds(order[-1] * size, size), :]
 
 
@@ -267,13 +278,11 @@
         outs[-1][pl.ds(pair, species // 2, stride=pairs), :] = kept
 
 
-def base_kernel(start, source, diag, upper, side, maps, products, partner, *outs):
-    rhs, base, step_maps, entry_maps, near_map, scratch = outs
-    planes, pairs = start.shape[:2]
-    size = pairs * LANES // 2
+def base_kernel(start, source, diag, upper, side, rhs, base):
+    planes = start.shape[0]
     vectors = [spread(start[p]) for p in range(planes)]
     for p in range(planes):
-        own = apply([(reader(diag, p, 0), spread(woven(source[p])))])
+        own = apply([(reader(diag, p, 0), spread_raw(source[p]))])
         terms = [
             (reader(side, 2, p, 0), shifted(vectors[p], True)),
             (reader(side, 3, p, 0), shifted(vectors[p], False)),
@@ -283,11 +292,18 @@
         around = apply(terms)
         rhs[p] = gather_pairs(own)
         base[p] = gather_pairs(own - around)
-    for p in range(planes):
-        if p:
-            diagonals(whole_tiles(maps, p * size, pairs), step_maps, p * size, scratch.at[0], pairs)
-        diagonals(whole_tiles(products, p * size, pairs), entry_maps, p * size, scratch.at[1], pairs)
-    diagonals(whole_tiles(partner, 0, pairs), near_map, 0, scratch.at[2], pairs)
+
+
+def convert(pairs, sources, outs, scratch):
+    size = pairs * LANES // 2
+    for source, out in zip(sources, outs):
+        for first in range(0, source.shape[0], size):
+            diagonals(whole_tiles(source, first, pairs), out, first, scratch, pairs)
+
+
+def near_kernel(pairs, *refs):
+    *refs, scratch = refs
+    convert(pairs, refs[: len(refs) // 2], refs[len(refs) // 2 :], scratch)
 
 
 def far_kernel(pairs, mine, other, out, scratch):
@@ -332,7 +348,7 @@
     return jnp.where(place == 0, 0.0, low), jnp.where(place == count - 1, 0.0, high)
 
 
-def forward_offset_kernel(base, other, paired, ahead, side, upper, step_maps, *rest):
+def forward_offset_kernel(base, paired, other, ahead, side, upper, step_maps, *rest):
     *partners, drive, offsets, slots = rest
     planes, pairs = base.shape[:2]
     size = pairs * LANES // 2
@@ -348,7 +364,7 @@
         fresh = base[p] - gather_pairs(apply(terms))
         drive[p] = fresh
         if previous is not None:
-            fresh = fresh - mapped(step_maps, previous, p * size)
+            fresh = fresh - mapped(step_maps, previous, (p - 1) * size)
         offsets[p] = fresh
         previous = fresh
     outgoing(previous, partners, here, slots)
@@ -366,11 +382,10 @@
         copy[p] = value
 
 
-def side_kernel(levels, base, vectors, side, maps, products, partner, *rest):
+def side_kernel(levels, base, vectors, side, steps, products, partner, *rest):
     parts = rest[: 2 * (levels - 2)]
     out, step_maps, entry_maps, near, *far, scratch = rest[2 * (levels - 2) :]
     planes, pairs = base.shape[:2]
-    size = pairs * LANES // 2
     for p in range(planes):
         vector = spread(vectors[p])
         around = apply(
@@ -380,15 +395,12 @@
             ]
         )
         out[p] = base[p] - gather_pairs(around)
-        if p + 1 < planes:
-            diagonals(whole_tiles(maps, p * size, pairs), step_maps, p * size, scratch.at[0], pairs)
-        diagonals(whole_tiles(products, p * size, pairs), entry_maps, p * size, scratch.at[1], pairs)
-    diagonals(whole_tiles(partner, 0, pairs), near, 0, scratch.at[2], pairs)
+    convert(pairs, (steps, products, partner), (step_maps, entry_maps, near), scratch.at[0])
     for level, ref in enumerate(far):
-        diagonals(part_tiles(*parts[2 * level : 2 * level + 2], pairs), ref, 0, scratch.at[3], pairs)
-
-
-def backward_offset_kernel(base, other, paired, side, step_maps, *rest):
+        diagonals(part_tiles(*parts[2 * level : 2 * level + 2], pairs), ref, 0, scratch.at[1], pairs)
+
+
+def backward_offset_kernel(base, paired, other, side, step_maps, *rest):
     *partners, offsets, slots = rest
     planes = base.shape[0]
     size = base.shape[1] * LANES // 2
@@ -399,7 +411,7 @@
         around = apply([(reader(side, 0, p, 0), spread(low)), (reader(side, 1, p, 0), spread(high))])
         fresh = base[p] - gather_pairs(around)
         if previous is not None:
-            fresh = fresh - mapped(step_maps, previous, p * size)
+            fresh = fresh - mapped(step_maps, previous, (planes - 2 - p) * size)
         offsets[p] = fresh
         previous = fresh
     outgoing(previous, partners, here, slots)
@@ -462,18 +474,18 @@
     size = species * pairs
     one = (pairs, LANES)
     vec = (planes,) + one
-    maps = (planes * size, LANES)
+    maps, steps = (planes * size, LANES), ((planes - 1) * size, LANES)
     whole, half = (size, LANES), (size // 2, LANES)
     slots = (count,) + one
     start = start.reshape(vec)
     source = source.reshape(vec)
 
-    def prepare(reverse, blocks, other):
-        *passed, maps_of, products, own = call(
+    def prepare(reverse, blocks, after=None):
+        *passed, step_maps, products, own = call(
             functools.partial(prep_kernel, reverse),
-            [blocks, (other, None) if reverse else other],
-            ([] if reverse else [vec]) + [maps, maps, whole],
-            [(depth * species // 2, LANES), (depth * species, LANES)],
+            [blocks] + ([start, (after, None)] if reverse else []),
+            ([vec] if reverse else []) + [steps, maps, whole],
+            [whole, (depth * species // 2, LANES), (depth * species, LANES)],
             1.0,
         )
         partners, kept = [], None
@@ -494,19 +506,18 @@
                     0.4,
                 )
                 own, kept = outs[0], outs[-1]
-        return [maps_of, products, *partners], passed
-
-    lower, (start,) = prepare(False, x_lower, start)
-    upper, _ = prepare(True, x_upper, lower[1])
+        return [step_maps, products, *partners], passed
+
+    lower, _ = prepare(False, x_lower)
+    upper, (start,) = prepare(True, x_upper, lower[1])
     paired, other = swaps(start)
     ahead = lax.ppermute(start[:1], "gx", [(i, (i - 1) % count) for i in range(count)])
 
-    rhs, base, step_maps, entry_maps, near = call(
-        base_kernel,
-        [start, source, diag_inverse, x_upper, side_blocks] + lower[:3],
-        [vec, vec, maps, maps, whole],
-        [(3,) + whole],
-        5.0,
+    rhs, base = call(
+        base_kernel, [start, source, diag_inverse, x_upper, side_blocks], [vec, vec], [], 5.0
+    )
+    step_maps, entry_maps, near = call(
+        functools.partial(near_kernel, pairs), lower[:3], [steps, maps, whole], [whole], 0.5
     )
     partners = [near]
     for level in range(levels - 2):
@@ -519,7 +530,7 @@
         )
     drive, offsets, sent = call(
         forward_offset_kernel,
-        [base, other, paired, ahead, side_blocks, x_upper, step_maps] + partners,
+        [base, paired, other, ahead, side_blocks, x_upper, step_maps] + partners,
         [vec, vec, slots],
         [],
         1.5,
@@ -535,13 +546,13 @@
     base, step_maps, entry_maps, *partners = call(
         functools.partial(side_kernel, levels),
         [base, copy, side_blocks] + upper,
-        [vec, maps, maps, whole] + [whole] * (levels - 2),
-        [(4,) + whole],
+        [vec, steps, maps, whole] + [whole] * (levels - 2),
+        [(2,) + whole],
         0.7,
     )
     offsets, sent = call(
         backward_offset_kernel,
-        [base, other, paired, side_blocks, step_maps] + partners,
+        [base, paired, other, side_blocks, step_maps] + partners,
         [vec, slots],
         [],
         1.5,

time: 43.9 us -> 41.4 us (0.943)
  local copies, waits for them, and re-layouts: 3.08 us -> 0.97 us
  Pallas kernels: 13.2 us -> 11.8 us
  waiting for transfers between devices: 4.67 us -> 5.91 us
    unnamed x16 -> x12, local copies, waits for them, and re-layouts: 3.08 us -> 0.97 us
    pallas_call x11 -> x12, Pallas kernels: 13.2 us -> 11.8 us  [call(): pl.pallas_call(kernel, out_shape=outs, in_specs=[pl.BlockSpec(memory_spac...]
    ppermute x8, waiting for transfers between devices: 0.33 us -> 1.57 us  [crossed(): lax.ppermute(block, axis, [(i, i ^ distance) for i in range(lax.axis_size...]
  transfers between devices with their start and end apart: 12 -> 12, of which waited for: 2 -> 3; matrix products, arithmetic and copies ran while one was open for 0% -> 0% of each run, Pallas kernels for 22% -> 19%
where the time goes in v9:
time: 41.4 us; the launch traced here: 41.2 us
  starting transfers between devices  14.6 us (35%)
  Pallas kernels  11.8 us (29%)
  blocking collectives  7.21 us (17%)
  waiting for transfers between devices  5.91 us (14%)
  local copies, waits for them, and re-layouts  0.97 us (2%)
  between operations  0.77 us (2%)
    pallas_call x12, Pallas kernels, call(): pl.pallas_call(kernel, out_shape=outs, in_specs=[pl.BlockSpec(memory_spac...  11.8 us
    ppermute x8, starting transfers between devices, crossed(): lax.ppermute(block, axis, [(i, i ^ distance) for i in range(lax.axis_size...  10.8 us
    all_to_all x1, blocking collectives, exchange(): return lax.all_to_all(slots, axis, 0, 0)  7.21 us
    all_to_all x1, waiting for transfers between devices, exchange(): return lax.all_to_all(slots, axis, 0, 0)  4.33 us
    all_to_all x1, starting transfers between devices, exchange(): return lax.all_to_all(slots, axis, 0, 0)  3.35 us
    ppermute x8, waiting for transfers between devices, crossed(): lax.ppermute(block, axis, [(i, i ^ distance) for i in range(lax.axis_size...  1.57 us
    unnamed x12, local copies, waits for them, and re-layouts  0.97 us
  transfers between devices with their start and end apart: 12, of which 3 were waited for; matrix products, arithmetic and copies ran while one was open for 0% of the time, Pallas kernels for 19%

profile of v9, /device:TPU:0, one launch (start us, length us, event | category | flops | bytes accessed | tf_op | source)
XLA Modules:
  0.0 41.2 jit_solution(3683675578668796588)
XLA Ops:
  0.6 0.9 %copy-done.1 = bf16[2,1,16,4096]{3,2,1,0:T(8,128)(2,1)S(1)} copy-done((bf16[2,1,16,4096]{3,2,1,0:T(8,128)(2,1)S(1)}, bf16[2,1,16,4096]{3,2,1,0:T(8,128)(2,1)}, u32[]{:S(2)}) %copy-start.1) | copy-done | bytes 262168
  1.6 1.3 %shard_map.77 = (f32[512,128]{1,0:T(8,128)S(1)}, f32[1024,128]{1,0:T(8,128)S(1)}, f32[512,128]{1,0:T(8,128)S(1)}) custom-call(bf16[2,1,16,4096]{3,2,1,0:T(8,128)(2,1)S(1)} %copy-done.1), custom_call_target="tpu_custom_call" | custom-call | flops 1150000000 | bytes 262144 | tf_op jit(solution)/shard_map/pallas_call | solution.py:434
  2.9 0.0 copy-start.3
  2.9 0.0 copy-start.4
  2.9 0.5 %collective-permute-start.3 = (f32[512,128]{1,0:T(8,128)S(1)}, f32[512,128]{1,0:T(8,128)S(1)}, u32[]{:S(2)}, u32[]{:S(2)}) collective-permute-start(f32[512,128]{1,0:T(8,128)S(1)} %get-tuple-element.31.own), channel_id=1, source_target_pairs={{0,4},{4,0},{8,12},{12,8},{16,20},{20,16},{24,28},{28,24},{1,5},{5... | collective-permute-start | bytes 786440 | tf_op jit(solution)/shard_map/ppermute | solution.py:461
  3.4 1.2 %collective-permute-done.3.refs_2_.refs_0_ = f32[512,128]{1,0:T(8,128)S(1)} collective-permute-done((f32[512,128]{1,0:T(8,128)S(1)}, f32[512,128]{1,0:T(8,128)S(1)}, u32[]{:S(2)}, u32[]{:S(2)}) %collective-permute-start.3) | collective-permute-done | bytes 262176 | tf_op jit(solution)/shard_map/ppermute | solution.py:461
  4.6 0.4 shard_map.81
  5.0 2.9 %collective-permute-start.4 = (f32[256,128]{1,0:T(8,128)S(1)}, f32[256,128]{1,0:T(8,128)S(1)}, u32[]{:S(2)}, u32[]{:S(2)}) collective-permute-start(f32[256,128]{1,0:T(8,128)S(1)} %shard_map.81), channel_id=1, source_target_pairs={{0,8},{4,12},{8,0},{12,4},{16,24},{20,28},{24,16},{28,20},{1,9},{5... | collective-permute-start | bytes 393224 | tf_op jit(solution)/shard_map/ppermute | solution.py:461
  7.9 1.3 %shard_map.78 = (f32[2,8,128]{2,1,0:T(8,128)S(1)}, f32[512,128]{1,0:T(8,128)S(1)}, f32[1024,128]{1,0:T(8,128)S(1)}, f32[512,128]{1,0:T(8,128)S(1)}) custom-call(bf16[2,1,16,4096]{3,2,1,0:T(8,128)(2,1)S(1)} %copy-done.3, f32[2,8,128]{2,1,0:T(8,128)S(1)} %bitcast.4, f32[1024,128]{1,0:T(8,128)S(1)} %get-tuple-element.27.refs_1_), custom_call_target="tpu_custom_call" | custom-call | flops 1150000000 | bytes 794624 | tf_op jit(solution)/shard_map/pallas_call | solution.py:434
  9.2 0.0 copy-start.5
  9.2 0.1 collective-permute-start.1
  9.3 3.1 %collective-permute-start = (f32[2,8,128]{2,1,0:T(8,128)S(1)}, f32[2,8,128]{2,1,0:T(8,128)S(1)}, u32[]{:S(2)}, u32[]{:S(2)}) collective-permute-start(f32[2,8,128]{2,1,0:T(8,128)S(1)} %get-tuple-element.28.start), channel_id=1, source_target_pairs={{0,1},{1,0},{2,3},{3,2},{4,5},{5,4},{6,7},{7,6},{8,9},{9,8},{10,11... | collective-permute-start | bytes 24584 | tf_op jit(solution)/shard_map/ppermute | solution.py:461
  12.4 0.4 collective-permute-start.2
  12.8 0.1 collective-permute-start.6
  12.9 0.0 collective-permute-done.4.mine
  12.9 0.4 collective-permute-start.5
  13.3 1.4 %shard_map.79 = (f32[2,8,128]{2,1,0:T(8,128)S(1)}, f32[2,8,128]{2,1,0:T(8,128)S(1)}) custom-call(f32[2,8,128]{2,1,0:T(8,128)S(1)} %get-tuple-element.28.start, f32[2,8,128]{2,1,0:T(8,128)S(1)} %bitcast.5, bf16[2,1,16,4096]{3,2,1,0:T(8,128)(2,1)S(1)} %copy-done.2, bf16[2,1,16,4096]{3,2,1,0:T(8,128)(2,1)S(1)} %copy-done.3, bf16[4,2,1,16,4096]{4,3,2,1,0:T(8,128)(2,1)S(1)} %copy-done), custom_call_target="tpu_custom_call" | custom-call | flops 5750000128 | bytes 1589248 | tf_op jit(solution)/shard_map/pallas_call | solution.py:434
  14.7 0.4 shard_map.85
  15.1 0.6 %collective-permute-start.7 = (f32[256,128]{1,0:T(8,128)S(1)}, f32[256,128]{1,0:T(8,128)S(1)}, u32[]{:S(2)}, u32[]{:S(2)}) collective-permute-start(f32[256,128]{1,0:T(8,128)S(1)} %shard_map.85), channel_id=1, source_target_pairs={{0,8},{4,12},{8,0},{12,4},{16,24},{20,28},{24,16},{28,20},{1,9},{5... | collective-permute-start | bytes 393224 | tf_op jit(solution)/shard_map/ppermute | solution.py:461
  15.6 0.4 shard_map.80
  16.0 0.2 shard_map.82.rest_1_
  16.2 1.8 %shard_map.83 = (f32[2,8,128]{2,1,0:T(8,128)S(1)}, f32[2,8,128]{2,1,0:T(8,128)S(1)}, f32[8,8,128]{2,1,0:T(8,128)}) custom-call(f32[2,8,128]{2,1,0:T(8,128)S(1)} %get-tuple-element.29.base, f32[2,8,128]{2,1,0:T(8,128)S(1)} %collective-permute-done.paired, f32[2,8,128]{2,1,0:T(8,128)S(1)} %collective-permute-done.1.other, ...), custom_call_target="tpu_custom_call" | custom-call | flops 1724999936 | bytes 2125824 | tf_op jit(solution)/shard_map/pallas_call | solution.py:434
  18.0 3.4 %all-to-all-start = ((f32[8,8,128]{2,1,0:T(8,128)}), f32[8,8,128]{2,1,0:T(8,128)S(1)}, u32[]{:S(2)}, u32[]{:S(2)}) async-start(f32[8,8,128]{2,1,0:T(8,128)} %get-tuple-element.34), calls=%async_computation | async-start | bytes 65536 | tf_op jit(solution)/shard_map/all_to_all | solution.py:465
  21.4 0.5 %collective-permute-start.8 = (f32[256,128]{1,0:T(8,128)S(1)}, f32[256,128]{1,0:T(8,128)S(1)}, u32[]{:S(2)}, u32[]{:S(2)}) collective-permute-start(f32[256,128]{1,0:T(8,128)S(1)} %collective-permute-done.7.rest_0_), channel_id=1, source_target_pairs={{0,4},{4,0},{8,12},{12,8},{16,20},{20,16},{24,28},{28,24},{1,5},{5... | collective-permute-start | bytes 393224 | tf_op jit(solution)/shard_map/ppermute | solution.py:461
  21.9 4.3 %all-to-all-done.got = f32[8,8,128]{2,1,0:T(8,128)S(1)} async-done(((f32[8,8,128]{2,1,0:T(8,128)}), f32[8,8,128]{2,1,0:T(8,128)S(1)}, u32[]{:S(2)}, u32[]{:S(2)}) %all-to-all-start) | async-done | bytes 32800 | tf_op jit(solution)/shard_map/all_to_all | solution.py:465
  26.2 1.2 %shard_map.84 = (f32[2,8,128]{2,1,0:T(8,128)}, f32[2,8,128]{2,1,0:T(8,128)S(1)}, f32[2,8,128]{2,1,0:T(8,128)S(1)}) custom-call(f32[8,8,128]{2,1,0:T(8,128)S(1)} %all-to-all-done.got, f32[2,8,128]{2,1,0:T(8,128)S(1)} %get-tuple-element.35.drive, f32[2,8,128]{2,1,0:T(8,128)S(1)} %get-tuple-element.36.offsets, f32[2,8,128]{2,1,0:T(8,128)S(1)} %get-tuple-element.37.rhs, ...), custom_call_target="tpu_custom_call" | custom-call | flops 1150000000 | bytes 1105920 | tf_op jit(solution)/shard_map/pallas_call | solution.py:434
  27.4 2.6 %collective-permute-start.9 = (f32[2,8,128]{2,1,0:T(8,128)S(1)}, f32[2,8,128]{2,1,0:T(8,128)S(1)}, u32[]{:S(2)}, u32[]{:S(2)}) collective-permute-start(f32[2,8,128]{2,1,0:T(8,128)S(1)} %get-tuple-element.41.vectors), channel_id=1, source_target_pairs={{0,1},{1,0},{2,3},{3,2},{4,5},{5,4},{6,7},{7,6},{8,9},{9,8},{10,11... | collective-permute-start | bytes 24584 | tf_op jit(solution)/shard_map/ppermute | solution.py:461
  30.0 1.2 %shard_map.86 = (f32[2,8,128]{2,1,0:T(8,128)S(1)}, f32[512,128]{1,0:T(8,128)S(1)}, f32[1024,128]{1,0:T(8,128)S(1)}, f32[512,128]{1,0:T(8,128)S(1)}, f32[512,128]{1,0:T(8,128)S(1)}) custom-call(f32[2,8,128]{2,1,0:T(8,128)S(1)} %get-tuple-element.40.base, f32[2,8,128]{2,1,0:T(8,128)S(1)} %get-tuple-element.41.vectors, ...), custom_call_target="tpu_custom_call" | custom-call | flops 805000000 | bytes 2375680 | tf_op jit(solution)/shard_map/pallas_call | solution.py:434
  31.2 0.4 collective-permute-done.9.paired
  31.6 1.2 %shard_map.87 = (f32[2,8,128]{2,1,0:T(8,128)S(1)}, f32[8,8,128]{2,1,0:T(8,128)S(1)}) custom-call(f32[2,8,128]{2,1,0:T(8,128)S(1)} %get-tuple-element.45.base, f32[2,8,128]{2,1,0:T(8,128)S(1)} %collective-permute-done.9.paired, f32[2,8,128]{2,1,0:T(8,128)S(1)} %collective-permute-done.10.other, bf16[4,2,1,16,4096]{4,3,2,1,0:T(8,128)(2,1)S(1)} %copy-done, ...), custom_call_target="tpu_custom_call" | custom-call | flops 1724999936 | bytes 1859584 | tf_op jit(solution)/shard_map/pallas_call | solution.py:434
  32.8 7.2 %all_to_all.10.got = f32[8,8,128]{2,1,0:T(8,128)S(1)} all-to-all(f32[8,8,128]{2,1,0:T(8,128)S(1)} %get-tuple-element.49), channel_id=1, replica_groups=mesh['gx'=8,'gy'=4] {'gx'}, dimensions={0} | all-to-all | bytes 65536 | tf_op jit(solution)/shard_map/all_to_all | solution.py:465
  40.0 1.2 %shard_map.88 = f32[2,8,128]{2,1,0:T(8,128)} custom-call(f32[8,8,128]{2,1,0:T(8,128)S(1)} %all_to_all.10.got, f32[2,8,128]{2,1,0:T(8,128)S(1)} %get-tuple-element.50.offsets, f32[1024,128]{1,0:T(8,128)S(1)} %get-tuple-element.51.entry_maps, f32[512,128]{1,0:T(8,128)S(1)} %get-tuple-element.47.rest_0_, f32[512,128]{1,0:T(8,128)S(1)} %get-tuple-element.48.rest_1_), custom_call_target="tpu_custom_call" | custom-call | flops 1150000000 | bytes 1089536 | tf_op jit(solution)/shard_map/pallas_call | solution.py:434
  (18 shorter events, 0.0 us)
Async XLA Ops:
  0.6 1.0 %copy-start.1 = (bf16[2,1,16,4096]{3,2,1,0:T(8,128)(2,1)S(1)}, bf16[2,1,16,4096]{3,2,1,0:T(8,128)(2,1)}, u32[]{:S(2)}) copy-start(bf16[2,1,16,4096]{3,2,1,0:T(8,128)(2,1)} %blocks.2) | copy-start | bytes 786436
  2.9 5.0 %copy-start.3 = (bf16[2,1,16,4096]{3,2,1,0:T(8,128)(2,1)S(1)}, bf16[2,1,16,4096]{3,2,1,0:T(8,128)(2,1)}, u32[]{:S(2)}) copy-start(bf16[2,1,16,4096]{3,2,1,0:T(8,128)(2,1)} %upper.3) | copy-start | bytes 786436
  2.9 5.0 %copy-start.4 = (f32[2,1,1024]{2,1,0:T(1,128)S(1)}, f32[2,1,1024]{2,1,0:T(1,128)}, u32[]{:S(2)}) copy-start(f32[2,1,1024]{2,1,0:T(1,128)} %param.6) | copy-start | bytes 24580
  2.9 1.7 %collective-permute-start.3 = (f32[512,128]{1,0:T(8,128)S(1)}, f32[512,128]{1,0:T(8,128)S(1)}, u32[]{:S(2)}, u32[]{:S(2)}) collective-permute-start(f32[512,128]{1,0:T(8,128)S(1)} %get-tuple-element.31.own), channel_id=1, source_target_pairs={{0,4},{4,0},{8,12},{12,8},{16,20},{20,16},{24,28},{28,24},{1,5},{5... | collective-permute-start | bytes 786440 | tf_op jit(solution)/shard_map/ppermute | solution.py:461
  5.0 8.0 %collective-permute-start.4 = (f32[256,128]{1,0:T(8,128)S(1)}, f32[256,128]{1,0:T(8,128)S(1)}, u32[]{:S(2)}, u32[]{:S(2)}) collective-permute-start(f32[256,128]{1,0:T(8,128)S(1)} %shard_map.81), channel_id=1, source_target_pairs={{0,8},{4,12},{8,0},{12,4},{16,24},{20,28},{24,16},{28,20},{1,9},{5... | collective-permute-start | bytes 393224 | tf_op jit(solution)/shard_map/ppermute | solution.py:461
  7.8 5.5 %copy-start = (bf16[4,2,1,16,4096]{4,3,2,1,0:T(8,128)(2,1)S(1)}, bf16[4,2,1,16,4096]{4,3,2,1,0:T(8,128)(2,1)}, u32[]{:S(2)}) copy-start(bf16[4,2,1,16,4096]{4,3,2,1,0:T(8,128)(2,1)} %side.7) | copy-start | bytes 3145732
  7.8 5.5 %copy-start.2 = (bf16[2,1,16,4096]{3,2,1,0:T(8,128)(2,1)S(1)}, bf16[2,1,16,4096]{3,2,1,0:T(8,128)(2,1)}, u32[]{:S(2)}) copy-start(bf16[2,1,16,4096]{3,2,1,0:T(8,128)(2,1)} %diag.1) | copy-start | bytes 786436
  9.2 4.1 %copy-start.5 = (f32[2,1,1024]{2,1,0:T(1,128)S(1)}, f32[2,1,1024]{2,1,0:T(1,128)}, u32[]{:S(2)}) copy-start(f32[2,1,1024]{2,1,0:T(1,128)} %param.7) | copy-start | bytes 24580
  9.2 7.0 %collective-permute-start.1 = (f32[2,8,128]{2,1,0:T(8,128)S(1)}, f32[2,8,128]{2,1,0:T(8,128)S(1)}, u32[]{:S(2)}, u32[]{:S(2)}) collective-permute-start(f32[2,8,128]{2,1,0:T(8,128)S(1)} %get-tuple-element.28.start), channel_id=1, source_target_pairs={{0,4},{1,2},{2,1},{3,7},{4,0},{5,6},{6,5},{7,3},{8,12},{9,10},{10,... | collective-permute-start | bytes 24584 | tf_op jit(solution)/shard_map/ppermute | solution.py:457
  9.3 7.0 %collective-permute-start = (f32[2,8,128]{2,1,0:T(8,128)S(1)}, f32[2,8,128]{2,1,0:T(8,128)S(1)}, u32[]{:S(2)}, u32[]{:S(2)}) collective-permute-start(f32[2,8,128]{2,1,0:T(8,128)S(1)} %get-tuple-element.28.start), channel_id=1, source_target_pairs={{0,1},{1,0},{2,3},{3,2},{4,5},{5,4},{6,7},{7,6},{8,9},{9,8},{10,11... | collective-permute-start | bytes 24584 | tf_op jit(solution)/shard_map/ppermute | solution.py:461
  12.4 3.8 %collective-permute-start.2 = (f32[1,8,128]{2,1,0:T(8,128)S(1)}, f32[1,8,128]{2,1,0:T(8,128)S(1)}, u32[]{:S(2)}, u32[]{:S(2)}) collective-permute-start(f32[1,8,128]{2,1,0:T(8,128)S(1)} %slice.3), channel_id=1, source_target_pairs={{0,28},{4,0},{8,4},{12,8},{16,12},{20,16},{24,20},{28,24},{1,29},{... | collective-permute-start | bytes 12296 | tf_op jit(solution)/shard_map/ppermute | solution.py:514
  12.8 1.9 %collective-permute-start.6 = (f32[512,128]{1,0:T(8,128)S(1)}, f32[512,128]{1,0:T(8,128)S(1)}, u32[]{:S(2)}, u32[]{:S(2)}) collective-permute-start(f32[512,128]{1,0:T(8,128)S(1)} %get-tuple-element.44.own), channel_id=1, source_target_pairs={{0,4},{4,0},{8,12},{12,8},{16,20},{20,16},{24,28},{28,24},{1,5},{5... | collective-permute-start | bytes 786440 | tf_op jit(solution)/shard_map/ppermute | solution.py:461
  12.9 3.1 %collective-permute-start.5 = (f32[256,128]{1,0:T(8,128)S(1)}, f32[256,128]{1,0:T(8,128)S(1)}, u32[]{:S(2)}, u32[]{:S(2)}) collective-permute-start(f32[256,128]{1,0:T(8,128)S(1)} %collective-permute-done.4.mine), channel_id=1, source_target_pairs={{0,4},{4,0},{8,12},{12,8},{16,20},{20,16},{24,28},{28,24},{1,5},{5... | collective-permute-start | bytes 393224 | tf_op jit(solution)/shard_map/ppermute | solution.py:461
  15.1 6.3 %collective-permute-start.7 = (f32[256,128]{1,0:T(8,128)S(1)}, f32[256,128]{1,0:T(8,128)S(1)}, u32[]{:S(2)}, u32[]{:S(2)}) collective-permute-start(f32[256,128]{1,0:T(8,128)S(1)} %shard_map.85), channel_id=1, source_target_pairs={{0,8},{4,12},{8,0},{12,4},{16,24},{20,28},{24,16},{28,20},{1,9},{5... | collective-permute-start | bytes 393224 | tf_op jit(solution)/shard_map/ppermute | solution.py:461
  18.0 8.2 %all-to-all-start = ((f32[8,8,128]{2,1,0:T(8,128)}), f32[8,8,128]{2,1,0:T(8,128)S(1)}, u32[]{:S(2)}, u32[]{:S(2)}) async-start(f32[8,8,128]{2,1,0:T(8,128)} %get-tuple-element.34), calls=%async_computation | async-start | bytes 65536 | tf_op jit(solution)/shard_map/all_to_all | solution.py:465
  21.4 8.6 %collective-permute-start.8 = (f32[256,128]{1,0:T(8,128)S(1)}, f32[256,128]{1,0:T(8,128)S(1)}, u32[]{:S(2)}, u32[]{:S(2)}) collective-permute-start(f32[256,128]{1,0:T(8,128)S(1)} %collective-permute-done.7.rest_0_), channel_id=1, source_target_pairs={{0,4},{4,0},{8,12},{12,8},{16,20},{20,16},{24,28},{28,24},{1,5},{5... | collective-permute-start | bytes 393224 | tf_op jit(solution)/shard_map/ppermute | solution.py:461
  27.4 3.9 %collective-permute-start.10 = (f32[2,8,128]{2,1,0:T(8,128)S(1)}, f32[2,8,128]{2,1,0:T(8,128)S(1)}, u32[]{:S(2)}, u32[]{:S(2)}) collective-permute-start(f32[2,8,128]{2,1,0:T(8,128)S(1)} %get-tuple-element.41.vectors), channel_id=1, source_target_pairs={{0,4},{1,2},{2,1},{3,7},{4,0},{5,6},{6,5},{7,3},{8,12},{9,10},{10,... | collective-permute-start | bytes 24584 | tf_op jit(solution)/shard_map/ppermute | solution.py:457
  27.4 4.3 %collective-permute-start.9 = (f32[2,8,128]{2,1,0:T(8,128)S(1)}, f32[2,8,128]{2,1,0:T(8,128)S(1)}, u32[]{:S(2)}, u32[]{:S(2)}) collective-permute-start(f32[2,8,128]{2,1,0:T(8,128)S(1)} %get-tuple-element.41.vectors), channel_id=1, source_target_pairs={{0,1},{1,0},{2,3},{3,2},{4,5},{5,4},{6,7},{7,6},{8,9},{9,8},{10,11... | collective-permute-start | bytes 24584 | tf_op jit(solution)/shard_map/ppermute | solution.py:461

commit v10 on v9

--- a/solution.py
+++ b/solution.py
@@ -252,7 +252,7 @@
     here = (lax.axis_index("gx") >> level) & 1
     core = lax.axis_index("gx") & 1
     species = LANES // 2
-    *refs, scratch = refs
+    _, *refs, scratch = refs
     outs = refs[-2:] if full else refs[-1:]
     partner = refs[: len(refs) - len(outs)]
     later_is_own = here == (0 if reverse else 1)
@@ -316,12 +316,8 @@
         passed = mapped(ref, vectors[-1])
         vectors.append(jnp.where((here >> level) & 1 == 0, passed, vectors[-1]))
     place = lax.axis_index("gx")
-    for target in range(slots.shape[0]):
-        apart = place ^ target
-        value = vectors[0]
-        for level in range(1, len(vectors)):
-            value = jnp.where(apart >= 1 << level, vectors[level], value)
-        slots[target] = value
+    for apart in range(slots.shape[0]):
+        slots[place ^ apart] = vectors[max(apart.bit_length() - 1, 0)]
 
 
 def incoming(got, partners, here, reverse):
@@ -329,9 +325,10 @@
     entering = None
     for level in range(len(partners) + 1)[::-1]:
         total = None
-        for source in range(count):
-            place = count - 1 - source if reverse else source
-            term = jnp.where((place >> level) == (here >> level) - 1, got[source], 0.0)
+        first = jnp.maximum((here >> level) - 1, 0) << level
+        for e in range(1 << level):
+            place = first + e
+            term = got[count - 1 - place if reverse else place]
             total = term if total is None else total + term
         if entering is not None:
             total = total + mapped(partners[level], entering)
@@ -481,13 +478,15 @@
     source = source.reshape(vec)
 
     def prepare(reverse, blocks, after=None):
-        *passed, step_maps, products, own = call(
+        return call(
             functools.partial(prep_kernel, reverse),
             [blocks] + ([start, (after, None)] if reverse else []),
             ([vec] if reverse else []) + [steps, maps, whole],
             [whole, (depth * species // 2, LANES), (depth * species, LANES)],
             1.0,
         )
+
+    def partner_maps(reverse, own, after):
         partners, kept = [], None
         for level in range(levels - 1):
             if level == 0:
@@ -500,16 +499,18 @@
                 full = level + 3 < levels
                 outs = call(
                     functools.partial(join_kernel, level, reverse, full, pairs),
-                    [own] + got,
+                    [own, (after, None)] + got,
                     [whole, half] if full else [half],
                     [(depth * species, LANES)],
                     0.4,
                 )
                 own, kept = outs[0], outs[-1]
-        return [step_maps, products, *partners], passed
-
-    lower, _ = prepare(False, x_lower)
-    upper, (start,) = prepare(True, x_upper, lower[1])
+        return partners
+
+    step_maps, products, own = prepare(False, x_lower)
+    start, upper_steps, upper_products, upper_own = prepare(True, x_upper, products)
+    lower = [step_maps, products, *partner_maps(False, own, start)]
+    upper = [upper_steps, upper_products, *partner_maps(True, upper_own, start)]
     paired, other = swaps(start)
     ahead = lax.ppermute(start[:1], "gx", [(i, (i - 1) % count) for i in range(count)])
 

time: 41.4 us -> 41.6 us (level)
  starting transfers between devices: 14.6 us -> 15.7 us
  waiting for transfers between devices: 5.91 us -> 5.03 us
    ppermute x8, starting transfers between devices: 10.8 us -> 11.7 us  [crossed(): lax.ppermute(block, axis, [(i, i ^ distance) for i in range(lax.axis_size...]
    ppermute x8, waiting for transfers between devices: 1.57 us -> 0.66 us  [crossed(): lax.ppermute(block, axis, [(i, i ^ distance) for i in range(lax.axis_size...]
where the time goes in v10:
time: 41.6 us; the launch traced here: 41.4 us
  starting transfers between devices  15.7 us (38%)
  Pallas kernels  11.7 us (28%)
  blocking collectives  7.21 us (17%)
  waiting for transfers between devices  5.03 us (12%)
  local copies, waits for them, and re-layouts  0.97 us (2%)
  between operations  0.77 us (2%)
    pallas_call x12, Pallas kernels, call(): pl.pallas_call(kernel, out_shape=outs, in_specs=[pl.BlockSpec(memory_spac...  11.7 us
    ppermute x8, starting transfers between devices, crossed(): lax.ppermute(block, axis, [(i, i ^ distance) for i in range(lax.axis_size...  11.7 us
    all_to_all x1, blocking collectives, exchange(): return lax.all_to_all(slots, axis, 0, 0)  7.21 us
    all_to_all x1, waiting for transfers between devices, exchange(): return lax.all_to_all(slots, axis, 0, 0)  4.36 us
    all_to_all x1, starting transfers between devices, exchange(): return lax.all_to_all(slots, axis, 0, 0)  3.34 us
    unnamed x12, local copies, waits for them, and re-layouts  0.97 us
  transfers between devices with their start and end apart: 12, of which 3 were waited for; matrix products, arithmetic and copies ran while one was open for 0% of the time, Pallas kernels for 19%

profile of v10, /device:TPU:0, one launch (start us, length us, event | category | flops | bytes accessed | tf_op | source)
XLA Modules:
  0.0 41.4 jit_solution(2208103371499892080)
XLA Ops:
  0.6 0.9 %copy-done.1 = bf16[2,1,16,4096]{3,2,1,0:T(8,128)(2,1)S(1)} copy-done((bf16[2,1,16,4096]{3,2,1,0:T(8,128)(2,1)S(1)}, bf16[2,1,16,4096]{3,2,1,0:T(8,128)(2,1)}, u32[]{:S(2)}) %copy-start.1) | copy-done | bytes 262168
  1.6 1.3 %shard_map.77 = (f32[512,128]{1,0:T(8,128)S(1)}, f32[1024,128]{1,0:T(8,128)S(1)}, f32[512,128]{1,0:T(8,128)S(1)}) custom-call(bf16[2,1,16,4096]{3,2,1,0:T(8,128)(2,1)S(1)} %copy-done.1), custom_call_target="tpu_custom_call" | custom-call | flops 1150000000 | bytes 262144 | tf_op jit(solution)/shard_map/pallas_call | solution.py:431
  2.9 0.5 %collective-permute-start.3 = (f32[512,128]{1,0:T(8,128)S(1)}, f32[512,128]{1,0:T(8,128)S(1)}, u32[]{:S(2)}, u32[]{:S(2)}) collective-permute-start(f32[512,128]{1,0:T(8,128)S(1)} %get-tuple-element.31.own), channel_id=1, source_target_pairs={{0,4},{4,0},{8,12},{12,8},{16,20},{20,16},{24,28},{28,24},{1,5},{5... | collective-permute-start | bytes 786440 | tf_op jit(solution)/shard_map/ppermute | solution.py:458
  3.4 1.3 %shard_map.78 = (f32[2,8,128]{2,1,0:T(8,128)S(1)}, f32[512,128]{1,0:T(8,128)S(1)}, f32[1024,128]{1,0:T(8,128)S(1)}, f32[512,128]{1,0:T(8,128)S(1)}) custom-call(bf16[2,1,16,4096]{3,2,1,0:T(8,128)(2,1)S(1)} %copy-done.3, f32[2,8,128]{2,1,0:T(8,128)S(1)} %bitcast.4, f32[1024,128]{1,0:T(8,128)S(1)} %get-tuple-element.27.refs_1_), custom_call_target="tpu_custom_call" | custom-call | flops 1150000000 | bytes 794624 | tf_op jit(solution)/shard_map/pallas_call | solution.py:431
  4.7 0.0 copy-start
  4.7 0.0 collective-permute-done.3.refs_2_.refs_1_
  4.7 0.0 copy-start.2
  4.7 0.4 shard_map.81
  5.1 2.7 %collective-permute-start.4 = (f32[256,128]{1,0:T(8,128)S(1)}, f32[256,128]{1,0:T(8,128)S(1)}, u32[]{:S(2)}, u32[]{:S(2)}) collective-permute-start(f32[256,128]{1,0:T(8,128)S(1)} %shard_map.81), channel_id=1, source_target_pairs={{0,8},{4,12},{8,0},{12,4},{16,24},{20,28},{24,16},{28,20},{1,9},{5... | collective-permute-start | bytes 393224 | tf_op jit(solution)/shard_map/ppermute | solution.py:458
  7.9 0.0 collective-permute-start.1
  7.9 3.1 %collective-permute-start = (f32[2,8,128]{2,1,0:T(8,128)S(1)}, f32[2,8,128]{2,1,0:T(8,128)S(1)}, u32[]{:S(2)}, u32[]{:S(2)}) collective-permute-start(f32[2,8,128]{2,1,0:T(8,128)S(1)} %get-tuple-element.28.start.refs_0_), channel_id=1, source_target_pairs={{0,1},{1,0},{2,3},{3,2},{4,5},{5,4},{6,7},{7,6},{8,9},{9,8},{10,11... | collective-permute-start | bytes 24584 | tf_op jit(solution)/shard_map/ppermute | solution.py:458
  11.0 0.6 %collective-permute-start.2 = (f32[1,8,128]{2,1,0:T(8,128)S(1)}, f32[1,8,128]{2,1,0:T(8,128)S(1)}, u32[]{:S(2)}, u32[]{:S(2)}) collective-permute-start(f32[1,8,128]{2,1,0:T(8,128)S(1)} %slice.3), channel_id=1, source_target_pairs={{0,28},{4,0},{8,4},{12,8},{16,12},{20,16},{24,20},{28,24},{1,29},{... | collective-permute-start | bytes 12296 | tf_op jit(solution)/shard_map/ppermute | solution.py:515
  11.6 0.0 collective-permute-start.6
  11.6 0.2 collective-permute-done.4.mine
  11.8 0.3 collective-permute-start.5
  12.1 1.4 %shard_map.79 = (f32[2,8,128]{2,1,0:T(8,128)S(1)}, f32[2,8,128]{2,1,0:T(8,128)S(1)}) custom-call(f32[2,8,128]{2,1,0:T(8,128)S(1)} %get-tuple-element.28.start.refs_0_, f32[2,8,128]{2,1,0:T(8,128)S(1)} %bitcast.5, bf16[2,1,16,4096]{3,2,1,0:T(8,128)(2,1)S(1)} %copy-done.2, bf16[2,1,16,4096]{3,2,1,0:T(8,128)(2,1)S(1)} %copy-done.3, ...), custom_call_target="tpu_custom_call" | custom-call | flops 5750000128 | bytes 1589248 | tf_op jit(solution)/shard_map/pallas_call | solution.py:431
  13.5 0.0 collective-permute-done.6.refs_1_.partner
  13.5 0.4 shard_map.85
  13.9 1.5 %collective-permute-start.7 = (f32[256,128]{1,0:T(8,128)S(1)}, f32[256,128]{1,0:T(8,128)S(1)}, u32[]{:S(2)}, u32[]{:S(2)}) collective-permute-start(f32[256,128]{1,0:T(8,128)S(1)} %shard_map.85), channel_id=1, source_target_pairs={{0,8},{4,12},{8,0},{12,4},{16,24},{20,28},{24,16},{28,20},{1,9},{5... | collective-permute-start | bytes 393224 | tf_op jit(solution)/shard_map/ppermute | solution.py:458
  15.4 0.4 shard_map.80
  15.8 0.2 shard_map.82.rest_1_
  16.0 1.8 %shard_map.83 = (f32[2,8,128]{2,1,0:T(8,128)S(1)}, f32[2,8,128]{2,1,0:T(8,128)S(1)}, f32[8,8,128]{2,1,0:T(8,128)}) custom-call(f32[2,8,128]{2,1,0:T(8,128)S(1)} %get-tuple-element.29.base, f32[2,8,128]{2,1,0:T(8,128)S(1)} %collective-permute-done.paired, f32[2,8,128]{2,1,0:T(8,128)S(1)} %collective-permute-done.1.other, ...), custom_call_target="tpu_custom_call" | custom-call | flops 1724999936 | bytes 2125824 | tf_op jit(solution)/shard_map/pallas_call | solution.py:431
  17.8 3.3 %all-to-all-start = ((f32[8,8,128]{2,1,0:T(8,128)}), f32[8,8,128]{2,1,0:T(8,128)S(1)}, u32[]{:S(2)}, u32[]{:S(2)}) async-start(f32[8,8,128]{2,1,0:T(8,128)} %get-tuple-element.34), calls=%async_computation | async-start | bytes 65536 | tf_op jit(solution)/shard_map/all_to_all | solution.py:462
  21.1 0.4 collective-permute-start.8
  21.5 4.4 %all-to-all-done.got = f32[8,8,128]{2,1,0:T(8,128)S(1)} async-done(((f32[8,8,128]{2,1,0:T(8,128)}), f32[8,8,128]{2,1,0:T(8,128)S(1)}, u32[]{:S(2)}, u32[]{:S(2)}) %all-to-all-start) | async-done | bytes 32800 | tf_op jit(solution)/shard_map/all_to_all | solution.py:462
  25.9 1.1 %shard_map.84 = (f32[2,8,128]{2,1,0:T(8,128)}, f32[2,8,128]{2,1,0:T(8,128)S(1)}, f32[2,8,128]{2,1,0:T(8,128)S(1)}) custom-call(f32[8,8,128]{2,1,0:T(8,128)S(1)} %all-to-all-done.got, f32[2,8,128]{2,1,0:T(8,128)S(1)} %get-tuple-element.35.drive, f32[2,8,128]{2,1,0:T(8,128)S(1)} %get-tuple-element.36.offsets, f32[2,8,128]{2,1,0:T(8,128)S(1)} %get-tuple-element.37.rhs, ...), custom_call_target="tpu_custom_call" | custom-call | flops 1150000000 | bytes 1105920 | tf_op jit(solution)/shard_map/pallas_call | solution.py:431
  27.1 3.2 %collective-permute-start.9 = (f32[2,8,128]{2,1,0:T(8,128)S(1)}, f32[2,8,128]{2,1,0:T(8,128)S(1)}, u32[]{:S(2)}, u32[]{:S(2)}) collective-permute-start(f32[2,8,128]{2,1,0:T(8,128)S(1)} %get-tuple-element.41.vectors), channel_id=1, source_target_pairs={{0,1},{1,0},{2,3},{3,2},{4,5},{5,4},{6,7},{7,6},{8,9},{9,8},{10,11... | collective-permute-start | bytes 24584 | tf_op jit(solution)/shard_map/ppermute | solution.py:458
  30.2 1.2 %shard_map.86 = (f32[2,8,128]{2,1,0:T(8,128)S(1)}, f32[512,128]{1,0:T(8,128)S(1)}, f32[1024,128]{1,0:T(8,128)S(1)}, f32[512,128]{1,0:T(8,128)S(1)}, f32[512,128]{1,0:T(8,128)S(1)}) custom-call(f32[2,8,128]{2,1,0:T(8,128)S(1)} %get-tuple-element.40.base, f32[2,8,128]{2,1,0:T(8,128)S(1)} %get-tuple-element.41.vectors, ...), custom_call_target="tpu_custom_call" | custom-call | flops 805000000 | bytes 2375680 | tf_op jit(solution)/shard_map/pallas_call | solution.py:431
  31.4 0.4 collective-permute-done.9.paired
  31.8 1.2 %shard_map.87 = (f32[2,8,128]{2,1,0:T(8,128)S(1)}, f32[8,8,128]{2,1,0:T(8,128)S(1)}) custom-call(f32[2,8,128]{2,1,0:T(8,128)S(1)} %get-tuple-element.45.base, f32[2,8,128]{2,1,0:T(8,128)S(1)} %collective-permute-done.9.paired, f32[2,8,128]{2,1,0:T(8,128)S(1)} %collective-permute-done.10.other, bf16[4,2,1,16,4096]{4,3,2,1,0:T(8,128)(2,1)S(1)} %copy-done, ...), custom_call_target="tpu_custom_call" | custom-call | flops 1724999936 | bytes 1859584 | tf_op jit(solution)/shard_map/pallas_call | solution.py:431
  33.0 7.2 %all_to_all.10.got = f32[8,8,128]{2,1,0:T(8,128)S(1)} all-to-all(f32[8,8,128]{2,1,0:T(8,128)S(1)} %get-tuple-element.49), channel_id=1, replica_groups=mesh['gx'=8,'gy'=4] {'gx'}, dimensions={0} | all-to-all | bytes 65536 | tf_op jit(solution)/shard_map/all_to_all | solution.py:462
  40.2 1.2 %shard_map.88 = f32[2,8,128]{2,1,0:T(8,128)} custom-call(f32[8,8,128]{2,1,0:T(8,128)S(1)} %all_to_all.10.got, f32[2,8,128]{2,1,0:T(8,128)S(1)} %get-tuple-element.50.offsets, f32[1024,128]{1,0:T(8,128)S(1)} %get-tuple-element.51.entry_maps, f32[512,128]{1,0:T(8,128)S(1)} %get-tuple-element.47.rest_0_, f32[512,128]{1,0:T(8,128)S(1)} %get-tuple-element.48.rest_1_), custom_call_target="tpu_custom_call" | custom-call | flops 1150000000 | bytes 1089536 | tf_op jit(solution)/shard_map/pallas_call | solution.py:431
  (18 shorter events, 0.0 us)
Async XLA Ops:
  0.6 1.0 %copy-start.1 = (bf16[2,1,16,4096]{3,2,1,0:T(8,128)(2,1)S(1)}, bf16[2,1,16,4096]{3,2,1,0:T(8,128)(2,1)}, u32[]{:S(2)}) copy-start(bf16[2,1,16,4096]{3,2,1,0:T(8,128)(2,1)} %blocks.2) | copy-start | bytes 786436
  1.6 1.8 %copy-start.3 = (bf16[2,1,16,4096]{3,2,1,0:T(8,128)(2,1)S(1)}, bf16[2,1,16,4096]{3,2,1,0:T(8,128)(2,1)}, u32[]{:S(2)}) copy-start(bf16[2,1,16,4096]{3,2,1,0:T(8,128)(2,1)} %upper.3) | copy-start | bytes 786436
  1.6 1.8 %copy-start.4 = (f32[2,1,1024]{2,1,0:T(1,128)S(1)}, f32[2,1,1024]{2,1,0:T(1,128)}, u32[]{:S(2)}) copy-start(f32[2,1,1024]{2,1,0:T(1,128)} %param.6) | copy-start | bytes 24580
  2.9 1.8 %collective-permute-start.3 = (f32[512,128]{1,0:T(8,128)S(1)}, f32[512,128]{1,0:T(8,128)S(1)}, u32[]{:S(2)}, u32[]{:S(2)}) collective-permute-start(f32[512,128]{1,0:T(8,128)S(1)} %get-tuple-element.31.own), channel_id=1, source_target_pairs={{0,4},{4,0},{8,12},{12,8},{16,20},{20,16},{24,28},{28,24},{1,5},{5... | collective-permute-start | bytes 786440 | tf_op jit(solution)/shard_map/ppermute | solution.py:458
  4.7 7.4 %copy-start = (bf16[4,2,1,16,4096]{4,3,2,1,0:T(8,128)(2,1)S(1)}, bf16[4,2,1,16,4096]{4,3,2,1,0:T(8,128)(2,1)}, u32[]{:S(2)}) copy-start(bf16[4,2,1,16,4096]{4,3,2,1,0:T(8,128)(2,1)} %side.7) | copy-start | bytes 3145732
  4.7 7.4 %copy-start.2 = (bf16[2,1,16,4096]{3,2,1,0:T(8,128)(2,1)S(1)}, bf16[2,1,16,4096]{3,2,1,0:T(8,128)(2,1)}, u32[]{:S(2)}) copy-start(bf16[2,1,16,4096]{3,2,1,0:T(8,128)(2,1)} %diag.1) | copy-start | bytes 786436
  5.1 7.0 %copy-start.5 = (f32[2,1,1024]{2,1,0:T(1,128)S(1)}, f32[2,1,1024]{2,1,0:T(1,128)}, u32[]{:S(2)}) copy-start(f32[2,1,1024]{2,1,0:T(1,128)} %param.7) | copy-start | bytes 24580
  5.1 6.7 %collective-permute-start.4 = (f32[256,128]{1,0:T(8,128)S(1)}, f32[256,128]{1,0:T(8,128)S(1)}, u32[]{:S(2)}, u32[]{:S(2)}) collective-permute-start(f32[256,128]{1,0:T(8,128)S(1)} %shard_map.81), channel_id=1, source_target_pairs={{0,8},{4,12},{8,0},{12,4},{16,24},{20,28},{24,16},{28,20},{1,9},{5... | collective-permute-start | bytes 393224 | tf_op jit(solution)/shard_map/ppermute | solution.py:458
  7.9 8.1 %collective-permute-start.1 = (f32[2,8,128]{2,1,0:T(8,128)S(1)}, f32[2,8,128]{2,1,0:T(8,128)S(1)}, u32[]{:S(2)}, u32[]{:S(2)}) collective-permute-start(f32[2,8,128]{2,1,0:T(8,128)S(1)} %get-tuple-element.28.start.refs_0_), channel_id=1, source_target_pairs={{0,4},{1,2},{2,1},{3,7},{4,0},{5,6},{6,5},{7,3},{8,12},{9,10},{10,... | collective-permute-start | bytes 24584 | tf_op jit(solution)/shard_map/ppermute | solution.py:454
  7.9 8.1 %collective-permute-start = (f32[2,8,128]{2,1,0:T(8,128)S(1)}, f32[2,8,128]{2,1,0:T(8,128)S(1)}, u32[]{:S(2)}, u32[]{:S(2)}) collective-permute-start(f32[2,8,128]{2,1,0:T(8,128)S(1)} %get-tuple-element.28.start.refs_0_), channel_id=1, source_target_pairs={{0,1},{1,0},{2,3},{3,2},{4,5},{5,4},{6,7},{7,6},{8,9},{9,8},{10,11... | collective-permute-start | bytes 24584 | tf_op jit(solution)/shard_map/ppermute | solution.py:458
  11.0 4.9 %collective-permute-start.2 = (f32[1,8,128]{2,1,0:T(8,128)S(1)}, f32[1,8,128]{2,1,0:T(8,128)S(1)}, u32[]{:S(2)}, u32[]{:S(2)}) collective-permute-start(f32[1,8,128]{2,1,0:T(8,128)S(1)} %slice.3), channel_id=1, source_target_pairs={{0,28},{4,0},{8,4},{12,8},{16,12},{20,16},{24,20},{28,24},{1,29},{... | collective-permute-start | bytes 12296 | tf_op jit(solution)/shard_map/ppermute | solution.py:515
  11.6 1.9 %collective-permute-start.6 = (f32[512,128]{1,0:T(8,128)S(1)}, f32[512,128]{1,0:T(8,128)S(1)}, u32[]{:S(2)}, u32[]{:S(2)}) collective-permute-start(f32[512,128]{1,0:T(8,128)S(1)} %get-tuple-element.44.own), channel_id=1, source_target_pairs={{0,4},{4,0},{8,12},{12,8},{16,20},{20,16},{24,28},{28,24},{1,5},{5... | collective-permute-start | bytes 786440 | tf_op jit(solution)/shard_map/ppermute | solution.py:458
  11.8 3.9 %collective-permute-start.5 = (f32[256,128]{1,0:T(8,128)S(1)}, f32[256,128]{1,0:T(8,128)S(1)}, u32[]{:S(2)}, u32[]{:S(2)}) collective-permute-start(f32[256,128]{1,0:T(8,128)S(1)} %collective-permute-done.4.mine), channel_id=1, source_target_pairs={{0,4},{4,0},{8,12},{12,8},{16,20},{20,16},{24,28},{28,24},{1,5},{5... | collective-permute-start | bytes 393224 | tf_op jit(solution)/shard_map/ppermute | solution.py:458
  13.9 7.3 %collective-permute-start.7 = (f32[256,128]{1,0:T(8,128)S(1)}, f32[256,128]{1,0:T(8,128)S(1)}, u32[]{:S(2)}, u32[]{:S(2)}) collective-permute-start(f32[256,128]{1,0:T(8,128)S(1)} %shard_map.85), channel_id=1, source_target_pairs={{0,8},{4,12},{8,0},{12,4},{16,24},{20,28},{24,16},{28,20},{1,9},{5... | collective-permute-start | bytes 393224 | tf_op jit(solution)/shard_map/ppermute | solution.py:458
  17.8 8.1 %all-to-all-start = ((f32[8,8,128]{2,1,0:T(8,128)}), f32[8,8,128]{2,1,0:T(8,128)S(1)}, u32[]{:S(2)}, u32[]{:S(2)}) async-start(f32[8,8,128]{2,1,0:T(8,128)} %get-tuple-element.34), calls=%async_computation | async-start | bytes 65536 | tf_op jit(solution)/shard_map/all_to_all | solution.py:462
  21.1 9.1 %collective-permute-start.8 = (f32[256,128]{1,0:T(8,128)S(1)}, f32[256,128]{1,0:T(8,128)S(1)}, u32[]{:S(2)}, u32[]{:S(2)}) collective-permute-start(f32[256,128]{1,0:T(8,128)S(1)} %collective-permute-done.7.rest_0_), channel_id=1, source_target_pairs={{0,4},{4,0},{8,12},{12,8},{16,20},{20,16},{24,28},{28,24},{1,5},{5... | collective-permute-start | bytes 393224 | tf_op jit(solution)/shard_map/ppermute | solution.py:458
  27.1 4.4 %collective-permute-start.10 = (f32[2,8,128]{2,1,0:T(8,128)S(1)}, f32[2,8,128]{2,1,0:T(8,128)S(1)}, u32[]{:S(2)}, u32[]{:S(2)}) collective-permute-start(f32[2,8,128]{2,1,0:T(8,128)S(1)} %get-tuple-element.41.vectors), channel_id=1, source_target_pairs={{0,4},{1,2},{2,1},{3,7},{4,0},{5,6},{6,5},{7,3},{8,12},{9,10},{10,... | collective-permute-start | bytes 24584 | tf_op jit(solution)/shard_map/ppermute | solution.py:454
  27.1 4.8 %collective-permute-start.9 = (f32[2,8,128]{2,1,0:T(8,128)S(1)}, f32[2,8,128]{2,1,0:T(8,128)S(1)}, u32[]{:S(2)}, u32[]{:S(2)}) collective-permute-start(f32[2,8,128]{2,1,0:T(8,128)S(1)} %get-tuple-element.41.vectors), channel_id=1, source_target_pairs={{0,1},{1,0},{2,3},{3,2},{4,5},{5,4},{6,7},{7,6},{8,9},{9,8},{10,11... | collective-permute-start | bytes 24584 | tf_op jit(solution)/shard_map/ppermute | solution.py:458

commit v11 on v10

--- a/solution.py
+++ b/solution.py
@@ -253,7 +253,7 @@
     core = lax.axis_index("gx") & 1
     species = LANES // 2
     _, *refs, scratch = refs
-    outs = refs[-2:] if full else refs[-1:]
+    outs = refs[-2:] if full and not reverse else refs[-1:]
     partner = refs[: len(refs) - len(outs)]
     later_is_own = here == (0 if reverse else 1)
     for pair in range(pairs):
@@ -271,6 +271,8 @@
         if full:
             kept = multiply(scratch, pair, earlier, later, False)
             outs[0][pl.ds(pair, species, stride=pairs), :] = kept
+            if reverse:
+                continue
             kept = jnp.where(core == 0, kept[: species // 2], kept[species // 2 :])
         else:
             kept = jnp.where(core == 0, earlier[: species // 2], earlier[species // 2 :])
@@ -379,9 +381,9 @@
         copy[p] = value
 
 
-def side_kernel(levels, base, vectors, side, steps, products, partner, *rest):
-    parts = rest[: 2 * (levels - 2)]
-    out, step_maps, entry_maps, near, *far, scratch = rest[2 * (levels - 2) :]
+def side_kernel(base, vectors, side, *rest):
+    *rest, scratch = rest
+    sources, (out, *converted) = rest[: len(rest) // 2], rest[len(rest) // 2 :]
     planes, pairs = base.shape[:2]
     for p in range(planes):
         vector = spread(vectors[p])
@@ -392,9 +394,7 @@
             ]
         )
         out[p] = base[p] - gather_pairs(around)
-    convert(pairs, (steps, products, partner), (step_maps, entry_maps, near), scratch.at[0])
-    for level, ref in enumerate(far):
-        diagonals(part_tiles(*parts[2 * level : 2 * level + 2], pairs), ref, 0, scratch.at[1], pairs)
+    convert(pairs, sources, converted, scratch)
 
 
 def backward_offset_kernel(base, paired, other, side, step_maps, *rest):
@@ -489,18 +489,18 @@
     def partner_maps(reverse, own, after):
         partners, kept = [], None
         for level in range(levels - 1):
-            if level == 0:
-                got = [crossed(own, "gx", 1)]
+            if level == 0 or reverse:
+                got = [crossed(own, "gx", 1 << level)]
             else:
                 mine = crossed(kept, "gx", 1 << level)
                 got = [mine, crossed(mine, "gx", 1)]
             partners += got
             if level + 2 < levels:
-                full = level + 3 < levels
+                full = reverse or level + 3 < levels
                 outs = call(
                     functools.partial(join_kernel, level, reverse, full, pairs),
                     [own, (after, None)] + got,
-                    [whole, half] if full else [half],
+                    [whole] if reverse else [whole, half] if full else [half],
                     [(depth * species, LANES)],
                     0.4,
                 )
@@ -509,14 +509,14 @@
 
     step_maps, products, own = prepare(False, x_lower)
     start, upper_steps, upper_products, upper_own = prepare(True, x_upper, products)
+    rhs, base = call(
+        base_kernel, [start, source, diag_inverse, x_upper, side_blocks], [vec, vec], [], 5.0
+    )
     lower = [step_maps, products, *partner_maps(False, own, start)]
     upper = [upper_steps, upper_products, *partner_maps(True, upper_own, start)]
     paired, other = swaps(start)
     ahead = lax.ppermute(start[:1], "gx", [(i, (i - 1) % count) for i in range(count)])
 
-    rhs, base = call(
-        base_kernel, [start, source, diag_inverse, x_upper, side_blocks], [vec, vec], [], 5.0
-    )
     step_maps, entry_maps, near = call(
         functools.partial(near_kernel, pairs), lower[:3], [steps, maps, whole], [whole], 0.5
     )
@@ -545,10 +545,10 @@
     )
     paired, other = swaps(copy)
     base, step_maps, entry_maps, *partners = call(
-        functools.partial(side_kernel, levels),
+        side_kernel,
         [base, copy, side_blocks] + upper,
-        [vec, steps, maps, whole] + [whole] * (levels - 2),
-        [(2,) + whole],
+        [vec, steps, maps] + [whole] * (levels - 1),
+        [whole],
         0.7,
     )
     offsets, sent = call(

time: 41.6 us -> 40.4 us (0.971)
  blocking collectives: 7.21 us -> 14.6 us
  waiting for transfers between devices: 5.03 us -> 0.66 us
  starting transfers between devices: 15.7 us -> 12 us
  Pallas kernels: 11.7 us -> 11.2 us
    all_to_all x1 -> x2, blocking collectives: 7.21 us -> 14.6 us  [exchange(): return lax.all_to_all(slots, axis, 0, 0)]
    all_to_all x1 -> x0, waiting for transfers between devices: 4.36 us -> none  [exchange(): return lax.all_to_all(slots, axis, 0, 0)]
    all_to_all x1 -> x0, starting transfers between devices: 3.34 us -> none  [exchange(): return lax.all_to_all(slots, axis, 0, 0)]
    pallas_call x12, Pallas kernels: 11.7 us -> 11.2 us  [call(): pl.pallas_call(kernel, out_shape=outs, in_specs=[pl.BlockSpec(memory_spac...]
    ppermute x8 -> x7, starting transfers between devices: 11.7 us -> 11.3 us  [crossed(): lax.ppermute(block, axis, [(i, i ^ distance) for i in range(lax.axis_size...]
  transfers between devices with their start and end apart: 12 -> 10, of which waited for: 3 -> 2; matrix products, arithmetic and copies ran while one was open for 0% -> 0% of each run, Pallas kernels for 19% -> 18%
where the time goes in v11:
time: 40.4 us; the launch traced here: 40.2 us
  blocking collectives  14.6 us (36%)
  starting transfers between devices  12 us (30%)
  Pallas kernels  11.2 us (28%)
  local copies, waits for them, and re-layouts  0.97 us (2%)
  between operations  0.76 us (2%)
  waiting for transfers between devices  0.66 us (2%)
    all_to_all x2, blocking collectives, exchange(): return lax.all_to_all(slots, axis, 0, 0)  14.6 us
    ppermute x7, starting transfers between devices, crossed(): lax.ppermute(block, axis, [(i, i ^ distance) for i in range(lax.axis_size...  11.3 us
    pallas_call x12, Pallas kernels, call(): pl.pallas_call(kernel, out_shape=outs, in_specs=[pl.BlockSpec(memory_spac...  11.2 us
    unnamed x12, local copies, waits for them, and re-layouts  0.97 us
  transfers between devices with their start and end apart: 10, of which 2 were waited for; matrix products, arithmetic and copies ran while one was open for 0% of the time, Pallas kernels for 18%

profile of v11, /device:TPU:0, one launch (start us, length us, event | category | flops | bytes accessed | tf_op | source)
XLA Modules:
  0.0 40.2 jit_solution(14370055071121676921)
XLA Ops:
  0.6 0.9 %copy-done.1 = bf16[2,1,16,4096]{3,2,1,0:T(8,128)(2,1)S(1)} copy-done((bf16[2,1,16,4096]{3,2,1,0:T(8,128)(2,1)S(1)}, bf16[2,1,16,4096]{3,2,1,0:T(8,128)(2,1)}, u32[]{:S(2)}) %copy-start.1) | copy-done | bytes 262168
  1.6 1.3 %shard_map.77 = (f32[512,128]{1,0:T(8,128)S(1)}, f32[1024,128]{1,0:T(8,128)S(1)}, f32[512,128]{1,0:T(8,128)S(1)}) custom-call(bf16[2,1,16,4096]{3,2,1,0:T(8,128)(2,1)S(1)} %copy-done.1), custom_call_target="tpu_custom_call" | custom-call | flops 1150000000 | bytes 262144 | tf_op jit(solution)/shard_map/pallas_call | solution.py:431
  2.9 0.5 %collective-permute-start.3 = (f32[512,128]{1,0:T(8,128)S(1)}, f32[512,128]{1,0:T(8,128)S(1)}, u32[]{:S(2)}, u32[]{:S(2)}) collective-permute-start(f32[512,128]{1,0:T(8,128)S(1)} %get-tuple-element.31.own), channel_id=1, source_target_pairs={{0,4},{4,0},{8,12},{12,8},{16,20},{20,16},{24,28},{28,24},{1,5},{5... | collective-permute-start | bytes 786440 | tf_op jit(solution)/shard_map/ppermute | solution.py:458
  3.4 1.3 %shard_map.78 = (f32[2,8,128]{2,1,0:T(8,128)S(1)}, f32[512,128]{1,0:T(8,128)S(1)}, f32[1024,128]{1,0:T(8,128)S(1)}, f32[512,128]{1,0:T(8,128)S(1)}) custom-call(bf16[2,1,16,4096]{3,2,1,0:T(8,128)(2,1)S(1)} %copy-done.3, f32[2,8,128]{2,1,0:T(8,128)S(1)} %bitcast.4, f32[1024,128]{1,0:T(8,128)S(1)} %get-tuple-element.27.refs_1_), custom_call_target="tpu_custom_call" | custom-call | flops 1150000000 | bytes 794624 | tf_op jit(solution)/shard_map/pallas_call | solution.py:431
  4.7 0.0 copy-start
  4.7 0.0 collective-permute-done.3.refs_2_.refs_1_
  4.7 0.0 copy-start.2
  4.7 0.4 shard_map.81
  5.1 2.7 %collective-permute-start.4 = (f32[256,128]{1,0:T(8,128)S(1)}, f32[256,128]{1,0:T(8,128)S(1)}, u32[]{:S(2)}, u32[]{:S(2)}) collective-permute-start(f32[256,128]{1,0:T(8,128)S(1)} %shard_map.81), channel_id=1, source_target_pairs={{0,8},{4,12},{8,0},{12,4},{16,24},{20,28},{24,16},{28,20},{1,9},{5... | collective-permute-start | bytes 393224 | tf_op jit(solution)/shard_map/ppermute | solution.py:458
  7.9 0.0 collective-permute-start.1
  7.9 3.1 %collective-permute-start = (f32[2,8,128]{2,1,0:T(8,128)S(1)}, f32[2,8,128]{2,1,0:T(8,128)S(1)}, u32[]{:S(2)}, u32[]{:S(2)}) collective-permute-start(f32[2,8,128]{2,1,0:T(8,128)S(1)} %get-tuple-element.28.start.refs_0_), channel_id=1, source_target_pairs={{0,1},{1,0},{2,3},{3,2},{4,5},{5,4},{6,7},{7,6},{8,9},{9,8},{10,11... | collective-permute-start | bytes 24584 | tf_op jit(solution)/shard_map/ppermute | solution.py:458
  11.0 0.6 %collective-permute-start.2 = (f32[1,8,128]{2,1,0:T(8,128)S(1)}, f32[1,8,128]{2,1,0:T(8,128)S(1)}, u32[]{:S(2)}, u32[]{:S(2)}) collective-permute-start(f32[1,8,128]{2,1,0:T(8,128)S(1)} %slice.3), channel_id=1, source_target_pairs={{0,28},{4,0},{8,4},{12,8},{16,12},{20,16},{24,20},{28,24},{1,29},{... | collective-permute-start | bytes 12296 | tf_op jit(solution)/shard_map/ppermute | solution.py:518
  11.6 0.0 collective-permute-start.6
  11.6 0.2 collective-permute-done.4.mine
  11.8 0.3 collective-permute-start.5
  12.1 1.4 %shard_map.79 = (f32[2,8,128]{2,1,0:T(8,128)S(1)}, f32[2,8,128]{2,1,0:T(8,128)S(1)}) custom-call(f32[2,8,128]{2,1,0:T(8,128)S(1)} %get-tuple-element.28.start.refs_0_, f32[2,8,128]{2,1,0:T(8,128)S(1)} %bitcast.5, bf16[2,1,16,4096]{3,2,1,0:T(8,128)(2,1)S(1)} %copy-done.2, bf16[2,1,16,4096]{3,2,1,0:T(8,128)(2,1)S(1)} %copy-done.3, ...), custom_call_target="tpu_custom_call" | custom-call | flops 5750000128 | bytes 1589248 | tf_op jit(solution)/shard_map/pallas_call | solution.py:431
  13.5 0.0 collective-permute-done.6.refs_1_.rest_2_
  13.5 0.4 %shard_map.85 = f32[512,128]{1,0:T(8,128)S(1)} custom-call(f32[512,128]{1,0:T(8,128)S(1)} %get-tuple-element.44.own, f32[2,8,128]{2,1,0:T(8,128)S(1)} %get-tuple-element.28.start.refs_0_, f32[512,128]{1,0:T(8,128)S(1)} %collective-permute-done.6.refs_1_.rest_2_), custom_call_target="tpu_custom_call" | custom-call | flops 460000000 | bytes 532480 | tf_op jit(solution)/shard_map/pallas_call | solution.py:431
  13.9 1.6 %collective-permute-start.7 = (f32[512,128]{1,0:T(8,128)S(1)}, f32[512,128]{1,0:T(8,128)S(1)}, u32[]{:S(2)}, u32[]{:S(2)}) collective-permute-start(f32[512,128]{1,0:T(8,128)S(1)} %shard_map.85), channel_id=1, source_target_pairs={{0,8},{4,12},{8,0},{12,4},{16,24},{20,28},{24,16},{28,20},{1,9},{5... | collective-permute-start | bytes 786440 | tf_op jit(solution)/shard_map/ppermute | solution.py:458
  15.5 0.4 shard_map.80
  15.9 0.2 shard_map.82.rest_1_
  16.0 0.0 collective-permute-done.2.ahead
  16.0 0.0 collective-permute-done.1.other
  16.1 1.2 %shard_map.83 = (f32[2,8,128]{2,1,0:T(8,128)S(1)}, f32[2,8,128]{2,1,0:T(8,128)S(1)}, f32[8,8,128]{2,1,0:T(8,128)S(1)}) custom-call(f32[2,8,128]{2,1,0:T(8,128)S(1)} %get-tuple-element.29.base, f32[2,8,128]{2,1,0:T(8,128)S(1)} %collective-permute-done.paired, f32[2,8,128]{2,1,0:T(8,128)S(1)} %collective-permute-done.1.other, ...), custom_call_target="tpu_custom_call" | custom-call | flops 1724999936 | bytes 2125824 | tf_op jit(solution)/shard_map/pallas_call | solution.py:431
  17.3 7.4 %all_to_all.10.got = f32[8,8,128]{2,1,0:T(8,128)S(1)} all-to-all(f32[8,8,128]{2,1,0:T(8,128)S(1)} %get-tuple-element.34), channel_id=1, replica_groups=mesh['gx'=8,'gy'=4] {'gx'}, dimensions={0} | all-to-all | bytes 65536 | tf_op jit(solution)/shard_map/all_to_all | solution.py:462
  24.7 1.1 %shard_map.84 = (f32[2,8,128]{2,1,0:T(8,128)}, f32[2,8,128]{2,1,0:T(8,128)S(1)}, f32[2,8,128]{2,1,0:T(8,128)S(1)}) custom-call(f32[8,8,128]{2,1,0:T(8,128)S(1)} %all_to_all.10.got, f32[2,8,128]{2,1,0:T(8,128)S(1)} %get-tuple-element.35.drive, f32[2,8,128]{2,1,0:T(8,128)S(1)} %get-tuple-element.36.offsets, f32[2,8,128]{2,1,0:T(8,128)S(1)} %get-tuple-element.37.rhs, ...), custom_call_target="tpu_custom_call" | custom-call | flops 1150000000 | bytes 1105920 | tf_op jit(solution)/shard_map/pallas_call | solution.py:431
  25.8 3.2 %collective-permute-start.8 = (f32[2,8,128]{2,1,0:T(8,128)S(1)}, f32[2,8,128]{2,1,0:T(8,128)S(1)}, u32[]{:S(2)}, u32[]{:S(2)}) collective-permute-start(f32[2,8,128]{2,1,0:T(8,128)S(1)} %get-tuple-element.41.vectors), channel_id=1, source_target_pairs={{0,1},{1,0},{2,3},{3,2},{4,5},{5,4},{6,7},{7,6},{8,9},{9,8},{10,11... | collective-permute-start | bytes 24584 | tf_op jit(solution)/shard_map/ppermute | solution.py:458
  29.0 1.2 %shard_map.86 = (f32[2,8,128]{2,1,0:T(8,128)S(1)}, f32[512,128]{1,0:T(8,128)S(1)}, f32[1024,128]{1,0:T(8,128)S(1)}, f32[512,128]{1,0:T(8,128)S(1)}, f32[512,128]{1,0:T(8,128)S(1)}) custom-call(f32[2,8,128]{2,1,0:T(8,128)S(1)} %get-tuple-element.40.base, f32[2,8,128]{2,1,0:T(8,128)S(1)} %get-tuple-element.41.vectors, ...), custom_call_target="tpu_custom_call" | custom-call | flops 805000000 | bytes 2375680 | tf_op jit(solution)/shard_map/pallas_call | solution.py:431
  30.2 0.4 collective-permute-done.8.paired
  30.6 1.2 %shard_map.87 = (f32[2,8,128]{2,1,0:T(8,128)S(1)}, f32[8,8,128]{2,1,0:T(8,128)S(1)}) custom-call(f32[2,8,128]{2,1,0:T(8,128)S(1)} %get-tuple-element.45.base, f32[2,8,128]{2,1,0:T(8,128)S(1)} %collective-permute-done.8.paired, f32[2,8,128]{2,1,0:T(8,128)S(1)} %collective-permute-done.9.other, bf16[4,2,1,16,4096]{4,3,2,1,0:T(8,128)(2,1)S(1)} %copy-done, ...), custom_call_target="tpu_custom_call" | custom-call | flops 1724999936 | bytes 1859584 | tf_op jit(solution)/shard_map/pallas_call | solution.py:431
  31.8 7.2 %all_to_all.11.got = f32[8,8,128]{2,1,0:T(8,128)S(1)} all-to-all(f32[8,8,128]{2,1,0:T(8,128)S(1)} %get-tuple-element.49), channel_id=1, replica_groups=mesh['gx'=8,'gy'=4] {'gx'}, dimensions={0} | all-to-all | bytes 65536 | tf_op jit(solution)/shard_map/all_to_all | solution.py:462
  39.0 1.2 %shard_map.88 = f32[2,8,128]{2,1,0:T(8,128)} custom-call(f32[8,8,128]{2,1,0:T(8,128)S(1)} %all_to_all.11.got, f32[2,8,128]{2,1,0:T(8,128)S(1)} %get-tuple-element.50.offsets, f32[1024,128]{1,0:T(8,128)S(1)} %get-tuple-element.51.entry_maps, f32[512,128]{1,0:T(8,128)S(1)} %get-tuple-element.47.rest_0_, f32[512,128]{1,0:T(8,128)S(1)} %get-tuple-element.48.rest_1_), custom_call_target="tpu_custom_call" | custom-call | flops 1150000000 | bytes 1089536 | tf_op jit(solution)/shard_map/pallas_call | solution.py:431
  (15 shorter events, 0.0 us)
Async XLA Ops:
  0.6 1.0 %copy-start.1 = (bf16[2,1,16,4096]{3,2,1,0:T(8,128)(2,1)S(1)}, bf16[2,1,16,4096]{3,2,1,0:T(8,128)(2,1)}, u32[]{:S(2)}) copy-start(bf16[2,1,16,4096]{3,2,1,0:T(8,128)(2,1)} %blocks.2) | copy-start | bytes 786436
  1.6 1.8 %copy-start.3 = (bf16[2,1,16,4096]{3,2,1,0:T(8,128)(2,1)S(1)}, bf16[2,1,16,4096]{3,2,1,0:T(8,128)(2,1)}, u32[]{:S(2)}) copy-start(bf16[2,1,16,4096]{3,2,1,0:T(8,128)(2,1)} %upper.3) | copy-start | bytes 786436
  1.6 1.8 %copy-start.4 = (f32[2,1,1024]{2,1,0:T(1,128)S(1)}, f32[2,1,1024]{2,1,0:T(1,128)}, u32[]{:S(2)}) copy-start(f32[2,1,1024]{2,1,0:T(1,128)} %param.6) | copy-start | bytes 24580
  2.9 1.8 %collective-permute-start.3 = (f32[512,128]{1,0:T(8,128)S(1)}, f32[512,128]{1,0:T(8,128)S(1)}, u32[]{:S(2)}, u32[]{:S(2)}) collective-permute-start(f32[512,128]{1,0:T(8,128)S(1)} %get-tuple-element.31.own), channel_id=1, source_target_pairs={{0,4},{4,0},{8,12},{12,8},{16,20},{20,16},{24,28},{28,24},{1,5},{5... | collective-permute-start | bytes 786440 | tf_op jit(solution)/shard_map/ppermute | solution.py:458
  4.7 7.4 %copy-start = (bf16[4,2,1,16,4096]{4,3,2,1,0:T(8,128)(2,1)S(1)}, bf16[4,2,1,16,4096]{4,3,2,1,0:T(8,128)(2,1)}, u32[]{:S(2)}) copy-start(bf16[4,2,1,16,4096]{4,3,2,1,0:T(8,128)(2,1)} %side.7) | copy-start | bytes 3145732
  4.7 7.4 %copy-start.2 = (bf16[2,1,16,4096]{3,2,1,0:T(8,128)(2,1)S(1)}, bf16[2,1,16,4096]{3,2,1,0:T(8,128)(2,1)}, u32[]{:S(2)}) copy-start(bf16[2,1,16,4096]{3,2,1,0:T(8,128)(2,1)} %diag.1) | copy-start | bytes 786436
  5.1 7.0 %copy-start.5 = (f32[2,1,1024]{2,1,0:T(1,128)S(1)}, f32[2,1,1024]{2,1,0:T(1,128)}, u32[]{:S(2)}) copy-start(f32[2,1,1024]{2,1,0:T(1,128)} %param.7) | copy-start | bytes 24580
  5.1 6.7 %collective-permute-start.4 = (f32[256,128]{1,0:T(8,128)S(1)}, f32[256,128]{1,0:T(8,128)S(1)}, u32[]{:S(2)}, u32[]{:S(2)}) collective-permute-start(f32[256,128]{1,0:T(8,128)S(1)} %shard_map.81), channel_id=1, source_target_pairs={{0,8},{4,12},{8,0},{12,4},{16,24},{20,28},{24,16},{28,20},{1,9},{5... | collective-permute-start | bytes 393224 | tf_op jit(solution)/shard_map/ppermute | solution.py:458
  7.9 8.2 %collective-permute-start.1 = (f32[2,8,128]{2,1,0:T(8,128)S(1)}, f32[2,8,128]{2,1,0:T(8,128)S(1)}, u32[]{:S(2)}, u32[]{:S(2)}) collective-permute-start(f32[2,8,128]{2,1,0:T(8,128)S(1)} %get-tuple-element.28.start.refs_0_), channel_id=1, source_target_pairs={{0,4},{1,2},{2,1},{3,7},{4,0},{5,6},{6,5},{7,3},{8,12},{9,10},{10,... | collective-permute-start | bytes 24584 | tf_op jit(solution)/shard_map/ppermute | solution.py:454
  7.9 8.2 %collective-permute-start = (f32[2,8,128]{2,1,0:T(8,128)S(1)}, f32[2,8,128]{2,1,0:T(8,128)S(1)}, u32[]{:S(2)}, u32[]{:S(2)}) collective-permute-start(f32[2,8,128]{2,1,0:T(8,128)S(1)} %get-tuple-element.28.start.refs_0_), channel_id=1, source_target_pairs={{0,1},{1,0},{2,3},{3,2},{4,5},{5,4},{6,7},{7,6},{8,9},{9,8},{10,11... | collective-permute-start | bytes 24584 | tf_op jit(solution)/shard_map/ppermute | solution.py:458
  11.0 5.0 %collective-permute-start.2 = (f32[1,8,128]{2,1,0:T(8,128)S(1)}, f32[1,8,128]{2,1,0:T(8,128)S(1)}, u32[]{:S(2)}, u32[]{:S(2)}) collective-permute-start(f32[1,8,128]{2,1,0:T(8,128)S(1)} %slice.3), channel_id=1, source_target_pairs={{0,28},{4,0},{8,4},{12,8},{16,12},{20,16},{24,20},{28,24},{1,29},{... | collective-permute-start | bytes 12296 | tf_op jit(solution)/shard_map/ppermute | solution.py:518
  11.6 1.9 %collective-permute-start.6 = (f32[512,128]{1,0:T(8,128)S(1)}, f32[512,128]{1,0:T(8,128)S(1)}, u32[]{:S(2)}, u32[]{:S(2)}) collective-permute-start(f32[512,128]{1,0:T(8,128)S(1)} %get-tuple-element.44.own), channel_id=1, source_target_pairs={{0,4},{4,0},{8,12},{12,8},{16,20},{20,16},{24,28},{28,24},{1,5},{5... | collective-permute-start | bytes 786440 | tf_op jit(solution)/shard_map/ppermute | solution.py:458
  11.8 4.0 %collective-permute-start.5 = (f32[256,128]{1,0:T(8,128)S(1)}, f32[256,128]{1,0:T(8,128)S(1)}, u32[]{:S(2)}, u32[]{:S(2)}) collective-permute-start(f32[256,128]{1,0:T(8,128)S(1)} %collective-permute-done.4.mine), channel_id=1, source_target_pairs={{0,4},{4,0},{8,12},{12,8},{16,20},{20,16},{24,28},{28,24},{1,5},{5... | collective-permute-start | bytes 393224 | tf_op jit(solution)/shard_map/ppermute | solution.py:458
  13.9 15.1 %collective-permute-start.7 = (f32[512,128]{1,0:T(8,128)S(1)}, f32[512,128]{1,0:T(8,128)S(1)}, u32[]{:S(2)}, u32[]{:S(2)}) collective-permute-start(f32[512,128]{1,0:T(8,128)S(1)} %shard_map.85), channel_id=1, source_target_pairs={{0,8},{4,12},{8,0},{12,4},{16,24},{20,28},{24,16},{28,20},{1,9},{5... | collective-permute-start | bytes 786440 | tf_op jit(solution)/shard_map/ppermute | solution.py:458
  25.8 4.4 %collective-permute-start.9 = (f32[2,8,128]{2,1,0:T(8,128)S(1)}, f32[2,8,128]{2,1,0:T(8,128)S(1)}, u32[]{:S(2)}, u32[]{:S(2)}) collective-permute-start(f32[2,8,128]{2,1,0:T(8,128)S(1)} %get-tuple-element.41.vectors), channel_id=1, source_target_pairs={{0,4},{1,2},{2,1},{3,7},{4,0},{5,6},{6,5},{7,3},{8,12},{9,10},{10,... | collective-permute-start | bytes 24584 | tf_op jit(solution)/shard_map/ppermute | solution.py:454
  25.8 4.8 %collective-permute-start.8 = (f32[2,8,128]{2,1,0:T(8,128)S(1)}, f32[2,8,128]{2,1,0:T(8,128)S(1)}, u32[]{:S(2)}, u32[]{:S(2)}) collective-permute-start(f32[2,8,128]{2,1,0:T(8,128)S(1)} %get-tuple-element.41.vectors), channel_id=1, source_target_pairs={{0,1},{1,0},{2,3},{3,2},{4,5},{5,4},{6,7},{7,6},{8,9},{9,8},{10,11... | collective-permute-start | bytes 24584 | tf_op jit(solution)/shard_map/ppermute | solution.py:458

commit v12 on v11

--- a/solution.py
+++ b/solution.py
@@ -222,11 +222,7 @@
 
 
 def prep_kernel(reverse, blocks, *refs):
-    if reverse:
-        start, _, passed, *refs = refs
-        for p in range(start.shape[0]):
-            passed[p] = woven(start[p])
-    steps, products, own, maps, native, rows_scratch = refs
+    steps, products, own, maps, native, rows_scratch = refs[1:] if reverse else refs
     planes, _, rows, width = blocks.shape
     species = LANES // 2
     pairs = rows // 2
@@ -248,11 +244,19 @@
     own[...] = products[pl.ds(order[-1] * size, size), :]
 
 
+def weave_kernel(start, passed):
+    for p in range(start.shape[0]):
+        passed[p] = woven(start[p])
+
+
 def join_kernel(level, reverse, full, pairs, own, *refs):
     here = (lax.axis_index("gx") >> level) & 1
     core = lax.axis_index("gx") & 1
     species = LANES // 2
     _, *refs, scratch = refs
+    if level == 0 and not reverse:
+        start, *refs, passed = refs
+        weave_kernel(start, passed)
     outs = refs[-2:] if full and not reverse else refs[-1:]
     partner = refs[: len(refs) - len(outs)]
     later_is_own = here == (0 if reverse else 1)
@@ -280,20 +284,18 @@
         outs[-1][pl.ds(pair, species // 2, stride=pairs), :] = kept
 
 
-def base_kernel(start, source, diag, upper, side, rhs, base):
+def base_kernel(start, source, diag, upper, side, base):
     planes = start.shape[0]
-    vectors = [spread(start[p]) for p in range(planes)]
+    vectors = [spread(-start[p]) for p in range(planes)]
     for p in range(planes):
-        own = apply([(reader(diag, p, 0), spread_raw(source[p]))])
         terms = [
+            (reader(diag, p, 0), spread_raw(source[p])),
             (reader(side, 2, p, 0), shifted(vectors[p], True)),
             (reader(side, 3, p, 0), shifted(vectors[p], False)),
         ]
         if p + 1 < planes:
             terms.append((reader(upper, p, 0), vectors[p + 1]))
-        around = apply(terms)
-        rhs[p] = gather_pairs(own)
-        base[p] = gather_pairs(own - around)
+        base[p] = gather_pairs(apply(terms))
 
 
 def convert(pairs, sources, outs, scratch):
@@ -347,53 +349,58 @@
     return jnp.where(place == 0, 0.0, low), jnp.where(place == count - 1, 0.0, high)
 
 
-def forward_offset_kernel(base, paired, other, ahead, side, upper, step_maps, *rest):
-    *partners, drive, offsets, slots = rest
-    planes, pairs = base.shape[:2]
-    size = pairs * LANES // 2
-    here = lax.axis_index("gx")
-    last = here == lax.axis_size("gx") - 1
-    previous = None
+def drive_kernel(base, paired, other, ahead, side, upper, drive):
+    planes = base.shape[0]
+    last = lax.axis_index("gx") == lax.axis_size("gx") - 1
     for p in range(planes):
         low, high = beside("gy", paired[p], other[p])
         terms = [(reader(side, 0, p, 0), spread(low)), (reader(side, 1, p, 0), spread(high))]
         if p + 1 == planes:
             beyond = jnp.where(last, 0.0, ahead[0])
             terms.append((reader(upper, p, 0), spread(beyond)))
-        fresh = base[p] - gather_pairs(apply(terms))
-        drive[p] = fresh
+        drive[p] = base[p] - gather_pairs(apply(terms))
+
+
+def forward_offset_kernel(drive, step_maps, *rest):
+    *partners, offsets, slots = rest
+    planes = drive.shape[0]
+    size = drive.shape[1] * LANES // 2
+    previous = None
+    for p in range(planes):
+        fresh = drive[p]
         if previous is not None:
             fresh = fresh - mapped(step_maps, previous, (p - 1) * size)
         offsets[p] = fresh
         previous = fresh
-    outgoing(previous, partners, here, slots)
-
-
-def forward_kernel(got, drive, offsets, rhs, entry_maps, *rest):
+    outgoing(previous, partners, lax.axis_index("gx"), slots)
+
+
+def forward_kernel(got, drive, offsets, entry_maps, *rest):
     *partners, out, copy, base = rest
     planes = drive.shape[0]
     size = drive.shape[1] * LANES // 2
     entering = incoming(got, partners, lax.axis_index("gx"), False)
     for p in range(planes):
         value = offsets[p] + mapped(entry_maps, entering, p * size)
-        base[p] = rhs[p] - (drive[p] - value)
+        base[p] = value - drive[p]
         out[p] = unwoven(value)
         copy[p] = value
 
 
-def side_kernel(base, vectors, side, *rest):
+def side_kernel(base, vectors, source, diag, side, *rest):
     *rest, scratch = rest
     sources, (out, *converted) = rest[: len(rest) // 2], rest[len(rest) // 2 :]
     planes, pairs = base.shape[:2]
     for p in range(planes):
-        vector = spread(vectors[p])
+        vector = spread(-vectors[p])
         around = apply(
             [
+                (reader(diag, p, 0), spread_raw(source[p])),
                 (reader(side, 2, p, 0), shifted(vector, True)),
                 (reader(side, 3, p, 0), shifted(vector, False)),
             ]
         )
-        out[p] = base[p] - gather_pairs(around)
+        out[p] = base[p] + gather_pairs(around)
     convert(pairs, sources, converted, scratch)
 
 
@@ -480,8 +487,8 @@
     def prepare(reverse, blocks, after=None):
         return call(
             functools.partial(prep_kernel, reverse),
-            [blocks] + ([start, (after, None)] if reverse else []),
-            ([vec] if reverse else []) + [steps, maps, whole],
+            [blocks] + ([(after, None)] if reverse else []),
+            [steps, maps, whole],
             [whole, (depth * species // 2, LANES), (depth * species, LANES)],
             1.0,
         )
@@ -497,23 +504,31 @@
             partners += got
             if level + 2 < levels:
                 full = reverse or level + 3 < levels
+                weave = level == 0 and not reverse
                 outs = call(
                     functools.partial(join_kernel, level, reverse, full, pairs),
-                    [own, (after, None)] + got,
-                    [whole] if reverse else [whole, half] if full else [half],
+                    [own, (after, None)] + ([start] if weave else []) + got,
+                    ([whole] if reverse else [whole, half] if full else [half]) + [vec] * weave,
                     [(depth * species, LANES)],
-                    0.4,
+                    0.02,
                 )
+                if weave:
+                    *outs, woven_start = outs
+                    partners.append(woven_start)
                 own, kept = outs[0], outs[-1]
         return partners
 
     step_maps, products, own = prepare(False, x_lower)
-    start, upper_steps, upper_products, upper_own = prepare(True, x_upper, products)
-    rhs, base = call(
-        base_kernel, [start, source, diag_inverse, x_upper, side_blocks], [vec, vec], [], 5.0
-    )
-    lower = [step_maps, products, *partner_maps(False, own, start)]
-    upper = [upper_steps, upper_products, *partner_maps(True, upper_own, start)]
+    upper_steps, upper_products, upper_own = prepare(True, x_upper, products)
+    lower = [step_maps, products, *partner_maps(False, own, upper_products)]
+    if levels > 2:
+        start = lower.pop(3)
+    else:
+        (start,) = call(weave_kernel, [start], [vec], [], 0.1)
+    (base,) = call(
+        base_kernel, [start, source, diag_inverse, x_upper, side_blocks], [vec], [], 0.05
+    )
+    upper = [upper_steps, upper_products, *partner_maps(True, upper_own, upper_products)]
     paired, other = swaps(start)
     ahead = lax.ppermute(start[:1], "gx", [(i, (i - 1) % count) for i in range(count)])
 
@@ -529,16 +544,15 @@
             [whole],
             0.3,
         )
-    drive, offsets, sent = call(
-        forward_offset_kernel,
-        [base, paired, other, ahead, side_blocks, x_upper, step_maps] + partners,
-        [vec, vec, slots],
-        [],
-        1.5,
+    (drive,) = call(
+        drive_kernel, [base, paired, other, ahead, side_blocks, x_upper], [vec], [], 1.0
+    )
+    offsets, sent = call(
+        forward_offset_kernel, [drive, step_maps] + partners, [vec, slots], [], 1.0
     )
     forward, copy, base = call(
         forward_kernel,
-        [exchange(sent, "gx"), drive, offsets, rhs, entry_maps] + partners,
+        [exchange(sent, "gx"), drive, offsets, entry_maps] + partners,
         [vec, vec, vec],
         [],
         1.0,
@@ -546,7 +560,7 @@
     paired, other = swaps(copy)
     base, step_maps, entry_maps, *partners = call(
         side_kernel,
-        [base, copy, side_blocks] + upper,
+        [base, copy, source, diag_inverse, side_blocks] + upper,
         [vec, steps, maps] + [whole] * (levels - 1),
         [whole],
         0.7,

time: 40.4 us -> 39.9 us (0.988)
  starting transfers between devices: 12 us -> 10.4 us
  blocking collectives: 14.6 us -> 15.5 us
  local copies, waits for them, and re-layouts: 0.97 us -> 1.86 us
  Pallas kernels: 11.2 us -> 10.7 us
    ppermute x7, starting transfers between devices: 11.3 us -> 10.2 us  [crossed(): lax.ppermute(block, axis, [(i, i ^ distance) for i in range(lax.axis_size...]
    unnamed x12, local copies, waits for them, and re-layouts: 0.97 us -> 1.86 us
    all_to_all x2, blocking collectives: 14.6 us -> 15.5 us  [exchange(): return lax.all_to_all(slots, axis, 0, 0)]
    pallas_call x12 -> x13, Pallas kernels: 11.2 us -> 10.7 us  [call(): pl.pallas_call(kernel, out_shape=outs, in_specs=[pl.BlockSpec(memory_spac...]
  transfers between devices with their start and end apart: 10 -> 10, of which waited for: 2 -> 1; matrix products, arithmetic and copies ran while one was open for 0% -> 0% of each run, Pallas kernels for 18% -> 18%
where the time goes in v12:
time: 39.9 us; the launch traced here: 39.7 us
  blocking collectives  15.5 us (39%)
  Pallas kernels  10.7 us (27%)
  starting transfers between devices  10.4 us (26%)
  local copies, waits for them, and re-layouts  1.86 us (5%)
  between operations  0.75 us (2%)
    all_to_all x2, blocking collectives, exchange(): return lax.all_to_all(slots, axis, 0, 0)  15.5 us
    pallas_call x13, Pallas kernels, call(): pl.pallas_call(kernel, out_shape=outs, in_specs=[pl.BlockSpec(memory_spac...  10.7 us
    ppermute x7, starting transfers between devices, crossed(): lax.ppermute(block, axis, [(i, i ^ distance) for i in range(lax.axis_size...  10.2 us
    unnamed x12, local copies, waits for them, and re-layouts  1.86 us
  transfers between devices with their start and end apart: 10, of which 1 were waited for; matrix products, arithmetic and copies ran while one was open for 0% of the time, Pallas kernels for 18%

profile of v12, /device:TPU:0, one launch (start us, length us, event | category | flops | bytes accessed | tf_op | source)
XLA Modules:
  0.0 39.7 jit_solution(2458354047679079296)
XLA Ops:
  0.6 1.0 %copy-done.5 = bf16[2,1,16,4096]{3,2,1,0:T(8,128)(2,1)S(1)} copy-done((bf16[2,1,16,4096]{3,2,1,0:T(8,128)(2,1)S(1)}, bf16[2,1,16,4096]{3,2,1,0:T(8,128)(2,1)}, u32[]{:S(2)}) %copy-start.5) | copy-done | bytes 262168
  1.6 1.3 %shard_map.77 = (f32[512,128]{1,0:T(8,128)S(1)}, f32[1024,128]{1,0:T(8,128)S(1)}, f32[512,128]{1,0:T(8,128)S(1)}) custom-call(bf16[2,1,16,4096]{3,2,1,0:T(8,128)(2,1)S(1)} %copy-done.5), custom_call_target="tpu_custom_call" | custom-call | flops 1150000000 | bytes 262144 | tf_op jit(solution)/shard_map/pallas_call | solution.py:438
  2.9 0.5 %collective-permute-start = (f32[512,128]{1,0:T(8,128)S(1)}, f32[512,128]{1,0:T(8,128)S(1)}, u32[]{:S(2)}, u32[]{:S(2)}) collective-permute-start(f32[512,128]{1,0:T(8,128)S(1)} %get-tuple-element.25.own), channel_id=1, source_target_pairs={{0,4},{4,0},{8,12},{12,8},{16,20},{20,16},{24,28},{28,24},{1,5},{5... | collective-permute-start | bytes 786440 | tf_op jit(solution)/shard_map/ppermute | solution.py:465
  3.5 1.3 %shard_map.78 = (f32[512,128]{1,0:T(8,128)S(1)}, f32[1024,128]{1,0:T(8,128)S(1)}, f32[512,128]{1,0:T(8,128)S(1)}) custom-call(bf16[2,1,16,4096]{3,2,1,0:T(8,128)(2,1)S(1)} %copy-done.1, f32[1024,128]{1,0:T(8,128)S(1)} %get-tuple-element.26.refs_0_.refs_1_), custom_call_target="tpu_custom_call" | custom-call | flops 1150000000 | bytes 786432 | tf_op jit(solution)/shard_map/pallas_call | solution.py:438
  4.8 0.1 collective-permute-start.6
  4.9 0.0 collective-permute-done.refs_2_
  4.9 0.4 shard_map.79
  5.3 3.0 %collective-permute-start.4 = (f32[256,128]{1,0:T(8,128)S(1)}, f32[256,128]{1,0:T(8,128)S(1)}, u32[]{:S(2)}, u32[]{:S(2)}) collective-permute-start(f32[256,128]{1,0:T(8,128)S(1)} %get-tuple-element.32), channel_id=1, source_target_pairs={{0,8},{4,12},{8,0},{12,4},{16,24},{20,28},{24,16},{28,20},{1,9},{5... | collective-permute-start | bytes 393224 | tf_op jit(solution)/shard_map/ppermute | solution.py:465
  8.2 3.1 %collective-permute-start.1 = (f32[2,8,128]{2,1,0:T(8,128)S(1)}, f32[2,8,128]{2,1,0:T(8,128)S(1)}, u32[]{:S(2)}, u32[]{:S(2)}) collective-permute-start(f32[2,8,128]{2,1,0:T(8,128)S(1)} %get-tuple-element.28.start), channel_id=1, source_target_pairs={{0,1},{1,0},{2,3},{3,2},{4,5},{5,4},{6,7},{7,6},{8,9},{9,8},{10,11... | collective-permute-start | bytes 24584 | tf_op jit(solution)/shard_map/ppermute | solution.py:465
  11.4 0.3 collective-permute-start.3
  11.7 0.0 collective-permute-done.6.refs_1_.rest_2_
  11.7 0.4 %shard_map.86 = f32[512,128]{1,0:T(8,128)S(1)} custom-call(f32[512,128]{1,0:T(8,128)S(1)} %get-tuple-element.40.own, f32[1024,128]{1,0:T(8,128)S(1)} %get-tuple-element.27.refs_0_.rest_1_, f32[512,128]{1,0:T(8,128)S(1)} %collective-permute-done.6.refs_1_.rest_2_), custom_call_target="tpu_custom_call" | custom-call | flops 23000000 | bytes 1048576 | tf_op jit(solution)/shard_map/pallas_call | solution.py:438
  12.1 0.6 %collective-permute-start.7 = (f32[512,128]{1,0:T(8,128)S(1)}, f32[512,128]{1,0:T(8,128)S(1)}, u32[]{:S(2)}, u32[]{:S(2)}) collective-permute-start(f32[512,128]{1,0:T(8,128)S(1)} %shard_map.86), channel_id=1, source_target_pairs={{0,8},{4,12},{8,0},{12,4},{16,24},{20,28},{24,16},{28,20},{1,9},{5... | collective-permute-start | bytes 786440 | tf_op jit(solution)/shard_map/ppermute | solution.py:465
  12.7 0.0 collective-permute-start.5
  12.7 0.0 copy-start.2
  12.7 0.0 copy-start.4
  12.7 0.4 shard_map.82
  13.1 0.8 %copy-done = bf16[4,2,1,16,4096]{4,3,2,1,0:T(8,128)(2,1)S(1)} copy-done((bf16[4,2,1,16,4096]{4,3,2,1,0:T(8,128)(2,1)S(1)}, bf16[4,2,1,16,4096]{4,3,2,1,0:T(8,128)(2,1)}, u32[]{:S(2)}) %copy-start) | copy-done | bytes 1048600
  13.9 0.0 copy-done.2
  14.0 0.8 %shard_map.80.base = f32[2,8,128]{2,1,0:T(8,128)S(1)} custom-call(f32[2,8,128]{2,1,0:T(8,128)S(1)} %get-tuple-element.28.start, f32[2,8,128]{2,1,0:T(8,128)S(1)} %bitcast.5, bf16[2,1,16,4096]{3,2,1,0:T(8,128)(2,1)S(1)} %copy-done.2, bf16[2,1,16,4096]{3,2,1,0:T(8,128)(2,1)S(1)} %copy-done.1, bf16[4,2,1,16,4096]{4,3,2,1,0:T(8,128)(2,1)S(1)} %copy-done), custom_call_target="tpu_custom_call" | custom-call | flops 57500000 | bytes 1589248 | tf_op jit(solution)/shard_map/pallas_call | solution.py:438
  14.8 0.0 collective-permute-done.3.ahead
  14.8 0.8 %shard_map.81.drive = f32[2,8,128]{2,1,0:T(8,128)S(1)} custom-call(f32[2,8,128]{2,1,0:T(8,128)S(1)} %shard_map.80.base, f32[2,8,128]{2,1,0:T(8,128)S(1)} %collective-permute-done.1.paired, f32[2,8,128]{2,1,0:T(8,128)S(1)} %collective-permute-done.2.other, f32[1,8,128]{2,1,0:T(8,128)S(1)} %collective-permute-done.3.ahead, ...), custom_call_target="tpu_custom_call" | custom-call | flops 1150000000 | bytes 1339392 | tf_op jit(solution)/shard_map/pallas_call | solution.py:438
  15.6 0.2 shard_map.83.rest_1_
  15.8 0.5 %shard_map.84 = (f32[2,8,128]{2,1,0:T(8,128)S(1)}, f32[8,8,128]{2,1,0:T(8,128)S(1)}) custom-call(f32[2,8,128]{2,1,0:T(8,128)S(1)} %shard_map.81.drive, f32[512,128]{1,0:T(8,128)S(1)} %get-tuple-element.30.step_maps, f32[512,128]{1,0:T(8,128)S(1)} %get-tuple-element.31.rest_0_, f32[512,128]{1,0:T(8,128)S(1)} %shard_map.83.rest_1_), custom_call_target="tpu_custom_call" | custom-call | flops 1150000000 | bytes 794624 | tf_op jit(solution)/shard_map/pallas_call | solution.py:438
  16.2 8.3 %all_to_all.10.got = f32[8,8,128]{2,1,0:T(8,128)S(1)} all-to-all(f32[8,8,128]{2,1,0:T(8,128)S(1)} %get-tuple-element.33), channel_id=1, replica_groups=mesh['gx'=8,'gy'=4] {'gx'}, dimensions={0} | all-to-all | bytes 65536 | tf_op jit(solution)/shard_map/all_to_all | solution.py:469
  24.5 1.1 %shard_map.85 = (f32[2,8,128]{2,1,0:T(8,128)}, f32[2,8,128]{2,1,0:T(8,128)S(1)}, f32[2,8,128]{2,1,0:T(8,128)S(1)}) custom-call(f32[8,8,128]{2,1,0:T(8,128)S(1)} %all_to_all.10.got, f32[2,8,128]{2,1,0:T(8,128)S(1)} %shard_map.81.drive, f32[2,8,128]{2,1,0:T(8,128)S(1)} %get-tuple-element.34.offsets, f32[1024,128]{1,0:T(8,128)S(1)} %get-tuple-element.35.entry_maps, ...), custom_call_target="tpu_custom_call" | custom-call | flops 1150000000 | bytes 1097728 | tf_op jit(solution)/shard_map/pallas_call | solution.py:438
  25.7 2.8 %collective-permute-start.8 = (f32[2,8,128]{2,1,0:T(8,128)S(1)}, f32[2,8,128]{2,1,0:T(8,128)S(1)}, u32[]{:S(2)}, u32[]{:S(2)}) collective-permute-start(f32[2,8,128]{2,1,0:T(8,128)S(1)} %get-tuple-element.38.vectors), channel_id=1, source_target_pairs={{0,1},{1,0},{2,3},{3,2},{4,5},{5,4},{6,7},{7,6},{8,9},{9,8},{10,11... | collective-permute-start | bytes 24584 | tf_op jit(solution)/shard_map/ppermute | solution.py:465
  28.5 1.3 %shard_map.87 = (f32[2,8,128]{2,1,0:T(8,128)S(1)}, f32[512,128]{1,0:T(8,128)S(1)}, f32[1024,128]{1,0:T(8,128)S(1)}, f32[512,128]{1,0:T(8,128)S(1)}, f32[512,128]{1,0:T(8,128)S(1)}) custom-call(f32[2,8,128]{2,1,0:T(8,128)S(1)} %get-tuple-element.37.base, f32[2,8,128]{2,1,0:T(8,128)S(1)} %get-tuple-element.38.vectors, f32[2,8,128]{2,1,0:T(8,128)S(1)} %bitcast.6, ...), custom_call_target="tpu_custom_call" | custom-call | flops 805000000 | bytes 2646016 | tf_op jit(solution)/shard_map/pallas_call | solution.py:438
  29.8 0.3 collective-permute-done.8.paired
  30.1 1.2 %shard_map.88 = (f32[2,8,128]{2,1,0:T(8,128)S(1)}, f32[8,8,128]{2,1,0:T(8,128)S(1)}) custom-call(f32[2,8,128]{2,1,0:T(8,128)S(1)} %get-tuple-element.41.base, f32[2,8,128]{2,1,0:T(8,128)S(1)} %collective-permute-done.8.paired, f32[2,8,128]{2,1,0:T(8,128)S(1)} %collective-permute-done.9.other, bf16[4,2,1,16,4096]{4,3,2,1,0:T(8,128)(2,1)S(1)} %copy-done, ...), custom_call_target="tpu_custom_call" | custom-call | flops 1724999936 | bytes 1859584 | tf_op jit(solution)/shard_map/pallas_call | solution.py:438
  31.3 7.2 %all_to_all.11.got = f32[8,8,128]{2,1,0:T(8,128)S(1)} all-to-all(f32[8,8,128]{2,1,0:T(8,128)S(1)} %get-tuple-element.45), channel_id=1, replica_groups=mesh['gx'=8,'gy'=4] {'gx'}, dimensions={0} | all-to-all | bytes 65536 | tf_op jit(solution)/shard_map/all_to_all | solution.py:469
  38.5 1.2 %shard_map.89 = f32[2,8,128]{2,1,0:T(8,128)} custom-call(f32[8,8,128]{2,1,0:T(8,128)S(1)} %all_to_all.11.got, f32[2,8,128]{2,1,0:T(8,128)S(1)} %get-tuple-element.46.offsets, f32[1024,128]{1,0:T(8,128)S(1)} %get-tuple-element.47.entry_maps, f32[512,128]{1,0:T(8,128)S(1)} %get-tuple-element.43.rest_0_, f32[512,128]{1,0:T(8,128)S(1)} %get-tuple-element.44.rest_1_), custom_call_target="tpu_custom_call" | custom-call | flops 1150000000 | bytes 1089536 | tf_op jit(solution)/shard_map/pallas_call | solution.py:438
  (16 shorter events, 0.0 us)
Async XLA Ops:
  0.6 2.8 %copy-start.1 = (bf16[2,1,16,4096]{3,2,1,0:T(8,128)(2,1)S(1)}, bf16[2,1,16,4096]{3,2,1,0:T(8,128)(2,1)}, u32[]{:S(2)}) copy-start(bf16[2,1,16,4096]{3,2,1,0:T(8,128)(2,1)} %upper.3) | copy-start | bytes 786436
  0.6 1.0 %copy-start.5 = (bf16[2,1,16,4096]{3,2,1,0:T(8,128)(2,1)S(1)}, bf16[2,1,16,4096]{3,2,1,0:T(8,128)(2,1)}, u32[]{:S(2)}) copy-start(bf16[2,1,16,4096]{3,2,1,0:T(8,128)(2,1)} %blocks.2) | copy-start | bytes 786436
  2.9 2.0 %collective-permute-start = (f32[512,128]{1,0:T(8,128)S(1)}, f32[512,128]{1,0:T(8,128)S(1)}, u32[]{:S(2)}, u32[]{:S(2)}) collective-permute-start(f32[512,128]{1,0:T(8,128)S(1)} %get-tuple-element.25.own), channel_id=1, source_target_pairs={{0,4},{4,0},{8,12},{12,8},{16,20},{20,16},{24,28},{28,24},{1,5},{5... | collective-permute-start | bytes 786440 | tf_op jit(solution)/shard_map/ppermute | solution.py:465
  3.5 1.4 %copy-start.3 = (f32[2,1,1024]{2,1,0:T(1,128)S(1)}, f32[2,1,1024]{2,1,0:T(1,128)}, u32[]{:S(2)}) copy-start(f32[2,1,1024]{2,1,0:T(1,128)} %param.6) | copy-start | bytes 24580
  4.8 6.9 %collective-permute-start.6 = (f32[512,128]{1,0:T(8,128)S(1)}, f32[512,128]{1,0:T(8,128)S(1)}, u32[]{:S(2)}, u32[]{:S(2)}) collective-permute-start(f32[512,128]{1,0:T(8,128)S(1)} %get-tuple-element.40.own), channel_id=1, source_target_pairs={{0,4},{4,0},{8,12},{12,8},{16,20},{20,16},{24,28},{28,24},{1,5},{5... | collective-permute-start | bytes 786440 | tf_op jit(solution)/shard_map/ppermute | solution.py:465
  5.3 7.4 %collective-permute-start.4 = (f32[256,128]{1,0:T(8,128)S(1)}, f32[256,128]{1,0:T(8,128)S(1)}, u32[]{:S(2)}, u32[]{:S(2)}) collective-permute-start(f32[256,128]{1,0:T(8,128)S(1)} %get-tuple-element.32), channel_id=1, source_target_pairs={{0,8},{4,12},{8,0},{12,4},{16,24},{20,28},{24,16},{28,20},{1,9},{5... | collective-permute-start | bytes 393224 | tf_op jit(solution)/shard_map/ppermute | solution.py:465
  8.2 6.6 %collective-permute-start.2 = (f32[2,8,128]{2,1,0:T(8,128)S(1)}, f32[2,8,128]{2,1,0:T(8,128)S(1)}, u32[]{:S(2)}, u32[]{:S(2)}) collective-permute-start(f32[2,8,128]{2,1,0:T(8,128)S(1)} %get-tuple-element.28.start), channel_id=1, source_target_pairs={{0,4},{1,2},{2,1},{3,7},{4,0},{5,6},{6,5},{7,3},{8,12},{9,10},{10,... | collective-permute-start | bytes 24584 | tf_op jit(solution)/shard_map/ppermute | solution.py:461
  8.2 6.6 %collective-permute-start.1 = (f32[2,8,128]{2,1,0:T(8,128)S(1)}, f32[2,8,128]{2,1,0:T(8,128)S(1)}, u32[]{:S(2)}, u32[]{:S(2)}) collective-permute-start(f32[2,8,128]{2,1,0:T(8,128)S(1)} %get-tuple-element.28.start), channel_id=1, source_target_pairs={{0,1},{1,0},{2,3},{3,2},{4,5},{5,4},{6,7},{7,6},{8,9},{9,8},{10,11... | collective-permute-start | bytes 24584 | tf_op jit(solution)/shard_map/ppermute | solution.py:465
  11.4 3.4 %collective-permute-start.3 = (f32[1,8,128]{2,1,0:T(8,128)S(1)}, f32[1,8,128]{2,1,0:T(8,128)S(1)}, u32[]{:S(2)}, u32[]{:S(2)}) collective-permute-start(f32[1,8,128]{2,1,0:T(8,128)S(1)} %slice.3), channel_id=1, source_target_pairs={{0,28},{4,0},{8,4},{12,8},{16,12},{20,16},{24,20},{28,24},{1,29},{... | collective-permute-start | bytes 12296 | tf_op jit(solution)/shard_map/ppermute | solution.py:533
  12.1 16.4 %collective-permute-start.7 = (f32[512,128]{1,0:T(8,128)S(1)}, f32[512,128]{1,0:T(8,128)S(1)}, u32[]{:S(2)}, u32[]{:S(2)}) collective-permute-start(f32[512,128]{1,0:T(8,128)S(1)} %shard_map.86), channel_id=1, source_target_pairs={{0,8},{4,12},{8,0},{12,4},{16,24},{20,28},{24,16},{28,20},{1,9},{5... | collective-permute-start | bytes 786440 | tf_op jit(solution)/shard_map/ppermute | solution.py:465
  12.7 2.9 %collective-permute-start.5 = (f32[256,128]{1,0:T(8,128)S(1)}, f32[256,128]{1,0:T(8,128)S(1)}, u32[]{:S(2)}, u32[]{:S(2)}) collective-permute-start(f32[256,128]{1,0:T(8,128)S(1)} %collective-permute-done.4.mine), channel_id=1, source_target_pairs={{0,4},{4,0},{8,12},{12,8},{16,20},{20,16},{24,28},{28,24},{1,5},{5... | collective-permute-start | bytes 393224 | tf_op jit(solution)/shard_map/ppermute | solution.py:465
  12.7 1.2 %copy-start = (bf16[4,2,1,16,4096]{4,3,2,1,0:T(8,128)(2,1)S(1)}, bf16[4,2,1,16,4096]{4,3,2,1,0:T(8,128)(2,1)}, u32[]{:S(2)}) copy-start(bf16[4,2,1,16,4096]{4,3,2,1,0:T(8,128)(2,1)} %side.7) | copy-start | bytes 3145732
  12.7 1.3 %copy-start.2 = (bf16[2,1,16,4096]{3,2,1,0:T(8,128)(2,1)S(1)}, bf16[2,1,16,4096]{3,2,1,0:T(8,128)(2,1)}, u32[]{:S(2)}) copy-start(bf16[2,1,16,4096]{3,2,1,0:T(8,128)(2,1)} %diag.3) | copy-start | bytes 786436
  12.7 1.3 %copy-start.4 = (f32[2,1,1024]{2,1,0:T(1,128)S(1)}, f32[2,1,1024]{2,1,0:T(1,128)}, u32[]{:S(2)}) copy-start(f32[2,1,1024]{2,1,0:T(1,128)} %param.7) | copy-start | bytes 24580
  25.7 4.1 %collective-permute-start.9 = (f32[2,8,128]{2,1,0:T(8,128)S(1)}, f32[2,8,128]{2,1,0:T(8,128)S(1)}, u32[]{:S(2)}, u32[]{:S(2)}) collective-permute-start(f32[2,8,128]{2,1,0:T(8,128)S(1)} %get-tuple-element.38.vectors), channel_id=1, source_target_pairs={{0,4},{1,2},{2,1},{3,7},{4,0},{5,6},{6,5},{7,3},{8,12},{9,10},{10,... | collective-permute-start | bytes 24584 | tf_op jit(solution)/shard_map/ppermute | solution.py:461
  25.7 4.4 %collective-permute-start.8 = (f32[2,8,128]{2,1,0:T(8,128)S(1)}, f32[2,8,128]{2,1,0:T(8,128)S(1)}, u32[]{:S(2)}, u32[]{:S(2)}) collective-permute-start(f32[2,8,128]{2,1,0:T(8,128)S(1)} %get-tuple-element.38.vectors), channel_id=1, source_target_pairs={{0,1},{1,0},{2,3},{3,2},{4,5},{5,4},{6,7},{7,6},{8,9},{9,8},{10,11... | collective-permute-start | bytes 24584 | tf_op jit(solution)/shard_map/ppermute | solution.py:465

commit v13 on v12

--- a/solution.py
+++ b/solution.py
@@ -526,14 +526,14 @@
     else:
         (start,) = call(weave_kernel, [start], [vec], [], 0.1)
     (base,) = call(
-        base_kernel, [start, source, diag_inverse, x_upper, side_blocks], [vec], [], 0.05
+        base_kernel, [start, source, diag_inverse, x_upper, side_blocks], [vec], [], 0.02
     )
     upper = [upper_steps, upper_products, *partner_maps(True, upper_own, upper_products)]
     paired, other = swaps(start)
     ahead = lax.ppermute(start[:1], "gx", [(i, (i - 1) % count) for i in range(count)])
 
     step_maps, entry_maps, near = call(
-        functools.partial(near_kernel, pairs), lower[:3], [steps, maps, whole], [whole], 0.5
+        functools.partial(near_kernel, pairs), lower[:3], [steps, maps, whole], [whole], 0.1
     )
     partners = [near]
     for level in range(levels - 2):
@@ -542,10 +542,10 @@
             lower[3 + 2 * level : 5 + 2 * level],
             [whole],
             [whole],
-            0.3,
+            0.1,
         )
     (drive,) = call(
-        drive_kernel, [base, paired, other, ahead, side_blocks, x_upper], [vec], [], 1.0
+        drive_kernel, [base, paired, other, ahead, side_blocks, x_upper], [vec], [], 1.2
     )
     offsets, sent = call(
         forward_offset_kernel, [drive, step_maps] + partners, [vec, slots], [], 1.0

time: 39.9 us -> 38.6 us (0.967)
  starting transfers between devices: 10.4 us -> 9.8 us
    ppermute x7, starting transfers between devices: 10.2 us -> 9.51 us  [crossed(): lax.ppermute(block, axis, [(i, i ^ distance) for i in range(lax.axis_size...]
where the time goes in v13:
time: 38.6 us; the launch traced here: 38.4 us
  blocking collectives  15.3 us (40%)
  Pallas kernels  10.7 us (28%)
  starting transfers between devices  9.8 us (25%)
  local copies, waits for them, and re-layouts  1.47 us (4%)
  between operations  0.76 us (2%)
    all_to_all x2, blocking collectives, exchange(): return lax.all_to_all(slots, axis, 0, 0)  15.3 us
    pallas_call x13, Pallas kernels, call(): pl.pallas_call(kernel, out_shape=outs, in_specs=[pl.BlockSpec(memory_spac...  10.7 us
    ppermute x7, starting transfers between devices, crossed(): lax.ppermute(block, axis, [(i, i ^ distance) for i in range(lax.axis_size...  9.51 us
    unnamed x12, local copies, waits for them, and re-layouts  1.47 us
  transfers between devices with their start and end apart: 10, of which 1 were waited for; matrix products, arithmetic and copies ran while one was open for 0% of the time, Pallas kernels for 18%

profile of v13, /device:TPU:0, one launch (start us, length us, event | category | flops | bytes accessed | tf_op | source)
XLA Modules:
  0.0 38.4 jit_solution(6940116624564490156)
XLA Ops:
  0.6 1.0 %copy-done.5 = bf16[2,1,16,4096]{3,2,1,0:T(8,128)(2,1)S(1)} copy-done((bf16[2,1,16,4096]{3,2,1,0:T(8,128)(2,1)S(1)}, bf16[2,1,16,4096]{3,2,1,0:T(8,128)(2,1)}, u32[]{:S(2)}) %copy-start.5) | copy-done | bytes 262168
  1.6 1.3 %shard_map.77 = (f32[512,128]{1,0:T(8,128)S(1)}, f32[1024,128]{1,0:T(8,128)S(1)}, f32[512,128]{1,0:T(8,128)S(1)}) custom-call(bf16[2,1,16,4096]{3,2,1,0:T(8,128)(2,1)S(1)} %copy-done.5), custom_call_target="tpu_custom_call" | custom-call | flops 1150000000 | bytes 262144 | tf_op jit(solution)/shard_map/pallas_call | solution.py:438
  2.9 0.5 %collective-permute-start = (f32[512,128]{1,0:T(8,128)S(1)}, f32[512,128]{1,0:T(8,128)S(1)}, u32[]{:S(2)}, u32[]{:S(2)}) collective-permute-start(f32[512,128]{1,0:T(8,128)S(1)} %get-tuple-element.25.own), channel_id=1, source_target_pairs={{0,4},{4,0},{8,12},{12,8},{16,20},{20,16},{24,28},{28,24},{1,5},{5... | collective-permute-start | bytes 786440 | tf_op jit(solution)/shard_map/ppermute | solution.py:465
  3.5 1.3 %shard_map.78 = (f32[512,128]{1,0:T(8,128)S(1)}, f32[1024,128]{1,0:T(8,128)S(1)}, f32[512,128]{1,0:T(8,128)S(1)}) custom-call(bf16[2,1,16,4096]{3,2,1,0:T(8,128)(2,1)S(1)} %copy-done.1, f32[1024,128]{1,0:T(8,128)S(1)} %get-tuple-element.26.refs_0_.refs_1_), custom_call_target="tpu_custom_call" | custom-call | flops 1150000000 | bytes 786432 | tf_op jit(solution)/shard_map/pallas_call | solution.py:438
  4.8 0.1 collective-permute-start.6
  4.9 0.0 collective-permute-done.refs_2_
  4.9 0.4 shard_map.79
  5.3 3.0 %collective-permute-start.4 = (f32[256,128]{1,0:T(8,128)S(1)}, f32[256,128]{1,0:T(8,128)S(1)}, u32[]{:S(2)}, u32[]{:S(2)}) collective-permute-start(f32[256,128]{1,0:T(8,128)S(1)} %get-tuple-element.32), channel_id=1, source_target_pairs={{0,8},{4,12},{8,0},{12,4},{16,24},{20,28},{24,16},{28,20},{1,9},{5... | collective-permute-start | bytes 393224 | tf_op jit(solution)/shard_map/ppermute | solution.py:465
  8.2 0.0 collective-permute-start.2
  8.2 3.1 %collective-permute-start.1 = (f32[2,8,128]{2,1,0:T(8,128)S(1)}, f32[2,8,128]{2,1,0:T(8,128)S(1)}, u32[]{:S(2)}, u32[]{:S(2)}) collective-permute-start(f32[2,8,128]{2,1,0:T(8,128)S(1)} %get-tuple-element.28.start), channel_id=1, source_target_pairs={{0,1},{1,0},{2,3},{3,2},{4,5},{5,4},{6,7},{7,6},{8,9},{9,8},{10,11... | collective-permute-start | bytes 24584 | tf_op jit(solution)/shard_map/ppermute | solution.py:465
  11.4 0.3 collective-permute-start.3
  11.7 0.0 collective-permute-done.6.refs_1_.rest_2_
  11.7 0.4 %shard_map.86 = f32[512,128]{1,0:T(8,128)S(1)} custom-call(f32[512,128]{1,0:T(8,128)S(1)} %get-tuple-element.40.own, f32[1024,128]{1,0:T(8,128)S(1)} %get-tuple-element.27.refs_0_.rest_1_, f32[512,128]{1,0:T(8,128)S(1)} %collective-permute-done.6.refs_1_.rest_2_), custom_call_target="tpu_custom_call" | custom-call | flops 23000000 | bytes 1048576 | tf_op jit(solution)/shard_map/pallas_call | solution.py:438
  12.1 0.6 %collective-permute-start.7 = (f32[512,128]{1,0:T(8,128)S(1)}, f32[512,128]{1,0:T(8,128)S(1)}, u32[]{:S(2)}, u32[]{:S(2)}) collective-permute-start(f32[512,128]{1,0:T(8,128)S(1)} %shard_map.86), channel_id=1, source_target_pairs={{0,8},{4,12},{8,0},{12,4},{16,24},{20,28},{24,16},{28,20},{1,9},{5... | collective-permute-start | bytes 786440 | tf_op jit(solution)/shard_map/ppermute | solution.py:465
  12.7 0.4 shard_map.82
  13.1 0.0 collective-permute-done.4.mine
  13.1 0.1 collective-permute-start.5
  13.2 0.5 %copy-done.2 = bf16[2,1,16,4096]{3,2,1,0:T(8,128)(2,1)S(1)} copy-done((bf16[2,1,16,4096]{3,2,1,0:T(8,128)(2,1)S(1)}, bf16[2,1,16,4096]{3,2,1,0:T(8,128)(2,1)}, u32[]{:S(2)}) %copy-start.2) | copy-done | bytes 262168
  13.6 0.8 %shard_map.80.base = f32[2,8,128]{2,1,0:T(8,128)S(1)} custom-call(f32[2,8,128]{2,1,0:T(8,128)S(1)} %get-tuple-element.28.start, f32[2,8,128]{2,1,0:T(8,128)S(1)} %bitcast.5, bf16[2,1,16,4096]{3,2,1,0:T(8,128)(2,1)S(1)} %copy-done.2, bf16[2,1,16,4096]{3,2,1,0:T(8,128)(2,1)S(1)} %copy-done.1, bf16[4,2,1,16,4096]{4,3,2,1,0:T(8,128)(2,1)S(1)} %copy-done), custom_call_target="tpu_custom_call" | custom-call | flops 23000000 | bytes 1589248 | tf_op jit(solution)/shard_map/pallas_call | solution.py:438
  14.4 0.0 collective-permute-done.3.ahead
  14.5 0.0 collective-permute-done.2.other
  14.5 0.8 %shard_map.81.drive = f32[2,8,128]{2,1,0:T(8,128)S(1)} custom-call(f32[2,8,128]{2,1,0:T(8,128)S(1)} %shard_map.80.base, f32[2,8,128]{2,1,0:T(8,128)S(1)} %collective-permute-done.1.paired, f32[2,8,128]{2,1,0:T(8,128)S(1)} %collective-permute-done.2.other, f32[1,8,128]{2,1,0:T(8,128)S(1)} %collective-permute-done.3.ahead, ...), custom_call_target="tpu_custom_call" | custom-call | flops 1380000000 | bytes 1339392 | tf_op jit(solution)/shard_map/pallas_call | solution.py:438
  15.3 0.2 shard_map.83.rest_1_
  15.4 0.5 %shard_map.84 = (f32[2,8,128]{2,1,0:T(8,128)S(1)}, f32[8,8,128]{2,1,0:T(8,128)S(1)}) custom-call(f32[2,8,128]{2,1,0:T(8,128)S(1)} %shard_map.81.drive, f32[512,128]{1,0:T(8,128)S(1)} %get-tuple-element.30.step_maps, f32[512,128]{1,0:T(8,128)S(1)} %get-tuple-element.31.rest_0_, f32[512,128]{1,0:T(8,128)S(1)} %shard_map.83.rest_1_), custom_call_target="tpu_custom_call" | custom-call | flops 1150000000 | bytes 794624 | tf_op jit(solution)/shard_map/pallas_call | solution.py:438
  15.9 8.1 %all_to_all.10.got = f32[8,8,128]{2,1,0:T(8,128)S(1)} all-to-all(f32[8,8,128]{2,1,0:T(8,128)S(1)} %get-tuple-element.33), channel_id=1, replica_groups=mesh['gx'=8,'gy'=4] {'gx'}, dimensions={0} | all-to-all | bytes 65536 | tf_op jit(solution)/shard_map/all_to_all | solution.py:469
  24.0 1.1 %shard_map.85 = (f32[2,8,128]{2,1,0:T(8,128)}, f32[2,8,128]{2,1,0:T(8,128)S(1)}, f32[2,8,128]{2,1,0:T(8,128)S(1)}) custom-call(f32[8,8,128]{2,1,0:T(8,128)S(1)} %all_to_all.10.got, f32[2,8,128]{2,1,0:T(8,128)S(1)} %shard_map.81.drive, f32[2,8,128]{2,1,0:T(8,128)S(1)} %get-tuple-element.34.offsets, f32[1024,128]{1,0:T(8,128)S(1)} %get-tuple-element.35.entry_maps, ...), custom_call_target="tpu_custom_call" | custom-call | flops 1150000000 | bytes 1097728 | tf_op jit(solution)/shard_map/pallas_call | solution.py:438
  25.1 2.1 %collective-permute-start.8 = (f32[2,8,128]{2,1,0:T(8,128)S(1)}, f32[2,8,128]{2,1,0:T(8,128)S(1)}, u32[]{:S(2)}, u32[]{:S(2)}) collective-permute-start(f32[2,8,128]{2,1,0:T(8,128)S(1)} %get-tuple-element.38.vectors), channel_id=1, source_target_pairs={{0,1},{1,0},{2,3},{3,2},{4,5},{5,4},{6,7},{7,6},{8,9},{9,8},{10,11... | collective-permute-start | bytes 24584 | tf_op jit(solution)/shard_map/ppermute | solution.py:465
  27.2 1.3 %shard_map.87 = (f32[2,8,128]{2,1,0:T(8,128)S(1)}, f32[512,128]{1,0:T(8,128)S(1)}, f32[1024,128]{1,0:T(8,128)S(1)}, f32[512,128]{1,0:T(8,128)S(1)}, f32[512,128]{1,0:T(8,128)S(1)}) custom-call(f32[2,8,128]{2,1,0:T(8,128)S(1)} %get-tuple-element.37.base, f32[2,8,128]{2,1,0:T(8,128)S(1)} %get-tuple-element.38.vectors, f32[2,8,128]{2,1,0:T(8,128)S(1)} %bitcast.6, ...), custom_call_target="tpu_custom_call" | custom-call | flops 805000000 | bytes 2646016 | tf_op jit(solution)/shard_map/pallas_call | solution.py:438
  28.5 0.3 collective-permute-done.8.paired
  28.8 1.2 %shard_map.88 = (f32[2,8,128]{2,1,0:T(8,128)S(1)}, f32[8,8,128]{2,1,0:T(8,128)S(1)}) custom-call(f32[2,8,128]{2,1,0:T(8,128)S(1)} %get-tuple-element.41.base, f32[2,8,128]{2,1,0:T(8,128)S(1)} %collective-permute-done.8.paired, f32[2,8,128]{2,1,0:T(8,128)S(1)} %collective-permute-done.9.other, bf16[4,2,1,16,4096]{4,3,2,1,0:T(8,128)(2,1)S(1)} %copy-done, ...), custom_call_target="tpu_custom_call" | custom-call | flops 1724999936 | bytes 1859584 | tf_op jit(solution)/shard_map/pallas_call | solution.py:438
  30.0 7.2 %all_to_all.11.got = f32[8,8,128]{2,1,0:T(8,128)S(1)} all-to-all(f32[8,8,128]{2,1,0:T(8,128)S(1)} %get-tuple-element.45), channel_id=1, replica_groups=mesh['gx'=8,'gy'=4] {'gx'}, dimensions={0} | all-to-all | bytes 65536 | tf_op jit(solution)/shard_map/all_to_all | solution.py:469
  37.2 1.2 %shard_map.89 = f32[2,8,128]{2,1,0:T(8,128)} custom-call(f32[8,8,128]{2,1,0:T(8,128)S(1)} %all_to_all.11.got, f32[2,8,128]{2,1,0:T(8,128)S(1)} %get-tuple-element.46.offsets, f32[1024,128]{1,0:T(8,128)S(1)} %get-tuple-element.47.entry_maps, f32[512,128]{1,0:T(8,128)S(1)} %get-tuple-element.43.rest_0_, f32[512,128]{1,0:T(8,128)S(1)} %get-tuple-element.44.rest_1_), custom_call_target="tpu_custom_call" | custom-call | flops 1150000000 | bytes 1089536 | tf_op jit(solution)/shard_map/pallas_call | solution.py:438
  (16 shorter events, 0.0 us)
Async XLA Ops:
  0.6 2.8 %copy-start.1 = (bf16[2,1,16,4096]{3,2,1,0:T(8,128)(2,1)S(1)}, bf16[2,1,16,4096]{3,2,1,0:T(8,128)(2,1)}, u32[]{:S(2)}) copy-start(bf16[2,1,16,4096]{3,2,1,0:T(8,128)(2,1)} %upper.3) | copy-start | bytes 786436
  0.6 1.0 %copy-start.5 = (bf16[2,1,16,4096]{3,2,1,0:T(8,128)(2,1)S(1)}, bf16[2,1,16,4096]{3,2,1,0:T(8,128)(2,1)}, u32[]{:S(2)}) copy-start(bf16[2,1,16,4096]{3,2,1,0:T(8,128)(2,1)} %blocks.2) | copy-start | bytes 786436
  2.9 2.0 %collective-permute-start = (f32[512,128]{1,0:T(8,128)S(1)}, f32[512,128]{1,0:T(8,128)S(1)}, u32[]{:S(2)}, u32[]{:S(2)}) collective-permute-start(f32[512,128]{1,0:T(8,128)S(1)} %get-tuple-element.25.own), channel_id=1, source_target_pairs={{0,4},{4,0},{8,12},{12,8},{16,20},{20,16},{24,28},{28,24},{1,5},{5... | collective-permute-start | bytes 786440 | tf_op jit(solution)/shard_map/ppermute | solution.py:465
  3.5 1.4 %copy-start.3 = (f32[2,1,1024]{2,1,0:T(1,128)S(1)}, f32[2,1,1024]{2,1,0:T(1,128)}, u32[]{:S(2)}) copy-start(f32[2,1,1024]{2,1,0:T(1,128)} %param.6) | copy-start | bytes 24580
  4.8 6.9 %collective-permute-start.6 = (f32[512,128]{1,0:T(8,128)S(1)}, f32[512,128]{1,0:T(8,128)S(1)}, u32[]{:S(2)}, u32[]{:S(2)}) collective-permute-start(f32[512,128]{1,0:T(8,128)S(1)} %get-tuple-element.40.own), channel_id=1, source_target_pairs={{0,4},{4,0},{8,12},{12,8},{16,20},{20,16},{24,28},{28,24},{1,5},{5... | collective-permute-start | bytes 786440 | tf_op jit(solution)/shard_map/ppermute | solution.py:465
  5.3 7.8 %collective-permute-start.4 = (f32[256,128]{1,0:T(8,128)S(1)}, f32[256,128]{1,0:T(8,128)S(1)}, u32[]{:S(2)}, u32[]{:S(2)}) collective-permute-start(f32[256,128]{1,0:T(8,128)S(1)} %get-tuple-element.32), channel_id=1, source_target_pairs={{0,8},{4,12},{8,0},{12,4},{16,24},{20,28},{24,16},{28,20},{1,9},{5... | collective-permute-start | bytes 393224 | tf_op jit(solution)/shard_map/ppermute | solution.py:465
  8.2 4.9 %copy-start = (bf16[4,2,1,16,4096]{4,3,2,1,0:T(8,128)(2,1)S(1)}, bf16[4,2,1,16,4096]{4,3,2,1,0:T(8,128)(2,1)}, u32[]{:S(2)}) copy-start(bf16[4,2,1,16,4096]{4,3,2,1,0:T(8,128)(2,1)} %side.7) | copy-start | bytes 3145732
  8.2 6.2 %collective-permute-start.2 = (f32[2,8,128]{2,1,0:T(8,128)S(1)}, f32[2,8,128]{2,1,0:T(8,128)S(1)}, u32[]{:S(2)}, u32[]{:S(2)}) collective-permute-start(f32[2,8,128]{2,1,0:T(8,128)S(1)} %get-tuple-element.28.start), channel_id=1, source_target_pairs={{0,4},{1,2},{2,1},{3,7},{4,0},{5,6},{6,5},{7,3},{8,12},{9,10},{10,... | collective-permute-start | bytes 24584 | tf_op jit(solution)/shard_map/ppermute | solution.py:461
  8.2 6.2 %collective-permute-start.1 = (f32[2,8,128]{2,1,0:T(8,128)S(1)}, f32[2,8,128]{2,1,0:T(8,128)S(1)}, u32[]{:S(2)}, u32[]{:S(2)}) collective-permute-start(f32[2,8,128]{2,1,0:T(8,128)S(1)} %get-tuple-element.28.start), channel_id=1, source_target_pairs={{0,1},{1,0},{2,3},{3,2},{4,5},{5,4},{6,7},{7,6},{8,9},{9,8},{10,11... | collective-permute-start | bytes 24584 | tf_op jit(solution)/shard_map/ppermute | solution.py:465
  11.4 3.1 %collective-permute-start.3 = (f32[1,8,128]{2,1,0:T(8,128)S(1)}, f32[1,8,128]{2,1,0:T(8,128)S(1)}, u32[]{:S(2)}, u32[]{:S(2)}) collective-permute-start(f32[1,8,128]{2,1,0:T(8,128)S(1)} %slice.3), channel_id=1, source_target_pairs={{0,28},{4,0},{8,4},{12,8},{16,12},{20,16},{24,20},{28,24},{1,29},{... | collective-permute-start | bytes 12296 | tf_op jit(solution)/shard_map/ppermute | solution.py:533
  12.1 15.1 %collective-permute-start.7 = (f32[512,128]{1,0:T(8,128)S(1)}, f32[512,128]{1,0:T(8,128)S(1)}, u32[]{:S(2)}, u32[]{:S(2)}) collective-permute-start(f32[512,128]{1,0:T(8,128)S(1)} %shard_map.86), channel_id=1, source_target_pairs={{0,8},{4,12},{8,0},{12,4},{16,24},{20,28},{24,16},{28,20},{1,9},{5... | collective-permute-start | bytes 786440 | tf_op jit(solution)/shard_map/ppermute | solution.py:465
  12.7 0.9 %copy-start.2 = (bf16[2,1,16,4096]{3,2,1,0:T(8,128)(2,1)S(1)}, bf16[2,1,16,4096]{3,2,1,0:T(8,128)(2,1)}, u32[]{:S(2)}) copy-start(bf16[2,1,16,4096]{3,2,1,0:T(8,128)(2,1)} %diag.3) | copy-start | bytes 786436
  12.7 1.0 %copy-start.4 = (f32[2,1,1024]{2,1,0:T(1,128)S(1)}, f32[2,1,1024]{2,1,0:T(1,128)}, u32[]{:S(2)}) copy-start(f32[2,1,1024]{2,1,0:T(1,128)} %param.7) | copy-start | bytes 24580
  13.1 2.2 %collective-permute-start.5 = (f32[256,128]{1,0:T(8,128)S(1)}, f32[256,128]{1,0:T(8,128)S(1)}, u32[]{:S(2)}, u32[]{:S(2)}) collective-permute-start(f32[256,128]{1,0:T(8,128)S(1)} %collective-permute-done.4.mine), channel_id=1, source_target_pairs={{0,4},{4,0},{8,12},{12,8},{16,20},{20,16},{24,28},{28,24},{1,5},{5... | collective-permute-start | bytes 393224 | tf_op jit(solution)/shard_map/ppermute | solution.py:465
  25.1 3.4 %collective-permute-start.9 = (f32[2,8,128]{2,1,0:T(8,128)S(1)}, f32[2,8,128]{2,1,0:T(8,128)S(1)}, u32[]{:S(2)}, u32[]{:S(2)}) collective-permute-start(f32[2,8,128]{2,1,0:T(8,128)S(1)} %get-tuple-element.38.vectors), channel_id=1, source_target_pairs={{0,4},{1,2},{2,1},{3,7},{4,0},{5,6},{6,5},{7,3},{8,12},{9,10},{10,... | collective-permute-start | bytes 24584 | tf_op jit(solution)/shard_map/ppermute | solution.py:461
  25.1 3.7 %collective-permute-start.8 = (f32[2,8,128]{2,1,0:T(8,128)S(1)}, f32[2,8,128]{2,1,0:T(8,128)S(1)}, u32[]{:S(2)}, u32[]{:S(2)}) collective-permute-start(f32[2,8,128]{2,1,0:T(8,128)S(1)} %get-tuple-element.38.vectors), channel_id=1, source_target_pairs={{0,1},{1,0},{2,3},{3,2},{4,5},{5,4},{6,7},{7,6},{8,9},{9,8},{10,11... | collective-permute-start | bytes 24584 | tf_op jit(solution)/shard_map/ppermute | solution.py:465

commit v14 on v13

--- a/solution.py
+++ b/solution.py
@@ -310,10 +310,6 @@
     convert(pairs, refs[: len(refs) // 2], refs[len(refs) // 2 :], scratch)
 
 
-def far_kernel(pairs, mine, other, out, scratch):
-    diagonals(part_tiles(mine, other, pairs), out, 0, scratch, pairs)
-
-
 def outgoing(offset, partners, here, slots):
     vectors = [offset]
     for level, ref in enumerate(partners):
@@ -361,10 +357,12 @@
         drive[p] = base[p] - gather_pairs(apply(terms))
 
 
-def forward_offset_kernel(drive, step_maps, *rest):
-    *partners, offsets, slots = rest
-    planes = drive.shape[0]
-    size = drive.shape[1] * LANES // 2
+def forward_offset_kernel(levels, drive, step_maps, near, *rest):
+    parts, (offsets, slots, *far, scratch) = rest[: 2 * (levels - 2)], rest[2 * (levels - 2) :]
+    planes, pairs = drive.shape[:2]
+    size = pairs * LANES // 2
+    for level, ref in enumerate(far):
+        diagonals(part_tiles(*parts[2 * level : 2 * level + 2], pairs), ref, 0, scratch, pairs)
     previous = None
     for p in range(planes):
         fresh = drive[p]
@@ -372,7 +370,7 @@
             fresh = fresh - mapped(step_maps, previous, (p - 1) * size)
         offsets[p] = fresh
         previous = fresh
-    outgoing(previous, partners, lax.axis_index("gx"), slots)
+    outgoing(previous, [near, *far], lax.axis_index("gx"), slots)
 
 
 def forward_kernel(got, drive, offsets, entry_maps, *rest):
@@ -535,21 +533,17 @@
     step_maps, entry_maps, near = call(
         functools.partial(near_kernel, pairs), lower[:3], [steps, maps, whole], [whole], 0.1
     )
-    partners = [near]
-    for level in range(levels - 2):
-        partners += call(
-            functools.partial(far_kernel, pairs),
-            lower[3 + 2 * level : 5 + 2 * level],
-            [whole],
-            [whole],
-            0.1,
-        )
     (drive,) = call(
         drive_kernel, [base, paired, other, ahead, side_blocks, x_upper], [vec], [], 1.2
     )
-    offsets, sent = call(
-        forward_offset_kernel, [drive, step_maps] + partners, [vec, slots], [], 1.0
-    )
+    offsets, sent, *far = call(
+        functools.partial(forward_offset_kernel, levels),
+        [drive, step_maps, near] + lower[3:],
+        [vec, slots] + [whole] * (levels - 2),
+        [whole],
+        1.0,
+    )
+    partners = [near, *far]
     forward, copy, base = call(
         forward_kernel,
         [exchange(sent, "gx"), drive, offsets, entry_maps] + partners,

time: 38.6 us -> 38.5 us (level)
    pallas_call x13 -> x12, Pallas kernels: 10.7 us -> 10.6 us  [call(): pl.pallas_call(kernel, out_shape=outs, in_specs=[pl.BlockSpec(memory_spac...]
where the time goes in v14:
time: 38.5 us; the launch traced here: 38.2 us
  blocking collectives  15.3 us (40%)
  Pallas kernels  10.6 us (28%)
  starting transfers between devices  9.8 us (25%)
  local copies, waits for them, and re-layouts  1.47 us (4%)
  between operations  0.75 us (2%)
    all_to_all x2, blocking collectives, exchange(): return lax.all_to_all(slots, axis, 0, 0)  15.3 us
    pallas_call x12, Pallas kernels, call(): pl.pallas_call(kernel, out_shape=outs, in_specs=[pl.BlockSpec(memory_spac...  10.6 us
    ppermute x7, starting transfers between devices, crossed(): lax.ppermute(block, axis, [(i, i ^ distance) for i in range(lax.axis_size...  9.51 us
    unnamed x12, local copies, waits for them, and re-layouts  1.47 us
  transfers between devices with their start and end apart: 10, of which 1 were waited for; matrix products, arithmetic and copies ran while one was open for 0% of the time, Pallas kernels for 18%

profile of v14, /device:TPU:0, one launch (start us, length us, event | category | flops | bytes accessed | tf_op | source)
XLA Modules:
  0.0 38.2 jit_solution(12458877760488030867)
XLA Ops:
  0.6 1.0 %copy-done.5 = bf16[2,1,16,4096]{3,2,1,0:T(8,128)(2,1)S(1)} copy-done((bf16[2,1,16,4096]{3,2,1,0:T(8,128)(2,1)S(1)}, bf16[2,1,16,4096]{3,2,1,0:T(8,128)(2,1)}, u32[]{:S(2)}) %copy-start.5) | copy-done | bytes 262168
  1.6 1.3 %shard_map.77 = (f32[512,128]{1,0:T(8,128)S(1)}, f32[1024,128]{1,0:T(8,128)S(1)}, f32[512,128]{1,0:T(8,128)S(1)}) custom-call(bf16[2,1,16,4096]{3,2,1,0:T(8,128)(2,1)S(1)} %copy-done.5), custom_call_target="tpu_custom_call" | custom-call | flops 1150000000 | bytes 262144 | tf_op jit(solution)/shard_map/pallas_call | solution.py:436
  2.9 0.5 %collective-permute-start = (f32[512,128]{1,0:T(8,128)S(1)}, f32[512,128]{1,0:T(8,128)S(1)}, u32[]{:S(2)}, u32[]{:S(2)}) collective-permute-start(f32[512,128]{1,0:T(8,128)S(1)} %get-tuple-element.26.own), channel_id=1, source_target_pairs={{0,4},{4,0},{8,12},{12,8},{16,20},{20,16},{24,28},{28,24},{1,5},{5... | collective-permute-start | bytes 786440 | tf_op jit(solution)/shard_map/ppermute | solution.py:463
  3.5 1.3 %shard_map.78 = (f32[512,128]{1,0:T(8,128)S(1)}, f32[1024,128]{1,0:T(8,128)S(1)}, f32[512,128]{1,0:T(8,128)S(1)}) custom-call(bf16[2,1,16,4096]{3,2,1,0:T(8,128)(2,1)S(1)} %copy-done.1, f32[1024,128]{1,0:T(8,128)S(1)} %get-tuple-element.27.refs_0_.refs_1_), custom_call_target="tpu_custom_call" | custom-call | flops 1150000000 | bytes 786432 | tf_op jit(solution)/shard_map/pallas_call | solution.py:436
  4.8 0.1 collective-permute-start.6
  4.9 0.0 collective-permute-done.refs_2_
  4.9 0.4 shard_map.79
  5.3 3.0 %collective-permute-start.4 = (f32[256,128]{1,0:T(8,128)S(1)}, f32[256,128]{1,0:T(8,128)S(1)}, u32[]{:S(2)}, u32[]{:S(2)}) collective-permute-start(f32[256,128]{1,0:T(8,128)S(1)} %get-tuple-element.33), channel_id=1, source_target_pairs={{0,8},{4,12},{8,0},{12,4},{16,24},{20,28},{24,16},{28,20},{1,9},{5... | collective-permute-start | bytes 393224 | tf_op jit(solution)/shard_map/ppermute | solution.py:463
  8.2 0.0 collective-permute-start.2
  8.2 3.1 %collective-permute-start.1 = (f32[2,8,128]{2,1,0:T(8,128)S(1)}, f32[2,8,128]{2,1,0:T(8,128)S(1)}, u32[]{:S(2)}, u32[]{:S(2)}) collective-permute-start(f32[2,8,128]{2,1,0:T(8,128)S(1)} %get-tuple-element.29.start), channel_id=1, source_target_pairs={{0,1},{1,0},{2,3},{3,2},{4,5},{5,4},{6,7},{7,6},{8,9},{9,8},{10,11... | collective-permute-start | bytes 24584 | tf_op jit(solution)/shard_map/ppermute | solution.py:463
  11.4 0.3 collective-permute-start.3
  11.7 0.0 collective-permute-done.6.refs_1_.rest_2_
  11.7 0.4 %shard_map.85 = f32[512,128]{1,0:T(8,128)S(1)} custom-call(f32[512,128]{1,0:T(8,128)S(1)} %get-tuple-element.42.own, f32[1024,128]{1,0:T(8,128)S(1)} %get-tuple-element.28.refs_0_.rest_1_, f32[512,128]{1,0:T(8,128)S(1)} %collective-permute-done.6.refs_1_.rest_2_), custom_call_target="tpu_custom_call" | custom-call | flops 23000000 | bytes 1048576 | tf_op jit(solution)/shard_map/pallas_call | solution.py:436
  12.1 0.6 %collective-permute-start.7 = (f32[512,128]{1,0:T(8,128)S(1)}, f32[512,128]{1,0:T(8,128)S(1)}, u32[]{:S(2)}, u32[]{:S(2)}) collective-permute-start(f32[512,128]{1,0:T(8,128)S(1)} %shard_map.85), channel_id=1, source_target_pairs={{0,8},{4,12},{8,0},{12,4},{16,24},{20,28},{24,16},{28,20},{1,9},{5... | collective-permute-start | bytes 786440 | tf_op jit(solution)/shard_map/ppermute | solution.py:463
  12.7 0.4 shard_map.82
  13.1 0.0 collective-permute-done.4.rest_0_
  13.1 0.1 collective-permute-start.5
  13.2 0.5 %copy-done.2 = bf16[2,1,16,4096]{3,2,1,0:T(8,128)(2,1)S(1)} copy-done((bf16[2,1,16,4096]{3,2,1,0:T(8,128)(2,1)S(1)}, bf16[2,1,16,4096]{3,2,1,0:T(8,128)(2,1)}, u32[]{:S(2)}) %copy-start.2) | copy-done | bytes 262168
  13.6 0.8 %shard_map.80.base = f32[2,8,128]{2,1,0:T(8,128)S(1)} custom-call(f32[2,8,128]{2,1,0:T(8,128)S(1)} %get-tuple-element.29.start, f32[2,8,128]{2,1,0:T(8,128)S(1)} %bitcast.5, bf16[2,1,16,4096]{3,2,1,0:T(8,128)(2,1)S(1)} %copy-done.2, bf16[2,1,16,4096]{3,2,1,0:T(8,128)(2,1)S(1)} %copy-done.1, bf16[4,2,1,16,4096]{4,3,2,1,0:T(8,128)(2,1)S(1)} %copy-done), custom_call_target="tpu_custom_call" | custom-call | flops 23000000 | bytes 1589248 | tf_op jit(solution)/shard_map/pallas_call | solution.py:436
  14.4 0.0 collective-permute-done.3.ahead
  14.5 0.8 %shard_map.81.drive = f32[2,8,128]{2,1,0:T(8,128)S(1)} custom-call(f32[2,8,128]{2,1,0:T(8,128)S(1)} %shard_map.80.base, f32[2,8,128]{2,1,0:T(8,128)S(1)} %collective-permute-done.1.paired, f32[2,8,128]{2,1,0:T(8,128)S(1)} %collective-permute-done.2.other, f32[1,8,128]{2,1,0:T(8,128)S(1)} %collective-permute-done.3.ahead, ...), custom_call_target="tpu_custom_call" | custom-call | flops 1380000000 | bytes 1339392 | tf_op jit(solution)/shard_map/pallas_call | solution.py:436
  15.3 0.0 collective-permute-done.5.rest_1_
  15.3 0.5 %shard_map.83 = (f32[2,8,128]{2,1,0:T(8,128)S(1)}, f32[8,8,128]{2,1,0:T(8,128)S(1)}, f32[512,128]{1,0:T(8,128)S(1)}) custom-call(f32[2,8,128]{2,1,0:T(8,128)S(1)} %shard_map.81.drive, f32[512,128]{1,0:T(8,128)S(1)} %get-tuple-element.31.step_maps, f32[512,128]{1,0:T(8,128)S(1)} %get-tuple-element.32.near.rest_0_, ...), custom_call_target="tpu_custom_call" | custom-call | flops 1150000000 | bytes 794624 | tf_op jit(solution)/shard_map/pallas_call | solution.py:436
  15.7 8.1 %all_to_all.10.got = f32[8,8,128]{2,1,0:T(8,128)S(1)} all-to-all(f32[8,8,128]{2,1,0:T(8,128)S(1)} %get-tuple-element.34), channel_id=1, replica_groups=mesh['gx'=8,'gy'=4] {'gx'}, dimensions={0} | all-to-all | bytes 65536 | tf_op jit(solution)/shard_map/all_to_all | solution.py:467
  23.8 1.1 %shard_map.84 = (f32[2,8,128]{2,1,0:T(8,128)}, f32[2,8,128]{2,1,0:T(8,128)S(1)}, f32[2,8,128]{2,1,0:T(8,128)S(1)}) custom-call(f32[8,8,128]{2,1,0:T(8,128)S(1)} %all_to_all.10.got, f32[2,8,128]{2,1,0:T(8,128)S(1)} %shard_map.81.drive, f32[2,8,128]{2,1,0:T(8,128)S(1)} %get-tuple-element.35.offsets, f32[1024,128]{1,0:T(8,128)S(1)} %get-tuple-element.36.entry_maps, ...), custom_call_target="tpu_custom_call" | custom-call | flops 1150000000 | bytes 1097728 | tf_op jit(solution)/shard_map/pallas_call | solution.py:436
  25.0 0.0 collective-permute-start.9
  25.0 2.1 %collective-permute-start.8 = (f32[2,8,128]{2,1,0:T(8,128)S(1)}, f32[2,8,128]{2,1,0:T(8,128)S(1)}, u32[]{:S(2)}, u32[]{:S(2)}) collective-permute-start(f32[2,8,128]{2,1,0:T(8,128)S(1)} %get-tuple-element.40.vectors), channel_id=1, source_target_pairs={{0,1},{1,0},{2,3},{3,2},{4,5},{5,4},{6,7},{7,6},{8,9},{9,8},{10,11... | collective-permute-start | bytes 24584 | tf_op jit(solution)/shard_map/ppermute | solution.py:463
  27.1 1.3 %shard_map.86 = (f32[2,8,128]{2,1,0:T(8,128)S(1)}, f32[512,128]{1,0:T(8,128)S(1)}, f32[1024,128]{1,0:T(8,128)S(1)}, f32[512,128]{1,0:T(8,128)S(1)}, f32[512,128]{1,0:T(8,128)S(1)}) custom-call(f32[2,8,128]{2,1,0:T(8,128)S(1)} %get-tuple-element.39.base, f32[2,8,128]{2,1,0:T(8,128)S(1)} %get-tuple-element.40.vectors, f32[2,8,128]{2,1,0:T(8,128)S(1)} %bitcast.6, ...), custom_call_target="tpu_custom_call" | custom-call | flops 805000000 | bytes 2646016 | tf_op jit(solution)/shard_map/pallas_call | solution.py:436
  28.3 0.3 collective-permute-done.8.paired
  28.7 1.2 %shard_map.87 = (f32[2,8,128]{2,1,0:T(8,128)S(1)}, f32[8,8,128]{2,1,0:T(8,128)S(1)}) custom-call(f32[2,8,128]{2,1,0:T(8,128)S(1)} %get-tuple-element.43.base, f32[2,8,128]{2,1,0:T(8,128)S(1)} %collective-permute-done.8.paired, f32[2,8,128]{2,1,0:T(8,128)S(1)} %collective-permute-done.9.other, bf16[4,2,1,16,4096]{4,3,2,1,0:T(8,128)(2,1)S(1)} %copy-done, ...), custom_call_target="tpu_custom_call" | custom-call | flops 1724999936 | bytes 1859584 | tf_op jit(solution)/shard_map/pallas_call | solution.py:436
  29.9 7.2 %all_to_all.11.got = f32[8,8,128]{2,1,0:T(8,128)S(1)} all-to-all(f32[8,8,128]{2,1,0:T(8,128)S(1)} %get-tuple-element.47), channel_id=1, replica_groups=mesh['gx'=8,'gy'=4] {'gx'}, dimensions={0} | all-to-all | bytes 65536 | tf_op jit(solution)/shard_map/all_to_all | solution.py:467
  37.1 1.2 %shard_map.88 = f32[2,8,128]{2,1,0:T(8,128)} custom-call(f32[8,8,128]{2,1,0:T(8,128)S(1)} %all_to_all.11.got, f32[2,8,128]{2,1,0:T(8,128)S(1)} %get-tuple-element.48.offsets, f32[1024,128]{1,0:T(8,128)S(1)} %get-tuple-element.49.entry_maps, f32[512,128]{1,0:T(8,128)S(1)} %get-tuple-element.45.rest_0_, f32[512,128]{1,0:T(8,128)S(1)} %get-tuple-element.46.rest_1_), custom_call_target="tpu_custom_call" | custom-call | flops 1150000000 | bytes 1089536 | tf_op jit(solution)/shard_map/pallas_call | solution.py:436
  (15 shorter events, 0.0 us)
Async XLA Ops:
  0.6 2.8 %copy-start.1 = (bf16[2,1,16,4096]{3,2,1,0:T(8,128)(2,1)S(1)}, bf16[2,1,16,4096]{3,2,1,0:T(8,128)(2,1)}, u32[]{:S(2)}) copy-start(bf16[2,1,16,4096]{3,2,1,0:T(8,128)(2,1)} %upper.3) | copy-start | bytes 786436
  0.6 1.0 %copy-start.5 = (bf16[2,1,16,4096]{3,2,1,0:T(8,128)(2,1)S(1)}, bf16[2,1,16,4096]{3,2,1,0:T(8,128)(2,1)}, u32[]{:S(2)}) copy-start(bf16[2,1,16,4096]{3,2,1,0:T(8,128)(2,1)} %blocks.2) | copy-start | bytes 786436
  2.9 2.0 %collective-permute-start = (f32[512,128]{1,0:T(8,128)S(1)}, f32[512,128]{1,0:T(8,128)S(1)}, u32[]{:S(2)}, u32[]{:S(2)}) collective-permute-start(f32[512,128]{1,0:T(8,128)S(1)} %get-tuple-element.26.own), channel_id=1, source_target_pairs={{0,4},{4,0},{8,12},{12,8},{16,20},{20,16},{24,28},{28,24},{1,5},{5... | collective-permute-start | bytes 786440 | tf_op jit(solution)/shard_map/ppermute | solution.py:463
  3.5 1.4 %copy-start.3 = (f32[2,1,1024]{2,1,0:T(1,128)S(1)}, f32[2,1,1024]{2,1,0:T(1,128)}, u32[]{:S(2)}) copy-start(f32[2,1,1024]{2,1,0:T(1,128)} %param.6) | copy-start | bytes 24580
  4.8 6.9 %collective-permute-start.6 = (f32[512,128]{1,0:T(8,128)S(1)}, f32[512,128]{1,0:T(8,128)S(1)}, u32[]{:S(2)}, u32[]{:S(2)}) collective-permute-start(f32[512,128]{1,0:T(8,128)S(1)} %get-tuple-element.42.own), channel_id=1, source_target_pairs={{0,4},{4,0},{8,12},{12,8},{16,20},{20,16},{24,28},{28,24},{1,5},{5... | collective-permute-start | bytes 786440 | tf_op jit(solution)/shard_map/ppermute | solution.py:463
  5.3 7.8 %collective-permute-start.4 = (f32[256,128]{1,0:T(8,128)S(1)}, f32[256,128]{1,0:T(8,128)S(1)}, u32[]{:S(2)}, u32[]{:S(2)}) collective-permute-start(f32[256,128]{1,0:T(8,128)S(1)} %get-tuple-element.33), channel_id=1, source_target_pairs={{0,8},{4,12},{8,0},{12,4},{16,24},{20,28},{24,16},{28,20},{1,9},{5... | collective-permute-start | bytes 393224 | tf_op jit(solution)/shard_map/ppermute | solution.py:463
  8.2 4.9 %copy-start = (bf16[4,2,1,16,4096]{4,3,2,1,0:T(8,128)(2,1)S(1)}, bf16[4,2,1,16,4096]{4,3,2,1,0:T(8,128)(2,1)}, u32[]{:S(2)}) copy-start(bf16[4,2,1,16,4096]{4,3,2,1,0:T(8,128)(2,1)} %side.7) | copy-start | bytes 3145732
  8.2 6.2 %collective-permute-start.2 = (f32[2,8,128]{2,1,0:T(8,128)S(1)}, f32[2,8,128]{2,1,0:T(8,128)S(1)}, u32[]{:S(2)}, u32[]{:S(2)}) collective-permute-start(f32[2,8,128]{2,1,0:T(8,128)S(1)} %get-tuple-element.29.start), channel_id=1, source_target_pairs={{0,4},{1,2},{2,1},{3,7},{4,0},{5,6},{6,5},{7,3},{8,12},{9,10},{10,... | collective-permute-start | bytes 24584 | tf_op jit(solution)/shard_map/ppermute | solution.py:459
  8.2 6.2 %collective-permute-start.1 = (f32[2,8,128]{2,1,0:T(8,128)S(1)}, f32[2,8,128]{2,1,0:T(8,128)S(1)}, u32[]{:S(2)}, u32[]{:S(2)}) collective-permute-start(f32[2,8,128]{2,1,0:T(8,128)S(1)} %get-tuple-element.29.start), channel_id=1, source_target_pairs={{0,1},{1,0},{2,3},{3,2},{4,5},{5,4},{6,7},{7,6},{8,9},{9,8},{10,11... | collective-permute-start | bytes 24584 | tf_op jit(solution)/shard_map/ppermute | solution.py:463
  11.4 3.1 %collective-permute-start.3 = (f32[1,8,128]{2,1,0:T(8,128)S(1)}, f32[1,8,128]{2,1,0:T(8,128)S(1)}, u32[]{:S(2)}, u32[]{:S(2)}) collective-permute-start(f32[1,8,128]{2,1,0:T(8,128)S(1)} %slice.3), channel_id=1, source_target_pairs={{0,28},{4,0},{8,4},{12,8},{16,12},{20,16},{24,20},{28,24},{1,29},{... | collective-permute-start | bytes 12296 | tf_op jit(solution)/shard_map/ppermute | solution.py:531
  12.1 15.0 %collective-permute-start.7 = (f32[512,128]{1,0:T(8,128)S(1)}, f32[512,128]{1,0:T(8,128)S(1)}, u32[]{:S(2)}, u32[]{:S(2)}) collective-permute-start(f32[512,128]{1,0:T(8,128)S(1)} %shard_map.85), channel_id=1, source_target_pairs={{0,8},{4,12},{8,0},{12,4},{16,24},{20,28},{24,16},{28,20},{1,9},{5... | collective-permute-start | bytes 786440 | tf_op jit(solution)/shard_map/ppermute | solution.py:463
  12.7 0.9 %copy-start.2 = (bf16[2,1,16,4096]{3,2,1,0:T(8,128)(2,1)S(1)}, bf16[2,1,16,4096]{3,2,1,0:T(8,128)(2,1)}, u32[]{:S(2)}) copy-start(bf16[2,1,16,4096]{3,2,1,0:T(8,128)(2,1)} %diag.3) | copy-start | bytes 786436
  12.7 1.0 %copy-start.4 = (f32[2,1,1024]{2,1,0:T(1,128)S(1)}, f32[2,1,1024]{2,1,0:T(1,128)}, u32[]{:S(2)}) copy-start(f32[2,1,1024]{2,1,0:T(1,128)} %param.7) | copy-start | bytes 24580
  13.1 2.2 %collective-permute-start.5 = (f32[256,128]{1,0:T(8,128)S(1)}, f32[256,128]{1,0:T(8,128)S(1)}, u32[]{:S(2)}, u32[]{:S(2)}) collective-permute-start(f32[256,128]{1,0:T(8,128)S(1)} %collective-permute-done.4.rest_0_), channel_id=1, source_target_pairs={{0,4},{4,0},{8,12},{12,8},{16,20},{20,16},{24,28},{28,24},{1,5},{5... | collective-permute-start | bytes 393224 | tf_op jit(solution)/shard_map/ppermute | solution.py:463
  25.0 3.4 %collective-permute-start.9 = (f32[2,8,128]{2,1,0:T(8,128)S(1)}, f32[2,8,128]{2,1,0:T(8,128)S(1)}, u32[]{:S(2)}, u32[]{:S(2)}) collective-permute-start(f32[2,8,128]{2,1,0:T(8,128)S(1)} %get-tuple-element.40.vectors), channel_id=1, source_target_pairs={{0,4},{1,2},{2,1},{3,7},{4,0},{5,6},{6,5},{7,3},{8,12},{9,10},{10,... | collective-permute-start | bytes 24584 | tf_op jit(solution)/shard_map/ppermute | solution.py:459
  25.0 3.7 %collective-permute-start.8 = (f32[2,8,128]{2,1,0:T(8,128)S(1)}, f32[2,8,128]{2,1,0:T(8,128)S(1)}, u32[]{:S(2)}, u32[]{:S(2)}) collective-permute-start(f32[2,8,128]{2,1,0:T(8,128)S(1)} %get-tuple-element.40.vectors), channel_id=1, source_target_pairs={{0,1},{1,0},{2,3},{3,2},{4,5},{5,4},{6,7},{7,6},{8,9},{9,8},{10,11... | collective-permute-start | bytes 24584 | tf_op jit(solution)/shard_map/ppermute | solution.py:463
